TPU v7x, 32 devices: a whole 2x2x4 slice. The times are simulated.
32 devices in a mesh: row: 8 (over y, x, core), col: 4 (over z).
Axes of the slice: x: 2, y: 2, z: 4, core: 2. Of those that a mesh axis runs over, the one named last changes fastest.
Arguments:
- ortho_in: bfloat16 [7168, 9216], P(('row', 'col')), may hold values from -6 to 6
Outputs:
- next_iterate: bfloat16 [7168, 9216], P(('row', 'col'))
All inputs are finite; a program needn't handle non-finite values.
Results may differ from a plain program's by a relative error of at most 0.024.
Values may be sent and summed in bfloat16 or wider, within the bound.
No kernel may reach another device: no remote copies, remote signals or barrier semaphores. Data moves between devices by JAX's collectives and lax.ppermute only.
A program may use at most 128 MiB of HBM per device.

v0:
```python
import math

import jax
import jax.numpy as jnp
from jax import lax
from jax.sharding import PartitionSpec as P

coef_a = 3.4445
coef_b = -4.775
coef_c = 2.0315


def per_device(ortho_in):
    tile = lax.all_to_all(ortho_in, "col", split_axis=1, concat_axis=0, tiled=True)
    tile_rows = tile.shape[0]
    tile_cols = tile.shape[1]
    full_rows = tile_rows * lax.axis_size("row")
    full_cols = tile_cols * lax.axis_size("col")
    inv_square = 1.0 / (math.sqrt(full_rows) + math.sqrt(full_cols)) ** 2
    panel = lax.all_gather(tile, "row", axis=0, tiled=True)
    partial_gram = lax.dot_general(
        tile, panel, (((1,), (1,)), ((), ())), preferred_element_type=jnp.float32
    )
    gram_total = lax.psum(partial_gram.astype(jnp.bfloat16), "col").astype(jnp.float32)
    gram = (gram_total * inv_square).astype(jnp.bfloat16)
    first_f = jnp.dot(gram, panel, preferred_element_type=jnp.float32)
    first_prod = first_f.astype(jnp.bfloat16)
    second_prod = jnp.dot(
        gram,
        lax.all_gather(first_prod, "row", axis=0, tiled=True),
        preferred_element_type=jnp.float32,
    )
    iterate = (
        coef_a * tile.astype(jnp.float32)
        + coef_b * first_prod.astype(jnp.float32)
        + coef_c * second_prod
    )
    result_tile = iterate.astype(jnp.bfloat16)
    return lax.all_to_all(result_tile, "col", split_axis=0, concat_axis=1, tiled=True)


def solution(mesh):
    in_specs = (P(("row", "col"), None),)
    out_specs = P(("row", "col"), None)
    return jax.shard_map(
        per_device, mesh=mesh, in_specs=in_specs, out_specs=out_specs, check_vma=False
    )
```

profile of v0, /device:TPU:0, one launch (start us, length us, event | category | flops | bytes accessed | tf_op | source)
XLA Modules:
  0.0 1080.5 jit_solution(1276086312446231835)
XLA Ops:
  6.5 0.0 all-gather.3.cloned.1.call-start
  6.5 2.4 copy.7
  9.0 98.0 %all_to_all.38 = bf16[224,4,2304]{2,0,1:T(8,128)(2,1)} all-to-all(bf16[224,4,2304]{2,0,1:T(8,128)(2,1)S(1)} %bitcast.19), channel_id=1, replica_groups=mesh['row'=8,'col'=4] {'col'}, dimensions={1} | all-to-all | bytes 8257536 | tf_op jit(solution)/shard_map/all_to_all | solution.py:14
  106.9 0.0 all-gather.3.cloned.1.call-update
  107.0 0.0 all-reduce.2.cloned.1.call-start
  107.0 158.1 %all-gather.3.cloned.1.call-done = bf16[7168,2304]{1,0:T(8,128)(2,1)} async-done(((bf16[896,2304]{1,0:T(8,128)(2,1)}), bf16[7168,2304]{1,0:T(8,128)(2,1)}) %all-gather.3.cloned.1.call-update) | async-done | bytes 33030160 | tf_op jit(solution)/shard_map/all_gather | solution.py:20
  265.1 36.9 %convolution_convert_fusion = bf16[896,7168]{1,0:T(8,128)(2,1)} fusion(bf16[896,2304]{1,0:T(8,128)(2,1)} %bitcast.16, bf16[7168,2304]{1,0:T(8,128)(2,1)} %all-gather.3.cloned.1.call-done), kind=kOutput, calls=%fused_computation.1 | convolution fusion | flops 29601431552 | bytes 50003968 | tf_op jit(solution)/shard_map/dot_general | solution.py:21
  301.9 0.0 all-reduce.2.cloned.1.call-update
  302.0 0.0 all-gather.5.cloned.1.call-start
  302.0 434.7 %all-reduce.2.cloned.1.call-done = bf16[896,7168]{1,0:T(8,128)(2,1)} async-done(((bf16[896,7168]{1,0:T(8,128)(2,1)}), bf16[896,7168]{1,0:T(8,128)(2,1)}) %all-reduce.2.cloned.1.call-update) | async-done | bytes 12845072 | tf_op jit(solution)/shard_map/psum | solution.py:24
  736.7 39.3 %fusion.2 = bf16[896,2304]{1,0:T(8,128)(2,1)} fusion(bf16[7168,2304]{1,0:T(8,128)(2,1)} %all-gather.3.cloned.1.call-done, bf16[896,7168]{1,0:T(8,128)(2,1)} %all-reduce.2.cloned.1.call-done), kind=kOutput, calls=%fused_computation.5 | convolution fusion | flops 29616340992 | bytes 50003968 | tf_op jit(solution)/shard_map/dot_general | solution.py:26
  776.0 0.0 all-gather.5.cloned.1.call-update
  776.0 157.7 %all-gather.5.cloned.1.call-done = bf16[7168,2304]{1,0:T(8,128)(2,1)} async-done(((bf16[896,2304]{1,0:T(8,128)(2,1)}), bf16[7168,2304]{1,0:T(8,128)(2,1)}) %all-gather.5.cloned.1.call-update) | async-done | bytes 33030160 | tf_op jit(solution)/shard_map/all_gather | solution.py:30
  933.7 41.1 %add_convert_fusion = bf16[896,2304]{1,0:T(8,128)(2,1)} fusion(bf16[896,2304]{1,0:T(8,128)(2,1)} %fusion.2, bf16[896,2304]{1,0:T(8,128)(2,1)} %bitcast.17, bf16[7168,2304]{1,0:T(8,128)(2,1)} %all-gather.5.cloned.1.call-done, bf16[896,7168]{1,0:T(8,128)(2,1)} %all-reduce.2.cloned.1.call-done), kind=kOutput, calls=%fused_computation.4 | convolution fusion | flops 29630791680 | bytes 58261504 | tf_op jit(solution)/shard_map/dot_general | solution.py:28
  974.8 96.8 %all_to_all.39 = bf16[4,224,2304]{2,1,0:T(8,128)(2,1)S(1)} all-to-all(bf16[4,224,2304]{2,1,0:T(8,128)(2,1)} %bitcast.21), channel_id=1, replica_groups=mesh['row'=8,'col'=4] {'col'}, dimensions={0} | all-to-all | bytes 8257536 | tf_op jit(solution)/shard_map/all_to_all | solution.py:39
  1071.5 2.5 copy.5
Async XLA Ops:
  6.5 258.5 %all-gather.3.cloned.1.call-start = ((), (), s32[]{:S(2)}) async-start(), calls=%async_computation.2 | async-start | bytes 37158912 | tf_op jit(solution)/shard_map/all_gather | solution.py:20
  107.0 629.7 %all-reduce.2.cloned.1.call-start = ((), (), s32[]{:S(2)}) async-start(), calls=%async_computation.3 | async-start | bytes 25690112 | tf_op jit(solution)/shard_map/psum | solution.py:24
  302.0 631.7 %all-gather.5.cloned.1.call-start = ((), (), s32[]{:S(2)}) async-start(), calls=%async_computation.4 | async-start | bytes 37158912 | tf_op jit(solution)/shard_map/all_gather | solution.py:30
Sparse Core Ops, SparseCore 0:
  107.1 157.9 all-gather.2
  302.1 434.5 all-reduce.1
  776.1 157.5 all-gather.4
where the time goes:
time: 1080 us
  waiting for transfers between devices  750 us (69%)
  blocking collectives  195 us (18%)
  matrix products  117 us (11%)
  between operations  13.1 us (1%)
    psum x1, waiting for transfers between devices, per_device(): lax.psum(partial_gram.astype(jnp.bfloat16), 'col').astype(jnp.float32)  435 us
    all_gather x1, waiting for transfers between devices, per_device(): panel = lax.all_gather(tile, 'row', axis=0, tiled=True)  158 us
    all_gather x1, waiting for transfers between devices, per_device(): lax.all_gather(first_prod, 'row', axis=0, tiled=True)  158 us
    all_to_all x1, blocking collectives, per_device(): lax.all_to_all(ortho_in, 'col', split_axis=1, concat_axis=0, tiled=True)  98 us
    all_to_all x1, blocking collectives, per_device(): lax.all_to_all(result_tile, 'col', split_axis=0, concat_axis=1, tiled=True)  96.8 us
    dot_general x1, matrix products, per_device(): jnp.dot(gram, lax.all_gather(first_prod, 'row', axis=0, tiled=True), pref...  41.1 us
    dot_general x1, matrix products, per_device(): first_f = jnp.dot(gram, panel, preferred_element_type=jnp.float32)  39.3 us
    dot_general x1, matrix products, per_device(): lax.dot_general(tile, panel, (((1,), (1,)), ((), ())), preferred_element_...  36.9 us
  transfers between devices with their start and end apart: 3, of which 3 were waited for; matrix products, arithmetic and copies ran while one was open for 0% of the time, Pallas kernels for 0%

commit v1 on v0

v1 whole, which is shorter than its diff:
```python
import functools
import math

import jax
import jax.numpy as jnp
from jax import lax
from jax.experimental import pallas as pl
from jax.experimental.pallas import tpu as pltpu
from jax.sharding import PartitionSpec as P

coef_a = 3.4445
coef_b = -4.775
coef_c = 2.0315
bf16 = jnp.bfloat16
f32 = jnp.float32
VMEM_BYTES = 48 * 1024 * 1024


def widths_of(width, count):
    unit = 256 if width % 256 == 0 else 128
    base, extra = divmod(width // unit, count)
    return [unit * (base + (i >= count - extra)) for i in range(count)]


def dot_t(a, b):
    return lax.dot_general(a, b, (((1,), (1,)), ((), ())), preferred_element_type=f32)


def after(value, *others):
    return lax.optimization_barrier((value, *others))[0]


def swap(value, bit):
    count = lax.axis_size("row")
    return lax.ppermute(value, "row", [(r, r ^ bit) for r in range(count)])


def gather_chips(own):
    count = lax.axis_size("row")
    bit_x, bit_y = count // 4, count // 2
    h = own.shape[0] // 2
    corner = bit_x | bit_y
    parts = {(0, 0): own}
    parts[(bit_x, 0)] = swap(own, bit_x)
    parts[(bit_y, 0)] = swap(own, bit_y)
    from_x, from_y = lax.optimization_barrier((parts[(bit_x, 0)], parts[(bit_y, 0)]))
    upper, lower = lax.optimization_barrier((from_x[:h], from_y[h:]))
    parts[(corner, 0)] = swap(upper, bit_y)
    parts[(corner, h)] = swap(lower, bit_x)
    return parts, (upper, lower)


def add_cores(parts, hold=None):
    bit_x = lax.axis_size("row") // 4
    parts = dict(parts)
    bit = 1
    while bit < bit_x:
        for j, offset in list(parts):
            if (j | bit, offset) not in parts:
                part = parts[(j, offset)]
                if hold is not None:
                    part = after(part, hold)
                parts[(j | bit, offset)] = swap(part, bit)
        bit *= 2
    return parts


def whole_block(parts, j):
    pieces = [parts[key] for key in sorted(parts) if key[0] == j]
    return pieces[0] if len(pieces) == 1 else jnp.concatenate(pieces, axis=0)


def pair_kernel(count, low_ref, *refs):
    own, peer, out = refs[:count], refs[count : 2 * count], refs[2 * count]
    h = out.shape[0]

    def product(left, right, first):
        total = None
        for a, b in zip(left, right):
            term = dot_t(a[first : first + h, :], b[...])
            total = term if total is None else total + term
        out[...] = total.astype(bf16)

    @pl.when(low_ref[0] == 1)
    def _():
        product(own, peer, 0)

    @pl.when(low_ref[0] == 0)
    def _():
        product(peer, own, h)


def pair_piece(low, own, peer):
    size = own[0].shape[0]
    flops = size * size * sum(o.shape[1] for o in own)
    return pl.pallas_call(
        functools.partial(pair_kernel, len(own)),
        out_shape=jax.ShapeDtypeStruct((size // 2, size), bf16),
        in_specs=[pl.BlockSpec(memory_space=pltpu.SMEM)]
        + [pl.BlockSpec(memory_space=pltpu.VMEM)] * (2 * len(own)),
        out_specs=pl.BlockSpec(memory_space=pltpu.VMEM),
        cost_estimate=pl.CostEstimate(
            flops=flops, bytes_accessed=4 * flops // size, transcendentals=0
        ),
        compiler_params=pltpu.CompilerParams(vmem_limit_bytes=VMEM_BYTES),
    )(low, *own, *peer)


def block_kernel(low_ref, mine, theirs, gram_in, out):
    h = mine.shape[0]

    @pl.when(low_ref[0] == 1)
    def _():
        out[:h, :] = mine[...]
        out[h:, :] = theirs[...]

    @pl.when(low_ref[0] == 0)
    def _():
        out[...] = jnp.concatenate([theirs[...], mine[...]], axis=0).T


def put_block(gram, low, mine, theirs, j):
    h, size = mine.shape
    return pl.pallas_call(
        block_kernel,
        grid=(1,),
        out_shape=jax.ShapeDtypeStruct(gram.shape, bf16),
        in_specs=[
            pl.BlockSpec(memory_space=pltpu.SMEM),
            pl.BlockSpec((h, size), lambda i: (0, 0)),
            pl.BlockSpec((h, size), lambda i: (0, 0)),
            pl.BlockSpec(memory_space=pl.ANY),
        ],
        out_specs=pl.BlockSpec((None, size, size), lambda i: (j, 0, 0)),
        input_output_aliases={3: 0},
        cost_estimate=pl.CostEstimate(
            flops=0, bytes_accessed=4 * size * size, transcendentals=0
        ),
        compiler_params=pltpu.CompilerParams(vmem_limit_bytes=VMEM_BYTES),
    )(low, mine, theirs, gram)


def product_kernel(keys, start, finish, *refs):
    gram, parts = refs[0], refs[1 : 1 + len(keys)]
    extra = refs[1 + len(keys) : -5]
    out, gbuf, xbuf, acc, sems = refs[-5:]
    count, size, width = xbuf.shape
    h = size // 2

    def piece(j, part):
        return xbuf.at[j, pl.ds(part * h, h)], sems.at[j, part]

    copies = []
    for j in range(count):
        copies.append(pltpu.make_async_copy(gram.at[j], gbuf.at[j], sems.at[j, 2]))
        for part in range(2):
            key = (j, part * h) if (j, part * h) in keys else (j, 0)
            first = part * h - key[1]
            source = parts[keys.index(key)].at[pl.ds(first, h), pl.ds(start, width)]
            copies.append(pltpu.make_async_copy(source, *piece(j, part)))
    for copy in copies:
        copy.start()
    acc[...] = jnp.zeros_like(acc)

    @pl.loop(0, count)
    def _(j):
        pltpu.make_async_copy(gbuf.at[j], gbuf.at[j], sems.at[j, 2]).wait()
        for part in range(2):
            there, sem = piece(j, part)
            pltpu.make_async_copy(there, there, sem).wait()
        acc[...] += jnp.dot(gbuf[j], xbuf[j], preferred_element_type=f32)

    if finish:
        tile, first = extra
        out[...] = (
            coef_a * tile[...].astype(f32)
            + coef_b * first[...].astype(f32)
            + coef_c * acc[...]
        ).astype(bf16)
    else:
        out[...] = acc[...].astype(bf16)


def product(gram, parts, start, width, extra=()):
    count, size, _ = gram.shape
    keys = sorted(parts)
    flops = 2 * count * size * size * width
    return pl.pallas_call(
        functools.partial(product_kernel, keys, start, bool(extra)),
        out_shape=jax.ShapeDtypeStruct((size, width), bf16),
        in_specs=[pl.BlockSpec(memory_space=pl.ANY)] * (1 + len(keys))
        + [pl.BlockSpec(memory_space=pltpu.VMEM)] * len(extra),
        out_specs=pl.BlockSpec(memory_space=pltpu.VMEM),
        scratch_shapes=[
            pltpu.VMEM((count, size, size), bf16),
            pltpu.VMEM((count, size, width), bf16),
            pltpu.VMEM((size, width), f32),
            pltpu.SemaphoreType.DMA((count, 3)),
        ],
        cost_estimate=pl.CostEstimate(
            flops=flops,
            bytes_accessed=2 * count * size * (size + width),
            transcendentals=0,
        ),
        compiler_params=pltpu.CompilerParams(vmem_limit_bytes=VMEM_BYTES),
    )(gram, *[parts[key] for key in keys], *extra)


def sum_on_line(piece, scale, arrivals, depth):
    count = lax.axis_size("col")
    me = lax.axis_index("col")
    half = count // 2

    def send(stage, value, pairs):
        done = arrivals.setdefault(stage, [])
        if len(done) >= depth:
            value = after(value, done[-depth])
        arrived = lax.ppermute(value, "col", pairs)
        done.append(arrived)
        return arrived

    for s in range(half - 1):
        pairs = [(s, s + 1), (count - 1 - s, count - 2 - s)]
        arrived = send(s, piece, pairs)
        piece = (piece.astype(f32) + arrived.astype(f32)).astype(bf16)
    arrived = send(half - 1, piece, [(half - 1, half), (half, half - 1)])
    total = ((piece.astype(f32) + arrived.astype(f32)) * scale).astype(bf16)
    for s in range(half - 2, -1, -1):
        pairs = [(s + 1, s), (count - 2 - s, count - 1 - s)]
        arrived = send(2 * half - 2 - s, total, pairs)
        total = jnp.where((me == s) | (me == count - 1 - s), arrived, total)
    return total


def per_device(ortho_in):
    rows, cols = ortho_in.shape
    n_row = lax.axis_size("row")
    n_col = lax.axis_size("col")
    me = lax.axis_index("row")
    block = rows * n_col
    width = cols // n_col
    scale = 1.0 / (math.sqrt(block * n_row) + math.sqrt(cols)) ** 2
    h = block // 2
    bit_x, bit_y = n_row // 4, n_row // 2
    cores = range(1, bit_x)
    chips = (bit_x, bit_y, bit_x | bit_y)

    def exchange(value):
        return lax.all_to_all(value, "col", split_axis=0, concat_axis=0, tiled=True)

    tiles, gathered, siblings = [], [], []
    start = 0
    thirds = widths_of(width, 3)
    for w in (thirds[0], thirds[1] + thirds[2]):
        first = [start + c * width for c in range(n_col)]
        tile = exchange(jnp.concatenate([ortho_in[:, f : f + w] for f in first], axis=0))
        tiles.append(tile)
        parts, tied = gather_chips(tile)
        gathered.append(parts)
        siblings.append(add_cores({(0, 0): tile}))
        start += w

    arrivals = {}

    def low_of(j):
        return ((me & (1 << (j.bit_length() - 1))) == 0).astype(jnp.int32).reshape(1)

    own_sums = []
    for part in range(2):
        total = sum(dot_t(t[part * h : (part + 1) * h], t) for t in tiles)
        own_sums.append(sum_on_line(total.astype(bf16), scale, arrivals, 1))
    pieces = {}
    for j in cores:
        piece = pair_piece(low_of(j), tiles, [s[(j, 0)] for s in siblings])
        pieces[j, 0] = sum_on_line(piece, scale, arrivals, 1)
    for j in chips:
        peers = [whole_block(parts, j) for parts in gathered]
        if j != chips[-1]:
            peers[0] = after(peers[0], *tied)
        for i in range(bit_x):
            left = [s[(i, 0)] for s in siblings]
            piece = pair_piece(low_of(j), left, peers)
            pieces[j, i] = sum_on_line(piece, scale, arrivals, 2)
    gram = jnp.zeros((n_row, block, block), bf16)
    for (j, i), mine in pieces.items():
        if j not in chips:
            gram = put_block(gram, low_of(j), mine, swap(mine, j), j)
            continue
        theirs = swap(mine, j)
        if i > 0:
            mine = swap(mine, i)
        gram = put_block(gram, low_of(j), mine, theirs, j | i)
    for part in range(2):
        gram = lax.dynamic_update_slice(gram, own_sums[part][None], (0, part * h, 0))
    panels = [
        add_cores({**parts, **sibling}, pieces[chips[-1], 0])
        for parts, sibling in zip(gathered, siblings)
    ]

    outs = [[] for _ in range(n_col)]
    hold = []
    for k, w in enumerate(thirds):
        source, start = (0, 0) if k == 0 else (1, 0 if k == 1 else thirds[1])
        parts = dict(panels[source])
        if hold:
            parts[(0, 0)] = after(parts[(0, 0)], *hold)
        first = product(gram, parts, start, w)
        first_parts = add_cores(gather_chips(first)[0])
        tile = tiles[source][:, start : start + w]
        result = product(gram, first_parts, 0, w, (tile, first))
        hold = [first_parts[(bit_x, 0)]] + ([] if k == 0 else [last])
        last = result
        back = exchange(result)
        for c in range(n_col):
            outs[c].append(back[c * rows : (c + 1) * rows])
    return jnp.concatenate([piece for out in outs for piece in out], axis=1)


def solution(mesh):
    in_specs = (P(("row", "col"), None),)
    out_specs = P(("row", "col"), None)
    return jax.shard_map(
        per_device, mesh=mesh, in_specs=in_specs, out_specs=out_specs, check_vma=False
    )
```

time: 1080 us -> 810 us (0.75)
  waiting for transfers between devices: 750 us -> 453 us
  blocking collectives: 195 us -> 0 us
  Pallas kernels: 0 us -> 144 us
  starting transfers between devices: 0.09 us -> 114 us
  matrix products: 117 us -> 8.72 us
  local copies, waits for them, and re-layouts: 4.92 us -> 54.8 us
  other arithmetic: 0 us -> 23.8 us
  between operations: 13.1 us -> 1.25 us
    psum x1 -> x0, waiting for transfers between devices: 435 us -> none  [per_device(): lax.psum(partial_gram.astype(jnp.bfloat16), 'col').astype(jnp.float32)]
    ppermute x0 -> x82, waiting for transfers between devices: none -> 316 us  [the longest x55 186 us: swap(): return lax.ppermute(value, 'row', [(r, r ^ bit) for r in range(count)])]
    all_gather x2 -> x0, waiting for transfers between devices: 316 us -> none  [the longest x1 158 us: per_device(): panel = lax.all_gather(tile, 'row', axis=0, tiled=True)]
    all_to_all x2 -> x0, blocking collectives: 195 us -> none  [the longest x1 98 us: per_device(): lax.all_to_all(ortho_in, 'col', split_axis=1, concat_axis=0, tiled=True)]
    pallas_call x0 -> x20, Pallas kernels: none -> 144 us  [the longest x6 97.2 us: product(): pl.pallas_call(functools.partial(product_kernel, keys, start, bool(extra)...]
    all_to_all x0 -> x5, waiting for transfers between devices: none -> 137 us  [exchange(): return lax.all_to_all(value, 'col', split_axis=0, concat_axis=0, tiled=True)]
    dot_general x3 -> x4, matrix products: 117 us -> 8.72 us  [dot_t(): lax.dot_general(a, b, (((1,), (1,)), ((), ())), preferred_element_type=f32)]
    ppermute x0 -> x82, starting transfers between devices: none -> 91 us  [the longest x27 56.1 us: send(): arrived = lax.ppermute(value, 'col', pairs)]
  transfers between devices with their start and end apart: 3 -> 87, of which waited for: 3 -> 29; matrix products, arithmetic and copies ran while one was open for 0% -> 8% of each run, Pallas kernels for 0% -> 16%
where the time goes in v1:
time: 810 us; the launch traced here: 800 us
  waiting for transfers between devices  453 us (56%)
  Pallas kernels  144 us (18%)
  starting transfers between devices  114 us (14%)
  local copies, waits for them, and re-layouts  54.8 us (7%)
  other arithmetic  23.8 us (3%)
  matrix products  8.72 us (1%)
    ppermute x55, waiting for transfers between devices, swap(): return lax.ppermute(value, 'row', [(r, r ^ bit) for r in range(count)])  186 us
    all_to_all x5, waiting for transfers between devices, exchange(): return lax.all_to_all(value, 'col', split_axis=0, concat_axis=0, tiled=True)  137 us
    ppermute x27, waiting for transfers between devices, send(): arrived = lax.ppermute(value, 'col', pairs)  130 us
    pallas_call x6, Pallas kernels, product(): pl.pallas_call(functools.partial(product_kernel, keys, start, bool(extra)...  97.2 us
    ppermute x27, starting transfers between devices, send(): arrived = lax.ppermute(value, 'col', pairs)  56.1 us
    pallas_call x7, Pallas kernels, pair_piece(): pl.pallas_call(functools.partial(pair_kernel, len(own)), out_shape=jax.Sh...  35.8 us
    ppermute x55, starting transfers between devices, swap(): return lax.ppermute(value, 'row', [(r, r ^ bit) for r in range(count)])  34.9 us
    unnamed x91, local copies, waits for them, and re-layouts  25.2 us
  transfers between devices with their start and end apart: 87, of which 29 were waited for; matrix products, arithmetic and copies ran while one was open for 8% of the time, Pallas kernels for 16%

profile of v1, /device:TPU:0, one launch (start us, length us, event | category | flops | bytes accessed | tf_op | source)
XLA Modules:
  0.0 800.0 jit_solution(2963608708716009835)
XLA Ops:
  2.6 6.3 all-to-all-start
  8.9 1.9 fusion.12
  12.4 29.2 %all-to-all-done = bf16[4,224,768]{2,1,0:T(8,128)(2,1)S(1)} async-done(((bf16[4,224,768]{2,1,0:T(8,128)(2,1)}), bf16[4,224,768]{2,1,0:T(8,128)(2,1)S(1)}, u32[]{:S(2)}, u32[]{:S(2)}) %all-to-all-start) | async-done | bytes 1376288 | tf_op jit(solution)/shard_map/all_to_all | solution.py:249
  41.6 4.6 all-to-all-start.1
  47.3 60.8 %all-to-all-done.1 = bf16[4,224,1536]{2,1,0:T(8,128)(2,1)} async-done(((bf16[4,224,1536]{2,1,0:T(8,128)(2,1)}), bf16[4,224,1536]{2,1,0:T(8,128)(2,1)}, u32[]{:S(2)}, u32[]{:S(2)}) %all-to-all-start.1) | async-done | bytes 2752544 | tf_op jit(solution)/shard_map/all_to_all | solution.py:249
  108.0 1.9 fusion.15
  110.0 3.5 fusion.18
  119.4 12.9 %collective-permute-done.10 = bf16[448,896]{1,0:T(8,128)(2,1)S(1)} collective-permute-done((bf16[448,896]{1,0:T(8,128)(2,1)S(1)}, bf16[448,896]{1,0:T(8,128)(2,1)S(1)}, u32[]{:S(2)}, u32[]{:S(2)}) %collective-permute-start.10) | collective-permute-done | bytes 802848 | tf_op jit(solution)/shard_map/ppermute | solution.py:218
  133.8 3.4 fusion.17
  138.2 10.7 %collective-permute-done.2.refs_2_.refs_3_ = bf16[896,768]{1,0:T(8,128)(2,1)S(1)} collective-permute-done((bf16[896,768]{1,0:T(8,128)(2,1)S(1)}, bf16[896,768]{1,0:T(8,128)(2,1)S(1)}, u32[]{:S(2)}, u32[]{:S(2)}) %collective-permute-start.2) | collective-permute-done | bytes 1376288 | tf_op jit(solution)/shard_map/ppermute | solution.py:35
  152.4 11.6 %collective-permute-done.11 = bf16[448,896]{1,0:T(8,128)(2,1)S(1)} collective-permute-done((bf16[448,896]{1,0:T(8,128)(2,1)S(1)}, bf16[448,896]{1,0:T(8,128)(2,1)S(1)}, u32[]{:S(2)}, u32[]{:S(2)}) %collective-permute-start.11) | collective-permute-done | bytes 802848 | tf_op jit(solution)/shard_map/ppermute | solution.py:218
  168.1 53.9 %collective-permute-done.4.refs_7_ = bf16[448,768]{1,0:T(8,128)(2,1)} collective-permute-done((bf16[448,768]{1,0:T(8,128)(2,1)S(1)}, bf16[448,768]{1,0:T(8,128)(2,1)}, u32[]{:S(2)}, u32[]{:S(2)}) %collective-permute-start.4) | collective-permute-done | bytes 688160 | tf_op jit(solution)/shard_map/ppermute | solution.py:35
  227.4 4.9 shard_map.20
  232.4 6.4 collective-permute-start.12
  240.2 2.5 slice.167
  244.2 2.5 multiply_convert_fusion.4
  248.6 5.1 shard_map.23
  253.7 6.3 collective-permute-start.30
  260.0 4.9 shard_map.19
  264.9 5.4 shard_map.22
  270.3 5.4 shard_map.18
  275.7 2.2 add_convert_fusion.5
  282.4 4.1 collective-permute-start.13
  286.5 2.2 collective-permute-start.31
  290.4 5.1 shard_map.21
  295.5 4.9 shard_map.17
  305.9 10.0 %collective-permute-done.31 = bf16[448,896]{1,0:T(8,128)(2,1)} collective-permute-done((bf16[448,896]{1,0:T(8,128)(2,1)S(1)}, bf16[448,896]{1,0:T(8,128)(2,1)}, u32[]{:S(2)}, u32[]{:S(2)}) %collective-permute-start.31) | collective-permute-done | bytes 802848 | tf_op jit(solution)/shard_map/ppermute | solution.py:218
  320.6 6.1 collective-permute-start.14
  330.1 7.3 collective-permute-done.36
  338.7 6.3 collective-permute-done.14
  345.0 6.3 collective-permute-start.15
  351.5 10.7 %collective-permute-done.32 = bf16[448,896]{1,0:T(8,128)(2,1)S(1)} collective-permute-done((bf16[448,896]{1,0:T(8,128)(2,1)S(1)}, bf16[448,896]{1,0:T(8,128)(2,1)S(1)}, u32[]{:S(2)}, u32[]{:S(2)}) %collective-permute-start.32) | collective-permute-done | bytes 802848 | tf_op jit(solution)/shard_map/ppermute | solution.py:218
  363.2 9.8 %collective-permute-done.15 = bf16[448,896]{1,0:T(8,128)(2,1)S(1)} collective-permute-done((bf16[448,896]{1,0:T(8,128)(2,1)S(1)}, bf16[448,896]{1,0:T(8,128)(2,1)S(1)}, u32[]{:S(2)}, u32[]{:S(2)}) %collective-permute-start.15) | collective-permute-done | bytes 802848 | tf_op jit(solution)/shard_map/ppermute | solution.py:218
  381.1 17.9 %collective-permute-done.26 = bf16[448,896]{1,0:T(8,128)(2,1)S(1)} collective-permute-done((bf16[448,896]{1,0:T(8,128)(2,1)S(1)}, bf16[448,896]{1,0:T(8,128)(2,1)S(1)}, u32[]{:S(2)}, u32[]{:S(2)}) %collective-permute-start.26) | collective-permute-done | bytes 802848 | tf_op jit(solution)/shard_map/ppermute | solution.py:218
  402.9 30.3 %collective-permute-done.38 = bf16[448,896]{1,0:T(8,128)(2,1)S(1)} collective-permute-done((bf16[448,896]{1,0:T(8,128)(2,1)S(1)}, bf16[448,896]{1,0:T(8,128)(2,1)S(1)}, u32[]{:S(2)}, u32[]{:S(2)}) %collective-permute-start.38) | collective-permute-done | bytes 802848 | tf_op jit(solution)/shard_map/ppermute | solution.py:218
  434.0 10.9 %collective-permute-done.27 = bf16[448,896]{1,0:T(8,128)(2,1)S(1)} collective-permute-done((bf16[448,896]{1,0:T(8,128)(2,1)S(1)}, bf16[448,896]{1,0:T(8,128)(2,1)S(1)}, u32[]{:S(2)}, u32[]{:S(2)}) %collective-permute-start.27) | collective-permute-done | bytes 802848 | tf_op jit(solution)/shard_map/ppermute | solution.py:218
  450.8 20.4 %collective-permute-done.41.theirs = bf16[448,896]{1,0:T(8,128)(2,1)S(1)} collective-permute-done((bf16[448,896]{1,0:T(8,128)(2,1)S(1)}, bf16[448,896]{1,0:T(8,128)(2,1)S(1)}, u32[]{:S(2)}, u32[]{:S(2)}) %collective-permute-start.41) | collective-permute-done | bytes 802848 | tf_op jit(solution)/shard_map/ppermute | solution.py:35
  475.9 6.3 broadcast_in_dim.9.gram_in
  494.0 2.7 shard_map.30
  496.7 2.2 bitcast_dynamic-update-slice_fusion.1
  498.9 2.2 bitcast_dynamic-update-slice_fusion.refs_0_
  501.2 14.7 %shard_map.31.refs_1_.refs_12_ = bf16[896,768]{1,0:T(8,128)(2,1)S(1)} custom-call(bf16[8,896,896]{2,1,0:T(8,128)(2,1)} %bitcast_dynamic-update-slice_fusion.refs_0_, bf16[896,768]{1,0:T(8,128)(2,1)S(1)} %bitcast.83, bf16[896,768]{1,0:T(8,128)(2,1)} %copy-done.1, bf16[896,768]{1,0:T(8,128)(2,1)} %copy-done.2, ...), custom_call_target="tpu_custom_call" | custom-call | flops 9865003008 | bytes 23855104 | tf_op jit(solution)/shard_map/pallas_call | solution.py:188
  518.1 30.2 %collective-permute-done.52.refs_3_ = bf16[896,768]{1,0:T(8,128)(2,1)S(1)} collective-permute-done((bf16[896,768]{1,0:T(8,128)(2,1)S(1)}, bf16[896,768]{1,0:T(8,128)(2,1)S(1)}, u32[]{:S(2)}, u32[]{:S(2)}) %collective-permute-start.52) | collective-permute-done | bytes 1376288 | tf_op jit(solution)/shard_map/ppermute | solution.py:35
  553.9 12.4 %collective-permute-done.56.refs_7_ = bf16[448,768]{1,0:T(8,128)(2,1)S(1)} collective-permute-done((bf16[448,768]{1,0:T(8,128)(2,1)S(1)}, bf16[448,768]{1,0:T(8,128)(2,1)S(1)}, u32[]{:S(2)}, u32[]{:S(2)}) %collective-permute-start.56) | collective-permute-done | bytes 688160 | tf_op jit(solution)/shard_map/ppermute | solution.py:35
  567.6 14.9 %shard_map.33.refs_1_.refs_12_ = bf16[896,768]{1,0:T(8,128)(2,1)S(1)} custom-call(bf16[8,896,896]{2,1,0:T(8,128)(2,1)} %bitcast_dynamic-update-slice_fusion.refs_0_, bf16[896,1536]{1,0:T(8,128)(2,1)} %bitcast.4.refs_1_, bf16[896,1536]{1,0:T(8,128)(2,1)} %collective-permute-done.1.refs_1_.refs_3_.refs_2_, bf16[896,1536]{1,0:T(8,128)(2,1)} %collective-permute-done.6.refs_3_, ...), custom_call_target="tpu_custom_call" | custom-call | flops 9865003008 | bytes 23855104 | tf_op jit(solution)/shard_map/pallas_call | solution.py:188
  584.3 17.7 %shard_map.32 = bf16[896,768]{1,0:T(8,128)(2,1)} custom-call(bf16[8,896,896]{2,1,0:T(8,128)(2,1)} %bitcast_dynamic-update-slice_fusion.refs_0_, bf16[896,768]{1,0:T(8,128)(2,1)S(1)} %shard_map.31.refs_1_.refs_12_, bf16[896,768]{1,0:T(8,128)(2,1)} %collective-permute-done.51.refs_2_, bf16[896,768]{1,0:T(8,128)(2,1)} %copy-done.34, ...), custom_call_target="tpu_custom_call" | custom-call | flops 9865003008 | bytes 23855104 | tf_op jit(solution)/shard_map/pallas_call | solution.py:188
  602.1 13.2 %collective-permute-done.65.refs_3_ = bf16[896,768]{1,0:T(8,128)(2,1)} collective-permute-done((bf16[896,768]{1,0:T(8,128)(2,1)S(1)}, bf16[896,768]{1,0:T(8,128)(2,1)}, u32[]{:S(2)}, u32[]{:S(2)}) %collective-permute-start.65) | collective-permute-done | bytes 1376288 | tf_op jit(solution)/shard_map/ppermute | solution.py:35
  615.3 14.9 %shard_map.35.refs_1_.refs_12_ = bf16[896,768]{1,0:T(8,128)(2,1)S(1)} custom-call(bf16[8,896,896]{2,1,0:T(8,128)(2,1)} %bitcast_dynamic-update-slice_fusion.refs_0_, bf16[896,1536]{1,0:T(8,128)(2,1)} %bitcast.4.refs_1_, bf16[896,1536]{1,0:T(8,128)(2,1)} %collective-permute-done.1.refs_1_.refs_3_.refs_2_, bf16[896,1536]{1,0:T(8,128)(2,1)} %collective-permute-done.6.refs_3_, ...), custom_call_target="tpu_custom_call" | custom-call | flops 9865003008 | bytes 23855104 | tf_op jit(solution)/shard_map/pallas_call | solution.py:188
  636.7 40.8 %collective-permute-done.69.refs_7_ = bf16[448,768]{1,0:T(8,128)(2,1)S(1)} collective-permute-done((bf16[448,768]{1,0:T(8,128)(2,1)S(1)}, bf16[448,768]{1,0:T(8,128)(2,1)S(1)}, u32[]{:S(2)}, u32[]{:S(2)}) %collective-permute-start.69) | collective-permute-done | bytes 688160 | tf_op jit(solution)/shard_map/ppermute | solution.py:35
  678.0 5.4 all-to-all-start.2
  683.9 3.5 fusion.14
  687.5 2.0 slice.185
  689.5 2.0 slice.186
  693.8 17.5 %shard_map.34 = bf16[896,768]{1,0:T(8,128)(2,1)} custom-call(bf16[8,896,896]{2,1,0:T(8,128)(2,1)} %bitcast_dynamic-update-slice_fusion.refs_0_, bf16[896,768]{1,0:T(8,128)(2,1)S(1)} %shard_map.33.refs_1_.refs_12_, bf16[896,768]{1,0:T(8,128)(2,1)} %collective-permute-done.64.refs_2_, bf16[896,768]{1,0:T(8,128)(2,1)} %collective-permute-done.65.refs_3_, ...), custom_call_target="tpu_custom_call" | custom-call | flops 9865003008 | bytes 23855104 | tf_op jit(solution)/shard_map/pallas_call | solution.py:188
  711.3 5.7 all-to-all-done.2
  717.0 3.5 all-to-all-start.3
  721.2 1.8 collective-permute-done.80.refs_9_
  724.0 17.5 %shard_map.36 = bf16[896,768]{1,0:T(8,128)(2,1)} custom-call(bf16[8,896,896]{2,1,0:T(8,128)(2,1)} %bitcast_dynamic-update-slice_fusion.refs_0_, bf16[896,768]{1,0:T(8,128)(2,1)S(1)} %shard_map.35.refs_1_.refs_12_, bf16[896,768]{1,0:T(8,128)(2,1)} %collective-permute-done.73.refs_2_, bf16[896,768]{1,0:T(8,128)(2,1)} %collective-permute-done.74.refs_3_, ...), custom_call_target="tpu_custom_call" | custom-call | flops 9865003008 | bytes 23855104 | tf_op jit(solution)/shard_map/pallas_call | solution.py:188
  741.5 12.0 %all-to-all-done.3 = bf16[4,224,768]{2,1,0:T(8,128)(2,1)S(1)} async-done(((bf16[4,224,768]{2,1,0:T(8,128)(2,1)}), bf16[4,224,768]{2,1,0:T(8,128)(2,1)S(1)}, u32[]{:S(2)}, u32[]{:S(2)}) %all-to-all-start.3) | async-done | bytes 1376288 | tf_op jit(solution)/shard_map/all_to_all | solution.py:249
  753.5 3.5 all-to-all-start.4
  757.1 1.7 fusion.11
  759.6 29.8 %all-to-all-done.4 = bf16[4,224,768]{2,1,0:T(8,128)(2,1)S(1)} async-done(((bf16[4,224,768]{2,1,0:T(8,128)(2,1)}), bf16[4,224,768]{2,1,0:T(8,128)(2,1)S(1)}, u32[]{:S(2)}, u32[]{:S(2)}) %all-to-all-start.4) | async-done | bytes 1376288 | tf_op jit(solution)/shard_map/all_to_all | solution.py:249
  790.1 1.7 fusion.8
  793.3 1.7 fusion.5
  (273 shorter events, 118.5 us)
Async XLA Ops:
  2.6 39.1 %all-to-all-start = ((bf16[4,224,768]{2,1,0:T(8,128)(2,1)}), bf16[4,224,768]{2,1,0:T(8,128)(2,1)S(1)}, u32[]{:S(2)}, u32[]{:S(2)}) async-start(bf16[4,224,768]{2,1,0:T(8,128)(2,1)} %bitcast.1), calls=%async_computation | async-start | bytes 2752512 | tf_op jit(solution)/shard_map/all_to_all | solution.py:249
  41.6 66.4 %all-to-all-start.1 = ((bf16[4,224,1536]{2,1,0:T(8,128)(2,1)}), bf16[4,224,1536]{2,1,0:T(8,128)(2,1)}, u32[]{:S(2)}, u32[]{:S(2)}) async-start(bf16[4,224,1536]{2,1,0:T(8,128)(2,1)} %bitcast.85), calls=%async_computation.1 | async-start | bytes 5505024 | tf_op jit(solution)/shard_map/all_to_all | solution.py:249
  46.2 72.6 %collective-permute-start = (bf16[896,768]{1,0:T(8,128)(2,1)S(1)}, bf16[896,768]{1,0:T(8,128)(2,1)S(1)}, u32[]{:S(2)}, u32[]{:S(2)}) collective-permute-start(bf16[896,768]{1,0:T(8,128)(2,1)S(1)} %bitcast.74), channel_id=1, source_target_pairs={{0,4},{4,0},{8,12},{12,8},{16,20},{20,16},{24,28},{28,24},{1,5},{5... | collective-permute-start | bytes 4128776 | tf_op jit(solution)/shard_map/ppermute | solution.py:35
  115.7 33.2 %collective-permute-start.2 = (bf16[896,768]{1,0:T(8,128)(2,1)S(1)}, bf16[896,768]{1,0:T(8,128)(2,1)S(1)}, u32[]{:S(2)}, u32[]{:S(2)}) collective-permute-start(bf16[896,768]{1,0:T(8,128)(2,1)S(1)} %bitcast.76), channel_id=1, source_target_pairs={{0,8},{4,12},{8,0},{12,4},{16,24},{20,28},{24,16},{28,20},{1,9},{5... | collective-permute-start | bytes 4128776 | tf_op jit(solution)/shard_map/ppermute | solution.py:35
  117.3 33.2 %collective-permute-start.3 = (bf16[896,768]{1,0:T(8,128)(2,1)S(1)}, bf16[896,768]{1,0:T(8,128)(2,1)}, u32[]{:S(2)}, u32[]{:S(2)}) collective-permute-start(bf16[896,768]{1,0:T(8,128)(2,1)S(1)} %bitcast.77), channel_id=1, source_target_pairs={{0,16},{4,20},{8,24},{12,28},{16,0},{20,4},{24,8},{28,12},{1,17},{... | collective-permute-start | bytes 4128776 | tf_op jit(solution)/shard_map/ppermute | solution.py:35
  118.8 108.6 %collective-permute-start.1 = (bf16[896,1536]{1,0:T(8,128)(2,1)}, bf16[896,1536]{1,0:T(8,128)(2,1)}, u32[]{:S(2)}, u32[]{:S(2)}) collective-permute-start(bf16[896,1536]{1,0:T(8,128)(2,1)} %bitcast.4.refs_1_), channel_id=1, source_target_pairs={{0,4},{4,0},{8,12},{12,8},{16,20},{20,16},{24,28},{28,24},{1,5},{5... | collective-permute-start | bytes 8257544 | tf_op jit(solution)/shard_map/ppermute | solution.py:35
  118.8 119.9 %collective-permute-start.6 = (bf16[896,1536]{1,0:T(8,128)(2,1)}, bf16[896,1536]{1,0:T(8,128)(2,1)}, u32[]{:S(2)}, u32[]{:S(2)}) collective-permute-start(bf16[896,1536]{1,0:T(8,128)(2,1)} %bitcast.4.refs_1_), channel_id=1, source_target_pairs={{0,8},{4,12},{8,0},{12,4},{16,24},{20,28},{24,16},{28,20},{1,9},{5... | collective-permute-start | bytes 8257544 | tf_op jit(solution)/shard_map/ppermute | solution.py:35
  132.3 106.4 %collective-permute-start.7 = (bf16[896,1536]{1,0:T(8,128)(2,1)}, bf16[896,1536]{1,0:T(8,128)(2,1)}, u32[]{:S(2)}, u32[]{:S(2)}) collective-permute-start(bf16[896,1536]{1,0:T(8,128)(2,1)} %bitcast.4.refs_1_), channel_id=1, source_target_pairs={{0,16},{4,20},{8,24},{12,28},{16,0},{20,4},{24,8},{28,12},{1,17},{... | collective-permute-start | bytes 8257544 | tf_op jit(solution)/shard_map/ppermute | solution.py:35
  164.0 57.9 %collective-permute-start.4 = (bf16[448,768]{1,0:T(8,128)(2,1)S(1)}, bf16[448,768]{1,0:T(8,128)(2,1)}, u32[]{:S(2)}, u32[]{:S(2)}) collective-permute-start(bf16[448,768]{1,0:T(8,128)(2,1)S(1)} %slice.164), channel_id=1, source_target_pairs={{0,16},{4,20},{8,24},{12,28},{16,0},{20,4},{24,8},{28,12},{1,17},{... | collective-permute-start | bytes 2064392 | tf_op jit(solution)/shard_map/ppermute | solution.py:35
  165.5 58.2 %collective-permute-start.5 = (bf16[448,768]{1,0:T(8,128)(2,1)S(1)}, bf16[448,768]{1,0:T(8,128)(2,1)}, u32[]{:S(2)}, u32[]{:S(2)}) collective-permute-start(bf16[448,768]{1,0:T(8,128)(2,1)S(1)} %slice.165), channel_id=1, source_target_pairs={{0,8},{4,12},{8,0},{12,4},{16,24},{20,28},{24,16},{28,20},{1,9},{5... | collective-permute-start | bytes 2064392 | tf_op jit(solution)/shard_map/ppermute | solution.py:35
  223.8 22.9 %collective-permute-start.22 = (bf16[448,896]{1,0:T(8,128)(2,1)S(1)}, bf16[448,896]{1,0:T(8,128)(2,1)}, u32[]{:S(2)}, u32[]{:S(2)}) collective-permute-start(bf16[448,896]{1,0:T(8,128)(2,1)S(1)} %multiply_convert_fusion.3), channel_id=1, source_target_pairs={{1,0},{2,3},{5,4},{6,7},{9,8},{10,11},{13,12},{14,15},{17,16},{18,... | collective-permute-start | bytes 2408456 | tf_op jit(solution)/shard_map/ppermute | solution.py:218
  232.4 43.3 %collective-permute-start.12 = (bf16[448,896]{1,0:T(8,128)(2,1)S(1)}, bf16[448,896]{1,0:T(8,128)(2,1)}, u32[]{:S(2)}, u32[]{:S(2)}) collective-permute-start(bf16[448,896]{1,0:T(8,128)(2,1)S(1)} %shard_map.20), channel_id=1, source_target_pairs={{0,1},{3,2},{4,5},{7,6},{8,9},{11,10},{12,13},{15,14},{16,17},{19,... | collective-permute-start | bytes 2408456 | tf_op jit(solution)/shard_map/ppermute | solution.py:218
  242.7 39.7 %collective-permute-start.8 = (bf16[448,1536]{1,0:T(8,128)(2,1)S(1)}, bf16[448,1536]{1,0:T(8,128)(2,1)S(1)}, u32[]{:S(2)}, u32[]{:S(2)}) collective-permute-start(bf16[448,1536]{1,0:T(8,128)(2,1)S(1)} %slice.166), channel_id=1, source_target_pairs={{0,16},{4,20},{8,24},{12,28},{16,0},{20,4},{24,8},{28,12},{1,17},{... | collective-permute-start | bytes 4128776 | tf_op jit(solution)/shard_map/ppermute | solution.py:35
  246.7 55.4 %collective-permute-start.23 = (bf16[448,896]{1,0:T(8,128)(2,1)}, bf16[448,896]{1,0:T(8,128)(2,1)}, u32[]{:S(2)}, u32[]{:S(2)}) collective-permute-start(bf16[448,896]{1,0:T(8,128)(2,1)} %multiply_convert_fusion.4), channel_id=1, source_target_pairs={{1,0},{2,3},{5,4},{6,7},{9,8},{10,11},{13,12},{14,15},{17,16},{18,... | collective-permute-start | bytes 2408456 | tf_op jit(solution)/shard_map/ppermute | solution.py:218
  248.0 38.5 %collective-permute-start.9 = (bf16[448,1536]{1,0:T(8,128)(2,1)}, bf16[448,1536]{1,0:T(8,128)(2,1)S(1)}, u32[]{:S(2)}, u32[]{:S(2)}) collective-permute-start(bf16[448,1536]{1,0:T(8,128)(2,1)} %slice.167), channel_id=1, source_target_pairs={{0,8},{4,12},{8,0},{12,4},{16,24},{20,28},{24,16},{28,20},{1,9},{5... | collective-permute-start | bytes 4128776 | tf_op jit(solution)/shard_map/ppermute | solution.py:35
  253.7 25.7 %collective-permute-start.30 = (bf16[448,896]{1,0:T(8,128)(2,1)S(1)}, bf16[448,896]{1,0:T(8,128)(2,1)}, u32[]{:S(2)}, u32[]{:S(2)}) collective-permute-start(bf16[448,896]{1,0:T(8,128)(2,1)S(1)} %shard_map.23), channel_id=1, source_target_pairs={{0,1},{3,2},{4,5},{7,6},{8,9},{11,10},{12,13},{15,14},{16,17},{19,... | collective-permute-start | bytes 2408456 | tf_op jit(solution)/shard_map/ppermute | solution.py:218
  280.8 36.5 %collective-permute-start.33 = (bf16[448,896]{1,0:T(8,128)(2,1)S(1)}, bf16[448,896]{1,0:T(8,128)(2,1)}, u32[]{:S(2)}, u32[]{:S(2)}) collective-permute-start(bf16[448,896]{1,0:T(8,128)(2,1)S(1)} %add_convert_fusion), channel_id=1, source_target_pairs={{1,2},{2,1},{5,6},{6,5},{9,10},{10,9},{13,14},{14,13},{17,18},{18,... | collective-permute-start | bytes 2408456 | tf_op jit(solution)/shard_map/ppermute | solution.py:218
  286.5 29.4 %collective-permute-start.31 = (bf16[448,896]{1,0:T(8,128)(2,1)S(1)}, bf16[448,896]{1,0:T(8,128)(2,1)}, u32[]{:S(2)}, u32[]{:S(2)}) collective-permute-start(bf16[448,896]{1,0:T(8,128)(2,1)S(1)} %shard_map.22), channel_id=1, source_target_pairs={{0,1},{3,2},{4,5},{7,6},{8,9},{11,10},{12,13},{15,14},{16,17},{19,... | collective-permute-start | bytes 2408456 | tf_op jit(solution)/shard_map/ppermute | solution.py:218
  302.1 24.6 %collective-permute-start.24 = (bf16[448,896]{1,0:T(8,128)(2,1)S(1)}, bf16[448,896]{1,0:T(8,128)(2,1)S(1)}, u32[]{:S(2)}, u32[]{:S(2)}) collective-permute-start(bf16[448,896]{1,0:T(8,128)(2,1)S(1)} %multiply_convert_fusion.5), channel_id=1, source_target_pairs={{1,0},{2,3},{5,4},{6,7},{9,8},{10,11},{13,12},{14,15},{17,16},{18,... | collective-permute-start | bytes 2408456 | tf_op jit(solution)/shard_map/ppermute | solution.py:218
  305.2 23.0 %collective-permute-start.19 = (bf16[448,896]{1,0:T(8,128)(2,1)S(1)}, bf16[448,896]{1,0:T(8,128)(2,1)S(1)}, u32[]{:S(2)}, u32[]{:S(2)}) collective-permute-start(bf16[448,896]{1,0:T(8,128)(2,1)S(1)} %add_convert_fusion.6), channel_id=1, source_target_pairs={{1,2},{2,1},{5,6},{6,5},{9,10},{10,9},{13,14},{14,13},{17,18},{18,... | collective-permute-start | bytes 2408456 | tf_op jit(solution)/shard_map/ppermute | solution.py:218
  320.6 24.4 %collective-permute-start.14 = (bf16[448,896]{1,0:T(8,128)(2,1)S(1)}, bf16[448,896]{1,0:T(8,128)(2,1)S(1)}, u32[]{:S(2)}, u32[]{:S(2)}) collective-permute-start(bf16[448,896]{1,0:T(8,128)(2,1)S(1)} %shard_map.18), channel_id=1, source_target_pairs={{0,1},{3,2},{4,5},{7,6},{8,9},{11,10},{12,13},{15,14},{16,17},{19,... | collective-permute-start | bytes 2408456 | tf_op jit(solution)/shard_map/ppermute | solution.py:218
  326.7 35.5 %collective-permute-start.32 = (bf16[448,896]{1,0:T(8,128)(2,1)S(1)}, bf16[448,896]{1,0:T(8,128)(2,1)S(1)}, u32[]{:S(2)}, u32[]{:S(2)}) collective-permute-start(bf16[448,896]{1,0:T(8,128)(2,1)S(1)} %shard_map.21), channel_id=1, source_target_pairs={{0,1},{3,2},{4,5},{7,6},{8,9},{11,10},{12,13},{15,14},{16,17},{19,... | collective-permute-start | bytes 2408456 | tf_op jit(solution)/shard_map/ppermute | solution.py:218
  328.2 72.6 %collective-permute-start.46 = (bf16[448,896]{1,0:T(8,128)(2,1)S(1)}, bf16[448,896]{1,0:T(8,128)(2,1)S(1)}, u32[]{:S(2)}, u32[]{:S(2)}) collective-permute-start(bf16[448,896]{1,0:T(8,128)(2,1)S(1)} %broadcast_select_fusion.mine), channel_id=1, source_target_pairs={{0,4},{4,0},{8,12},{12,8},{16,20},{20,16},{24,28},{28,24},{1,5},{5... | collective-permute-start | bytes 2408456 | tf_op jit(solution)/shard_map/ppermute | solution.py:35
  328.5 46.4 %collective-permute-start.25 = (bf16[448,896]{1,0:T(8,128)(2,1)S(1)}, bf16[448,896]{1,0:T(8,128)(2,1)S(1)}, u32[]{:S(2)}, u32[]{:S(2)}) collective-permute-start(bf16[448,896]{1,0:T(8,128)(2,1)S(1)} %multiply_convert_fusion.6), channel_id=1, source_target_pairs={{1,0},{2,3},{5,4},{6,7},{9,8},{10,11},{13,12},{14,15},{17,16},{18,... | collective-permute-start | bytes 2408456 | tf_op jit(solution)/shard_map/ppermute | solution.py:218
  337.4 42.1 %collective-permute-start.37 = (bf16[448,896]{1,0:T(8,128)(2,1)S(1)}, bf16[448,896]{1,0:T(8,128)(2,1)S(1)}, u32[]{:S(2)}, u32[]{:S(2)}) collective-permute-start(bf16[448,896]{1,0:T(8,128)(2,1)S(1)} %multiply_convert_fusion.1), channel_id=1, source_target_pairs={{1,0},{2,3},{5,4},{6,7},{9,8},{10,11},{13,12},{14,15},{17,16},{18,... | collective-permute-start | bytes 2408456 | tf_op jit(solution)/shard_map/ppermute | solution.py:218
  345.0 28.0 %collective-permute-start.15 = (bf16[448,896]{1,0:T(8,128)(2,1)S(1)}, bf16[448,896]{1,0:T(8,128)(2,1)S(1)}, u32[]{:S(2)}, u32[]{:S(2)}) collective-permute-start(bf16[448,896]{1,0:T(8,128)(2,1)S(1)} %shard_map.17), channel_id=1, source_target_pairs={{0,1},{3,2},{4,5},{7,6},{8,9},{11,10},{12,13},{15,14},{16,17},{19,... | collective-permute-start | bytes 2408456 | tf_op jit(solution)/shard_map/ppermute | solution.py:218
  375.0 24.0 %collective-permute-start.26 = (bf16[448,896]{1,0:T(8,128)(2,1)S(1)}, bf16[448,896]{1,0:T(8,128)(2,1)S(1)}, u32[]{:S(2)}, u32[]{:S(2)}) collective-permute-start(bf16[448,896]{1,0:T(8,128)(2,1)S(1)} %multiply_convert_fusion.7), channel_id=1, source_target_pairs={{1,0},{2,3},{5,4},{6,7},{9,8},{10,11},{13,12},{14,15},{17,16},{18,... | collective-permute-start | bytes 2408456 | tf_op jit(solution)/shard_map/ppermute | solution.py:218
  376.4 25.9 %collective-permute-start.45 = (bf16[448,896]{1,0:T(8,128)(2,1)S(1)}, bf16[448,896]{1,0:T(8,128)(2,1)S(1)}, u32[]{:S(2)}, u32[]{:S(2)}) collective-permute-start(bf16[448,896]{1,0:T(8,128)(2,1)S(1)} %broadcast_select_fusion.1.mine), channel_id=1, source_target_pairs={{0,8},{4,12},{8,0},{12,4},{16,24},{20,28},{24,16},{28,20},{1,9},{5... | collective-permute-start | bytes 2408456 | tf_op jit(solution)/shard_map/ppermute | solution.py:35
  379.5 23.3 %collective-permute-start.43 = (bf16[448,896]{1,0:T(8,128)(2,1)S(1)}, bf16[448,896]{1,0:T(8,128)(2,1)S(1)}, u32[]{:S(2)}, u32[]{:S(2)}) collective-permute-start(bf16[448,896]{1,0:T(8,128)(2,1)S(1)} %broadcast_select_fusion.2), channel_id=1, source_target_pairs={{0,4},{4,0},{8,12},{12,8},{16,20},{20,16},{24,28},{28,24},{1,5},{5... | collective-permute-start | bytes 2408456 | tf_op jit(solution)/shard_map/ppermute | solution.py:35
  379.5 53.7 %collective-permute-start.38 = (bf16[448,896]{1,0:T(8,128)(2,1)S(1)}, bf16[448,896]{1,0:T(8,128)(2,1)S(1)}, u32[]{:S(2)}, u32[]{:S(2)}) collective-permute-start(bf16[448,896]{1,0:T(8,128)(2,1)S(1)} %multiply_convert_fusion.2), channel_id=1, source_target_pairs={{1,0},{2,3},{5,4},{6,7},{9,8},{10,11},{13,12},{14,15},{17,16},{18,... | collective-permute-start | bytes 2408456 | tf_op jit(solution)/shard_map/ppermute | solution.py:218
  399.0 45.9 %collective-permute-start.27 = (bf16[448,896]{1,0:T(8,128)(2,1)S(1)}, bf16[448,896]{1,0:T(8,128)(2,1)S(1)}, u32[]{:S(2)}, u32[]{:S(2)}) collective-permute-start(bf16[448,896]{1,0:T(8,128)(2,1)S(1)} %multiply_convert_fusion.8), channel_id=1, source_target_pairs={{1,0},{2,3},{5,4},{6,7},{9,8},{10,11},{13,12},{14,15},{17,16},{18,... | collective-permute-start | bytes 2408456 | tf_op jit(solution)/shard_map/ppermute | solution.py:218
  400.8 46.8 %collective-permute-start.44 = (bf16[448,896]{1,0:T(8,128)(2,1)S(1)}, bf16[448,896]{1,0:T(8,128)(2,1)S(1)}, u32[]{:S(2)}, u32[]{:S(2)}) collective-permute-start(bf16[448,896]{1,0:T(8,128)(2,1)S(1)} %broadcast_select_fusion.2), channel_id=1, source_target_pairs={{0,8},{4,12},{8,0},{12,4},{16,24},{20,28},{24,16},{28,20},{1,9},{5... | collective-permute-start | bytes 2408456 | tf_op jit(solution)/shard_map/ppermute | solution.py:35
  402.3 46.2 %collective-permute-start.42 = (bf16[448,896]{1,0:T(8,128)(2,1)S(1)}, bf16[448,896]{1,0:T(8,128)(2,1)S(1)}, u32[]{:S(2)}, u32[]{:S(2)}) collective-permute-start(bf16[448,896]{1,0:T(8,128)(2,1)S(1)} %broadcast_select_fusion.3.mine), channel_id=1, source_target_pairs={{0,16},{4,20},{8,24},{12,28},{16,0},{20,4},{24,8},{28,12},{1,17},{... | collective-permute-start | bytes 2408456 | tf_op jit(solution)/shard_map/ppermute | solution.py:35
  402.8 47.1 %collective-permute-start.40 = (bf16[448,896]{1,0:T(8,128)(2,1)S(1)}, bf16[448,896]{1,0:T(8,128)(2,1)S(1)}, u32[]{:S(2)}, u32[]{:S(2)}) collective-permute-start(bf16[448,896]{1,0:T(8,128)(2,1)S(1)} %broadcast_select_fusion.4), channel_id=1, source_target_pairs={{0,4},{4,0},{8,12},{12,8},{16,20},{20,16},{24,28},{28,24},{1,5},{5... | collective-permute-start | bytes 2408456 | tf_op jit(solution)/shard_map/ppermute | solution.py:35
  433.2 38.0 %collective-permute-start.41 = (bf16[448,896]{1,0:T(8,128)(2,1)S(1)}, bf16[448,896]{1,0:T(8,128)(2,1)S(1)}, u32[]{:S(2)}, u32[]{:S(2)}) collective-permute-start(bf16[448,896]{1,0:T(8,128)(2,1)S(1)} %broadcast_select_fusion.4), channel_id=1, source_target_pairs={{0,16},{4,20},{8,24},{12,28},{16,0},{20,4},{24,8},{28,12},{1,17},{... | collective-permute-start | bytes 2408456 | tf_op jit(solution)/shard_map/ppermute | solution.py:35
  444.9 28.7 %collective-permute-start.39 = (bf16[448,896]{1,0:T(8,128)(2,1)S(1)}, bf16[448,896]{1,0:T(8,128)(2,1)S(1)}, u32[]{:S(2)}, u32[]{:S(2)}) collective-permute-start(bf16[448,896]{1,0:T(8,128)(2,1)S(1)} %broadcast_select_fusion.5.mine), channel_id=1, source_target_pairs={{0,24},{4,28},{8,16},{12,20},{16,8},{20,12},{24,0},{28,4},{1,25},{... | collective-permute-start | bytes 2408456 | tf_op jit(solution)/shard_map/ppermute | solution.py:35
  448.5 26.0 %collective-permute-start.28 = (bf16[448,896]{1,0:T(8,128)(2,1)}, bf16[448,896]{1,0:T(8,128)(2,1)S(1)}, u32[]{:S(2)}, u32[]{:S(2)}) collective-permute-start(bf16[448,896]{1,0:T(8,128)(2,1)} %broadcast_select_fusion.6), channel_id=1, source_target_pairs={{0,4},{4,0},{8,12},{12,8},{16,20},{20,16},{24,28},{28,24},{1,5},{5... | collective-permute-start | bytes 2408456 | tf_op jit(solution)/shard_map/ppermute | solution.py:35
  449.4 51.8 %collective-permute-start.47 = (bf16[896,768]{1,0:T(8,128)(2,1)S(1)}, bf16[896,768]{1,0:T(8,128)(2,1)}, u32[]{:S(2)}, u32[]{:S(2)}) collective-permute-start(bf16[896,768]{1,0:T(8,128)(2,1)S(1)} %copy-done.3), channel_id=1, source_target_pairs={{0,4},{4,0},{8,12},{12,8},{16,20},{20,16},{24,28},{28,24},{1,5},{5... | collective-permute-start | bytes 4128776 | tf_op jit(solution)/shard_map/ppermute | solution.py:35
  450.8 50.3 %collective-permute-start.48 = (bf16[896,768]{1,0:T(8,128)(2,1)}, bf16[896,768]{1,0:T(8,128)(2,1)}, u32[]{:S(2)}, u32[]{:S(2)}) collective-permute-start(bf16[896,768]{1,0:T(8,128)(2,1)} %collective-permute-done.3.refs_2_.refs_5_), channel_id=1, source_target_pairs={{0,4},{4,0},{8,12},{12,8},{16,20},{20,16},{24,28},{28,24},{1,5},{5... | collective-permute-start | bytes 4128776 | tf_op jit(solution)/shard_map/ppermute | solution.py:35
  474.5 26.6 %collective-permute-start.49 = (bf16[448,768]{1,0:T(8,128)(2,1)}, bf16[448,768]{1,0:T(8,128)(2,1)}, u32[]{:S(2)}, u32[]{:S(2)}) collective-permute-start(bf16[448,768]{1,0:T(8,128)(2,1)} %collective-permute-done.4.refs_7_), channel_id=1, source_target_pairs={{0,4},{4,0},{8,12},{12,8},{16,20},{20,16},{24,28},{28,24},{1,5},{5... | collective-permute-start | bytes 2064392 | tf_op jit(solution)/shard_map/ppermute | solution.py:35
  475.4 25.7 %collective-permute-start.50 = (bf16[448,768]{1,0:T(8,128)(2,1)}, bf16[448,768]{1,0:T(8,128)(2,1)}, u32[]{:S(2)}, u32[]{:S(2)}) collective-permute-start(bf16[448,768]{1,0:T(8,128)(2,1)} %collective-permute-done.5.refs_8_), channel_id=1, source_target_pairs={{0,4},{4,0},{8,12},{12,8},{16,20},{20,16},{24,28},{28,24},{1,5},{5... | collective-permute-start | bytes 2064392 | tf_op jit(solution)/shard_map/ppermute | solution.py:35
  515.9 32.4 %collective-permute-start.52 = (bf16[896,768]{1,0:T(8,128)(2,1)S(1)}, bf16[896,768]{1,0:T(8,128)(2,1)S(1)}, u32[]{:S(2)}, u32[]{:S(2)}) collective-permute-start(bf16[896,768]{1,0:T(8,128)(2,1)S(1)} %shard_map.31.refs_1_.refs_12_), channel_id=1, source_target_pairs={{0,8},{4,12},{8,0},{12,4},{16,24},{20,28},{24,16},{28,20},{1,9},{5... | collective-permute-start | bytes 4128776 | tf_op jit(solution)/shard_map/ppermute | solution.py:35
  516.0 36.3 %collective-permute-start.60 = (bf16[896,1536]{1,0:T(8,128)(2,1)}, bf16[896,1536]{1,0:T(8,128)(2,1)S(1)}, u32[]{:S(2)}, u32[]{:S(2)}) collective-permute-start(bf16[896,1536]{1,0:T(8,128)(2,1)} %collective-permute-done.6.refs_3_), channel_id=1, source_target_pairs={{0,4},{4,0},{8,12},{12,8},{16,20},{20,16},{24,28},{28,24},{1,5},{5... | collective-permute-start | bytes 8257544 | tf_op jit(solution)/shard_map/ppermute | solution.py:35
  516.3 36.6 %collective-permute-start.61 = (bf16[896,1536]{1,0:T(8,128)(2,1)}, bf16[896,1536]{1,0:T(8,128)(2,1)S(1)}, u32[]{:S(2)}, u32[]{:S(2)}) collective-permute-start(bf16[896,1536]{1,0:T(8,128)(2,1)} %collective-permute-done.7.refs_3_.refs_5_), channel_id=1, source_target_pairs={{0,4},{4,0},{8,12},{12,8},{16,20},{20,16},{24,28},{28,24},{1,5},{5... | collective-permute-start | bytes 8257544 | tf_op jit(solution)/shard_map/ppermute | solution.py:35
  516.5 32.3 %collective-permute-start.54 = (bf16[896,768]{1,0:T(8,128)(2,1)S(1)}, bf16[896,768]{1,0:T(8,128)(2,1)S(1)}, u32[]{:S(2)}, u32[]{:S(2)}) collective-permute-start(bf16[896,768]{1,0:T(8,128)(2,1)S(1)} %shard_map.31.refs_1_.refs_12_), channel_id=1, source_target_pairs={{0,16},{4,20},{8,24},{12,28},{16,0},{20,4},{24,8},{28,12},{1,17},{... | collective-permute-start | bytes 4128776 | tf_op jit(solution)/shard_map/ppermute | solution.py:35
  518.1 32.5 %collective-permute-start.62 = (bf16[448,1536]{1,0:T(8,128)(2,1)S(1)}, bf16[448,1536]{1,0:T(8,128)(2,1)S(1)}, u32[]{:S(2)}, u32[]{:S(2)}) collective-permute-start(bf16[448,1536]{1,0:T(8,128)(2,1)S(1)} %copy-done.9), channel_id=1, source_target_pairs={{0,4},{4,0},{8,12},{12,8},{16,20},{20,16},{24,28},{28,24},{1,5},{5... | collective-permute-start | bytes 4128776 | tf_op jit(solution)/shard_map/ppermute | solution.py:35
  552.3 30.2 %collective-permute-start.51 = (bf16[896,768]{1,0:T(8,128)(2,1)S(1)}, bf16[896,768]{1,0:T(8,128)(2,1)}, u32[]{:S(2)}, u32[]{:S(2)}) collective-permute-start(bf16[896,768]{1,0:T(8,128)(2,1)S(1)} %shard_map.31.refs_1_.refs_12_), channel_id=1, source_target_pairs={{0,4},{4,0},{8,12},{12,8},{16,20},{20,16},{24,28},{28,24},{1,5},{5... | collective-permute-start | bytes 4128776 | tf_op jit(solution)/shard_map/ppermute | solution.py:35
  552.3 32.0 %collective-permute-start.53 = (bf16[896,768]{1,0:T(8,128)(2,1)S(1)}, bf16[896,768]{1,0:T(8,128)(2,1)}, u32[]{:S(2)}, u32[]{:S(2)}) collective-permute-start(bf16[896,768]{1,0:T(8,128)(2,1)S(1)} %collective-permute-done.52.refs_3_), channel_id=1, source_target_pairs={{0,4},{4,0},{8,12},{12,8},{16,20},{20,16},{24,28},{28,24},{1,5},{5... | collective-permute-start | bytes 4128776 | tf_op jit(solution)/shard_map/ppermute | solution.py:35
  552.8 31.5 %collective-permute-start.55 = (bf16[896,768]{1,0:T(8,128)(2,1)S(1)}, bf16[896,768]{1,0:T(8,128)(2,1)}, u32[]{:S(2)}, u32[]{:S(2)}) collective-permute-start(bf16[896,768]{1,0:T(8,128)(2,1)S(1)} %collective-permute-done.54.refs_5_), channel_id=1, source_target_pairs={{0,4},{4,0},{8,12},{12,8},{16,20},{20,16},{24,28},{28,24},{1,5},{5... | collective-permute-start | bytes 4128776 | tf_op jit(solution)/shard_map/ppermute | solution.py:35
  582.5 32.8 %collective-permute-start.65 = (bf16[896,768]{1,0:T(8,128)(2,1)S(1)}, bf16[896,768]{1,0:T(8,128)(2,1)}, u32[]{:S(2)}, u32[]{:S(2)}) collective-permute-start(bf16[896,768]{1,0:T(8,128)(2,1)S(1)} %shard_map.33.refs_1_.refs_12_), channel_id=1, source_target_pairs={{0,8},{4,12},{8,0},{12,4},{16,24},{20,28},{24,16},{28,20},{1,9},{5... | collective-permute-start | bytes 4128776 | tf_op jit(solution)/shard_map/ppermute | solution.py:35
  583.5 48.1 %collective-permute-start.67 = (bf16[896,768]{1,0:T(8,128)(2,1)S(1)}, bf16[896,768]{1,0:T(8,128)(2,1)}, u32[]{:S(2)}, u32[]{:S(2)}) collective-permute-start(bf16[896,768]{1,0:T(8,128)(2,1)S(1)} %shard_map.33.refs_1_.refs_12_), channel_id=1, source_target_pairs={{0,16},{4,20},{8,24},{12,28},{16,0},{20,4},{24,8},{28,12},{1,17},{... | collective-permute-start | bytes 4128776 | tf_op jit(solution)/shard_map/ppermute | solution.py:35
  630.2 53.2 %collective-permute-start.74 = (bf16[896,768]{1,0:T(8,128)(2,1)S(1)}, bf16[896,768]{1,0:T(8,128)(2,1)}, u32[]{:S(2)}, u32[]{:S(2)}) collective-permute-start(bf16[896,768]{1,0:T(8,128)(2,1)S(1)} %shard_map.35.refs_1_.refs_12_), channel_id=1, source_target_pairs={{0,8},{4,12},{8,0},{12,4},{16,24},{20,28},{24,16},{28,20},{1,9},{5... | collective-permute-start | bytes 4128776 | tf_op jit(solution)/shard_map/ppermute | solution.py:35
  631.2 52.3 %collective-permute-start.76 = (bf16[896,768]{1,0:T(8,128)(2,1)S(1)}, bf16[896,768]{1,0:T(8,128)(2,1)}, u32[]{:S(2)}, u32[]{:S(2)}) collective-permute-start(bf16[896,768]{1,0:T(8,128)(2,1)S(1)} %shard_map.35.refs_1_.refs_12_), channel_id=1, source_target_pairs={{0,16},{4,20},{8,24},{12,28},{16,0},{20,4},{24,8},{28,12},{1,17},{... | collective-permute-start | bytes 4128776 | tf_op jit(solution)/shard_map/ppermute | solution.py:35
  633.9 43.5 %collective-permute-start.69 = (bf16[448,768]{1,0:T(8,128)(2,1)S(1)}, bf16[448,768]{1,0:T(8,128)(2,1)S(1)}, u32[]{:S(2)}, u32[]{:S(2)}) collective-permute-start(bf16[448,768]{1,0:T(8,128)(2,1)S(1)} %slice.180), channel_id=1, source_target_pairs={{0,16},{4,20},{8,24},{12,28},{16,0},{20,4},{24,8},{28,12},{1,17},{... | collective-permute-start | bytes 2064392 | tf_op jit(solution)/shard_map/ppermute | solution.py:35
  635.6 41.9 %collective-permute-start.70 = (bf16[448,768]{1,0:T(8,128)(2,1)S(1)}, bf16[448,768]{1,0:T(8,128)(2,1)}, u32[]{:S(2)}, u32[]{:S(2)}) collective-permute-start(bf16[448,768]{1,0:T(8,128)(2,1)S(1)} %slice.181), channel_id=1, source_target_pairs={{0,8},{4,12},{8,0},{12,4},{16,24},{20,28},{24,16},{28,20},{1,9},{5... | collective-permute-start | bytes 2064392 | tf_op jit(solution)/shard_map/ppermute | solution.py:35
  636.7 54.8 %collective-permute-start.64 = (bf16[896,768]{1,0:T(8,128)(2,1)S(1)}, bf16[896,768]{1,0:T(8,128)(2,1)}, u32[]{:S(2)}, u32[]{:S(2)}) collective-permute-start(bf16[896,768]{1,0:T(8,128)(2,1)S(1)} %shard_map.33.refs_1_.refs_12_), channel_id=1, source_target_pairs={{0,4},{4,0},{8,12},{12,8},{16,20},{20,16},{24,28},{28,24},{1,5},{5... | collective-permute-start | bytes 4128776 | tf_op jit(solution)/shard_map/ppermute | solution.py:35
  678.0 39.1 %all-to-all-start.2 = ((bf16[4,224,768]{2,1,0:T(8,128)(2,1)}), bf16[4,224,768]{2,1,0:T(8,128)(2,1)}, u32[]{:S(2)}, u32[]{:S(2)}) async-start(bf16[4,224,768]{2,1,0:T(8,128)(2,1)} %bitcast.13), calls=%async_computation.2 | async-start | bytes 2752512 | tf_op jit(solution)/shard_map/all_to_all | solution.py:249
  691.5 29.7 %collective-permute-start.73 = (bf16[896,768]{1,0:T(8,128)(2,1)S(1)}, bf16[896,768]{1,0:T(8,128)(2,1)}, u32[]{:S(2)}, u32[]{:S(2)}) collective-permute-start(bf16[896,768]{1,0:T(8,128)(2,1)S(1)} %shard_map.35.refs_1_.refs_12_), channel_id=1, source_target_pairs={{0,4},{4,0},{8,12},{12,8},{16,20},{20,16},{24,28},{28,24},{1,5},{5... | collective-permute-start | bytes 4128776 | tf_op jit(solution)/shard_map/ppermute | solution.py:35
  691.6 29.0 %collective-permute-start.78 = (bf16[448,768]{1,0:T(8,128)(2,1)}, bf16[448,768]{1,0:T(8,128)(2,1)}, u32[]{:S(2)}, u32[]{:S(2)}) collective-permute-start(bf16[448,768]{1,0:T(8,128)(2,1)} %slice.185), channel_id=1, source_target_pairs={{0,16},{4,20},{8,24},{12,28},{16,0},{20,4},{24,8},{28,12},{1,17},{... | collective-permute-start | bytes 2064392 | tf_op jit(solution)/shard_map/ppermute | solution.py:35
  692.2 28.5 %collective-permute-start.79 = (bf16[448,768]{1,0:T(8,128)(2,1)}, bf16[448,768]{1,0:T(8,128)(2,1)}, u32[]{:S(2)}, u32[]{:S(2)}) collective-permute-start(bf16[448,768]{1,0:T(8,128)(2,1)} %slice.186), channel_id=1, source_target_pairs={{0,8},{4,12},{8,0},{12,4},{16,24},{20,28},{24,16},{28,20},{1,9},{5... | collective-permute-start | bytes 2064392 | tf_op jit(solution)/shard_map/ppermute | solution.py:35
  693.3 30.7 %collective-permute-start.75 = (bf16[896,768]{1,0:T(8,128)(2,1)}, bf16[896,768]{1,0:T(8,128)(2,1)}, u32[]{:S(2)}, u32[]{:S(2)}) collective-permute-start(bf16[896,768]{1,0:T(8,128)(2,1)} %collective-permute-done.74.refs_3_), channel_id=1, source_target_pairs={{0,4},{4,0},{8,12},{12,8},{16,20},{20,16},{24,28},{28,24},{1,5},{5... | collective-permute-start | bytes 4128776 | tf_op jit(solution)/shard_map/ppermute | solution.py:35
  693.3 30.7 %collective-permute-start.77 = (bf16[896,768]{1,0:T(8,128)(2,1)}, bf16[896,768]{1,0:T(8,128)(2,1)}, u32[]{:S(2)}, u32[]{:S(2)}) collective-permute-start(bf16[896,768]{1,0:T(8,128)(2,1)} %collective-permute-done.76.refs_5_), channel_id=1, source_target_pairs={{0,4},{4,0},{8,12},{12,8},{16,20},{20,16},{24,28},{28,24},{1,5},{5... | collective-permute-start | bytes 4128776 | tf_op jit(solution)/shard_map/ppermute | solution.py:35
  717.0 36.5 %all-to-all-start.3 = ((bf16[4,224,768]{2,1,0:T(8,128)(2,1)}), bf16[4,224,768]{2,1,0:T(8,128)(2,1)S(1)}, u32[]{:S(2)}, u32[]{:S(2)}) async-start(bf16[4,224,768]{2,1,0:T(8,128)(2,1)} %bitcast.15), calls=%async_computation.3 | async-start | bytes 2752512 | tf_op jit(solution)/shard_map/all_to_all | solution.py:249
  753.5 35.8 %all-to-all-start.4 = ((bf16[4,224,768]{2,1,0:T(8,128)(2,1)}), bf16[4,224,768]{2,1,0:T(8,128)(2,1)S(1)}, u32[]{:S(2)}, u32[]{:S(2)}) async-start(bf16[4,224,768]{2,1,0:T(8,128)(2,1)} %bitcast.17), calls=%async_computation.4 | async-start | bytes 2752512 | tf_op jit(solution)/shard_map/all_to_all | solution.py:249
  (62 other events, 1334.4 us)

commit v2 on v1

v2 whole, which is shorter than its diff:
```python
import functools
import math

import jax
import jax.numpy as jnp
from jax import lax
from jax.experimental import pallas as pl
from jax.experimental.pallas import tpu as pltpu
from jax.sharding import PartitionSpec as P

coef_a = 3.4445
coef_b = -4.775
coef_c = 2.0315
bf16 = jnp.bfloat16
f32 = jnp.float32
VMEM_BYTES = 48 * 1024 * 1024


def widths_of(width, count):
    unit = 256 if width % 256 == 0 else 128
    base, extra = divmod(width // unit, count)
    return [unit * (base + (i >= count - extra)) for i in range(count)]


def dot_t(a, b):
    return lax.dot_general(a, b, (((1,), (1,)), ((), ())), preferred_element_type=f32)


def after(value, *others):
    return lax.optimization_barrier((value, *others))[0]


def swap(value, bit):
    count = lax.axis_size("row")
    return lax.ppermute(value, "row", [(r, r ^ bit) for r in range(count)])


def gather_chips(own):
    count = lax.axis_size("row")
    bit_x, bit_y = count // 4, count // 2
    h = own.shape[0] // 2
    corner = bit_x | bit_y
    parts = {(0, 0): own}
    parts[(bit_x, 0)] = swap(own, bit_x)
    parts[(bit_y, 0)] = swap(own, bit_y)
    from_x, from_y = lax.optimization_barrier((parts[(bit_x, 0)], parts[(bit_y, 0)]))
    upper, lower = lax.optimization_barrier((from_x[:h], from_y[h:]))
    parts[(corner, 0)] = swap(upper, bit_y)
    parts[(corner, h)] = swap(lower, bit_x)
    return parts, (upper, lower)


def add_cores(parts, hold=None):
    bit_x = lax.axis_size("row") // 4
    parts = dict(parts)
    bit = 1
    while bit < bit_x:
        for j, offset in list(parts):
            if (j | bit, offset) not in parts:
                part = parts[(j, offset)]
                if hold is not None:
                    part = after(part, hold)
                parts[(j | bit, offset)] = swap(part, bit)
        bit *= 2
    return parts


def whole_block(parts, j):
    pieces = [parts[key] for key in sorted(parts) if key[0] == j]
    return pieces[0] if len(pieces) == 1 else jnp.concatenate(pieces, axis=0)


def pieces_kernel(count, jobs, scale, low_ref, *refs):
    out = refs[-1]
    h = out.shape[1]

    def product(n, left, right, first):
        total = None
        for k in range(count):
            rows = refs[left * count + k][first : first + h, :]
            term = dot_t(rows, refs[right * count + k][...])
            total = term if total is None else total + term
        out[n] = (total * scale).astype(bf16)

    for n, (left, right, low, first) in enumerate(jobs):
        if low is None:
            product(n, left, right, first)
            continue

        @pl.when(low_ref[low] == 1)
        def _():
            product(n, left, right, 0)

        @pl.when(low_ref[low] == 0)
        def _():
            product(n, right, left, h)


def gram_pieces(blocks, jobs, lows, scale):
    count = len(blocks[0])
    size = blocks[0][0].shape[0]
    width = sum(part.shape[1] for part in blocks[0])
    return pl.pallas_call(
        functools.partial(pieces_kernel, count, jobs, scale),
        out_shape=jax.ShapeDtypeStruct((len(jobs), size // 2, size), bf16),
        in_specs=[pl.BlockSpec(memory_space=pltpu.SMEM)]
        + [pl.BlockSpec(memory_space=pltpu.VMEM)] * (count * len(blocks)),
        out_specs=pl.BlockSpec(memory_space=pltpu.VMEM),
        cost_estimate=pl.CostEstimate(
            flops=len(jobs) * size * size * width,
            bytes_accessed=2 * size * (len(blocks) * width + len(jobs) * size // 2),
            transcendentals=0,
        ),
        compiler_params=pltpu.CompilerParams(vmem_limit_bytes=VMEM_BYTES),
    )(jnp.stack(lows).astype(jnp.int32), *[part for block in blocks for part in block])


def block_kernel(low_ref, mine, theirs, gram_in, out):
    h = mine.shape[0]

    @pl.when(low_ref[0] == 1)
    def _():
        out[:h, :] = mine[...]
        out[h:, :] = theirs[...]

    @pl.when(low_ref[0] == 0)
    def _():
        out[...] = jnp.concatenate([theirs[...], mine[...]], axis=0).T


def put_block(gram, low, mine, theirs, j):
    h, size = mine.shape
    return pl.pallas_call(
        block_kernel,
        grid=(1,),
        out_shape=jax.ShapeDtypeStruct(gram.shape, bf16),
        in_specs=[
            pl.BlockSpec(memory_space=pltpu.SMEM),
            pl.BlockSpec((h, size), lambda i: (0, 0)),
            pl.BlockSpec((h, size), lambda i: (0, 0)),
            pl.BlockSpec(memory_space=pl.ANY),
        ],
        out_specs=pl.BlockSpec((None, size, size), lambda i: (j, 0, 0)),
        input_output_aliases={3: 0},
        cost_estimate=pl.CostEstimate(
            flops=0, bytes_accessed=4 * size * size, transcendentals=0
        ),
        compiler_params=pltpu.CompilerParams(vmem_limit_bytes=VMEM_BYTES),
    )(low, mine, theirs, gram)


def product_kernel(keys, start, finish, me_ref, *refs):
    gram, parts = refs[0], refs[1 : 1 + len(keys)]
    extra = refs[1 + len(keys) : -5]
    out, gbuf, xbuf, acc, sems = refs[-5:]
    count, size, width = xbuf.shape
    h = size // 2

    def piece(j, part):
        return xbuf.at[j, pl.ds(part * h, h)], sems.at[j, part]

    copies = []
    for j in range(count):
        copies.append(pltpu.make_async_copy(gram.at[j], gbuf.at[j], sems.at[j, 2]))
        for part in range(2):
            if keys[0] is None:
                first = pl.multiple_of((me_ref[0] ^ j) * size + part * h, 16)
                source = parts[0].at[pl.ds(first, h), pl.ds(start, width)]
            else:
                key = (j, part * h) if (j, part * h) in keys else (j, 0)
                first = part * h - key[1]
                source = parts[keys.index(key)].at[pl.ds(first, h), pl.ds(start, width)]
            copies.append(pltpu.make_async_copy(source, *piece(j, part)))
    for copy in copies:
        copy.start()
    acc[...] = jnp.zeros_like(acc)

    @pl.loop(0, count)
    def _(j):
        pltpu.make_async_copy(gbuf.at[j], gbuf.at[j], sems.at[j, 2]).wait()
        for part in range(2):
            there, sem = piece(j, part)
            pltpu.make_async_copy(there, there, sem).wait()
        acc[...] += jnp.dot(gbuf[j], xbuf[j], preferred_element_type=f32)

    if finish:
        tile, first = extra
        out[...] = (
            coef_a * tile[...].astype(f32)
            + coef_b * first[...].astype(f32)
            + coef_c * acc[...]
        ).astype(bf16)
    else:
        out[...] = acc[...].astype(bf16)


def product(gram, me, parts, start, width, extra=()):
    count, size, _ = gram.shape
    keys = sorted(parts)
    flops = 2 * count * size * size * width
    return pl.pallas_call(
        functools.partial(product_kernel, keys, start, bool(extra)),
        out_shape=jax.ShapeDtypeStruct((size, width), bf16),
        in_specs=[pl.BlockSpec(memory_space=pltpu.SMEM)]
        + [pl.BlockSpec(memory_space=pl.ANY)] * (1 + len(keys))
        + [pl.BlockSpec(memory_space=pltpu.VMEM)] * len(extra),
        out_specs=pl.BlockSpec(memory_space=pltpu.VMEM),
        scratch_shapes=[
            pltpu.VMEM((count, size, size), bf16),
            pltpu.VMEM((count, size, width), bf16),
            pltpu.VMEM((size, width), f32),
            pltpu.SemaphoreType.DMA((count, 3)),
        ],
        cost_estimate=pl.CostEstimate(
            flops=flops,
            bytes_accessed=2 * count * size * (size + width),
            transcendentals=0,
        ),
        compiler_params=pltpu.CompilerParams(vmem_limit_bytes=VMEM_BYTES),
    )(me.astype(jnp.int32).reshape(1), gram, *[parts[key] for key in keys], *extra)


def per_device(ortho_in):
    rows, cols = ortho_in.shape
    n_row = lax.axis_size("row")
    n_col = lax.axis_size("col")
    me = lax.axis_index("row")
    block = rows * n_col
    width = cols // n_col
    scale = 1.0 / (math.sqrt(block * n_row) + math.sqrt(cols)) ** 2
    h = block // 2
    bit_x, bit_y = n_row // 4, n_row // 2
    cores = range(1, bit_x)
    chips = (bit_x, bit_y, bit_x | bit_y)

    def exchange(value):
        return lax.all_to_all(value, "col", split_axis=0, concat_axis=0, tiled=True)

    tiles, gathered, siblings, tied = [], [], [], []
    start = 0
    thirds = widths_of(width, 3)
    for k, w in enumerate(thirds):
        first = [start + c * width for c in range(n_col)]
        part = jnp.concatenate([ortho_in[:, f : f + w] for f in first], axis=0)
        if k == 2:
            part = after(part, gathered[0][(bit_x, 0)], gathered[0][(bit_y, 0)])
        tile = exchange(part)
        tiles.append(tile)
        parts, tie = gather_chips(tile)
        gathered.append(parts)
        tied.extend(tie)
        siblings.append(add_cores({(0, 0): tile}))
        start += w

    def low_of(j):
        return ((me & (1 << (j.bit_length() - 1))) == 0).astype(jnp.int32).reshape(1)

    gram = jnp.zeros((n_row, block, block), bf16)
    lefts = [[s[(i, 0)] for s in siblings] for i in range(bit_x)]
    jobs = [(0, 0, None, 0), (0, 0, None, h)] + [(0, j, j - 1, 0) for j in cores]
    near = gram_pieces(lefts, jobs, [low_of(j)[0] for j in cores], scale)
    last = near = lax.psum(near, "col")
    gram = lax.dynamic_update_slice(gram, near[:2].reshape(1, block, block), (0, 0, 0))
    for j in cores:
        gram = put_block(gram, low_of(j), near[1 + j], swap(near[1 + j], j), j)
    for stage in (chips[:2], chips[2:]):
        blocks = list(lefts)
        for j in stage:
            peers = [whole_block(parts, j) for parts in gathered]
            if j != chips[-1]:
                peers[0] = after(peers[0], *tied)
            blocks.append(peers)
        jobs = [(i, bit_x + n, n, 0) for n in range(len(stage)) for i in range(bit_x)]
        pieces = gram_pieces(blocks, jobs, [low_of(j)[0] for j in stage], scale)
        last = sums = lax.psum(after(pieces, last), "col")
        for n, j in enumerate(stage):
            for i in range(bit_x):
                mine = sums[n * bit_x + i]
                theirs = swap(mine, j)
                if i > 0:
                    mine = swap(mine, i)
                gram = put_block(gram, low_of(j), mine, theirs, j | i)
    panels = [
        add_cores({**parts, **sibling}) for parts, sibling in zip(gathered, siblings)
    ]

    outs = [[] for _ in range(n_col)]
    for k, w in enumerate(thirds):
        first = product(gram, me, panels[k], 0, w)
        first_panel = lax.all_gather(first, "row", axis=0, tiled=True)
        result = product(gram, me, {None: first_panel}, 0, w, (tiles[k], first))
        back = exchange(result)
        for c in range(n_col):
            outs[c].append(back[c * rows : (c + 1) * rows])
    return jnp.concatenate([piece for out in outs for piece in out], axis=1)


def solution(mesh):
    in_specs = (P(("row", "col"), None),)
    out_specs = P(("row", "col"), None)
    return jax.shard_map(
        per_device, mesh=mesh, in_specs=in_specs, out_specs=out_specs, check_vma=False
    )
```

time: 810 us -> 787 us (0.972)
  starting transfers between devices: 114 us -> 54.8 us
  waiting for transfers between devices: 453 us -> 478 us
  local copies, waits for them, and re-layouts: 54.8 us -> 75 us
  other arithmetic: 23.8 us -> 9.63 us
  between operations: 1.25 us -> 14.2 us
  matrix products: 8.72 us -> 0 us
    ppermute x27 -> x0, waiting for transfers between devices: 130 us -> none  [send(): arrived = lax.ppermute(value, 'col', pairs)]
    psum x0 -> x3, waiting for transfers between devices: none -> 121 us  [the longest x2 107 us: per_device(): last = sums = lax.psum(after(pieces, last), 'col')]
    all_gather x0 -> x3, waiting for transfers between devices: none -> 99.6 us  [per_device(): first_panel = lax.all_gather(first, 'row', axis=0, tiled=True)]
    ppermute x27 -> x0, starting transfers between devices: 56.1 us -> none  [send(): arrived = lax.ppermute(value, 'col', pairs)]
    all_to_all x5 -> x6, waiting for transfers between devices: 137 us -> 92.4 us  [exchange(): return lax.all_to_all(value, 'col', split_axis=0, concat_axis=0, tiled=True)]
    ppermute x55 -> x37, waiting for transfers between devices: 186 us -> 166 us  [swap(): return lax.ppermute(value, 'row', [(r, r ^ bit) for r in range(count)])]
    unnamed x91 -> x81, local copies, waits for them, and re-layouts: 25.2 us -> 43.5 us
    convert_element_type x18 -> x0, other arithmetic: 15 us -> none  [the longest x9 8.03 us: sum_on_line(): piece = (piece.astype(f32) + arrived.astype(f32)).astype(bf16)]
  transfers between devices with their start and end apart: 87 -> 49, of which waited for: 29 -> 25; matrix products, arithmetic and copies ran while one was open for 8% -> 5% of each run, Pallas kernels for 16% -> 15%
where the time goes in v2:
time: 787 us; the launch traced here: 777 us
  waiting for transfers between devices  478 us (61%)
  Pallas kernels  145 us (18%)
  local copies, waits for them, and re-layouts  75 us (10%)
  starting transfers between devices  54.8 us (7%)
  between operations  14.2 us (2%)
  other arithmetic  9.63 us (1%)
    ppermute x37, waiting for transfers between devices, swap(): return lax.ppermute(value, 'row', [(r, r ^ bit) for r in range(count)])  166 us
    psum x2, waiting for transfers between devices, per_device(): last = sums = lax.psum(after(pieces, last), 'col')  107 us
    all_gather x3, waiting for transfers between devices, per_device(): first_panel = lax.all_gather(first, 'row', axis=0, tiled=True)  99.6 us
    pallas_call x6, Pallas kernels, product(): pl.pallas_call(functools.partial(product_kernel, keys, start, bool(extra)...  93.9 us
    all_to_all x6, waiting for transfers between devices, exchange(): return lax.all_to_all(value, 'col', split_axis=0, concat_axis=0, tiled=True)  92.4 us
    unnamed x81, local copies, waits for them, and re-layouts  43.5 us
    pallas_call x3, Pallas kernels, gram_pieces(): pl.pallas_call(functools.partial(pieces_kernel, count, jobs, scale), out_...  36.8 us
    all_to_all x6, starting transfers between devices, exchange(): return lax.all_to_all(value, 'col', split_axis=0, concat_axis=0, tiled=True)  28.4 us
  transfers between devices with their start and end apart: 49, of which 25 were waited for; matrix products, arithmetic and copies ran while one was open for 5% of the time, Pallas kernels for 15%

profile of v2, /device:TPU:0, one launch (start us, length us, event | category | flops | bytes accessed | tf_op | source)
XLA Modules:
  0.0 777.1 jit_solution(15964552961371182666)
XLA Ops:
  6.5 3.3 fusion.12
  11.0 6.3 all-to-all-start
  18.4 31.6 %all-to-all-done = bf16[4,224,768]{2,1,0:T(8,128)(2,1)S(1)} async-done(((bf16[4,224,768]{2,1,0:T(8,128)(2,1)}), bf16[4,224,768]{2,1,0:T(8,128)(2,1)S(1)}, u32[]{:S(2)}, u32[]{:S(2)}) %all-to-all-start) | async-done | bytes 1376288 | tf_op jit(solution)/shard_map/all_to_all | solution.py:237
  50.0 3.5 all-to-all-start.1
  53.6 1.6 collective-permute-start
  56.7 2.2 pad_maximum_fusion.2
  58.9 25.9 %collective-permute-done.refs_6_.refs_3_ = bf16[896,768]{1,0:T(8,128)(2,1)S(1)} collective-permute-done((bf16[896,768]{1,0:T(8,128)(2,1)S(1)}, bf16[896,768]{1,0:T(8,128)(2,1)S(1)}, u32[]{:S(2)}, u32[]{:S(2)}) %collective-permute-start) | collective-permute-done | bytes 1376288 | tf_op jit(solution)/shard_map/ppermute | solution.py:35
  86.1 4.7 all-to-all-start.2
  91.3 31.1 %all-to-all-done.2 = bf16[4,224,768]{2,1,0:T(8,128)(2,1)} async-done(((bf16[4,224,768]{2,1,0:T(8,128)(2,1)}), bf16[4,224,768]{2,1,0:T(8,128)(2,1)}, u32[]{:S(2)}, u32[]{:S(2)}) %all-to-all-start.2) | async-done | bytes 1376288 | tf_op jit(solution)/shard_map/all_to_all | solution.py:237
  122.4 3.5 collective-permute-done.4.refs_5_.refs_2_
  125.9 10.8 %shard_map.19 = bf16[3,448,896]{2,1,0:T(8,128)(2,1)} custom-call(s32[1]{0:T(128)} %bitcast.9.low_ref, bf16[896,768]{1,0:T(8,128)(2,1)S(1)} %bitcast.79, bf16[896,768]{1,0:T(8,128)(2,1)S(1)} %bitcast.85, bf16[896,768]{1,0:T(8,128)(2,1)} %bitcast.7.refs_2_.refs_1_, bf16[896,768]{1,0:T(8,128)(2,1)} %collective-permute-done.2.refs_3_.refs_2_, ...), custom_call_target="tpu_custom_call" | custom-call | flops 5549064192 | bytes 10665984 | tf_op jit(solution)/shard_map/pallas_call | solution.py:103
  136.7 1.6 collective-permute-start.7
  140.9 2.2 slice.163
  144.3 25.7 %collective-permute-done.7.refs_7_.refs_3_ = bf16[896,768]{1,0:T(8,128)(2,1)} collective-permute-done((bf16[896,768]{1,0:T(8,128)(2,1)S(1)}, bf16[896,768]{1,0:T(8,128)(2,1)}, u32[]{:S(2)}, u32[]{:S(2)}) %collective-permute-start.7) | collective-permute-done | bytes 1376288 | tf_op jit(solution)/shard_map/ppermute | solution.py:35
  169.9 1.5 collective-permute-done.8.refs_10_.refs_5_
  171.5 2.0 slice.165
  173.5 2.0 slice.166
  175.5 23.1 %collective-permute-done.11.refs_8_.refs_3_ = bf16[896,768]{1,0:T(8,128)(2,1)} collective-permute-done((bf16[896,768]{1,0:T(8,128)(2,1)}, bf16[896,768]{1,0:T(8,128)(2,1)}, u32[]{:S(2)}, u32[]{:S(2)}) %collective-permute-start.11) | collective-permute-done | bytes 1376288 | tf_op jit(solution)/shard_map/ppermute | solution.py:35
  199.8 2.0 slice.167
  201.8 2.0 slice.168
  203.8 16.2 %shard_map.18 = bf16[4,448,896]{2,1,0:T(8,128)(2,1)} custom-call(s32[2]{0:T(128)S(1)} %pad_add_fusion.low_ref, bf16[896,768]{1,0:T(8,128)(2,1)S(1)} %bitcast.80, bf16[896,768]{1,0:T(8,128)(2,1)S(1)} %bitcast.88, bf16[896,768]{1,0:T(8,128)(2,1)} %bitcast.7.refs_2_.refs_1_, bf16[896,768]{1,0:T(8,128)(2,1)} %collective-permute-done.2.refs_3_.refs_2_, ...), custom_call_target="tpu_custom_call" | custom-call | flops 7398752256 | bytes 19726336 | tf_op jit(solution)/shard_map/pallas_call | solution.py:103
  220.0 13.3 %all-reduce.5.cloned.1.call-done = bf16[3,448,896]{2,1,0:T(8,128)(2,1)} async-done(((bf16[3,448,896]{2,1,0:T(8,128)(2,1)}), bf16[3,448,896]{2,1,0:T(8,128)(2,1)}) %all-reduce.5.cloned.1.call-update) | async-done | bytes 2408464 | tf_op jit(solution)/shard_map/psum | solution.py:262
  233.3 1.5 collective-permute-start.10
  238.9 13.1 %collective-permute-done.10.refs_8_ = bf16[448,768]{1,0:T(8,128)(2,1)} collective-permute-done((bf16[448,768]{1,0:T(8,128)(2,1)}, bf16[448,768]{1,0:T(8,128)(2,1)}, u32[]{:S(2)}, u32[]{:S(2)}) %collective-permute-start.10) | collective-permute-done | bytes 688160 | tf_op jit(solution)/shard_map/ppermute | solution.py:35
  253.6 2.5 pad_maximum_fusion.4.refs_7_
  256.1 12.1 %collective-permute-done.5.refs_7_ = bf16[448,768]{1,0:T(8,128)(2,1)S(1)} collective-permute-done((bf16[448,768]{1,0:T(8,128)(2,1)}, bf16[448,768]{1,0:T(8,128)(2,1)S(1)}, u32[]{:S(2)}, u32[]{:S(2)}) %collective-permute-start.5) | collective-permute-done | bytes 688160 | tf_op jit(solution)/shard_map/ppermute | solution.py:35
  269.5 12.0 %collective-permute-done.13.refs_7_ = bf16[448,768]{1,0:T(8,128)(2,1)S(1)} collective-permute-done((bf16[448,768]{1,0:T(8,128)(2,1)}, bf16[448,768]{1,0:T(8,128)(2,1)S(1)}, u32[]{:S(2)}, u32[]{:S(2)}) %collective-permute-start.13) | collective-permute-done | bytes 688160 | tf_op jit(solution)/shard_map/ppermute | solution.py:35
  284.4 9.9 %shard_map.17 = bf16[2,448,896]{2,1,0:T(8,128)(2,1)} custom-call(s32[1]{0:T(128)} %bitcast.1.low_ref, bf16[896,768]{1,0:T(8,128)(2,1)S(1)} %bitcast.81, bf16[896,768]{1,0:T(8,128)(2,1)S(1)} %bitcast.89, bf16[896,768]{1,0:T(8,128)(2,1)} %bitcast.7.refs_2_.refs_1_, bf16[896,768]{1,0:T(8,128)(2,1)} %collective-permute-done.2.refs_3_.refs_2_, ...), custom_call_target="tpu_custom_call" | custom-call | flops 3699376128 | bytes 13991936 | tf_op jit(solution)/shard_map/pallas_call | solution.py:103
  294.2 63.8 %all-reduce.7.cloned.1.call-done = bf16[4,448,896]{2,1,0:T(8,128)(2,1)} async-done(((bf16[4,448,896]{2,1,0:T(8,128)(2,1)}), bf16[4,448,896]{2,1,0:T(8,128)(2,1)}) %all-reduce.7.cloned.1.call-update) | async-done | bytes 3211280 | tf_op jit(solution)/shard_map/psum | solution.py:275
  359.4 3.5 slice_bitcast_fusion.1
  368.2 15.4 %collective-permute-done.23.theirs = bf16[448,896]{1,0:T(8,128)(2,1)S(1)} collective-permute-done((bf16[448,896]{1,0:T(8,128)(2,1)S(1)}, bf16[448,896]{1,0:T(8,128)(2,1)S(1)}, u32[]{:S(2)}, u32[]{:S(2)}) %collective-permute-start.23) | collective-permute-done | bytes 802848 | tf_op jit(solution)/shard_map/ppermute | solution.py:35
  386.0 43.7 %all-reduce.9.cloned.1.call-done = bf16[2,448,896]{2,1,0:T(8,128)(2,1)} async-done(((bf16[2,448,896]{2,1,0:T(8,128)(2,1)}), bf16[2,448,896]{2,1,0:T(8,128)(2,1)}) %all-reduce.9.cloned.1.call-update) | async-done | bytes 1605648 | tf_op jit(solution)/shard_map/psum | solution.py:275
  429.7 2.5 slice_bitcast_fusion.5
  432.2 2.4 collective-permute-start.17
  436.7 17.3 %collective-permute-done.17.theirs = bf16[448,896]{1,0:T(8,128)(2,1)S(1)} collective-permute-done((bf16[448,896]{1,0:T(8,128)(2,1)S(1)}, bf16[448,896]{1,0:T(8,128)(2,1)S(1)}, u32[]{:S(2)}, u32[]{:S(2)}) %collective-permute-start.17) | collective-permute-done | bytes 802848 | tf_op jit(solution)/shard_map/ppermute | solution.py:35
  457.7 7.6 dynamic_update_slice.3.gram_in
  470.8 2.6 shard_map.22.gram_in
  473.5 2.5 shard_map.23.gram_in
  476.0 2.8 shard_map.24.gram_in
  480.2 2.5 shard_map.26.refs_0_
  482.6 14.5 %shard_map.29.refs_3_ = bf16[896,768]{1,0:T(8,128)(2,1)S(1)} custom-call(s32[1]{0:T(128)} %bitcast.me_ref, bf16[8,896,896]{2,1,0:T(8,128)(2,1)} %shard_map.26.refs_0_, bf16[896,768]{1,0:T(8,128)(2,1)S(1)} %bitcast.90, bf16[896,768]{1,0:T(8,128)(2,1)} %collective-permute-done.3.refs_4_.refs_2_, bf16[896,768]{1,0:T(8,128)(2,1)} %collective-permute-done.7.refs_7_.refs_3_, ...), custom_call_target="tpu_custom_call" | custom-call | flops 9865003008 | bytes 23855104 | tf_op jit(solution)/shard_map/pallas_call | solution.py:201
  499.7 5.3 collective-permute-done.27.refs_9_
  510.4 14.8 %shard_map.27.refs_3_ = bf16[896,768]{1,0:T(8,128)(2,1)S(1)} custom-call(s32[1]{0:T(128)} %bitcast.me_ref, bf16[8,896,896]{2,1,0:T(8,128)(2,1)} %shard_map.26.refs_0_, bf16[896,768]{1,0:T(8,128)(2,1)S(1)} %bitcast.82, bf16[896,768]{1,0:T(8,128)(2,1)} %collective-permute-done.2.refs_3_.refs_2_, bf16[896,768]{1,0:T(8,128)(2,1)} %copy-done.30, ...), custom_call_target="tpu_custom_call" | custom-call | flops 9865003008 | bytes 23855104 | tf_op jit(solution)/shard_map/pallas_call | solution.py:201
  527.5 4.1 collective-permute-done.35.refs_9_
  531.5 4.1 collective-permute-done.36.refs_10_
  539.0 14.9 %shard_map.31.refs_3_ = bf16[896,768]{1,0:T(8,128)(2,1)S(1)} custom-call(s32[1]{0:T(128)} %bitcast.me_ref, bf16[8,896,896]{2,1,0:T(8,128)(2,1)} %shard_map.26.refs_0_, bf16[896,768]{1,0:T(8,128)(2,1)} %bitcast.7.refs_2_.refs_1_, bf16[896,768]{1,0:T(8,128)(2,1)} %collective-permute-done.4.refs_5_.refs_2_, ...), custom_call_target="tpu_custom_call" | custom-call | flops 9865003008 | bytes 23855104 | tf_op jit(solution)/shard_map/pallas_call | solution.py:201
  555.0 10.0 %all-gather.6.cloned.1.call-done.refs_1_ = bf16[7168,768]{1,0:T(8,128)(2,1)} async-done(((bf16[896,768]{1,0:T(8,128)(2,1)}), bf16[7168,768]{1,0:T(8,128)(2,1)}) %all-gather.6.cloned.1.call-update) | async-done | bytes 11010064 | tf_op jit(solution)/shard_map/all_gather | solution.py:290
  566.3 15.4 %shard_map.30 = bf16[896,768]{1,0:T(8,128)(2,1)S(1)} custom-call(s32[1]{0:T(128)} %bitcast.me_ref, bf16[8,896,896]{2,1,0:T(8,128)(2,1)} %shard_map.26.refs_0_, bf16[7168,768]{1,0:T(8,128)(2,1)} %all-gather.6.cloned.1.call-done.refs_1_, bf16[896,768]{1,0:T(8,128)(2,1)S(1)} %bitcast.91, bf16[896,768]{1,0:T(8,128)(2,1)S(1)} %copy-done.8), custom_call_target="tpu_custom_call" | custom-call | flops 9865003008 | bytes 23855104 | tf_op jit(solution)/shard_map/pallas_call | solution.py:201
  582.9 4.6 all-to-all-start.4
  587.5 44.8 %all-gather.4.cloned.1.call-done.refs_1_ = bf16[7168,768]{1,0:T(8,128)(2,1)} async-done(((bf16[896,768]{1,0:T(8,128)(2,1)}), bf16[7168,768]{1,0:T(8,128)(2,1)}) %all-gather.4.cloned.1.call-update) | async-done | bytes 11010064 | tf_op jit(solution)/shard_map/all_gather | solution.py:290
  633.6 16.5 %shard_map.28 = bf16[896,768]{1,0:T(8,128)(2,1)} custom-call(s32[1]{0:T(128)} %bitcast.me_ref, bf16[8,896,896]{2,1,0:T(8,128)(2,1)} %shard_map.26.refs_0_, bf16[7168,768]{1,0:T(8,128)(2,1)} %all-gather.4.cloned.1.call-done.refs_1_, bf16[896,768]{1,0:T(8,128)(2,1)S(1)} %bitcast.83, bf16[896,768]{1,0:T(8,128)(2,1)S(1)} %copy-done.10), custom_call_target="tpu_custom_call" | custom-call | flops 9865003008 | bytes 23855104 | tf_op jit(solution)/shard_map/pallas_call | solution.py:201
  650.1 4.6 all-to-all-start.3
  654.7 44.8 %all-gather.8.cloned.1.call-done.refs_1_ = bf16[7168,768]{1,0:T(8,128)(2,1)} async-done(((bf16[896,768]{1,0:T(8,128)(2,1)}), bf16[7168,768]{1,0:T(8,128)(2,1)}) %all-gather.8.cloned.1.call-update) | async-done | bytes 11010064 | tf_op jit(solution)/shard_map/all_gather | solution.py:290
  700.8 17.8 %shard_map.32 = bf16[896,768]{1,0:T(8,128)(2,1)} custom-call(s32[1]{0:T(128)} %bitcast.me_ref, bf16[8,896,896]{2,1,0:T(8,128)(2,1)} %shard_map.26.refs_0_, bf16[7168,768]{1,0:T(8,128)(2,1)} %all-gather.8.cloned.1.call-done.refs_1_, bf16[896,768]{1,0:T(8,128)(2,1)} %bitcast.7.refs_2_.refs_1_, bf16[896,768]{1,0:T(8,128)(2,1)S(1)} %copy-done.12), custom_call_target="tpu_custom_call" | custom-call | flops 9865003008 | bytes 23855104 | tf_op jit(solution)/shard_map/pallas_call | solution.py:201
  718.7 4.6 all-to-all-start.5
  723.3 1.7 fusion.11
  725.0 1.7 fusion.10
  726.8 29.7 %all-to-all-done.5 = bf16[4,224,768]{2,1,0:T(8,128)(2,1)S(1)} async-done(((bf16[4,224,768]{2,1,0:T(8,128)(2,1)}), bf16[4,224,768]{2,1,0:T(8,128)(2,1)S(1)}, u32[]{:S(2)}, u32[]{:S(2)}) %all-to-all-start.5) | async-done | bytes 1376288 | tf_op jit(solution)/shard_map/all_to_all | solution.py:237
  757.2 1.7 fusion.8
  759.0 1.7 fusion.7
  761.4 1.7 fusion.5
  763.2 1.7 fusion.4
  765.6 1.7 fusion.2
  767.4 1.7 fusion.1
  (157 shorter events, 64.8 us)
Async XLA Ops:
  11.0 39.1 %all-to-all-start = ((bf16[4,224,768]{2,1,0:T(8,128)(2,1)}), bf16[4,224,768]{2,1,0:T(8,128)(2,1)S(1)}, u32[]{:S(2)}, u32[]{:S(2)}) async-start(bf16[4,224,768]{2,1,0:T(8,128)(2,1)} %bitcast.2), calls=%async_computation | async-start | bytes 2752512 | tf_op jit(solution)/shard_map/all_to_all | solution.py:237
  50.0 36.1 %all-to-all-start.1 = ((bf16[4,224,768]{2,1,0:T(8,128)(2,1)}), bf16[4,224,768]{2,1,0:T(8,128)(2,1)S(1)}, u32[]{:S(2)}, u32[]{:S(2)}) async-start(bf16[4,224,768]{2,1,0:T(8,128)(2,1)} %bitcast.94), calls=%async_computation.1 | async-start | bytes 2752512 | tf_op jit(solution)/shard_map/all_to_all | solution.py:237
  53.6 31.2 %collective-permute-start = (bf16[896,768]{1,0:T(8,128)(2,1)S(1)}, bf16[896,768]{1,0:T(8,128)(2,1)S(1)}, u32[]{:S(2)}, u32[]{:S(2)}) collective-permute-start(bf16[896,768]{1,0:T(8,128)(2,1)S(1)} %bitcast.76), channel_id=1, source_target_pairs={{0,8},{4,12},{8,0},{12,4},{16,24},{20,28},{24,16},{28,20},{1,9},{5... | collective-permute-start | bytes 4128776 | tf_op jit(solution)/shard_map/ppermute | solution.py:35
  55.1 31.0 %collective-permute-start.1 = (bf16[896,768]{1,0:T(8,128)(2,1)S(1)}, bf16[896,768]{1,0:T(8,128)(2,1)}, u32[]{:S(2)}, u32[]{:S(2)}) collective-permute-start(bf16[896,768]{1,0:T(8,128)(2,1)S(1)} %bitcast.77), channel_id=1, source_target_pairs={{0,16},{4,20},{8,24},{12,28},{16,0},{20,4},{24,8},{28,12},{1,17},{... | collective-permute-start | bytes 4128776 | tf_op jit(solution)/shard_map/ppermute | solution.py:35
  86.1 36.3 %all-to-all-start.2 = ((bf16[4,224,768]{2,1,0:T(8,128)(2,1)}), bf16[4,224,768]{2,1,0:T(8,128)(2,1)}, u32[]{:S(2)}, u32[]{:S(2)}) async-start(bf16[4,224,768]{2,1,0:T(8,128)(2,1)} %bitcast.95), calls=%async_computation.2 | async-start | bytes 2752512 | tf_op jit(solution)/shard_map/all_to_all | solution.py:237
  90.8 142.5 %all-reduce.5.cloned.1.call-start = ((), (), s32[]{:S(2)}) async-start(), calls=%async_computation.6 | async-start | bytes 4816896 | tf_op jit(solution)/shard_map/psum | solution.py:262
  90.8 31.6 %collective-permute-start.2 = (bf16[896,768]{1,0:T(8,128)(2,1)S(1)}, bf16[896,768]{1,0:T(8,128)(2,1)}, u32[]{:S(2)}, u32[]{:S(2)}) collective-permute-start(bf16[896,768]{1,0:T(8,128)(2,1)S(1)} %bitcast.78), channel_id=1, source_target_pairs={{0,4},{4,0},{8,12},{12,8},{16,20},{20,16},{24,28},{28,24},{1,5},{5... | collective-permute-start | bytes 4128776 | tf_op jit(solution)/shard_map/ppermute | solution.py:35
  90.8 31.6 %collective-permute-start.3 = (bf16[896,768]{1,0:T(8,128)(2,1)S(1)}, bf16[896,768]{1,0:T(8,128)(2,1)}, u32[]{:S(2)}, u32[]{:S(2)}) collective-permute-start(bf16[896,768]{1,0:T(8,128)(2,1)S(1)} %bitcast.84), channel_id=1, source_target_pairs={{0,4},{4,0},{8,12},{12,8},{16,20},{20,16},{24,28},{28,24},{1,5},{5... | collective-permute-start | bytes 4128776 | tf_op jit(solution)/shard_map/ppermute | solution.py:35
  122.4 3.5 collective-permute-start.4
  136.7 221.4 %all-reduce.7.cloned.1.call-start = ((), (), s32[]{:S(2)}) async-start(), calls=%async_computation.7 | async-start | bytes 6422528 | tf_op jit(solution)/shard_map/psum | solution.py:275
  136.7 33.2 %collective-permute-start.7 = (bf16[896,768]{1,0:T(8,128)(2,1)S(1)}, bf16[896,768]{1,0:T(8,128)(2,1)}, u32[]{:S(2)}, u32[]{:S(2)}) collective-permute-start(bf16[896,768]{1,0:T(8,128)(2,1)S(1)} %bitcast.86), channel_id=1, source_target_pairs={{0,8},{4,12},{8,0},{12,4},{16,24},{20,28},{24,16},{28,20},{1,9},{5... | collective-permute-start | bytes 4128776 | tf_op jit(solution)/shard_map/ppermute | solution.py:35
  138.3 33.2 %collective-permute-start.8 = (bf16[896,768]{1,0:T(8,128)(2,1)S(1)}, bf16[896,768]{1,0:T(8,128)(2,1)}, u32[]{:S(2)}, u32[]{:S(2)}) collective-permute-start(bf16[896,768]{1,0:T(8,128)(2,1)S(1)} %bitcast.87), channel_id=1, source_target_pairs={{0,16},{4,20},{8,24},{12,28},{16,0},{20,4},{24,8},{28,12},{1,17},{... | collective-permute-start | bytes 4128776 | tf_op jit(solution)/shard_map/ppermute | solution.py:35
  139.8 58.8 %collective-permute-start.11 = (bf16[896,768]{1,0:T(8,128)(2,1)}, bf16[896,768]{1,0:T(8,128)(2,1)}, u32[]{:S(2)}, u32[]{:S(2)}) collective-permute-start(bf16[896,768]{1,0:T(8,128)(2,1)} %bitcast.7.refs_2_.refs_1_), channel_id=1, source_target_pairs={{0,8},{4,12},{8,0},{12,4},{16,24},{20,28},{24,16},{28,20},{1,9},{5... | collective-permute-start | bytes 4128776 | tf_op jit(solution)/shard_map/ppermute | solution.py:35
  140.3 59.5 %collective-permute-start.12 = (bf16[896,768]{1,0:T(8,128)(2,1)}, bf16[896,768]{1,0:T(8,128)(2,1)}, u32[]{:S(2)}, u32[]{:S(2)}) collective-permute-start(bf16[896,768]{1,0:T(8,128)(2,1)} %bitcast.7.refs_2_.refs_1_), channel_id=1, source_target_pairs={{0,16},{4,20},{8,24},{12,28},{16,0},{20,4},{24,8},{28,12},{1,17},{... | collective-permute-start | bytes 4128776 | tf_op jit(solution)/shard_map/ppermute | solution.py:35
  233.3 196.4 %all-reduce.9.cloned.1.call-start = ((), (), s32[]{:S(2)}) async-start(), calls=%async_computation.8 | async-start | bytes 3211264 | tf_op jit(solution)/shard_map/psum | solution.py:275
  233.3 18.7 %collective-permute-start.10 = (bf16[448,768]{1,0:T(8,128)(2,1)}, bf16[448,768]{1,0:T(8,128)(2,1)}, u32[]{:S(2)}, u32[]{:S(2)}) collective-permute-start(bf16[448,768]{1,0:T(8,128)(2,1)} %slice.166), channel_id=1, source_target_pairs={{0,8},{4,12},{8,0},{12,4},{16,24},{20,28},{24,16},{28,20},{1,9},{5... | collective-permute-start | bytes 2064392 | tf_op jit(solution)/shard_map/ppermute | solution.py:35
  234.9 18.7 %collective-permute-start.9 = (bf16[448,768]{1,0:T(8,128)(2,1)}, bf16[448,768]{1,0:T(8,128)(2,1)}, u32[]{:S(2)}, u32[]{:S(2)}) collective-permute-start(bf16[448,768]{1,0:T(8,128)(2,1)} %slice.165), channel_id=1, source_target_pairs={{0,16},{4,20},{8,24},{12,28},{16,0},{20,4},{24,8},{28,12},{1,17},{... | collective-permute-start | bytes 2064392 | tf_op jit(solution)/shard_map/ppermute | solution.py:35
  236.4 31.9 %collective-permute-start.5 = (bf16[448,768]{1,0:T(8,128)(2,1)}, bf16[448,768]{1,0:T(8,128)(2,1)S(1)}, u32[]{:S(2)}, u32[]{:S(2)}) collective-permute-start(bf16[448,768]{1,0:T(8,128)(2,1)} %slice.163), channel_id=1, source_target_pairs={{0,16},{4,20},{8,24},{12,28},{16,0},{20,4},{24,8},{28,12},{1,17},{... | collective-permute-start | bytes 2064392 | tf_op jit(solution)/shard_map/ppermute | solution.py:35
  236.9 31.3 %collective-permute-start.6 = (bf16[448,768]{1,0:T(8,128)(2,1)S(1)}, bf16[448,768]{1,0:T(8,128)(2,1)S(1)}, u32[]{:S(2)}, u32[]{:S(2)}) collective-permute-start(bf16[448,768]{1,0:T(8,128)(2,1)S(1)} %slice.164), channel_id=1, source_target_pairs={{0,8},{4,12},{8,0},{12,4},{16,24},{20,28},{24,16},{28,20},{1,9},{5... | collective-permute-start | bytes 2064392 | tf_op jit(solution)/shard_map/ppermute | solution.py:35
  237.5 44.0 %collective-permute-start.13 = (bf16[448,768]{1,0:T(8,128)(2,1)}, bf16[448,768]{1,0:T(8,128)(2,1)S(1)}, u32[]{:S(2)}, u32[]{:S(2)}) collective-permute-start(bf16[448,768]{1,0:T(8,128)(2,1)} %slice.167), channel_id=1, source_target_pairs={{0,16},{4,20},{8,24},{12,28},{16,0},{20,4},{24,8},{28,12},{1,17},{... | collective-permute-start | bytes 2064392 | tf_op jit(solution)/shard_map/ppermute | solution.py:35
  252.1 29.4 %collective-permute-start.14 = (bf16[448,768]{1,0:T(8,128)(2,1)}, bf16[448,768]{1,0:T(8,128)(2,1)S(1)}, u32[]{:S(2)}, u32[]{:S(2)}) collective-permute-start(bf16[448,768]{1,0:T(8,128)(2,1)} %slice.168), channel_id=1, source_target_pairs={{0,8},{4,12},{8,0},{12,4},{16,24},{20,28},{24,16},{28,20},{1,9},{5... | collective-permute-start | bytes 2064392 | tf_op jit(solution)/shard_map/ppermute | solution.py:35
  268.2 13.2 %copy-start.25 = (bf16[448,768]{1,0:T(8,128)(2,1)}, bf16[448,768]{1,0:T(8,128)(2,1)S(1)}, u32[]{:S(2)}) copy-start(bf16[448,768]{1,0:T(8,128)(2,1)S(1)} %collective-permute-done.5.refs_7_) | copy-start | bytes 2064388
  268.2 13.2 %copy-start.27 = (bf16[448,768]{1,0:T(8,128)(2,1)}, bf16[448,768]{1,0:T(8,128)(2,1)S(1)}, u32[]{:S(2)}) copy-start(bf16[448,768]{1,0:T(8,128)(2,1)S(1)} %collective-permute-done.6.refs_8_) | copy-start | bytes 2064388
  358.1 206.9 %all-gather.6.cloned.1.call-start = ((), (), s32[]{:S(2)}) async-start(), calls=%async_computation.10 | async-start | bytes 12386304 | tf_op jit(solution)/shard_map/all_gather | solution.py:290
  359.3 3.6 copy-start.2
  359.3 8.0 %collective-permute-start.24 = (bf16[448,896]{1,0:T(8,128)(2,1)S(1)}, bf16[448,896]{1,0:T(8,128)(2,1)S(1)}, u32[]{:S(2)}, u32[]{:S(2)}) collective-permute-start(bf16[448,896]{1,0:T(8,128)(2,1)S(1)} %slice_bitcast_fusion.mine), channel_id=1, source_target_pairs={{0,4},{4,0},{8,12},{12,8},{16,20},{20,16},{24,28},{28,24},{1,5},{5... | collective-permute-start | bytes 2408456 | tf_op jit(solution)/shard_map/ppermute | solution.py:35
  362.9 20.7 %collective-permute-start.23 = (bf16[448,896]{1,0:T(8,128)(2,1)S(1)}, bf16[448,896]{1,0:T(8,128)(2,1)S(1)}, u32[]{:S(2)}, u32[]{:S(2)}) collective-permute-start(bf16[448,896]{1,0:T(8,128)(2,1)S(1)} %get-tuple-element.51.mine), channel_id=1, source_target_pairs={{0,8},{4,12},{8,0},{12,4},{16,24},{20,28},{24,16},{28,20},{1,9},{5... | collective-permute-start | bytes 2408456 | tf_op jit(solution)/shard_map/ppermute | solution.py:35
  365.3 67.0 %collective-permute-start.21 = (bf16[448,896]{1,0:T(8,128)(2,1)}, bf16[448,896]{1,0:T(8,128)(2,1)}, u32[]{:S(2)}, u32[]{:S(2)}) collective-permute-start(bf16[448,896]{1,0:T(8,128)(2,1)} %get-tuple-element.52), channel_id=1, source_target_pairs={{0,4},{4,0},{8,12},{12,8},{16,20},{20,16},{24,28},{28,24},{1,5},{5... | collective-permute-start | bytes 2408456 | tf_op jit(solution)/shard_map/ppermute | solution.py:35
  365.3 70.2 %collective-permute-start.22 = (bf16[448,896]{1,0:T(8,128)(2,1)}, bf16[448,896]{1,0:T(8,128)(2,1)}, u32[]{:S(2)}, u32[]{:S(2)}) collective-permute-start(bf16[448,896]{1,0:T(8,128)(2,1)} %get-tuple-element.52), channel_id=1, source_target_pairs={{0,8},{4,12},{8,0},{12,4},{16,24},{20,28},{24,16},{28,20},{1,9},{5... | collective-permute-start | bytes 2408456 | tf_op jit(solution)/shard_map/ppermute | solution.py:35
  365.8 69.7 %collective-permute-start.20 = (bf16[448,896]{1,0:T(8,128)(2,1)S(1)}, bf16[448,896]{1,0:T(8,128)(2,1)}, u32[]{:S(2)}, u32[]{:S(2)}) collective-permute-start(bf16[448,896]{1,0:T(8,128)(2,1)S(1)} %get-tuple-element.53.mine), channel_id=1, source_target_pairs={{0,16},{4,20},{8,24},{12,28},{16,0},{20,4},{24,8},{28,12},{1,17},{... | collective-permute-start | bytes 2408456 | tf_op jit(solution)/shard_map/ppermute | solution.py:35
  368.2 67.8 %collective-permute-start.18 = (bf16[448,896]{1,0:T(8,128)(2,1)}, bf16[448,896]{1,0:T(8,128)(2,1)}, u32[]{:S(2)}, u32[]{:S(2)}) collective-permute-start(bf16[448,896]{1,0:T(8,128)(2,1)} %get-tuple-element.54), channel_id=1, source_target_pairs={{0,4},{4,0},{8,12},{12,8},{16,20},{20,16},{24,28},{28,24},{1,5},{5... | collective-permute-start | bytes 2408456 | tf_op jit(solution)/shard_map/ppermute | solution.py:35
  384.5 51.6 %collective-permute-start.19 = (bf16[448,896]{1,0:T(8,128)(2,1)}, bf16[448,896]{1,0:T(8,128)(2,1)}, u32[]{:S(2)}, u32[]{:S(2)}) collective-permute-start(bf16[448,896]{1,0:T(8,128)(2,1)} %get-tuple-element.54), channel_id=1, source_target_pairs={{0,16},{4,20},{8,24},{12,28},{16,0},{20,4},{24,8},{28,12},{1,17},{... | collective-permute-start | bytes 2408456 | tf_op jit(solution)/shard_map/ppermute | solution.py:35
  429.7 26.7 %copy-start.29 = (bf16[3,448,896]{2,1,0:T(8,128)(2,1)S(1)}, bf16[3,448,896]{2,1,0:T(8,128)(2,1)}, u32[]{:S(2)}) copy-start(bf16[3,448,896]{2,1,0:T(8,128)(2,1)} %all-reduce.5.cloned.1.call-done) | copy-start | bytes 7225348
  432.2 21.7 %collective-permute-start.17 = (bf16[448,896]{1,0:T(8,128)(2,1)S(1)}, bf16[448,896]{1,0:T(8,128)(2,1)S(1)}, u32[]{:S(2)}, u32[]{:S(2)}) collective-permute-start(bf16[448,896]{1,0:T(8,128)(2,1)S(1)} %get-tuple-element.55.mine), channel_id=1, source_target_pairs={{0,24},{4,28},{8,16},{12,20},{16,8},{20,12},{24,0},{28,4},{1,25},{... | collective-permute-start | bytes 2408456 | tf_op jit(solution)/shard_map/ppermute | solution.py:35
  435.5 19.4 %collective-permute-start.15 = (bf16[448,896]{1,0:T(8,128)(2,1)}, bf16[448,896]{1,0:T(8,128)(2,1)S(1)}, u32[]{:S(2)}, u32[]{:S(2)}) collective-permute-start(bf16[448,896]{1,0:T(8,128)(2,1)} %get-tuple-element.56), channel_id=1, source_target_pairs={{0,4},{4,0},{8,12},{12,8},{16,20},{20,16},{24,28},{28,24},{1,5},{5... | collective-permute-start | bytes 2408456 | tf_op jit(solution)/shard_map/ppermute | solution.py:35
  435.5 47.1 %collective-permute-start.29 = (bf16[896,768]{1,0:T(8,128)(2,1)}, bf16[896,768]{1,0:T(8,128)(2,1)}, u32[]{:S(2)}, u32[]{:S(2)}) collective-permute-start(bf16[896,768]{1,0:T(8,128)(2,1)} %collective-permute-done.7.refs_7_.refs_3_), channel_id=1, source_target_pairs={{0,4},{4,0},{8,12},{12,8},{16,20},{20,16},{24,28},{28,24},{1,5},{5... | collective-permute-start | bytes 4128776 | tf_op jit(solution)/shard_map/ppermute | solution.py:35
  436.0 46.6 %collective-permute-start.30 = (bf16[896,768]{1,0:T(8,128)(2,1)}, bf16[896,768]{1,0:T(8,128)(2,1)}, u32[]{:S(2)}, u32[]{:S(2)}) collective-permute-start(bf16[896,768]{1,0:T(8,128)(2,1)} %collective-permute-done.8.refs_10_.refs_5_), channel_id=1, source_target_pairs={{0,4},{4,0},{8,12},{12,8},{16,20},{20,16},{24,28},{28,24},{1,5},{5... | collective-permute-start | bytes 4128776 | tf_op jit(solution)/shard_map/ppermute | solution.py:35
  436.1 44.0 %collective-permute-start.16 = (bf16[448,896]{1,0:T(8,128)(2,1)}, bf16[448,896]{1,0:T(8,128)(2,1)}, u32[]{:S(2)}, u32[]{:S(2)}) collective-permute-start(bf16[448,896]{1,0:T(8,128)(2,1)} %get-tuple-element.56), channel_id=1, source_target_pairs={{0,24},{4,28},{8,16},{12,20},{16,8},{20,12},{24,0},{28,4},{1,25},{... | collective-permute-start | bytes 2408456 | tf_op jit(solution)/shard_map/ppermute | solution.py:35
  454.9 27.7 %collective-permute-start.31 = (bf16[448,768]{1,0:T(8,128)(2,1)}, bf16[448,768]{1,0:T(8,128)(2,1)}, u32[]{:S(2)}, u32[]{:S(2)}) collective-permute-start(bf16[448,768]{1,0:T(8,128)(2,1)} %collective-permute-done.9.refs_7_), channel_id=1, source_target_pairs={{0,4},{4,0},{8,12},{12,8},{16,20},{20,16},{24,28},{28,24},{1,5},{5... | collective-permute-start | bytes 2064392 | tf_op jit(solution)/shard_map/ppermute | solution.py:35
  455.9 26.8 %collective-permute-start.32 = (bf16[448,768]{1,0:T(8,128)(2,1)}, bf16[448,768]{1,0:T(8,128)(2,1)}, u32[]{:S(2)}, u32[]{:S(2)}) collective-permute-start(bf16[448,768]{1,0:T(8,128)(2,1)} %collective-permute-done.10.refs_8_), channel_id=1, source_target_pairs={{0,4},{4,0},{8,12},{12,8},{16,20},{20,16},{24,28},{28,24},{1,5},{5... | collective-permute-start | bytes 2064392 | tf_op jit(solution)/shard_map/ppermute | solution.py:35
  465.3 1.1 copy-start.3
  467.6 1.4 copy-start.1
  467.6 2.0 copy-start.16
  476.0 2.8 copy-start.5
  476.0 2.8 copy-start.18
  478.8 1.4 copy-start.20
  498.3 28.7 %copy-start.22 = (bf16[448,768]{1,0:T(8,128)(2,1)S(1)}, bf16[448,768]{1,0:T(8,128)(2,1)}, u32[]{:S(2)}) copy-start(bf16[448,768]{1,0:T(8,128)(2,1)} %copy-done.21) | copy-start | bytes 2064388
  498.3 133.9 %all-gather.4.cloned.1.call-start = ((), (), s32[]{:S(2)}) async-start(), calls=%async_computation.9 | async-start | bytes 12386304 | tf_op jit(solution)/shard_map/all_gather | solution.py:290
  498.6 7.3 collective-permute-start.25
  498.7 7.3 collective-permute-start.26
  499.2 5.8 collective-permute-start.27
  499.3 6.7 collective-permute-start.28
  509.2 1.2 copy-start.28
  526.3 173.2 %all-gather.8.cloned.1.call-start = ((), (), s32[]{:S(2)}) async-start(), calls=%async_computation.11 | async-start | bytes 12386304 | tf_op jit(solution)/shard_map/all_gather | solution.py:290
  526.4 9.3 %collective-permute-start.33 = (bf16[896,768]{1,0:T(8,128)(2,1)}, bf16[896,768]{1,0:T(8,128)(2,1)S(1)}, u32[]{:S(2)}, u32[]{:S(2)}) collective-permute-start(bf16[896,768]{1,0:T(8,128)(2,1)} %collective-permute-done.11.refs_8_.refs_3_), channel_id=1, source_target_pairs={{0,4},{4,0},{8,12},{12,8},{16,20},{20,16},{24,28},{28,24},{1,5},{5... | collective-permute-start | bytes 4128776 | tf_op jit(solution)/shard_map/ppermute | solution.py:35
  526.6 9.1 %collective-permute-start.34 = (bf16[896,768]{1,0:T(8,128)(2,1)}, bf16[896,768]{1,0:T(8,128)(2,1)S(1)}, u32[]{:S(2)}, u32[]{:S(2)}) collective-permute-start(bf16[896,768]{1,0:T(8,128)(2,1)} %collective-permute-done.12.refs_11_.refs_5_), channel_id=1, source_target_pairs={{0,4},{4,0},{8,12},{12,8},{16,20},{20,16},{24,28},{28,24},{1,5},{5... | collective-permute-start | bytes 4128776 | tf_op jit(solution)/shard_map/ppermute | solution.py:35
  526.9 4.6 collective-permute-start.35
  527.1 8.5 %collective-permute-start.36 = (bf16[448,768]{1,0:T(8,128)(2,1)}, bf16[448,768]{1,0:T(8,128)(2,1)S(1)}, u32[]{:S(2)}, u32[]{:S(2)}) collective-permute-start(bf16[448,768]{1,0:T(8,128)(2,1)} %copy-done.23), channel_id=1, source_target_pairs={{0,4},{4,0},{8,12},{12,8},{16,20},{20,16},{24,28},{28,24},{1,5},{5... | collective-permute-start | bytes 2064392 | tf_op jit(solution)/shard_map/ppermute | solution.py:35
  565.0 1.3 copy-start.8
  582.9 67.2 %all-to-all-start.4 = ((bf16[4,224,768]{2,1,0:T(8,128)(2,1)}), bf16[4,224,768]{2,1,0:T(8,128)(2,1)}, u32[]{:S(2)}, u32[]{:S(2)}) async-start(bf16[4,224,768]{2,1,0:T(8,128)(2,1)} %bitcast.92), calls=%async_computation.4 | async-start | bytes 2752512 | tf_op jit(solution)/shard_map/all_to_all | solution.py:237
  632.2 1.3 copy-start.10
  650.1 68.6 %all-to-all-start.3 = ((bf16[4,224,768]{2,1,0:T(8,128)(2,1)}), bf16[4,224,768]{2,1,0:T(8,128)(2,1)}, u32[]{:S(2)}, u32[]{:S(2)}) async-start(bf16[4,224,768]{2,1,0:T(8,128)(2,1)} %bitcast.18), calls=%async_computation.3 | async-start | bytes 2752512 | tf_op jit(solution)/shard_map/all_to_all | solution.py:237
  699.5 1.3 copy-start.12
  718.7 37.8 %all-to-all-start.5 = ((bf16[4,224,768]{2,1,0:T(8,128)(2,1)}), bf16[4,224,768]{2,1,0:T(8,128)(2,1)S(1)}, u32[]{:S(2)}, u32[]{:S(2)}) async-start(bf16[4,224,768]{2,1,0:T(8,128)(2,1)} %bitcast.22), calls=%async_computation.5 | async-start | bytes 2752512 | tf_op jit(solution)/shard_map/all_to_all | solution.py:237
  (20 other events, 20.4 us)
Sparse Core Ops, SparseCore 0:
  136.8 96.4 all-reduce.4
  235.8 122.2 all-reduce.6
  360.4 69.2 all-reduce.8
  498.4 66.5 all-gather.5
  566.7 65.4 all-gather.3
  634.0 65.4 all-gather.7

commit v3 on v2

--- a/solution.py
+++ b/solution.py
@@ -220,6 +220,33 @@
     )(me.astype(jnp.int32).reshape(1), gram, *[parts[key] for key in keys], *extra)
 
 
+def sum_on_line(piece, arrivals):
+    count = lax.axis_size("col")
+    me = lax.axis_index("col")
+    half = count // 2
+
+    def send(stage, value, pairs):
+        done = arrivals.setdefault(stage, [])
+        if len(done) > 1:
+            value = after(value, done[-2])
+        arrived = lax.ppermute(value, "col", pairs)
+        done.append(arrived)
+        return arrived
+
+    def add(left, right):
+        return (left.astype(f32) + right.astype(f32)).astype(bf16)
+
+    for s in range(half - 1):
+        pairs = [(s, s + 1), (count - 1 - s, count - 2 - s)]
+        piece = add(piece, send(s, piece, pairs))
+    piece = add(piece, send(half - 1, piece, [(half - 1, half), (half, half - 1)]))
+    for s in range(half - 2, -1, -1):
+        pairs = [(s + 1, s), (count - 2 - s, count - 1 - s)]
+        arrived = send(2 * half - 2 - s, piece, pairs)
+        piece = jnp.where((me == s) | (me == count - 1 - s), arrived, piece)
+    return piece
+
+
 def per_device(ortho_in):
     rows, cols = ortho_in.shape
     n_row = lax.axis_size("row")
@@ -255,44 +282,62 @@
     def low_of(j):
         return ((me & (1 << (j.bit_length() - 1))) == 0).astype(jnp.int32).reshape(1)
 
-    gram = jnp.zeros((n_row, block, block), bf16)
     lefts = [[s[(i, 0)] for s in siblings] for i in range(bit_x)]
-    jobs = [(0, 0, None, 0), (0, 0, None, h)] + [(0, j, j - 1, 0) for j in cores]
+    arrivals = {}
+
+    def on_line(pieces):
+        return [sum_on_line(pieces[n], arrivals) for n in range(pieces.shape[0])]
+
+    own = gram_pieces(lefts[:1], [(0, 0, None, 0), (0, 0, None, h)], [me], scale)
+    own = last = lax.psum(own, "col")
+    sums = {}
+    jobs = [(0, j, j - 1, 0) for j in cores]
     near = gram_pieces(lefts, jobs, [low_of(j)[0] for j in cores], scale)
-    last = near = lax.psum(near, "col")
-    gram = lax.dynamic_update_slice(gram, near[:2].reshape(1, block, block), (0, 0, 0))
-    for j in cores:
-        gram = put_block(gram, low_of(j), near[1 + j], swap(near[1 + j], j), j)
-    for stage in (chips[:2], chips[2:]):
-        blocks = list(lefts)
-        for j in stage:
-            peers = [whole_block(parts, j) for parts in gathered]
-            if j != chips[-1]:
-                peers[0] = after(peers[0], *tied)
-            blocks.append(peers)
-        jobs = [(i, bit_x + n, n, 0) for n in range(len(stage)) for i in range(bit_x)]
-        pieces = gram_pieces(blocks, jobs, [low_of(j)[0] for j in stage], scale)
-        last = sums = lax.psum(after(pieces, last), "col")
-        for n, j in enumerate(stage):
-            for i in range(bit_x):
-                mine = sums[n * bit_x + i]
-                theirs = swap(mine, j)
-                if i > 0:
-                    mine = swap(mine, i)
-                gram = put_block(gram, low_of(j), mine, theirs, j | i)
+    for j, piece in zip(cores, on_line(near)):
+        sums[j, 0] = piece
+    for j in chips:
+        peers = [whole_block(parts, j) for parts in gathered]
+        if j != chips[-1]:
+            peers[0] = after(peers[0], *tied, gathered[0][(chips[-1], 0)])
+        jobs = [(i, bit_x, 0, 0) for i in range(bit_x)]
+        if j == chips[-1]:
+            parts = [
+                gram_pieces(lefts + [peers], jobs[:1], [low_of(j)[0]], scale),
+                gram_pieces(lefts + [peers], jobs[1:], [low_of(j)[0]], scale),
+            ]
+            head = last = lax.psum(after(parts[0], last), "col")
+            total = [head[0]] + on_line(parts[1])
+        else:
+            pieces = gram_pieces(lefts + [peers], jobs, [low_of(j)[0]], scale)
+            if j == bit_x:
+                total = last = lax.psum(after(pieces, last), "col")
+            else:
+                total = on_line(pieces)
+        for i in range(bit_x):
+            sums[j, i] = total[i]
+    gram = lax.dynamic_update_slice(
+        jnp.zeros((n_row, block, block), bf16), own.reshape(1, block, block), (0, 0, 0)
+    )
+    for (j, i), mine in sums.items():
+        theirs = swap(mine, j)
+        if i > 0:
+            mine = swap(mine, i)
+        gram = put_block(gram, low_of(j), mine, theirs, j | i)
     panels = [
         add_cores({**parts, **sibling}) for parts, sibling in zip(gathered, siblings)
     ]
 
-    outs = [[] for _ in range(n_col)]
+    outs = []
     for k, w in enumerate(thirds):
         first = product(gram, me, panels[k], 0, w)
-        first_panel = lax.all_gather(first, "row", axis=0, tiled=True)
-        result = product(gram, me, {None: first_panel}, 0, w, (tiles[k], first))
-        back = exchange(result)
-        for c in range(n_col):
-            outs[c].append(back[c * rows : (c + 1) * rows])
-    return jnp.concatenate([piece for out in outs for piece in out], axis=1)
+        if k == 1:
+            first_parts = add_cores(gather_chips(first)[0])
+        else:
+            first_parts = {None: lax.all_gather(first, "row", axis=0, tiled=True)}
+        result = product(gram, me, first_parts, 0, w, (tiles[k], first))
+        back = lax.all_to_all(result, "col", split_axis=0, concat_axis=1, tiled=True)
+        outs.append(back.reshape(rows, n_col, w))
+    return jnp.concatenate(outs, axis=2).reshape(rows, cols)
 
 
 def solution(mesh):

time: 787 us -> 831 us (1.056)
  blocking collectives: 0 us -> 35.8 us
  waiting for transfers between devices: 478 us -> 443 us
  starting transfers between devices: 54.8 us -> 85 us
  other arithmetic: 9.63 us -> 30.5 us
  local copies, waits for them, and re-layouts: 75 us -> 66.3 us
    all_gather x3 -> x2, waiting for transfers between devices: 99.6 us -> 0.02 us  [per_device(): first_parts = {None: lax.all_gather(first, 'row', axis=0, tiled=True)}]
    ppermute x0 -> x12, waiting for transfers between devices: none -> 45.3 us  [send(): arrived = lax.ppermute(value, 'col', pairs)]
    all_to_all x0 -> x1, blocking collectives: none -> 35.8 us  [per_device(): lax.all_to_all(result, 'col', split_axis=0, concat_axis=1, tiled=True)]
    all_to_all x6 -> x3, waiting for transfers between devices: 92.4 us -> 59.7 us  [exchange(): return lax.all_to_all(value, 'col', split_axis=0, concat_axis=0, tiled=True)]
    all_to_all x0 -> x2, waiting for transfers between devices: none -> 30.9 us  [per_device(): lax.all_to_all(result, 'col', split_axis=0, concat_axis=1, tiled=True)]
    ppermute x0 -> x12, starting transfers between devices: none -> 24.4 us  [send(): arrived = lax.ppermute(value, 'col', pairs)]
    ppermute x37 -> x46, waiting for transfers between devices: 166 us -> 186 us  [swap(): return lax.ppermute(value, 'row', [(r, r ^ bit) for r in range(count)])]
    convert_element_type x0 -> x7, other arithmetic: none -> 16.4 us  [add(): return (left.astype(f32) + right.astype(f32)).astype(bf16)]
  transfers between devices with their start and end apart: 49 -> 68, of which waited for: 25 -> 28; matrix products, arithmetic and copies ran while one was open for 5% -> 7% of each run, Pallas kernels for 15% -> 16%
where the time goes in v3:
time: 831 us; the launch traced here: 821 us
  waiting for transfers between devices  443 us (53%)
  Pallas kernels  147 us (18%)
  starting transfers between devices  85 us (10%)
  local copies, waits for them, and re-layouts  66.3 us (8%)
  blocking collectives  35.8 us (4%)
  other arithmetic  30.5 us (4%)
  between operations  13.9 us (2%)
    ppermute x46, waiting for transfers between devices, swap(): return lax.ppermute(value, 'row', [(r, r ^ bit) for r in range(count)])  186 us
    pallas_call x6, Pallas kernels, product(): pl.pallas_call(functools.partial(product_kernel, keys, start, bool(extra)...  91.5 us
    all_to_all x3, waiting for transfers between devices, exchange(): return lax.all_to_all(value, 'col', split_axis=0, concat_axis=0, tiled=True)  59.7 us
    psum x1, waiting for transfers between devices, per_device(): own = last = lax.psum(own, 'col')  45.8 us
    ppermute x12, waiting for transfers between devices, send(): arrived = lax.ppermute(value, 'col', pairs)  45.3 us
    psum x1, waiting for transfers between devices, per_device(): total = last = lax.psum(after(pieces, last), 'col')  44.5 us
    pallas_call x6, Pallas kernels, gram_pieces(): pl.pallas_call(functools.partial(pieces_kernel, count, jobs, scale), out_...  40.8 us
    ppermute x46, starting transfers between devices, swap(): return lax.ppermute(value, 'row', [(r, r ^ bit) for r in range(count)])  36.7 us
  transfers between devices with their start and end apart: 68, of which 28 were waited for; matrix products, arithmetic and copies ran while one was open for 7% of the time, Pallas kernels for 16%

profile of v3, /device:TPU:0, one launch (start us, length us, event | category | flops | bytes accessed | tf_op | source)
XLA Modules:
  0.0 821.3 jit_solution(454737176399252056)
XLA Ops:
  6.5 3.3 fusion
  11.0 6.3 all-to-all-start
  18.4 31.6 %all-to-all-done = bf16[4,224,768]{2,1,0:T(8,128)(2,1)S(1)} async-done(((bf16[4,224,768]{2,1,0:T(8,128)(2,1)}), bf16[4,224,768]{2,1,0:T(8,128)(2,1)S(1)}, u32[]{:S(2)}, u32[]{:S(2)}) %all-to-all-start) | async-done | bytes 1376288 | tf_op jit(solution)/shard_map/all_to_all | solution.py:264
  50.0 3.5 all-to-all-start.1
  56.7 2.2 pad_maximum_fusion.2
  58.9 26.0 %collective-permute-done.refs_6_.refs_3_ = bf16[896,768]{1,0:T(8,128)(2,1)} collective-permute-done((bf16[896,768]{1,0:T(8,128)(2,1)S(1)}, bf16[896,768]{1,0:T(8,128)(2,1)}, u32[]{:S(2)}, u32[]{:S(2)}) %collective-permute-start) | collective-permute-done | bytes 1376288 | tf_op jit(solution)/shard_map/ppermute | solution.py:35
  87.3 4.7 all-to-all-start.2
  94.5 28.2 %all-to-all-done.2 = bf16[4,224,768]{2,1,0:T(8,128)(2,1)S(1)} async-done(((bf16[4,224,768]{2,1,0:T(8,128)(2,1)}), bf16[4,224,768]{2,1,0:T(8,128)(2,1)S(1)}, u32[]{:S(2)}, u32[]{:S(2)}) %all-to-all-start.2) | async-done | bytes 1376288 | tf_op jit(solution)/shard_map/all_to_all | solution.py:264
  135.8 9.5 %collective-permute-done.5.refs_7_ = bf16[448,768]{1,0:T(8,128)(2,1)} collective-permute-done((bf16[448,768]{1,0:T(8,128)(2,1)}, bf16[448,768]{1,0:T(8,128)(2,1)}, u32[]{:S(2)}, u32[]{:S(2)}) %collective-permute-start.5) | collective-permute-done | bytes 688160 | tf_op jit(solution)/shard_map/ppermute | solution.py:35
  146.8 13.1 %collective-permute-done.9.refs_7_ = bf16[448,768]{1,0:T(8,128)(2,1)S(1)} collective-permute-done((bf16[448,768]{1,0:T(8,128)(2,1)}, bf16[448,768]{1,0:T(8,128)(2,1)S(1)}, u32[]{:S(2)}, u32[]{:S(2)}) %collective-permute-start.9) | collective-permute-done | bytes 688160 | tf_op jit(solution)/shard_map/ppermute | solution.py:35
  162.7 4.5 shard_map.21
  170.0 4.5 shard_map.22
  175.9 4.8 collective-permute-done.10.refs_8_
  181.8 12.6 %collective-permute-done.6.refs_8_ = bf16[448,768]{1,0:T(8,128)(2,1)} collective-permute-done((bf16[448,768]{1,0:T(8,128)(2,1)}, bf16[448,768]{1,0:T(8,128)(2,1)}, u32[]{:S(2)}, u32[]{:S(2)}) %collective-permute-start.6) | collective-permute-done | bytes 688160 | tf_op jit(solution)/shard_map/ppermute | solution.py:35
  203.7 9.7 %shard_map.18 = bf16[2,448,896]{2,1,0:T(8,128)(2,1)} custom-call(s32[1]{0:T(128)} %bitcast.1.low_ref, bf16[896,768]{1,0:T(8,128)(2,1)S(1)} %bitcast.42, bf16[896,768]{1,0:T(8,128)(2,1)S(1)} %bitcast.65, bf16[896,768]{1,0:T(8,128)(2,1)S(1)} %bitcast.53, bf16[896,768]{1,0:T(8,128)(2,1)} %collective-permute-done.2.refs_3_.refs_2_, ...), custom_call_target="tpu_custom_call" | custom-call | flops 3699376128 | bytes 13991936 | tf_op jit(solution)/shard_map/pallas_call | solution.py:103
  213.3 2.7 slice_bitcast_fusion.2
  216.1 2.2 collective-permute-start.15
  219.2 2.2 collective-permute-start.25
  221.4 9.2 %shard_map.20 = bf16[2,448,896]{2,1,0:T(8,128)(2,1)} custom-call(s32[1]{0:T(128)} %bitcast.10.low_ref, bf16[896,768]{1,0:T(8,128)(2,1)S(1)} %bitcast.43, bf16[896,768]{1,0:T(8,128)(2,1)S(1)} %bitcast.66, bf16[896,768]{1,0:T(8,128)(2,1)S(1)} %bitcast.54, bf16[896,768]{1,0:T(8,128)(2,1)} %collective-permute-done.2.refs_3_.refs_2_, ...), custom_call_target="tpu_custom_call" | custom-call | flops 3699376128 | bytes 13991936 | tf_op jit(solution)/shard_map/pallas_call | solution.py:103
  230.6 45.8 %all-reduce.5.cloned.1.call-done = bf16[2,448,896]{2,1,0:T(8,128)(2,1)} async-done(((bf16[2,448,896]{2,1,0:T(8,128)(2,1)}), bf16[2,448,896]{2,1,0:T(8,128)(2,1)}) %all-reduce.5.cloned.1.call-update) | async-done | bytes 1605648 | tf_op jit(solution)/shard_map/psum | solution.py:292
  282.8 6.1 shard_map.17
  288.9 7.2 collective-permute-start.16
  296.1 3.0 add_convert_fusion.3
  302.1 6.8 shard_map.19
  308.9 2.5 add_convert_fusion
  314.3 14.1 %collective-permute-done.16 = bf16[448,896]{1,0:T(8,128)(2,1)} collective-permute-done((bf16[448,896]{1,0:T(8,128)(2,1)S(1)}, bf16[448,896]{1,0:T(8,128)(2,1)}, u32[]{:S(2)}, u32[]{:S(2)}) %collective-permute-start.16) | collective-permute-done | bytes 802848 | tf_op jit(solution)/shard_map/ppermute | solution.py:232
  328.5 2.2 add_convert_fusion.7
  332.3 2.5 add_convert_fusion.4
  336.0 44.5 %all-reduce.7.cloned.1.call-done = bf16[2,448,896]{2,1,0:T(8,128)(2,1)} async-done(((bf16[2,448,896]{2,1,0:T(8,128)(2,1)}), bf16[2,448,896]{2,1,0:T(8,128)(2,1)}) %all-reduce.7.cloned.1.call-update) | async-done | bytes 1605648 | tf_op jit(solution)/shard_map/psum | solution.py:313
  380.6 2.4 slice_bitcast_fusion
  384.6 2.5 add_convert_fusion.1
  388.9 2.5 add_convert_fusion.5
  391.4 7.2 collective-permute-done.19
  399.9 2.2 broadcast_select_fusion.mine
  406.9 31.1 %all-reduce.9.cloned.1.call-done.mine = bf16[448,896]{1,0:T(8,128)(2,1)} async-done(((bf16[448,896]{1,0:T(8,128)(2,1)}), bf16[448,896]{1,0:T(8,128)(2,1)}) %all-reduce.9.cloned.1.call-update) | async-done | bytes 802832 | tf_op jit(solution)/shard_map/psum | solution.py:308
  438.0 2.4 collective-permute-start.23
  440.4 9.7 %collective-permute-done.29 = bf16[448,896]{1,0:T(8,128)(2,1)} collective-permute-done((bf16[448,896]{1,0:T(8,128)(2,1)}, bf16[448,896]{1,0:T(8,128)(2,1)}, u32[]{:S(2)}, u32[]{:S(2)}) %collective-permute-start.29) | collective-permute-done | bytes 802848 | tf_op jit(solution)/shard_map/ppermute | solution.py:232
  452.9 14.2 %collective-permute-done.20 = bf16[448,896]{1,0:T(8,128)(2,1)} collective-permute-done((bf16[448,896]{1,0:T(8,128)(2,1)}, bf16[448,896]{1,0:T(8,128)(2,1)}, u32[]{:S(2)}, u32[]{:S(2)}) %collective-permute-start.20) | collective-permute-done | bytes 802848 | tf_op jit(solution)/shard_map/ppermute | solution.py:232
  472.0 4.0 collective-permute-done.32.theirs
  477.9 2.4 collective-permute-start.22
  480.3 30.0 %collective-permute-done.31.theirs = bf16[448,896]{1,0:T(8,128)(2,1)S(1)} collective-permute-done((bf16[448,896]{1,0:T(8,128)(2,1)S(1)}, bf16[448,896]{1,0:T(8,128)(2,1)S(1)}, u32[]{:S(2)}, u32[]{:S(2)}) %collective-permute-start.31) | collective-permute-done | bytes 802848 | tf_op jit(solution)/shard_map/ppermute | solution.py:35
  512.7 7.6 dynamic_update_slice.3.gram_in
  520.3 2.7 shard_map.23.gram_in
  523.0 2.6 shard_map.24.gram_in
  525.6 2.5 shard_map.25.gram_in
  533.5 2.6 shard_map.29.refs_0_
  536.1 14.5 %shard_map.30.refs_3_ = bf16[896,768]{1,0:T(8,128)(2,1)S(1)} custom-call(s32[1]{0:T(128)} %bitcast.low_ref.me_ref, bf16[8,896,896]{2,1,0:T(8,128)(2,1)} %shard_map.29.refs_0_, bf16[896,768]{1,0:T(8,128)(2,1)S(1)} %bitcast.46, bf16[896,768]{1,0:T(8,128)(2,1)} %collective-permute-done.2.refs_3_.refs_2_, bf16[896,768]{1,0:T(8,128)(2,1)} %collective-permute-done.refs_6_.refs_3_, ...), custom_call_target="tpu_custom_call" | custom-call | flops 9865003008 | bytes 23855104 | tf_op jit(solution)/shard_map/pallas_call | solution.py:201
  552.9 5.3 collective-permute-done.56.refs_9_
  561.3 14.8 %shard_map.34.refs_3_ = bf16[896,768]{1,0:T(8,128)(2,1)S(1)} custom-call(s32[1]{0:T(128)} %bitcast.low_ref.me_ref, bf16[8,896,896]{2,1,0:T(8,128)(2,1)} %shard_map.29.refs_0_, bf16[896,768]{1,0:T(8,128)(2,1)S(1)} %bitcast.57, bf16[896,768]{1,0:T(8,128)(2,1)} %collective-permute-done.4.refs_5_.refs_2_, ...), custom_call_target="tpu_custom_call" | custom-call | flops 9865003008 | bytes 23855104 | tf_op jit(solution)/shard_map/pallas_call | solution.py:201
  578.4 4.1 collective-permute-done.43.refs_9_
  588.2 14.5 %shard_map.32.refs_1_.refs_12_ = bf16[896,768]{1,0:T(8,128)(2,1)S(1)} custom-call(s32[1]{0:T(128)} %bitcast.low_ref.me_ref, bf16[8,896,896]{2,1,0:T(8,128)(2,1)} %shard_map.29.refs_0_, bf16[896,768]{1,0:T(8,128)(2,1)S(1)} %bitcast.69, bf16[896,768]{1,0:T(8,128)(2,1)} %collective-permute-done.3.refs_4_.refs_2_, ...), custom_call_target="tpu_custom_call" | custom-call | flops 9865003008 | bytes 23855104 | tf_op jit(solution)/shard_map/pallas_call | solution.py:201
  602.7 2.2 collective-permute-start.46
  606.5 42.9 %collective-permute-done.46.refs_3_ = bf16[896,768]{1,0:T(8,128)(2,1)S(1)} collective-permute-done((bf16[896,768]{1,0:T(8,128)(2,1)S(1)}, bf16[896,768]{1,0:T(8,128)(2,1)S(1)}, u32[]{:S(2)}, u32[]{:S(2)}) %collective-permute-start.46) | collective-permute-done | bytes 1376288 | tf_op jit(solution)/shard_map/ppermute | solution.py:35
  652.2 22.4 %collective-permute-done.50.refs_7_ = bf16[448,768]{1,0:T(8,128)(2,1)S(1)} collective-permute-done((bf16[448,768]{1,0:T(8,128)(2,1)S(1)}, bf16[448,768]{1,0:T(8,128)(2,1)S(1)}, u32[]{:S(2)}, u32[]{:S(2)}) %collective-permute-start.50) | collective-permute-done | bytes 688160 | tf_op jit(solution)/shard_map/ppermute | solution.py:35
  675.2 2.6 collective-permute-done.52.refs_9_
  682.0 16.6 %shard_map.33 = bf16[896,768]{1,0:T(8,128)(2,1)S(1)} custom-call(s32[1]{0:T(128)} %bitcast.low_ref.me_ref, bf16[8,896,896]{2,1,0:T(8,128)(2,1)} %shard_map.29.refs_0_, bf16[896,768]{1,0:T(8,128)(2,1)S(1)} %shard_map.32.refs_1_.refs_12_, bf16[896,768]{1,0:T(8,128)(2,1)} %copy-done.38, bf16[896,768]{1,0:T(8,128)(2,1)} %copy-done.36, ...), custom_call_target="tpu_custom_call" | custom-call | flops 9865003008 | bytes 23855104 | tf_op jit(solution)/shard_map/pallas_call | solution.py:201
  699.7 4.6 all-to-all-start.4
  705.7 15.6 %shard_map.31 = bf16[896,768]{1,0:T(8,128)(2,1)S(1)} custom-call(s32[1]{0:T(128)} %bitcast.low_ref.me_ref, bf16[8,896,896]{2,1,0:T(8,128)(2,1)} %shard_map.29.refs_0_, bf16[7168,768]{1,0:T(8,128)(2,1)} %all-gather.3.cloned.1.call-done.refs_1_, bf16[896,768]{1,0:T(8,128)(2,1)S(1)} %bitcast.47, bf16[896,768]{1,0:T(8,128)(2,1)S(1)} %copy-done.12), custom_call_target="tpu_custom_call" | custom-call | flops 9865003008 | bytes 23855104 | tf_op jit(solution)/shard_map/pallas_call | solution.py:201
  722.3 15.1 %all-to-all-done.4 = bf16[4,224,768]{2,1,0:T(8,128)(2,1)} async-done(((bf16[4,224,768]{2,1,0:T(8,128)(2,1)}), bf16[4,224,768]{2,1,0:T(8,128)(2,1)}, u32[]{:S(2)}, u32[]{:S(2)}) %all-to-all-start.4) | async-done | bytes 1376288 | tf_op jit(solution)/shard_map/all_to_all | solution.py:338
  737.5 4.6 all-to-all-start.3
  742.1 15.4 %shard_map.35 = bf16[896,768]{1,0:T(8,128)(2,1)S(1)} custom-call(s32[1]{0:T(128)} %bitcast.low_ref.me_ref, bf16[8,896,896]{2,1,0:T(8,128)(2,1)} %shard_map.29.refs_0_, bf16[7168,768]{1,0:T(8,128)(2,1)} %all-gather.5.cloned.1.call-done.refs_1_, bf16[896,768]{1,0:T(8,128)(2,1)S(1)} %bitcast.58, bf16[896,768]{1,0:T(8,128)(2,1)S(1)} %copy-done.14), custom_call_target="tpu_custom_call" | custom-call | flops 9865003008 | bytes 23855104 | tf_op jit(solution)/shard_map/pallas_call | solution.py:201
  758.6 15.8 %all-to-all-done.3 = bf16[4,224,768]{2,1,0:T(8,128)(2,1)} async-done(((bf16[4,224,768]{2,1,0:T(8,128)(2,1)}), bf16[4,224,768]{2,1,0:T(8,128)(2,1)}, u32[]{:S(2)}, u32[]{:S(2)}) %all-to-all-start.3) | async-done | bytes 1376288 | tf_op jit(solution)/shard_map/all_to_all | solution.py:338
  774.4 35.8 %all_to_all.81 = bf16[4,224,768]{2,1,0:T(8,128)(2,1)S(1)} all-to-all(bf16[4,224,768]{2,1,0:T(8,128)(2,1)} %bitcast.74), channel_id=1, replica_groups=mesh['row'=8,'col'=4] {'col'}, dimensions={0} | all-to-all | bytes 2752512 | tf_op jit(solution)/shard_map/all_to_all | solution.py:338
  812.1 2.5 copy.10
  (221 shorter events, 113.5 us)
Async XLA Ops:
  11.0 39.1 %all-to-all-start = ((bf16[4,224,768]{2,1,0:T(8,128)(2,1)}), bf16[4,224,768]{2,1,0:T(8,128)(2,1)S(1)}, u32[]{:S(2)}, u32[]{:S(2)}) async-start(bf16[4,224,768]{2,1,0:T(8,128)(2,1)} %bitcast.2), calls=%async_computation | async-start | bytes 2752512 | tf_op jit(solution)/shard_map/all_to_all | solution.py:264
  50.0 36.1 %all-to-all-start.1 = ((bf16[4,224,768]{2,1,0:T(8,128)(2,1)}), bf16[4,224,768]{2,1,0:T(8,128)(2,1)S(1)}, u32[]{:S(2)}, u32[]{:S(2)}) async-start(bf16[4,224,768]{2,1,0:T(8,128)(2,1)} %bitcast.76), calls=%async_computation.1 | async-start | bytes 2752512 | tf_op jit(solution)/shard_map/all_to_all | solution.py:264
  53.6 31.3 %collective-permute-start = (bf16[896,768]{1,0:T(8,128)(2,1)S(1)}, bf16[896,768]{1,0:T(8,128)(2,1)}, u32[]{:S(2)}, u32[]{:S(2)}) collective-permute-start(bf16[896,768]{1,0:T(8,128)(2,1)S(1)} %bitcast.37), channel_id=1, source_target_pairs={{0,8},{4,12},{8,0},{12,4},{16,24},{20,28},{24,16},{28,20},{1,9},{5... | collective-permute-start | bytes 4128776 | tf_op jit(solution)/shard_map/ppermute | solution.py:35
  55.1 31.0 %collective-permute-start.1 = (bf16[896,768]{1,0:T(8,128)(2,1)S(1)}, bf16[896,768]{1,0:T(8,128)(2,1)}, u32[]{:S(2)}, u32[]{:S(2)}) collective-permute-start(bf16[896,768]{1,0:T(8,128)(2,1)S(1)} %bitcast.38), channel_id=1, source_target_pairs={{0,16},{4,20},{8,24},{12,28},{16,0},{20,4},{24,8},{28,12},{1,17},{... | collective-permute-start | bytes 4128776 | tf_op jit(solution)/shard_map/ppermute | solution.py:35
  87.3 35.4 %all-to-all-start.2 = ((bf16[4,224,768]{2,1,0:T(8,128)(2,1)}), bf16[4,224,768]{2,1,0:T(8,128)(2,1)S(1)}, u32[]{:S(2)}, u32[]{:S(2)}) async-start(bf16[4,224,768]{2,1,0:T(8,128)(2,1)} %bitcast.75), calls=%async_computation.2 | async-start | bytes 2752512 | tf_op jit(solution)/shard_map/all_to_all | solution.py:264
  92.0 184.5 %all-reduce.5.cloned.1.call-start = ((), (), s32[]{:S(2)}) async-start(), calls=%async_computation.6 | async-start | bytes 3211264 | tf_op jit(solution)/shard_map/psum | solution.py:292
  92.0 34.7 %collective-permute-start.7 = (bf16[896,768]{1,0:T(8,128)(2,1)}, bf16[896,768]{1,0:T(8,128)(2,1)}, u32[]{:S(2)}, u32[]{:S(2)}) collective-permute-start(bf16[896,768]{1,0:T(8,128)(2,1)} %bitcast.59), channel_id=1, source_target_pairs={{0,8},{4,12},{8,0},{12,4},{16,24},{20,28},{24,16},{28,20},{1,9},{5... | collective-permute-start | bytes 4128776 | tf_op jit(solution)/shard_map/ppermute | solution.py:35
  92.5 35.7 %collective-permute-start.8 = (bf16[896,768]{1,0:T(8,128)(2,1)}, bf16[896,768]{1,0:T(8,128)(2,1)}, u32[]{:S(2)}, u32[]{:S(2)}) collective-permute-start(bf16[896,768]{1,0:T(8,128)(2,1)} %bitcast.60), channel_id=1, source_target_pairs={{0,16},{4,20},{8,24},{12,28},{16,0},{20,4},{24,8},{28,12},{1,17},{... | collective-permute-start | bytes 4128776 | tf_op jit(solution)/shard_map/ppermute | solution.py:35
  94.0 38.7 %collective-permute-start.3 = (bf16[896,768]{1,0:T(8,128)(2,1)}, bf16[896,768]{1,0:T(8,128)(2,1)}, u32[]{:S(2)}, u32[]{:S(2)}) collective-permute-start(bf16[896,768]{1,0:T(8,128)(2,1)} %bitcast.61), channel_id=1, source_target_pairs={{0,4},{4,0},{8,12},{12,8},{16,20},{20,16},{24,28},{28,24},{1,5},{5... | collective-permute-start | bytes 4128776 | tf_op jit(solution)/shard_map/ppermute | solution.py:35
  94.0 40.2 %collective-permute-start.2 = (bf16[896,768]{1,0:T(8,128)(2,1)S(1)}, bf16[896,768]{1,0:T(8,128)(2,1)}, u32[]{:S(2)}, u32[]{:S(2)}) collective-permute-start(bf16[896,768]{1,0:T(8,128)(2,1)S(1)} %bitcast.39), channel_id=1, source_target_pairs={{0,4},{4,0},{8,12},{12,8},{16,20},{20,16},{24,28},{28,24},{1,5},{5... | collective-permute-start | bytes 4128776 | tf_op jit(solution)/shard_map/ppermute | solution.py:35
  122.7 47.0 %collective-permute-start.4 = (bf16[896,768]{1,0:T(8,128)(2,1)S(1)}, bf16[896,768]{1,0:T(8,128)(2,1)}, u32[]{:S(2)}, u32[]{:S(2)}) collective-permute-start(bf16[896,768]{1,0:T(8,128)(2,1)S(1)} %bitcast.48), channel_id=1, source_target_pairs={{0,4},{4,0},{8,12},{12,8},{16,20},{20,16},{24,28},{28,24},{1,5},{5... | collective-permute-start | bytes 4128776 | tf_op jit(solution)/shard_map/ppermute | solution.py:35
  126.7 18.5 %collective-permute-start.5 = (bf16[448,768]{1,0:T(8,128)(2,1)}, bf16[448,768]{1,0:T(8,128)(2,1)}, u32[]{:S(2)}, u32[]{:S(2)}) collective-permute-start(bf16[448,768]{1,0:T(8,128)(2,1)} %slice.84), channel_id=1, source_target_pairs={{0,16},{4,20},{8,24},{12,28},{16,0},{20,4},{24,8},{28,12},{1,17},{... | collective-permute-start | bytes 2064392 | tf_op jit(solution)/shard_map/ppermute | solution.py:35
  132.2 27.7 %collective-permute-start.9 = (bf16[448,768]{1,0:T(8,128)(2,1)}, bf16[448,768]{1,0:T(8,128)(2,1)S(1)}, u32[]{:S(2)}, u32[]{:S(2)}) collective-permute-start(bf16[448,768]{1,0:T(8,128)(2,1)} %slice.86), channel_id=1, source_target_pairs={{0,16},{4,20},{8,24},{12,28},{16,0},{20,4},{24,8},{28,12},{1,17},{... | collective-permute-start | bytes 2064392 | tf_op jit(solution)/shard_map/ppermute | solution.py:35
  132.7 62.8 %collective-permute-start.11 = (bf16[896,768]{1,0:T(8,128)(2,1)S(1)}, bf16[896,768]{1,0:T(8,128)(2,1)}, u32[]{:S(2)}, u32[]{:S(2)}) collective-permute-start(bf16[896,768]{1,0:T(8,128)(2,1)S(1)} %bitcast.49), channel_id=1, source_target_pairs={{0,8},{4,12},{8,0},{12,4},{16,24},{20,28},{24,16},{28,20},{1,9},{5... | collective-permute-start | bytes 4128776 | tf_op jit(solution)/shard_map/ppermute | solution.py:35
  134.2 61.3 %collective-permute-start.12 = (bf16[896,768]{1,0:T(8,128)(2,1)S(1)}, bf16[896,768]{1,0:T(8,128)(2,1)}, u32[]{:S(2)}, u32[]{:S(2)}) collective-permute-start(bf16[896,768]{1,0:T(8,128)(2,1)S(1)} %bitcast.50), channel_id=1, source_target_pairs={{0,16},{4,20},{8,24},{12,28},{16,0},{20,4},{24,8},{28,12},{1,17},{... | collective-permute-start | bytes 4128776 | tf_op jit(solution)/shard_map/ppermute | solution.py:35
  145.3 35.4 %collective-permute-start.10 = (bf16[448,768]{1,0:T(8,128)(2,1)}, bf16[448,768]{1,0:T(8,128)(2,1)}, u32[]{:S(2)}, u32[]{:S(2)}) collective-permute-start(bf16[448,768]{1,0:T(8,128)(2,1)} %slice.87), channel_id=1, source_target_pairs={{0,8},{4,12},{8,0},{12,4},{16,24},{20,28},{24,16},{28,20},{1,9},{5... | collective-permute-start | bytes 2064392 | tf_op jit(solution)/shard_map/ppermute | solution.py:35
  159.9 34.5 %collective-permute-start.6 = (bf16[448,768]{1,0:T(8,128)(2,1)}, bf16[448,768]{1,0:T(8,128)(2,1)}, u32[]{:S(2)}, u32[]{:S(2)}) collective-permute-start(bf16[448,768]{1,0:T(8,128)(2,1)} %slice.85), channel_id=1, source_target_pairs={{0,8},{4,12},{8,0},{12,4},{16,24},{20,28},{24,16},{28,20},{1,9},{5... | collective-permute-start | bytes 2064392 | tf_op jit(solution)/shard_map/ppermute | solution.py:35
  168.4 212.2 %all-reduce.7.cloned.1.call-start = ((), (), s32[]{:S(2)}) async-start(), calls=%async_computation.7 | async-start | bytes 3211264 | tf_op jit(solution)/shard_map/psum | solution.py:313
  174.5 43.8 %collective-permute-start.24 = (bf16[448,896]{1,0:T(8,128)(2,1)S(1)}, bf16[448,896]{1,0:T(8,128)(2,1)S(1)}, u32[]{:S(2)}, u32[]{:S(2)}) collective-permute-start(bf16[448,896]{1,0:T(8,128)(2,1)S(1)} %bitcast.70), channel_id=1, source_target_pairs={{0,1},{3,2},{4,5},{7,6},{8,9},{11,10},{12,13},{15,14},{16,17},{19,... | collective-permute-start | bytes 2408456 | tf_op jit(solution)/shard_map/ppermute | solution.py:232
  200.7 75.8 %collective-permute-start.13 = (bf16[448,768]{1,0:T(8,128)(2,1)}, bf16[448,768]{1,0:T(8,128)(2,1)}, u32[]{:S(2)}, u32[]{:S(2)}) collective-permute-start(bf16[448,768]{1,0:T(8,128)(2,1)} %slice.88), channel_id=1, source_target_pairs={{0,16},{4,20},{8,24},{12,28},{16,0},{20,4},{24,8},{28,12},{1,17},{... | collective-permute-start | bytes 2064392 | tf_op jit(solution)/shard_map/ppermute | solution.py:35
  202.2 78.4 %collective-permute-start.14 = (bf16[448,768]{1,0:T(8,128)(2,1)}, bf16[448,768]{1,0:T(8,128)(2,1)}, u32[]{:S(2)}, u32[]{:S(2)}) collective-permute-start(bf16[448,768]{1,0:T(8,128)(2,1)} %slice.89), channel_id=1, source_target_pairs={{0,8},{4,12},{8,0},{12,4},{16,24},{20,28},{24,16},{28,20},{1,9},{5... | collective-permute-start | bytes 2064392 | tf_op jit(solution)/shard_map/ppermute | solution.py:35
  216.1 72.9 %collective-permute-start.15 = (bf16[448,896]{1,0:T(8,128)(2,1)}, bf16[448,896]{1,0:T(8,128)(2,1)}, u32[]{:S(2)}, u32[]{:S(2)}) collective-permute-start(bf16[448,896]{1,0:T(8,128)(2,1)} %get-tuple-element.76), channel_id=1, source_target_pairs={{0,1},{3,2},{4,5},{7,6},{8,9},{11,10},{12,13},{15,14},{16,17},{19,... | collective-permute-start | bytes 2408456 | tf_op jit(solution)/shard_map/ppermute | solution.py:232
  219.2 76.9 %collective-permute-start.25 = (bf16[448,896]{1,0:T(8,128)(2,1)}, bf16[448,896]{1,0:T(8,128)(2,1)}, u32[]{:S(2)}, u32[]{:S(2)}) collective-permute-start(bf16[448,896]{1,0:T(8,128)(2,1)} %get-tuple-element.52), channel_id=1, source_target_pairs={{0,1},{3,2},{4,5},{7,6},{8,9},{11,10},{12,13},{15,14},{16,17},{19,... | collective-permute-start | bytes 2408456 | tf_op jit(solution)/shard_map/ppermute | solution.py:232
  276.5 161.5 %all-reduce.9.cloned.1.call-start = ((), (), s32[]{:S(2)}) async-start(), calls=%async_computation.8 | async-start | bytes 1605632 | tf_op jit(solution)/shard_map/psum | solution.py:308
  279.0 29.9 %collective-permute-start.26 = (bf16[448,896]{1,0:T(8,128)(2,1)}, bf16[448,896]{1,0:T(8,128)(2,1)}, u32[]{:S(2)}, u32[]{:S(2)}) collective-permute-start(bf16[448,896]{1,0:T(8,128)(2,1)} %add_convert_fusion.2), channel_id=1, source_target_pairs={{1,2},{2,1},{5,6},{6,5},{9,10},{10,9},{13,14},{14,13},{17,18},{18,... | collective-permute-start | bytes 2408456 | tf_op jit(solution)/shard_map/ppermute | solution.py:232
  288.9 39.5 %collective-permute-start.16 = (bf16[448,896]{1,0:T(8,128)(2,1)S(1)}, bf16[448,896]{1,0:T(8,128)(2,1)}, u32[]{:S(2)}, u32[]{:S(2)}) collective-permute-start(bf16[448,896]{1,0:T(8,128)(2,1)S(1)} %bitcast.71), channel_id=1, source_target_pairs={{0,1},{3,2},{4,5},{7,6},{8,9},{11,10},{12,13},{15,14},{16,17},{19,... | collective-permute-start | bytes 2408456 | tf_op jit(solution)/shard_map/ppermute | solution.py:232
  299.1 31.6 %collective-permute-start.17 = (bf16[448,896]{1,0:T(8,128)(2,1)}, bf16[448,896]{1,0:T(8,128)(2,1)}, u32[]{:S(2)}, u32[]{:S(2)}) collective-permute-start(bf16[448,896]{1,0:T(8,128)(2,1)} %get-tuple-element.74), channel_id=1, source_target_pairs={{1,2},{2,1},{5,6},{6,5},{9,10},{10,9},{13,14},{14,13},{17,18},{18,... | collective-permute-start | bytes 2408456 | tf_op jit(solution)/shard_map/ppermute | solution.py:232
  311.4 75.7 %collective-permute-start.28 = (bf16[448,896]{1,0:T(8,128)(2,1)}, bf16[448,896]{1,0:T(8,128)(2,1)}, u32[]{:S(2)}, u32[]{:S(2)}) collective-permute-start(bf16[448,896]{1,0:T(8,128)(2,1)} %add_convert_fusion), channel_id=1, source_target_pairs={{1,0},{2,3},{5,4},{6,7},{9,8},{10,11},{13,12},{14,15},{17,16},{18,... | collective-permute-start | bytes 2408456 | tf_op jit(solution)/shard_map/ppermute | solution.py:232
  312.7 71.8 %collective-permute-start.27 = (bf16[448,896]{1,0:T(8,128)(2,1)}, bf16[448,896]{1,0:T(8,128)(2,1)}, u32[]{:S(2)}, u32[]{:S(2)}) collective-permute-start(bf16[448,896]{1,0:T(8,128)(2,1)} %get-tuple-element.53), channel_id=1, source_target_pairs={{1,2},{2,1},{5,6},{6,5},{9,10},{10,9},{13,14},{14,13},{17,18},{18,... | collective-permute-start | bytes 2408456 | tf_op jit(solution)/shard_map/ppermute | solution.py:232
  330.7 57.0 %collective-permute-start.18 = (bf16[448,896]{1,0:T(8,128)(2,1)}, bf16[448,896]{1,0:T(8,128)(2,1)}, u32[]{:S(2)}, u32[]{:S(2)}) collective-permute-start(bf16[448,896]{1,0:T(8,128)(2,1)} %add_convert_fusion.7), channel_id=1, source_target_pairs={{1,2},{2,1},{5,6},{6,5},{9,10},{10,9},{13,14},{14,13},{17,18},{18,... | collective-permute-start | bytes 2408456 | tf_op jit(solution)/shard_map/ppermute | solution.py:232
  334.7 63.9 %collective-permute-start.19 = (bf16[448,896]{1,0:T(8,128)(2,1)}, bf16[448,896]{1,0:T(8,128)(2,1)}, u32[]{:S(2)}, u32[]{:S(2)}) collective-permute-start(bf16[448,896]{1,0:T(8,128)(2,1)} %add_convert_fusion.4), channel_id=1, source_target_pairs={{1,0},{2,3},{5,4},{6,7},{9,8},{10,11},{13,12},{14,15},{17,16},{18,... | collective-permute-start | bytes 2408456 | tf_op jit(solution)/shard_map/ppermute | solution.py:232
  383.0 20.9 %collective-permute-start.35 = (bf16[448,896]{1,0:T(8,128)(2,1)S(1)}, bf16[448,896]{1,0:T(8,128)(2,1)}, u32[]{:S(2)}, u32[]{:S(2)}) collective-permute-start(bf16[448,896]{1,0:T(8,128)(2,1)S(1)} %get-tuple-element.71.mine), channel_id=1, source_target_pairs={{0,8},{4,12},{8,0},{12,4},{16,24},{20,28},{24,16},{28,20},{1,9},{5... | collective-permute-start | bytes 2408456 | tf_op jit(solution)/shard_map/ppermute | solution.py:35
  384.5 319.9 %all-gather.3.cloned.1.call-start = ((), (), s32[]{:S(2)}) async-start(), calls=%async_computation.9 | async-start | bytes 12386304 | tf_op jit(solution)/shard_map/all_gather | solution.py:336
  384.5 21.4 %collective-permute-start.33 = (bf16[448,896]{1,0:T(8,128)(2,1)}, bf16[448,896]{1,0:T(8,128)(2,1)S(1)}, u32[]{:S(2)}, u32[]{:S(2)}) collective-permute-start(bf16[448,896]{1,0:T(8,128)(2,1)} %get-tuple-element.72), channel_id=1, source_target_pairs={{0,4},{4,0},{8,12},{12,8},{16,20},{20,16},{24,28},{28,24},{1,5},{5... | collective-permute-start | bytes 2408456 | tf_op jit(solution)/shard_map/ppermute | solution.py:35
  387.1 82.0 %collective-permute-start.34 = (bf16[448,896]{1,0:T(8,128)(2,1)}, bf16[448,896]{1,0:T(8,128)(2,1)}, u32[]{:S(2)}, u32[]{:S(2)}) collective-permute-start(bf16[448,896]{1,0:T(8,128)(2,1)} %get-tuple-element.72), channel_id=1, source_target_pairs={{0,8},{4,12},{8,0},{12,4},{16,24},{20,28},{24,16},{28,20},{1,9},{5... | collective-permute-start | bytes 2408456 | tf_op jit(solution)/shard_map/ppermute | solution.py:35
  387.7 62.5 %collective-permute-start.29 = (bf16[448,896]{1,0:T(8,128)(2,1)}, bf16[448,896]{1,0:T(8,128)(2,1)}, u32[]{:S(2)}, u32[]{:S(2)}) collective-permute-start(bf16[448,896]{1,0:T(8,128)(2,1)} %add_convert_fusion.1), channel_id=1, source_target_pairs={{1,0},{2,3},{5,4},{6,7},{9,8},{10,11},{13,12},{14,15},{17,16},{18,... | collective-permute-start | bytes 2408456 | tf_op jit(solution)/shard_map/ppermute | solution.py:232
  398.6 68.4 %collective-permute-start.20 = (bf16[448,896]{1,0:T(8,128)(2,1)}, bf16[448,896]{1,0:T(8,128)(2,1)}, u32[]{:S(2)}, u32[]{:S(2)}) collective-permute-start(bf16[448,896]{1,0:T(8,128)(2,1)} %add_convert_fusion.5), channel_id=1, source_target_pairs={{1,0},{2,3},{5,4},{6,7},{9,8},{10,11},{13,12},{14,15},{17,16},{18,... | collective-permute-start | bytes 2408456 | tf_op jit(solution)/shard_map/ppermute | solution.py:232
  403.8 66.8 %collective-permute-start.36 = (bf16[448,896]{1,0:T(8,128)(2,1)}, bf16[448,896]{1,0:T(8,128)(2,1)}, u32[]{:S(2)}, u32[]{:S(2)}) collective-permute-start(bf16[448,896]{1,0:T(8,128)(2,1)} %broadcast_select_fusion.mine), channel_id=1, source_target_pairs={{0,4},{4,0},{8,12},{12,8},{16,20},{20,16},{24,28},{28,24},{1,5},{5... | collective-permute-start | bytes 2408456 | tf_op jit(solution)/shard_map/ppermute | solution.py:35
  438.0 32.9 %collective-permute-start.23 = (bf16[448,896]{1,0:T(8,128)(2,1)}, bf16[448,896]{1,0:T(8,128)(2,1)S(1)}, u32[]{:S(2)}, u32[]{:S(2)}) collective-permute-start(bf16[448,896]{1,0:T(8,128)(2,1)} %all-reduce.9.cloned.1.call-done.mine), channel_id=1, source_target_pairs={{0,24},{4,28},{8,16},{12,20},{16,8},{20,12},{24,0},{28,4},{1,25},{... | collective-permute-start | bytes 2408456 | tf_op jit(solution)/shard_map/ppermute | solution.py:35
  450.1 25.9 %collective-permute-start.32 = (bf16[448,896]{1,0:T(8,128)(2,1)}, bf16[448,896]{1,0:T(8,128)(2,1)S(1)}, u32[]{:S(2)}, u32[]{:S(2)}) collective-permute-start(bf16[448,896]{1,0:T(8,128)(2,1)} %broadcast_select_fusion.1.mine), channel_id=1, source_target_pairs={{0,16},{4,20},{8,24},{12,28},{16,0},{20,4},{24,8},{28,12},{1,17},{... | collective-permute-start | bytes 2408456 | tf_op jit(solution)/shard_map/ppermute | solution.py:35
  467.0 10.0 %collective-permute-start.30 = (bf16[448,896]{1,0:T(8,128)(2,1)S(1)}, bf16[448,896]{1,0:T(8,128)(2,1)S(1)}, u32[]{:S(2)}, u32[]{:S(2)}) collective-permute-start(bf16[448,896]{1,0:T(8,128)(2,1)S(1)} %broadcast_select_fusion.2), channel_id=1, source_target_pairs={{0,4},{4,0},{8,12},{12,8},{16,20},{20,16},{24,28},{28,24},{1,5},{5... | collective-permute-start | bytes 2408456 | tf_op jit(solution)/shard_map/ppermute | solution.py:35
  469.1 41.3 %collective-permute-start.31 = (bf16[448,896]{1,0:T(8,128)(2,1)S(1)}, bf16[448,896]{1,0:T(8,128)(2,1)S(1)}, u32[]{:S(2)}, u32[]{:S(2)}) collective-permute-start(bf16[448,896]{1,0:T(8,128)(2,1)S(1)} %broadcast_select_fusion.2), channel_id=1, source_target_pairs={{0,16},{4,20},{8,24},{12,28},{16,0},{20,4},{24,8},{28,12},{1,17},{... | collective-permute-start | bytes 2408456 | tf_op jit(solution)/shard_map/ppermute | solution.py:35
  470.6 40.7 %collective-permute-start.21 = (bf16[448,896]{1,0:T(8,128)(2,1)}, bf16[448,896]{1,0:T(8,128)(2,1)S(1)}, u32[]{:S(2)}, u32[]{:S(2)}) collective-permute-start(bf16[448,896]{1,0:T(8,128)(2,1)} %broadcast_select_fusion.3), channel_id=1, source_target_pairs={{0,4},{4,0},{8,12},{12,8},{16,20},{20,16},{24,28},{28,24},{1,5},{5... | collective-permute-start | bytes 2408456 | tf_op jit(solution)/shard_map/ppermute | solution.py:35
  471.8 64.4 %collective-permute-start.37 = (bf16[896,768]{1,0:T(8,128)(2,1)}, bf16[896,768]{1,0:T(8,128)(2,1)}, u32[]{:S(2)}, u32[]{:S(2)}) collective-permute-start(bf16[896,768]{1,0:T(8,128)(2,1)} %collective-permute-done.refs_6_.refs_3_), channel_id=1, source_target_pairs={{0,4},{4,0},{8,12},{12,8},{16,20},{20,16},{24,28},{28,24},{1,5},{5... | collective-permute-start | bytes 4128776 | tf_op jit(solution)/shard_map/ppermute | solution.py:35
  477.0 59.1 %collective-permute-start.38 = (bf16[896,768]{1,0:T(8,128)(2,1)}, bf16[896,768]{1,0:T(8,128)(2,1)}, u32[]{:S(2)}, u32[]{:S(2)}) collective-permute-start(bf16[896,768]{1,0:T(8,128)(2,1)} %collective-permute-done.1.refs_6_.refs_5_), channel_id=1, source_target_pairs={{0,4},{4,0},{8,12},{12,8},{16,20},{20,16},{24,28},{28,24},{1,5},{5... | collective-permute-start | bytes 4128776 | tf_op jit(solution)/shard_map/ppermute | solution.py:35
  477.9 55.5 %collective-permute-start.22 = (bf16[448,896]{1,0:T(8,128)(2,1)}, bf16[448,896]{1,0:T(8,128)(2,1)}, u32[]{:S(2)}, u32[]{:S(2)}) collective-permute-start(bf16[448,896]{1,0:T(8,128)(2,1)} %broadcast_select_fusion.3), channel_id=1, source_target_pairs={{0,24},{4,28},{8,16},{12,20},{16,8},{20,12},{24,0},{28,4},{1,25},{... | collective-permute-start | bytes 2408456 | tf_op jit(solution)/shard_map/ppermute | solution.py:35
  511.3 24.8 %collective-permute-start.39 = (bf16[448,768]{1,0:T(8,128)(2,1)}, bf16[448,768]{1,0:T(8,128)(2,1)}, u32[]{:S(2)}, u32[]{:S(2)}) collective-permute-start(bf16[448,768]{1,0:T(8,128)(2,1)} %collective-permute-done.5.refs_7_), channel_id=1, source_target_pairs={{0,4},{4,0},{8,12},{12,8},{16,20},{20,16},{24,28},{28,24},{1,5},{5... | collective-permute-start | bytes 2064392 | tf_op jit(solution)/shard_map/ppermute | solution.py:35
  512.2 23.9 %collective-permute-start.40 = (bf16[448,768]{1,0:T(8,128)(2,1)}, bf16[448,768]{1,0:T(8,128)(2,1)}, u32[]{:S(2)}, u32[]{:S(2)}) collective-permute-start(bf16[448,768]{1,0:T(8,128)(2,1)} %collective-permute-done.6.refs_8_), channel_id=1, source_target_pairs={{0,4},{4,0},{8,12},{12,8},{16,20},{20,16},{24,28},{28,24},{1,5},{5... | collective-permute-start | bytes 2064392 | tf_op jit(solution)/shard_map/ppermute | solution.py:35
  551.8 190.3 %all-gather.5.cloned.1.call-start = ((), (), s32[]{:S(2)}) async-start(), calls=%async_computation.10 | async-start | bytes 12386304 | tf_op jit(solution)/shard_map/all_gather | solution.py:336
  551.8 7.3 collective-permute-start.54
  552.3 6.9 collective-permute-start.55
  552.8 6.4 collective-permute-start.57
  577.3 7.4 collective-permute-start.41
  577.7 6.9 collective-permute-start.42
  578.2 6.4 collective-permute-start.44
  602.7 46.7 %collective-permute-start.46 = (bf16[896,768]{1,0:T(8,128)(2,1)S(1)}, bf16[896,768]{1,0:T(8,128)(2,1)S(1)}, u32[]{:S(2)}, u32[]{:S(2)}) collective-permute-start(bf16[896,768]{1,0:T(8,128)(2,1)S(1)} %shard_map.32.refs_1_.refs_12_), channel_id=1, source_target_pairs={{0,8},{4,12},{8,0},{12,4},{16,24},{20,28},{24,16},{28,20},{1,9},{5... | collective-permute-start | bytes 4128776 | tf_op jit(solution)/shard_map/ppermute | solution.py:35
  604.9 44.5 %collective-permute-start.48 = (bf16[896,768]{1,0:T(8,128)(2,1)S(1)}, bf16[896,768]{1,0:T(8,128)(2,1)S(1)}, u32[]{:S(2)}, u32[]{:S(2)}) collective-permute-start(bf16[896,768]{1,0:T(8,128)(2,1)S(1)} %shard_map.32.refs_1_.refs_12_), channel_id=1, source_target_pairs={{0,16},{4,20},{8,24},{12,28},{16,0},{20,4},{24,8},{28,12},{1,17},{... | collective-permute-start | bytes 4128776 | tf_op jit(solution)/shard_map/ppermute | solution.py:35
  606.5 68.7 %collective-permute-start.45 = (bf16[896,768]{1,0:T(8,128)(2,1)S(1)}, bf16[896,768]{1,0:T(8,128)(2,1)S(1)}, u32[]{:S(2)}, u32[]{:S(2)}) collective-permute-start(bf16[896,768]{1,0:T(8,128)(2,1)S(1)} %shard_map.32.refs_1_.refs_12_), channel_id=1, source_target_pairs={{0,4},{4,0},{8,12},{12,8},{16,20},{20,16},{24,28},{28,24},{1,5},{5... | collective-permute-start | bytes 4128776 | tf_op jit(solution)/shard_map/ppermute | solution.py:35
  649.5 25.1 %collective-permute-start.50 = (bf16[448,768]{1,0:T(8,128)(2,1)S(1)}, bf16[448,768]{1,0:T(8,128)(2,1)S(1)}, u32[]{:S(2)}, u32[]{:S(2)}) collective-permute-start(bf16[448,768]{1,0:T(8,128)(2,1)S(1)} %slice.94), channel_id=1, source_target_pairs={{0,16},{4,20},{8,24},{12,28},{16,0},{20,4},{24,8},{28,12},{1,17},{... | collective-permute-start | bytes 2064392 | tf_op jit(solution)/shard_map/ppermute | solution.py:35
  651.0 23.6 %collective-permute-start.51 = (bf16[448,768]{1,0:T(8,128)(2,1)S(1)}, bf16[448,768]{1,0:T(8,128)(2,1)S(1)}, u32[]{:S(2)}, u32[]{:S(2)}) collective-permute-start(bf16[448,768]{1,0:T(8,128)(2,1)S(1)} %slice.95), channel_id=1, source_target_pairs={{0,8},{4,12},{8,0},{12,4},{16,24},{20,28},{24,16},{28,20},{1,9},{5... | collective-permute-start | bytes 2064392 | tf_op jit(solution)/shard_map/ppermute | solution.py:35
  651.7 28.1 %collective-permute-start.47 = (bf16[896,768]{1,0:T(8,128)(2,1)S(1)}, bf16[896,768]{1,0:T(8,128)(2,1)S(1)}, u32[]{:S(2)}, u32[]{:S(2)}) collective-permute-start(bf16[896,768]{1,0:T(8,128)(2,1)S(1)} %collective-permute-done.46.refs_3_), channel_id=1, source_target_pairs={{0,4},{4,0},{8,12},{12,8},{16,20},{20,16},{24,28},{28,24},{1,5},{5... | collective-permute-start | bytes 4128776 | tf_op jit(solution)/shard_map/ppermute | solution.py:35
  651.7 28.1 %collective-permute-start.49 = (bf16[896,768]{1,0:T(8,128)(2,1)S(1)}, bf16[896,768]{1,0:T(8,128)(2,1)S(1)}, u32[]{:S(2)}, u32[]{:S(2)}) collective-permute-start(bf16[896,768]{1,0:T(8,128)(2,1)S(1)} %collective-permute-done.48.refs_5_), channel_id=1, source_target_pairs={{0,4},{4,0},{8,12},{12,8},{16,20},{20,16},{24,28},{28,24},{1,5},{5... | collective-permute-start | bytes 4128776 | tf_op jit(solution)/shard_map/ppermute | solution.py:35
  699.7 37.7 %all-to-all-start.4 = ((bf16[4,224,768]{2,1,0:T(8,128)(2,1)}), bf16[4,224,768]{2,1,0:T(8,128)(2,1)}, u32[]{:S(2)}, u32[]{:S(2)}) async-start(bf16[4,224,768]{2,1,0:T(8,128)(2,1)} %bitcast.72), calls=%async_computation.4 | async-start | bytes 2752512 | tf_op jit(solution)/shard_map/all_to_all | solution.py:338
  737.5 36.9 %all-to-all-start.3 = ((bf16[4,224,768]{2,1,0:T(8,128)(2,1)}), bf16[4,224,768]{2,1,0:T(8,128)(2,1)}, u32[]{:S(2)}, u32[]{:S(2)}) async-start(bf16[4,224,768]{2,1,0:T(8,128)(2,1)} %bitcast.73), calls=%async_computation.3 | async-start | bytes 2752512 | tf_op jit(solution)/shard_map/all_to_all | solution.py:338
  (49 other events, 222.3 us)
Sparse Core Ops, SparseCore 0:
  168.5 107.9 all-reduce.4
  278.8 101.6 all-reduce.6
  384.6 53.3 all-reduce.8
  551.9 75.1 all-gather.2
  628.9 78.5 all-gather.4

commit v4 on v2

--- a/solution.py
+++ b/solution.py
@@ -129,15 +129,16 @@
 
 
 def put_block(gram, low, mine, theirs, j):
-    h, size = mine.shape
+    (mine, m), (theirs, t) = mine, theirs
+    _, h, size = mine.shape
     return pl.pallas_call(
         block_kernel,
         grid=(1,),
         out_shape=jax.ShapeDtypeStruct(gram.shape, bf16),
         in_specs=[
             pl.BlockSpec(memory_space=pltpu.SMEM),
-            pl.BlockSpec((h, size), lambda i: (0, 0)),
-            pl.BlockSpec((h, size), lambda i: (0, 0)),
+            pl.BlockSpec((None, h, size), lambda i: (m, 0, 0)),
+            pl.BlockSpec((None, h, size), lambda i: (t, 0, 0)),
             pl.BlockSpec(memory_space=pl.ANY),
         ],
         out_specs=pl.BlockSpec((None, size, size), lambda i: (j, 0, 0)),
@@ -147,6 +148,27 @@
         ),
         compiler_params=pltpu.CompilerParams(vmem_limit_bytes=VMEM_BYTES),
     )(low, mine, theirs, gram)
+
+
+def own_kernel(halves, out):
+    h = halves.shape[1]
+    out[:h, :] = halves[0]
+    out[h:, :] = halves[1]
+
+
+def start_gram(halves, count):
+    _, h, size = halves.shape
+    return pl.pallas_call(
+        own_kernel,
+        grid=(1,),
+        out_shape=jax.ShapeDtypeStruct((count, size, size), bf16),
+        in_specs=[pl.BlockSpec((2, h, size), lambda i: (0, 0, 0))],
+        out_specs=pl.BlockSpec((None, size, size), lambda i: (0, 0, 0)),
+        cost_estimate=pl.CostEstimate(
+            flops=0, bytes_accessed=4 * size * size, transcendentals=0
+        ),
+        compiler_params=pltpu.CompilerParams(vmem_limit_bytes=VMEM_BYTES),
+    )(halves)
 
 
 def product_kernel(keys, start, finish, me_ref, *refs):
@@ -239,6 +261,8 @@
     tiles, gathered, siblings, tied = [], [], [], []
     start = 0
     thirds = widths_of(width, 3)
+    if width % (9 * 256) == 0:
+        thirds = [width // 9 * n for n in (3, 4, 2)]
     for k, w in enumerate(thirds):
         first = [start + c * width for c in range(n_col)]
         part = jnp.concatenate([ortho_in[:, f : f + w] for f in first], axis=0)
@@ -255,14 +279,17 @@
     def low_of(j):
         return ((me & (1 << (j.bit_length() - 1))) == 0).astype(jnp.int32).reshape(1)
 
-    gram = jnp.zeros((n_row, block, block), bf16)
     lefts = [[s[(i, 0)] for s in siblings] for i in range(bit_x)]
     jobs = [(0, 0, None, 0), (0, 0, None, h)] + [(0, j, j - 1, 0) for j in cores]
     near = gram_pieces(lefts, jobs, [low_of(j)[0] for j in cores], scale)
     last = near = lax.psum(near, "col")
-    gram = lax.dynamic_update_slice(gram, near[:2].reshape(1, block, block), (0, 0, 0))
+    gram = start_gram(near, n_row)
     for j in cores:
-        gram = put_block(gram, low_of(j), near[1 + j], swap(near[1 + j], j), j)
+        theirs = swap(near[1 + j : 2 + j], j)
+        gram = put_block(gram, low_of(j), (near, 1 + j), (theirs, 0), j)
+    panels = [
+        add_cores({**parts, **sibling}) for parts, sibling in zip(gathered, siblings)
+    ]
     for stage in (chips[:2], chips[2:]):
         blocks = list(lefts)
         for j in stage:
@@ -272,27 +299,23 @@
             blocks.append(peers)
         jobs = [(i, bit_x + n, n, 0) for n in range(len(stage)) for i in range(bit_x)]
         pieces = gram_pieces(blocks, jobs, [low_of(j)[0] for j in stage], scale)
-        last = sums = lax.psum(after(pieces, last), "col")
+        held = list(panels[0].values()) if len(stage) == 1 else []
+        last = sums = lax.psum(after(pieces, last, *held), "col")
         for n, j in enumerate(stage):
-            for i in range(bit_x):
-                mine = sums[n * bit_x + i]
-                theirs = swap(mine, j)
-                if i > 0:
-                    mine = swap(mine, i)
-                gram = put_block(gram, low_of(j), mine, theirs, j | i)
-    panels = [
-        add_cores({**parts, **sibling}) for parts, sibling in zip(gathered, siblings)
-    ]
-
-    outs = [[] for _ in range(n_col)]
+            theirs = swap(sums[n * bit_x : (n + 1) * bit_x], j)
+            gram = put_block(gram, low_of(j), (sums, n * bit_x), (theirs, 0), j)
+            for i in cores:
+                mine = swap(sums[n * bit_x + i : n * bit_x + i + 1], i)
+                gram = put_block(gram, low_of(j), (mine, 0), (theirs, i), j | i)
+
+    outs = []
     for k, w in enumerate(thirds):
         first = product(gram, me, panels[k], 0, w)
         first_panel = lax.all_gather(first, "row", axis=0, tiled=True)
         result = product(gram, me, {None: first_panel}, 0, w, (tiles[k], first))
-        back = exchange(result)
-        for c in range(n_col):
-            outs[c].append(back[c * rows : (c + 1) * rows])
-    return jnp.concatenate([piece for out in outs for piece in out], axis=1)
+        back = lax.all_to_all(result, "col", split_axis=0, concat_axis=1, tiled=True)
+        outs.append(back.reshape(rows, n_col, w))
+    return jnp.concatenate(outs, axis=2).reshape(rows, cols)
 
 
 def solution(mesh):

time: 787 us -> 787 us (level)
  blocking collectives: 0 us -> 47.6 us
  local copies, waits for them, and re-layouts: 75 us -> 35.3 us
  Pallas kernels: 145 us -> 155 us
    all_to_all x0 -> x1, blocking collectives: none -> 47.6 us  [per_device(): lax.all_to_all(result, 'col', split_axis=0, concat_axis=1, tiled=True)]
    unnamed x81 -> x56, local copies, waits for them, and re-layouts: 43.5 us -> 10.9 us
    all_to_all x6 -> x3, waiting for transfers between devices: 92.4 us -> 61.1 us  [exchange(): return lax.all_to_all(value, 'col', split_axis=0, concat_axis=0, tiled=True)]
    ppermute x37 -> x34, waiting for transfers between devices: 166 us -> 144 us  [swap(): return lax.ppermute(value, 'row', [(r, r ^ bit) for r in range(count)])]
    psum x2, waiting for transfers between devices: 107 us -> 128 us  [per_device(): last = sums = lax.psum(after(pieces, last, *held), 'col')]
    all_to_all x6 -> x3, starting transfers between devices: 28.4 us -> 14.1 us  [exchange(): return lax.all_to_all(value, 'col', split_axis=0, concat_axis=0, tiled=True)]
    psum x1, waiting for transfers between devices: 13.3 us -> 26.5 us  [per_device(): last = near = lax.psum(near, 'col')]
    all_gather x3, waiting for transfers between devices: 99.6 us -> 111 us  [per_device(): first_panel = lax.all_gather(first, 'row', axis=0, tiled=True)]
  transfers between devices with their start and end apart: 49 -> 45, of which waited for: 25 -> 25; matrix products, arithmetic and copies ran while one was open for 5% -> 3% of each run, Pallas kernels for 15% -> 18%
where the time goes in v4:
time: 787 us; the launch traced here: 778 us
  waiting for transfers between devices  471 us (60%)
  Pallas kernels  155 us (20%)
  starting transfers between devices  48 us (6%)
  blocking collectives  47.6 us (6%)
  local copies, waits for them, and re-layouts  35.3 us (4%)
  between operations  14 us (2%)
    ppermute x34, waiting for transfers between devices, swap(): return lax.ppermute(value, 'row', [(r, r ^ bit) for r in range(count)])  144 us
    psum x2, waiting for transfers between devices, per_device(): last = sums = lax.psum(after(pieces, last, *held), 'col')  128 us
    all_gather x3, waiting for transfers between devices, per_device(): first_panel = lax.all_gather(first, 'row', axis=0, tiled=True)  111 us
    pallas_call x6, Pallas kernels, product(): pl.pallas_call(functools.partial(product_kernel, keys, start, bool(extra)...  100 us
    all_to_all x3, waiting for transfers between devices, exchange(): return lax.all_to_all(value, 'col', split_axis=0, concat_axis=0, tiled=True)  61.1 us
    all_to_all x1, blocking collectives, per_device(): lax.all_to_all(result, 'col', split_axis=0, concat_axis=1, tiled=True)  47.6 us
    pallas_call x3, Pallas kernels, gram_pieces(): pl.pallas_call(functools.partial(pieces_kernel, count, jobs, scale), out_...  37.9 us
    psum x1, waiting for transfers between devices, per_device(): last = near = lax.psum(near, 'col')  26.5 us
  transfers between devices with their start and end apart: 45, of which 25 were waited for; matrix products, arithmetic and copies ran while one was open for 3% of the time, Pallas kernels for 18%

profile of v4, /device:TPU:0, one launch (start us, length us, event | category | flops | bytes accessed | tf_op | source)
XLA Modules:
  0.0 778.0 jit_solution(9287592432951813205)
XLA Ops:
  6.5 1.4 fusion.2
  9.1 6.3 all-to-all-start
  15.4 1.6 fusion.1
  17.0 1.4 pad_maximum_fusion
  18.4 29.8 %all-to-all-done = bf16[4,224,768]{2,1,0:T(8,128)(2,1)S(1)} async-done(((bf16[4,224,768]{2,1,0:T(8,128)(2,1)}), bf16[4,224,768]{2,1,0:T(8,128)(2,1)S(1)}, u32[]{:S(2)}, u32[]{:S(2)}) %all-to-all-start) | async-done | bytes 1376288 | tf_op jit(solution)/shard_map/all_to_all | solution.py:259
  48.2 3.6 all-to-all-start.1
  51.8 1.6 collective-permute-start
  53.3 1.5 collective-permute-start.1
  57.2 25.8 %collective-permute-done.refs_6_.refs_3_ = bf16[896,768]{1,0:T(8,128)(2,1)S(1)} collective-permute-done((bf16[896,768]{1,0:T(8,128)(2,1)S(1)}, bf16[896,768]{1,0:T(8,128)(2,1)S(1)}, u32[]{:S(2)}, u32[]{:S(2)}) %collective-permute-start) | collective-permute-done | bytes 1376288 | tf_op jit(solution)/shard_map/ppermute | solution.py:35
  84.3 9.5 %all-to-all-done.1 = bf16[4,224,1024]{2,1,0:T(8,128)(2,1)S(1)} async-done(((bf16[4,224,1024]{2,1,0:T(8,128)(2,1)}), bf16[4,224,1024]{2,1,0:T(8,128)(2,1)S(1)}, u32[]{:S(2)}, u32[]{:S(2)}) %all-to-all-start.1) | async-done | bytes 1835040 | tf_op jit(solution)/shard_map/all_to_all | solution.py:259
  93.8 4.2 all-to-all-start.2
  98.7 21.8 %all-to-all-done.2 = bf16[4,224,512]{2,1,0:T(8,128)(2,1)} async-done(((bf16[4,224,512]{2,1,0:T(8,128)(2,1)}), bf16[4,224,512]{2,1,0:T(8,128)(2,1)}, u32[]{:S(2)}, u32[]{:S(2)}) %all-to-all-start.2) | async-done | bytes 917536 | tf_op jit(solution)/shard_map/all_to_all | solution.py:259
  120.5 1.5 collective-permute-start.7
  122.0 1.5 collective-permute-start.8
  123.5 11.2 %shard_map.19 = bf16[3,448,896]{2,1,0:T(8,128)(2,1)} custom-call(s32[1]{0:T(128)} %bitcast.9.low_ref, bf16[896,768]{1,0:T(8,128)(2,1)S(1)} %bitcast.30, bf16[896,1024]{1,0:T(8,128)(2,1)} %bitcast.22, bf16[896,512]{1,0:T(8,128)(2,1)} %bitcast.7.refs_2_.refs_1_, bf16[896,768]{1,0:T(8,128)(2,1)} %collective-permute-done.2.refs_3_.refs_2_, ...), custom_call_target="tpu_custom_call" | custom-call | flops 5549064192 | bytes 10665984 | tf_op jit(solution)/shard_map/pallas_call | solution.py:103
  136.1 1.5 collective-permute-start.12
  137.7 2.0 slice.84
  139.7 2.0 slice.85
  141.7 21.7 %collective-permute-done.7.refs_7_.refs_3_ = bf16[896,1024]{1,0:T(8,128)(2,1)} collective-permute-done((bf16[896,1024]{1,0:T(8,128)(2,1)S(1)}, bf16[896,1024]{1,0:T(8,128)(2,1)}, u32[]{:S(2)}, u32[]{:S(2)}) %collective-permute-start.7) | collective-permute-done | bytes 1835040 | tf_op jit(solution)/shard_map/ppermute | solution.py:35
  163.4 1.5 collective-permute-done.8.refs_10_.refs_5_
  165.0 2.2 slice.86
  167.2 2.2 slice.87
  169.3 13.4 %collective-permute-done.11.refs_8_.refs_3_ = bf16[896,512]{1,0:T(8,128)(2,1)} collective-permute-done((bf16[896,512]{1,0:T(8,128)(2,1)}, bf16[896,512]{1,0:T(8,128)(2,1)}, u32[]{:S(2)}, u32[]{:S(2)}) %collective-permute-start.11) | collective-permute-done | bytes 917536 | tf_op jit(solution)/shard_map/ppermute | solution.py:35
  183.9 1.8 slice.88
  185.8 1.8 slice.89
  187.6 17.0 %shard_map.18 = bf16[4,448,896]{2,1,0:T(8,128)(2,1)} custom-call(s32[2]{0:T(128)S(1)} %pad_add_fusion.low_ref, bf16[896,768]{1,0:T(8,128)(2,1)S(1)} %bitcast.31, bf16[896,1024]{1,0:T(8,128)(2,1)} %bitcast.23, bf16[896,512]{1,0:T(8,128)(2,1)} %bitcast.7.refs_2_.refs_1_, bf16[896,768]{1,0:T(8,128)(2,1)} %collective-permute-done.2.refs_3_.refs_2_, ...), custom_call_target="tpu_custom_call" | custom-call | flops 7398752256 | bytes 19726336 | tf_op jit(solution)/shard_map/pallas_call | solution.py:103
  204.6 26.5 %all-reduce.4.cloned.1.call-done.halves.mine = bf16[3,448,896]{2,1,0:T(8,128)(2,1)} async-done(((bf16[3,448,896]{2,1,0:T(8,128)(2,1)}), bf16[3,448,896]{2,1,0:T(8,128)(2,1)}) %all-reduce.4.cloned.1.call-update) | async-done | bytes 2408464 | tf_op jit(solution)/shard_map/psum | solution.py:285
  231.4 1.5 collective-permute-start.5
  232.9 1.5 collective-permute-start.6
  235.5 14.5 %collective-permute-done.5.refs_7_ = bf16[448,768]{1,0:T(8,128)(2,1)S(1)} collective-permute-done((bf16[448,768]{1,0:T(8,128)(2,1)}, bf16[448,768]{1,0:T(8,128)(2,1)S(1)}, u32[]{:S(2)}, u32[]{:S(2)}) %collective-permute-start.5) | collective-permute-done | bytes 688160 | tf_op jit(solution)/shard_map/ppermute | solution.py:35
  251.8 17.6 %collective-permute-done.10.refs_8_ = bf16[448,1024]{1,0:T(8,128)(2,1)S(1)} collective-permute-done((bf16[448,1024]{1,0:T(8,128)(2,1)}, bf16[448,1024]{1,0:T(8,128)(2,1)S(1)}, u32[]{:S(2)}, u32[]{:S(2)}) %collective-permute-start.10) | collective-permute-done | bytes 917536 | tf_op jit(solution)/shard_map/ppermute | solution.py:35
  269.4 1.5 collective-permute-start.14
  270.9 7.4 collective-permute-done.13.refs_7_
  279.5 1.4 pad_maximum_fusion.1.refs_7_
  281.8 9.8 %shard_map.17 = bf16[2,448,896]{2,1,0:T(8,128)(2,1)} custom-call(s32[1]{0:T(128)} %bitcast.1.low_ref, bf16[896,768]{1,0:T(8,128)(2,1)S(1)} %bitcast.32, bf16[896,1024]{1,0:T(8,128)(2,1)} %bitcast.24, bf16[896,512]{1,0:T(8,128)(2,1)} %bitcast.7.refs_2_.refs_1_, bf16[896,768]{1,0:T(8,128)(2,1)} %collective-permute-done.2.refs_3_.refs_2_, ...), custom_call_target="tpu_custom_call" | custom-call | flops 3699376128 | bytes 13991936 | tf_op jit(solution)/shard_map/pallas_call | solution.py:103
  292.4 63.5 %all-reduce.6.cloned.1.call-done.mine = bf16[4,448,896]{2,1,0:T(8,128)(2,1)} async-done(((bf16[4,448,896]{2,1,0:T(8,128)(2,1)}), bf16[4,448,896]{2,1,0:T(8,128)(2,1)}) %all-reduce.6.cloned.1.call-update) | async-done | bytes 3211280 | tf_op jit(solution)/shard_map/psum | solution.py:303
  355.9 2.2 slice.101
  358.2 1.9 fusion.3
  360.1 1.5 collective-permute-start.24
  361.6 1.5 collective-permute-start.22
  363.1 64.4 %all-reduce.8.cloned.1.call-done.mine = bf16[2,448,896]{2,1,0:T(8,128)(2,1)} async-done(((bf16[2,448,896]{2,1,0:T(8,128)(2,1)}), bf16[2,448,896]{2,1,0:T(8,128)(2,1)}) %all-reduce.8.cloned.1.call-update) | async-done | bytes 1605648 | tf_op jit(solution)/shard_map/psum | solution.py:303
  427.5 2.4 collective-permute-start.20
  430.6 1.8 collective-permute-done.23.mine
  435.5 28.8 %collective-permute-done.20.theirs = bf16[2,448,896]{2,1,0:T(8,128)(2,1)S(1)} collective-permute-done((bf16[2,448,896]{2,1,0:T(8,128)(2,1)}, bf16[2,448,896]{2,1,0:T(8,128)(2,1)S(1)}, u32[]{:S(2)}, u32[]{:S(2)}) %collective-permute-start.20) | collective-permute-done | bytes 1605664 | tf_op jit(solution)/shard_map/ppermute | solution.py:35
  465.5 2.4 shard_map.21.gram_in
  468.0 2.4 shard_map.22.gram_in
  470.4 2.4 shard_map.23.gram_in
  472.8 2.5 shard_map.24.gram_in
  475.3 3.0 shard_map.25.gram_in
  482.2 12.0 %shard_map.32.refs_3_ = bf16[896,512]{1,0:T(8,128)(2,1)} custom-call(s32[1]{0:T(128)} %bitcast.me_ref, bf16[8,896,896]{2,1,0:T(8,128)(2,1)} %shard_map.27.refs_0_, bf16[896,512]{1,0:T(8,128)(2,1)} %bitcast.7.refs_2_.refs_1_, bf16[896,512]{1,0:T(8,128)(2,1)} %collective-permute-done.4.refs_5_.refs_2_, ...), custom_call_target="tpu_custom_call" | custom-call | flops 6576668672 | bytes 20185088 | tf_op jit(solution)/shard_map/pallas_call | solution.py:223
  497.7 15.6 %shard_map.28.refs_3_ = bf16[896,768]{1,0:T(8,128)(2,1)} custom-call(s32[1]{0:T(128)} %bitcast.me_ref, bf16[8,896,896]{2,1,0:T(8,128)(2,1)} %shard_map.27.refs_0_, bf16[896,768]{1,0:T(8,128)(2,1)S(1)} %bitcast.33, bf16[896,768]{1,0:T(8,128)(2,1)} %collective-permute-done.2.refs_3_.refs_2_, bf16[896,768]{1,0:T(8,128)(2,1)} %copy-done.23, ...), custom_call_target="tpu_custom_call" | custom-call | flops 9865003008 | bytes 23855104 | tf_op jit(solution)/shard_map/pallas_call | solution.py:223
  514.9 5.4 collective-permute-done.28.refs_9_
  520.4 2.6 collective-permute-done.29.refs_10_
  525.5 20.1 %shard_map.30.refs_3_ = bf16[896,1024]{1,0:T(8,128)(2,1)} custom-call(s32[1]{0:T(128)} %bitcast.me_ref, bf16[8,896,896]{2,1,0:T(8,128)(2,1)} %shard_map.27.refs_0_, bf16[896,1024]{1,0:T(8,128)(2,1)} %bitcast.25, bf16[896,1024]{1,0:T(8,128)(2,1)} %collective-permute-done.3.refs_4_.refs_2_, bf16[896,1024]{1,0:T(8,128)(2,1)} %collective-permute-done.7.refs_7_.refs_3_, ...), custom_call_target="tpu_custom_call" | custom-call | flops 13153337344 | bytes 27525120 | tf_op jit(solution)/shard_map/pallas_call | solution.py:223
  545.6 1.6 all-gather.8.cloned.1.call-done.refs_1_
  547.3 13.6 %shard_map.33 = bf16[896,512]{1,0:T(8,128)(2,1)} custom-call(s32[1]{0:T(128)} %bitcast.me_ref, bf16[8,896,896]{2,1,0:T(8,128)(2,1)} %shard_map.27.refs_0_, bf16[7168,512]{1,0:T(8,128)(2,1)} %all-gather.8.cloned.1.call-done.refs_1_, bf16[896,512]{1,0:T(8,128)(2,1)} %bitcast.7.refs_2_.refs_1_, bf16[896,512]{1,0:T(8,128)(2,1)} %shard_map.32.refs_3_), custom_call_target="tpu_custom_call" | custom-call | flops 6576668672 | bytes 20185088 | tf_op jit(solution)/shard_map/pallas_call | solution.py:223
  560.9 4.6 all-to-all-start.5
  565.5 49.0 %all-gather.4.cloned.1.call-done.refs_1_ = bf16[7168,768]{1,0:T(8,128)(2,1)} async-done(((bf16[896,768]{1,0:T(8,128)(2,1)}), bf16[7168,768]{1,0:T(8,128)(2,1)}) %all-gather.4.cloned.1.call-update) | async-done | bytes 11010064 | tf_op jit(solution)/shard_map/all_gather | solution.py:314
  614.5 17.8 %shard_map.29 = bf16[896,768]{1,0:T(8,128)(2,1)} custom-call(s32[1]{0:T(128)} %bitcast.me_ref, bf16[8,896,896]{2,1,0:T(8,128)(2,1)} %shard_map.27.refs_0_, bf16[7168,768]{1,0:T(8,128)(2,1)} %all-gather.4.cloned.1.call-done.refs_1_, bf16[896,768]{1,0:T(8,128)(2,1)S(1)} %bitcast.34, bf16[896,768]{1,0:T(8,128)(2,1)} %shard_map.28.refs_3_), custom_call_target="tpu_custom_call" | custom-call | flops 9865003008 | bytes 23855104 | tf_op jit(solution)/shard_map/pallas_call | solution.py:223
  632.4 4.9 all-to-all-start.3
  637.3 60.0 %all-gather.6.cloned.1.call-done.refs_1_ = bf16[7168,1024]{1,0:T(8,128)(2,1)} async-done(((bf16[896,1024]{1,0:T(8,128)(2,1)}), bf16[7168,1024]{1,0:T(8,128)(2,1)}) %all-gather.6.cloned.1.call-update) | async-done | bytes 14680080 | tf_op jit(solution)/shard_map/all_gather | solution.py:314
  697.3 21.1 %shard_map.31 = bf16[896,1024]{1,0:T(8,128)(2,1)S(1)} custom-call(s32[1]{0:T(128)} %bitcast.me_ref, bf16[8,896,896]{2,1,0:T(8,128)(2,1)} %shard_map.27.refs_0_, bf16[7168,1024]{1,0:T(8,128)(2,1)} %all-gather.6.cloned.1.call-done.refs_1_, bf16[896,1024]{1,0:T(8,128)(2,1)S(1)} %bitcast.26, bf16[896,1024]{1,0:T(8,128)(2,1)} %shard_map.30.refs_3_), custom_call_target="tpu_custom_call" | custom-call | flops 13153337344 | bytes 27525120 | tf_op jit(solution)/shard_map/pallas_call | solution.py:223
  719.6 47.6 %all_to_all.81 = bf16[4,224,1024]{2,1,0:T(8,128)(2,1)S(1)} all-to-all(bf16[4,224,1024]{2,1,0:T(8,128)(2,1)} %bitcast.35), channel_id=1, replica_groups=mesh['row'=8,'col'=4] {'col'}, dimensions={0} | all-to-all | bytes 3670016 | tf_op jit(solution)/shard_map/all_to_all | solution.py:316
  768.5 2.5 copy.10
  (128 shorter events, 33.4 us)
Async XLA Ops:
  9.1 39.1 %all-to-all-start = ((bf16[4,224,768]{2,1,0:T(8,128)(2,1)}), bf16[4,224,768]{2,1,0:T(8,128)(2,1)S(1)}, u32[]{:S(2)}, u32[]{:S(2)}) async-start(bf16[4,224,768]{2,1,0:T(8,128)(2,1)} %bitcast.2), calls=%async_computation | async-start | bytes 2752512 | tf_op jit(solution)/shard_map/all_to_all | solution.py:259
  48.2 233.6 %copy-start.4 = (bf16[4,224,768]{2,1,0:T(8,128)(2,1)}, bf16[4,224,768]{2,1,0:T(8,128)(2,1)S(1)}, u32[]{:S(2)}) copy-start(bf16[4,224,768]{2,1,0:T(8,128)(2,1)S(1)} %all-to-all-done) | copy-start | bytes 4128772
  48.2 45.6 %all-to-all-start.1 = ((bf16[4,224,1024]{2,1,0:T(8,128)(2,1)}), bf16[4,224,1024]{2,1,0:T(8,128)(2,1)S(1)}, u32[]{:S(2)}, u32[]{:S(2)}) async-start(bf16[4,224,1024]{2,1,0:T(8,128)(2,1)} %bitcast.36), calls=%async_computation.1 | async-start | bytes 3670016 | tf_op jit(solution)/shard_map/all_to_all | solution.py:259
  51.8 31.2 %collective-permute-start = (bf16[896,768]{1,0:T(8,128)(2,1)S(1)}, bf16[896,768]{1,0:T(8,128)(2,1)S(1)}, u32[]{:S(2)}, u32[]{:S(2)}) collective-permute-start(bf16[896,768]{1,0:T(8,128)(2,1)S(1)} %bitcast.27), channel_id=1, source_target_pairs={{0,8},{4,12},{8,0},{12,4},{16,24},{20,28},{24,16},{28,20},{1,9},{5... | collective-permute-start | bytes 4128776 | tf_op jit(solution)/shard_map/ppermute | solution.py:35
  53.3 31.0 %collective-permute-start.1 = (bf16[896,768]{1,0:T(8,128)(2,1)S(1)}, bf16[896,768]{1,0:T(8,128)(2,1)}, u32[]{:S(2)}, u32[]{:S(2)}) collective-permute-start(bf16[896,768]{1,0:T(8,128)(2,1)S(1)} %bitcast.28), channel_id=1, source_target_pairs={{0,16},{4,20},{8,24},{12,28},{16,0},{20,4},{24,8},{28,12},{1,17},{... | collective-permute-start | bytes 4128776 | tf_op jit(solution)/shard_map/ppermute | solution.py:35
  93.8 29.7 %copy-start.2 = (bf16[4,224,1024]{2,1,0:T(8,128)(2,1)}, bf16[4,224,1024]{2,1,0:T(8,128)(2,1)S(1)}, u32[]{:S(2)}) copy-start(bf16[4,224,1024]{2,1,0:T(8,128)(2,1)S(1)} %all-to-all-done.1) | copy-start | bytes 5505028
  93.8 26.7 %all-to-all-start.2 = ((bf16[4,224,512]{2,1,0:T(8,128)(2,1)}), bf16[4,224,512]{2,1,0:T(8,128)(2,1)}, u32[]{:S(2)}, u32[]{:S(2)}) async-start(bf16[4,224,512]{2,1,0:T(8,128)(2,1)} %bitcast.39), calls=%async_computation.2 | async-start | bytes 1835008 | tf_op jit(solution)/shard_map/all_to_all | solution.py:259
  98.0 133.0 %all-reduce.4.cloned.1.call-start = ((), (), s32[]{:S(2)}) async-start(), calls=%async_computation.6 | async-start | bytes 4816896 | tf_op jit(solution)/shard_map/psum | solution.py:285
  98.1 25.4 %collective-permute-start.3 = (bf16[896,1024]{1,0:T(8,128)(2,1)S(1)}, bf16[896,1024]{1,0:T(8,128)(2,1)}, u32[]{:S(2)}, u32[]{:S(2)}) collective-permute-start(bf16[896,1024]{1,0:T(8,128)(2,1)S(1)} %bitcast.19), channel_id=1, source_target_pairs={{0,4},{4,0},{8,12},{12,8},{16,20},{20,16},{24,28},{28,24},{1,5},{5... | collective-permute-start | bytes 5505032 | tf_op jit(solution)/shard_map/ppermute | solution.py:35
  98.2 25.4 %collective-permute-start.2 = (bf16[896,768]{1,0:T(8,128)(2,1)S(1)}, bf16[896,768]{1,0:T(8,128)(2,1)}, u32[]{:S(2)}, u32[]{:S(2)}) collective-permute-start(bf16[896,768]{1,0:T(8,128)(2,1)S(1)} %bitcast.29), channel_id=1, source_target_pairs={{0,4},{4,0},{8,12},{12,8},{16,20},{20,16},{24,28},{28,24},{1,5},{5... | collective-permute-start | bytes 4128776 | tf_op jit(solution)/shard_map/ppermute | solution.py:35
  120.5 3.0 collective-permute-start.4
  120.5 42.9 %collective-permute-start.7 = (bf16[896,1024]{1,0:T(8,128)(2,1)S(1)}, bf16[896,1024]{1,0:T(8,128)(2,1)}, u32[]{:S(2)}, u32[]{:S(2)}) collective-permute-start(bf16[896,1024]{1,0:T(8,128)(2,1)S(1)} %bitcast.20), channel_id=1, source_target_pairs={{0,8},{4,12},{8,0},{12,4},{16,24},{20,28},{24,16},{28,20},{1,9},{5... | collective-permute-start | bytes 5505032 | tf_op jit(solution)/shard_map/ppermute | solution.py:35
  122.0 43.0 %collective-permute-start.8 = (bf16[896,1024]{1,0:T(8,128)(2,1)S(1)}, bf16[896,1024]{1,0:T(8,128)(2,1)}, u32[]{:S(2)}, u32[]{:S(2)}) collective-permute-start(bf16[896,1024]{1,0:T(8,128)(2,1)S(1)} %bitcast.21), channel_id=1, source_target_pairs={{0,16},{4,20},{8,24},{12,28},{16,0},{20,4},{24,8},{28,12},{1,17},{... | collective-permute-start | bytes 5505032 | tf_op jit(solution)/shard_map/ppermute | solution.py:35
  134.7 221.1 %all-reduce.6.cloned.1.call-start = ((), (), s32[]{:S(2)}) async-start(), calls=%async_computation.7 | async-start | bytes 6422528 | tf_op jit(solution)/shard_map/psum | solution.py:303
  134.8 47.9 %collective-permute-start.11 = (bf16[896,512]{1,0:T(8,128)(2,1)}, bf16[896,512]{1,0:T(8,128)(2,1)}, u32[]{:S(2)}, u32[]{:S(2)}) collective-permute-start(bf16[896,512]{1,0:T(8,128)(2,1)} %bitcast.7.refs_2_.refs_1_), channel_id=1, source_target_pairs={{0,8},{4,12},{8,0},{12,4},{16,24},{20,28},{24,16},{28,20},{1,9},{5... | collective-permute-start | bytes 2752520 | tf_op jit(solution)/shard_map/ppermute | solution.py:35
  136.1 47.8 %collective-permute-start.12 = (bf16[896,512]{1,0:T(8,128)(2,1)}, bf16[896,512]{1,0:T(8,128)(2,1)}, u32[]{:S(2)}, u32[]{:S(2)}) collective-permute-start(bf16[896,512]{1,0:T(8,128)(2,1)} %bitcast.7.refs_2_.refs_1_), channel_id=1, source_target_pairs={{0,16},{4,20},{8,24},{12,28},{16,0},{20,4},{24,8},{28,12},{1,17},{... | collective-permute-start | bytes 2752520 | tf_op jit(solution)/shard_map/ppermute | solution.py:35
  204.6 28.3 %copy-start.22 = (bf16[448,768]{1,0:T(8,128)(2,1)S(1)}, bf16[448,768]{1,0:T(8,128)(2,1)}, u32[]{:S(2)}) copy-start(bf16[448,768]{1,0:T(8,128)(2,1)} %slice.85) | copy-start | bytes 2064388
  231.1 196.4 %all-reduce.8.cloned.1.call-start = ((), (), s32[]{:S(2)}) async-start(), calls=%async_computation.8 | async-start | bytes 3211264 | tf_op jit(solution)/shard_map/psum | solution.py:303
  231.4 18.6 %collective-permute-start.5 = (bf16[448,768]{1,0:T(8,128)(2,1)}, bf16[448,768]{1,0:T(8,128)(2,1)S(1)}, u32[]{:S(2)}, u32[]{:S(2)}) collective-permute-start(bf16[448,768]{1,0:T(8,128)(2,1)} %slice.84), channel_id=1, source_target_pairs={{0,16},{4,20},{8,24},{12,28},{16,0},{20,4},{24,8},{28,12},{1,17},{... | collective-permute-start | bytes 2064392 | tf_op jit(solution)/shard_map/ppermute | solution.py:35
  232.9 18.4 %collective-permute-start.6 = (bf16[448,768]{1,0:T(8,128)(2,1)S(1)}, bf16[448,768]{1,0:T(8,128)(2,1)S(1)}, u32[]{:S(2)}, u32[]{:S(2)}) collective-permute-start(bf16[448,768]{1,0:T(8,128)(2,1)S(1)} %copy-done.22), channel_id=1, source_target_pairs={{0,8},{4,12},{8,0},{12,4},{16,24},{20,28},{24,16},{28,20},{1,9},{5... | collective-permute-start | bytes 2064392 | tf_op jit(solution)/shard_map/ppermute | solution.py:35
  234.4 35.0 %collective-permute-start.10 = (bf16[448,1024]{1,0:T(8,128)(2,1)}, bf16[448,1024]{1,0:T(8,128)(2,1)S(1)}, u32[]{:S(2)}, u32[]{:S(2)}) collective-permute-start(bf16[448,1024]{1,0:T(8,128)(2,1)} %slice.87), channel_id=1, source_target_pairs={{0,8},{4,12},{8,0},{12,4},{16,24},{20,28},{24,16},{28,20},{1,9},{5... | collective-permute-start | bytes 2752520 | tf_op jit(solution)/shard_map/ppermute | solution.py:35
  234.9 36.0 %collective-permute-start.9 = (bf16[448,1024]{1,0:T(8,128)(2,1)}, bf16[448,1024]{1,0:T(8,128)(2,1)S(1)}, u32[]{:S(2)}, u32[]{:S(2)}) collective-permute-start(bf16[448,1024]{1,0:T(8,128)(2,1)} %slice.86), channel_id=1, source_target_pairs={{0,16},{4,20},{8,24},{12,28},{16,0},{20,4},{24,8},{28,12},{1,17},{... | collective-permute-start | bytes 2752520 | tf_op jit(solution)/shard_map/ppermute | solution.py:35
  235.5 56.9 %collective-permute-start.15 = (bf16[896,768]{1,0:T(8,128)(2,1)}, bf16[896,768]{1,0:T(8,128)(2,1)}, u32[]{:S(2)}, u32[]{:S(2)}) collective-permute-start(bf16[896,768]{1,0:T(8,128)(2,1)} %copy-done.23), channel_id=1, source_target_pairs={{0,4},{4,0},{8,12},{12,8},{16,20},{20,16},{24,28},{28,24},{1,5},{5... | collective-permute-start | bytes 4128776 | tf_op jit(solution)/shard_map/ppermute | solution.py:35
  250.0 30.9 %copy-start.12 = (bf16[448,768]{1,0:T(8,128)(2,1)}, bf16[448,768]{1,0:T(8,128)(2,1)S(1)}, u32[]{:S(2)}) copy-start(bf16[448,768]{1,0:T(8,128)(2,1)S(1)} %collective-permute-done.5.refs_7_) | copy-start | bytes 2064388
  250.0 42.4 %collective-permute-start.16 = (bf16[896,768]{1,0:T(8,128)(2,1)}, bf16[896,768]{1,0:T(8,128)(2,1)}, u32[]{:S(2)}, u32[]{:S(2)}) collective-permute-start(bf16[896,768]{1,0:T(8,128)(2,1)} %collective-permute-done.1.refs_9_.refs_5_), channel_id=1, source_target_pairs={{0,4},{4,0},{8,12},{12,8},{16,20},{20,16},{24,28},{28,24},{1,5},{5... | collective-permute-start | bytes 4128776 | tf_op jit(solution)/shard_map/ppermute | solution.py:35
  251.3 29.6 %copy-start.14 = (bf16[448,768]{1,0:T(8,128)(2,1)}, bf16[448,768]{1,0:T(8,128)(2,1)S(1)}, u32[]{:S(2)}) copy-start(bf16[448,768]{1,0:T(8,128)(2,1)S(1)} %collective-permute-done.6.refs_8_) | copy-start | bytes 2064388
  251.3 27.0 %collective-permute-start.13 = (bf16[448,512]{1,0:T(8,128)(2,1)}, bf16[448,512]{1,0:T(8,128)(2,1)S(1)}, u32[]{:S(2)}, u32[]{:S(2)}) collective-permute-start(bf16[448,512]{1,0:T(8,128)(2,1)} %slice.88), channel_id=1, source_target_pairs={{0,16},{4,20},{8,24},{12,28},{16,0},{20,4},{24,8},{28,12},{1,17},{... | collective-permute-start | bytes 1376264 | tf_op jit(solution)/shard_map/ppermute | solution.py:35
  269.4 11.5 %copy-start.8 = (bf16[448,1024]{1,0:T(8,128)(2,1)}, bf16[448,1024]{1,0:T(8,128)(2,1)S(1)}, u32[]{:S(2)}) copy-start(bf16[448,1024]{1,0:T(8,128)(2,1)S(1)} %collective-permute-done.10.refs_8_) | copy-start | bytes 2752516
  269.4 11.5 %collective-permute-start.14 = (bf16[448,512]{1,0:T(8,128)(2,1)}, bf16[448,512]{1,0:T(8,128)(2,1)S(1)}, u32[]{:S(2)}, u32[]{:S(2)}) collective-permute-start(bf16[448,512]{1,0:T(8,128)(2,1)} %slice.89), channel_id=1, source_target_pairs={{0,8},{4,12},{8,0},{12,4},{16,24},{20,28},{24,16},{28,20},{1,9},{5... | collective-permute-start | bytes 1376264 | tf_op jit(solution)/shard_map/ppermute | solution.py:35
  270.9 10.0 %copy-start.10 = (bf16[448,1024]{1,0:T(8,128)(2,1)}, bf16[448,1024]{1,0:T(8,128)(2,1)S(1)}, u32[]{:S(2)}) copy-start(bf16[448,1024]{1,0:T(8,128)(2,1)S(1)} %collective-permute-done.9.refs_7_) | copy-start | bytes 2752516
  270.9 20.6 %collective-permute-start.17 = (bf16[448,768]{1,0:T(8,128)(2,1)S(1)}, bf16[448,768]{1,0:T(8,128)(2,1)S(1)}, u32[]{:S(2)}, u32[]{:S(2)}) collective-permute-start(bf16[448,768]{1,0:T(8,128)(2,1)S(1)} %collective-permute-done.5.refs_7_), channel_id=1, source_target_pairs={{0,4},{4,0},{8,12},{12,8},{16,20},{20,16},{24,28},{28,24},{1,5},{5... | collective-permute-start | bytes 2064392 | tf_op jit(solution)/shard_map/ppermute | solution.py:35
  278.3 2.7 copy-start.16
  278.3 14.1 %collective-permute-start.18 = (bf16[448,768]{1,0:T(8,128)(2,1)S(1)}, bf16[448,768]{1,0:T(8,128)(2,1)}, u32[]{:S(2)}, u32[]{:S(2)}) collective-permute-start(bf16[448,768]{1,0:T(8,128)(2,1)S(1)} %collective-permute-done.6.refs_8_), channel_id=1, source_target_pairs={{0,4},{4,0},{8,12},{12,8},{16,20},{20,16},{24,28},{28,24},{1,5},{5... | collective-permute-start | bytes 2064392 | tf_op jit(solution)/shard_map/ppermute | solution.py:35
  355.9 2.3 copy-start
  355.9 191.4 %all-gather.8.cloned.1.call-start = ((), (), s32[]{:S(2)}) async-start(), calls=%async_computation.11 | async-start | bytes 8257536 | tf_op jit(solution)/shard_map/all_gather | solution.py:314
  358.2 71.9 %collective-permute-start.25 = (bf16[1,448,896]{2,1,0:T(8,128)(2,1)}, bf16[1,448,896]{2,1,0:T(8,128)(2,1)}, u32[]{:S(2)}, u32[]{:S(2)}) collective-permute-start(bf16[1,448,896]{2,1,0:T(8,128)(2,1)} %slice.101), channel_id=1, source_target_pairs={{0,4},{4,0},{8,12},{12,8},{16,20},{20,16},{24,28},{28,24},{1,5},{5... | collective-permute-start | bytes 2408456 | tf_op jit(solution)/shard_map/ppermute | solution.py:35
  360.1 74.8 %collective-permute-start.24 = (bf16[2,448,896]{2,1,0:T(8,128)(2,1)}, bf16[2,448,896]{2,1,0:T(8,128)(2,1)}, u32[]{:S(2)}, u32[]{:S(2)}) collective-permute-start(bf16[2,448,896]{2,1,0:T(8,128)(2,1)} %get-tuple-element.51), channel_id=1, source_target_pairs={{0,8},{4,12},{8,0},{12,4},{16,24},{20,28},{24,16},{28,20},{1,9},{5... | collective-permute-start | bytes 4816904 | tf_op jit(solution)/shard_map/ppermute | solution.py:35
  361.6 73.7 %collective-permute-start.22 = (bf16[2,448,896]{2,1,0:T(8,128)(2,1)}, bf16[2,448,896]{2,1,0:T(8,128)(2,1)}, u32[]{:S(2)}, u32[]{:S(2)}) collective-permute-start(bf16[2,448,896]{2,1,0:T(8,128)(2,1)} %get-tuple-element.52), channel_id=1, source_target_pairs={{0,16},{4,20},{8,24},{12,28},{16,0},{20,4},{24,8},{28,12},{1,17},{... | collective-permute-start | bytes 4816904 | tf_op jit(solution)/shard_map/ppermute | solution.py:35
  427.5 7.8 %copy-start.17 = (bf16[448,512]{1,0:T(8,128)(2,1)S(1)}, bf16[448,512]{1,0:T(8,128)(2,1)}, u32[]{:S(2)}) copy-start(bf16[448,512]{1,0:T(8,128)(2,1)} %copy-done.16) | copy-start | bytes 1376260
  427.5 36.8 %copy-start.19 = (bf16[448,512]{1,0:T(8,128)(2,1)S(1)}, bf16[448,512]{1,0:T(8,128)(2,1)}, u32[]{:S(2)}) copy-start(bf16[448,512]{1,0:T(8,128)(2,1)} %copy-done.18) | copy-start | bytes 1376260
  427.5 36.8 %copy-start.1 = (bf16[3,448,896]{2,1,0:T(8,128)(2,1)S(1)}, bf16[3,448,896]{2,1,0:T(8,128)(2,1)}, u32[]{:S(2)}) copy-start(bf16[3,448,896]{2,1,0:T(8,128)(2,1)} %all-reduce.4.cloned.1.call-done.halves.mine) | copy-start | bytes 7225348
  427.5 36.8 %collective-permute-start.20 = (bf16[2,448,896]{2,1,0:T(8,128)(2,1)}, bf16[2,448,896]{2,1,0:T(8,128)(2,1)S(1)}, u32[]{:S(2)}, u32[]{:S(2)}) collective-permute-start(bf16[2,448,896]{2,1,0:T(8,128)(2,1)} %all-reduce.8.cloned.1.call-done.mine), channel_id=1, source_target_pairs={{0,24},{4,28},{8,16},{12,20},{16,8},{20,12},{24,0},{28,4},{1,25},{... | collective-permute-start | bytes 4816904 | tf_op jit(solution)/shard_map/ppermute | solution.py:35
  430.0 2.4 collective-permute-start.23
  430.1 3.4 collective-permute-start.21
  432.4 48.5 %collective-permute-start.30 = (bf16[896,512]{1,0:T(8,128)(2,1)}, bf16[896,512]{1,0:T(8,128)(2,1)S(1)}, u32[]{:S(2)}, u32[]{:S(2)}) collective-permute-start(bf16[896,512]{1,0:T(8,128)(2,1)} %collective-permute-done.11.refs_8_.refs_3_), channel_id=1, source_target_pairs={{0,4},{4,0},{8,12},{12,8},{16,20},{20,16},{24,28},{28,24},{1,5},{5... | collective-permute-start | bytes 2752520 | tf_op jit(solution)/shard_map/ppermute | solution.py:35
  433.5 47.4 %collective-permute-start.31 = (bf16[896,512]{1,0:T(8,128)(2,1)}, bf16[896,512]{1,0:T(8,128)(2,1)S(1)}, u32[]{:S(2)}, u32[]{:S(2)}) collective-permute-start(bf16[896,512]{1,0:T(8,128)(2,1)} %collective-permute-done.12.refs_11_.refs_5_), channel_id=1, source_target_pairs={{0,4},{4,0},{8,12},{12,8},{16,20},{20,16},{24,28},{28,24},{1,5},{5... | collective-permute-start | bytes 2752520 | tf_op jit(solution)/shard_map/ppermute | solution.py:35
  434.9 44.7 %collective-permute-start.19 = (bf16[1,448,896]{2,1,0:T(8,128)(2,1)S(1)}, bf16[1,448,896]{2,1,0:T(8,128)(2,1)S(1)}, u32[]{:S(2)}, u32[]{:S(2)}) collective-permute-start(bf16[1,448,896]{2,1,0:T(8,128)(2,1)S(1)} %slice.96), channel_id=1, source_target_pairs={{0,4},{4,0},{8,12},{12,8},{16,20},{20,16},{24,28},{28,24},{1,5},{5... | collective-permute-start | bytes 2408456 | tf_op jit(solution)/shard_map/ppermute | solution.py:35
  435.3 45.6 %collective-permute-start.32 = (bf16[448,512]{1,0:T(8,128)(2,1)S(1)}, bf16[448,512]{1,0:T(8,128)(2,1)S(1)}, u32[]{:S(2)}, u32[]{:S(2)}) collective-permute-start(bf16[448,512]{1,0:T(8,128)(2,1)S(1)} %copy-done.17), channel_id=1, source_target_pairs={{0,4},{4,0},{8,12},{12,8},{16,20},{20,16},{24,28},{28,24},{1,5},{5... | collective-permute-start | bytes 1376264 | tf_op jit(solution)/shard_map/ppermute | solution.py:35
  464.3 16.7 %collective-permute-start.33 = (bf16[448,512]{1,0:T(8,128)(2,1)S(1)}, bf16[448,512]{1,0:T(8,128)(2,1)S(1)}, u32[]{:S(2)}, u32[]{:S(2)}) collective-permute-start(bf16[448,512]{1,0:T(8,128)(2,1)S(1)} %copy-done.19), channel_id=1, source_target_pairs={{0,4},{4,0},{8,12},{12,8},{16,20},{20,16},{24,28},{28,24},{1,5},{5... | collective-permute-start | bytes 1376264 | tf_op jit(solution)/shard_map/ppermute | solution.py:35
  475.3 3.0 copy-start.6
  480.9 1.3 copy-start.27
  482.2 12.1 %copy-start.5 = (bf16[4,224,768]{2,1,0:T(8,128)(2,1)S(1)}, bf16[4,224,768]{2,1,0:T(8,128)(2,1)}, u32[]{:S(2)}) copy-start(bf16[4,224,768]{2,1,0:T(8,128)(2,1)} %copy-done.4) | copy-start | bytes 4128772
  494.2 20.2 %copy-start.11 = (bf16[448,1024]{1,0:T(8,128)(2,1)S(1)}, bf16[448,1024]{1,0:T(8,128)(2,1)}, u32[]{:S(2)}) copy-start(bf16[448,1024]{1,0:T(8,128)(2,1)} %copy-done.10) | copy-start | bytes 2752516
  494.2 20.6 %copy-start.9 = (bf16[448,1024]{1,0:T(8,128)(2,1)S(1)}, bf16[448,1024]{1,0:T(8,128)(2,1)}, u32[]{:S(2)}) copy-start(bf16[448,1024]{1,0:T(8,128)(2,1)} %copy-done.8) | copy-start | bytes 2752516
  494.2 120.3 %all-gather.4.cloned.1.call-start = ((), (), s32[]{:S(2)}) async-start(), calls=%async_computation.9 | async-start | bytes 12386304 | tf_op jit(solution)/shard_map/all_gather | solution.py:314
  513.4 183.9 %all-gather.6.cloned.1.call-start = ((), (), s32[]{:S(2)}) async-start(), calls=%async_computation.10 | async-start | bytes 16515072 | tf_op jit(solution)/shard_map/all_gather | solution.py:314
  513.4 9.6 %collective-permute-start.26 = (bf16[896,1024]{1,0:T(8,128)(2,1)}, bf16[896,1024]{1,0:T(8,128)(2,1)S(1)}, u32[]{:S(2)}, u32[]{:S(2)}) collective-permute-start(bf16[896,1024]{1,0:T(8,128)(2,1)} %collective-permute-done.7.refs_7_.refs_3_), channel_id=1, source_target_pairs={{0,4},{4,0},{8,12},{12,8},{16,20},{20,16},{24,28},{28,24},{1,5},{5... | collective-permute-start | bytes 5505032 | tf_op jit(solution)/shard_map/ppermute | solution.py:35
  514.3 8.9 %collective-permute-start.27 = (bf16[896,1024]{1,0:T(8,128)(2,1)}, bf16[896,1024]{1,0:T(8,128)(2,1)S(1)}, u32[]{:S(2)}, u32[]{:S(2)}) collective-permute-start(bf16[896,1024]{1,0:T(8,128)(2,1)} %collective-permute-done.8.refs_10_.refs_5_), channel_id=1, source_target_pairs={{0,4},{4,0},{8,12},{12,8},{16,20},{20,16},{24,28},{28,24},{1,5},{5... | collective-permute-start | bytes 5505032 | tf_op jit(solution)/shard_map/ppermute | solution.py:35
  514.4 6.0 collective-permute-start.28
  514.8 8.1 %collective-permute-start.29 = (bf16[448,1024]{1,0:T(8,128)(2,1)S(1)}, bf16[448,1024]{1,0:T(8,128)(2,1)S(1)}, u32[]{:S(2)}, u32[]{:S(2)}) collective-permute-start(bf16[448,1024]{1,0:T(8,128)(2,1)S(1)} %copy-done.9), channel_id=1, source_target_pairs={{0,4},{4,0},{8,12},{12,8},{16,20},{20,16},{24,28},{28,24},{1,5},{5... | collective-permute-start | bytes 2752520 | tf_op jit(solution)/shard_map/ppermute | solution.py:35
  524.2 1.3 copy-start.25
  560.9 71.5 %all-to-all-start.5 = ((bf16[4,224,512]{2,1,0:T(8,128)(2,1)}), bf16[4,224,512]{2,1,0:T(8,128)(2,1)}, u32[]{:S(2)}, u32[]{:S(2)}) async-start(bf16[4,224,512]{2,1,0:T(8,128)(2,1)} %bitcast.14), calls=%async_computation.5 | async-start | bytes 1835008 | tf_op jit(solution)/shard_map/all_to_all | solution.py:316
  632.4 64.9 %copy-start.3 = (bf16[4,224,1024]{2,1,0:T(8,128)(2,1)S(1)}, bf16[4,224,1024]{2,1,0:T(8,128)(2,1)}, u32[]{:S(2)}) copy-start(bf16[4,224,1024]{2,1,0:T(8,128)(2,1)} %copy-done.2) | copy-start | bytes 5505028
  632.4 87.2 %all-to-all-start.3 = ((bf16[4,224,768]{2,1,0:T(8,128)(2,1)}), bf16[4,224,768]{2,1,0:T(8,128)(2,1)S(1)}, u32[]{:S(2)}, u32[]{:S(2)}) async-start(bf16[4,224,768]{2,1,0:T(8,128)(2,1)} %bitcast.10), calls=%async_computation.3 | async-start | bytes 2752512 | tf_op jit(solution)/shard_map/all_to_all | solution.py:316
  (9 other events, 9.5 us)
Sparse Core Ops, SparseCore 0:
  134.9 96.1 all-reduce.3
  233.6 122.2 all-reduce.5
  358.2 69.2 all-reduce.7
  494.3 52.9 all-gather.7
  549.0 65.4 all-gather.3
  616.3 80.9 all-gather.5

commit v5 on v4

--- a/solution.py
+++ b/solution.py
@@ -301,6 +301,8 @@
         pieces = gram_pieces(blocks, jobs, [low_of(j)[0] for j in stage], scale)
         held = list(panels[0].values()) if len(stage) == 1 else []
         last = sums = lax.psum(after(pieces, last, *held), "col")
+        if len(stage) == 1:
+            sums, gram = lax.optimization_barrier((sums, gram))
         for n, j in enumerate(stage):
             theirs = swap(sums[n * bit_x : (n + 1) * bit_x], j)
             gram = put_block(gram, low_of(j), (sums, n * bit_x), (theirs, 0), j)
@@ -310,8 +312,13 @@
 
     outs = []
     for k, w in enumerate(thirds):
-        first = product(gram, me, panels[k], 0, w)
+        parts = dict(panels[k])
+        if k > 0:
+            parts[(0, 0)] = after(parts[(0, 0)], first)
+        first = product(gram, me, parts, 0, w)
         first_panel = lax.all_gather(first, "row", axis=0, tiled=True)
+        if k > 0:
+            first_panel = after(first_panel, result)
         result = product(gram, me, {None: first_panel}, 0, w, (tiles[k], first))
         back = lax.all_to_all(result, "col", split_axis=0, concat_axis=1, tiled=True)
         outs.append(back.reshape(rows, n_col, w))

time: 787 us -> 792 us (level)
  blocking collectives: 47.6 us -> 72.6 us
  waiting for transfers between devices: 471 us -> 458 us
    psum x2, waiting for transfers between devices: 128 us -> 87.4 us  [per_device(): last = sums = lax.psum(after(pieces, last, *held), 'col')]
    ppermute x34, waiting for transfers between devices: 144 us -> 180 us  [swap(): return lax.ppermute(value, 'row', [(r, r ^ bit) for r in range(count)])]
    all_to_all x1 -> x2, blocking collectives: 47.6 us -> 72.6 us  [per_device(): lax.all_to_all(result, 'col', split_axis=0, concat_axis=1, tiled=True)]
    all_gather x3, waiting for transfers between devices: 111 us -> 103 us  [per_device(): first_panel = lax.all_gather(first, 'row', axis=0, tiled=True)]
  transfers between devices with their start and end apart: 45 -> 44, of which waited for: 25 -> 27; matrix products, arithmetic and copies ran while one was open for 3% -> 3% of each run, Pallas kernels for 18% -> 17%
where the time goes in v5:
time: 792 us; the launch traced here: 783 us
  waiting for transfers between devices  458 us (58%)
  Pallas kernels  152 us (19%)
  blocking collectives  72.6 us (9%)
  starting transfers between devices  44.5 us (6%)
  local copies, waits for them, and re-layouts  32 us (4%)
  between operations  13.9 us (2%)
  other arithmetic  9.12 us (1%)
    ppermute x34, waiting for transfers between devices, swap(): return lax.ppermute(value, 'row', [(r, r ^ bit) for r in range(count)])  180 us
    all_gather x3, waiting for transfers between devices, per_device(): first_panel = lax.all_gather(first, 'row', axis=0, tiled=True)  103 us
    pallas_call x6, Pallas kernels, product(): pl.pallas_call(functools.partial(product_kernel, keys, start, bool(extra)...  99.2 us
    psum x2, waiting for transfers between devices, per_device(): last = sums = lax.psum(after(pieces, last, *held), 'col')  87.4 us
    all_to_all x2, blocking collectives, per_device(): lax.all_to_all(result, 'col', split_axis=0, concat_axis=1, tiled=True)  72.6 us
    all_to_all x3, waiting for transfers between devices, exchange(): return lax.all_to_all(value, 'col', split_axis=0, concat_axis=0, tiled=True)  61.1 us
    pallas_call x3, Pallas kernels, gram_pieces(): pl.pallas_call(functools.partial(pieces_kernel, count, jobs, scale), out_...  38 us
    psum x1, waiting for transfers between devices, per_device(): last = near = lax.psum(near, 'col')  26.5 us
  transfers between devices with their start and end apart: 44, of which 27 were waited for; matrix products, arithmetic and copies ran while one was open for 3% of the time, Pallas kernels for 17%

profile of v5, /device:TPU:0, one launch (start us, length us, event | category | flops | bytes accessed | tf_op | source)
XLA Modules:
  0.0 782.9 jit_solution(15397646182433479582)
XLA Ops:
  9.1 6.3 all-to-all-start
  15.4 1.6 fusion.1
  18.4 29.8 %all-to-all-done = bf16[4,224,768]{2,1,0:T(8,128)(2,1)S(1)} async-done(((bf16[4,224,768]{2,1,0:T(8,128)(2,1)}), bf16[4,224,768]{2,1,0:T(8,128)(2,1)S(1)}, u32[]{:S(2)}, u32[]{:S(2)}) %all-to-all-start) | async-done | bytes 1376288 | tf_op jit(solution)/shard_map/all_to_all | solution.py:259
  48.2 3.6 all-to-all-start.1
  51.8 1.6 collective-permute-start
  53.3 1.5 collective-permute-start.1
  57.2 25.8 %collective-permute-done.refs_6_.refs_3_ = bf16[896,768]{1,0:T(8,128)(2,1)S(1)} collective-permute-done((bf16[896,768]{1,0:T(8,128)(2,1)S(1)}, bf16[896,768]{1,0:T(8,128)(2,1)S(1)}, u32[]{:S(2)}, u32[]{:S(2)}) %collective-permute-start) | collective-permute-done | bytes 1376288 | tf_op jit(solution)/shard_map/ppermute | solution.py:35
  84.3 9.5 %all-to-all-done.1 = bf16[4,224,1024]{2,1,0:T(8,128)(2,1)S(1)} async-done(((bf16[4,224,1024]{2,1,0:T(8,128)(2,1)}), bf16[4,224,1024]{2,1,0:T(8,128)(2,1)S(1)}, u32[]{:S(2)}, u32[]{:S(2)}) %all-to-all-start.1) | async-done | bytes 1835040 | tf_op jit(solution)/shard_map/all_to_all | solution.py:259
  93.8 4.2 all-to-all-start.2
  98.7 21.8 %all-to-all-done.2 = bf16[4,224,512]{2,1,0:T(8,128)(2,1)} async-done(((bf16[4,224,512]{2,1,0:T(8,128)(2,1)}), bf16[4,224,512]{2,1,0:T(8,128)(2,1)}, u32[]{:S(2)}, u32[]{:S(2)}) %all-to-all-start.2) | async-done | bytes 917536 | tf_op jit(solution)/shard_map/all_to_all | solution.py:259
  120.5 1.5 collective-permute-start.7
  122.0 1.5 collective-permute-start.8
  123.6 11.2 %shard_map.19 = bf16[3,448,896]{2,1,0:T(8,128)(2,1)} custom-call(s32[1]{0:T(128)} %bitcast.9.low_ref, bf16[896,768]{1,0:T(8,128)(2,1)S(1)} %bitcast.30, bf16[896,1024]{1,0:T(8,128)(2,1)} %bitcast.22, bf16[896,512]{1,0:T(8,128)(2,1)} %bitcast.7.refs_2_.refs_1_, bf16[896,768]{1,0:T(8,128)(2,1)} %collective-permute-done.2.refs_3_.refs_2_, ...), custom_call_target="tpu_custom_call" | custom-call | flops 5549064192 | bytes 10665984 | tf_op jit(solution)/shard_map/pallas_call | solution.py:103
  136.1 1.5 collective-permute-start.12
  137.7 2.0 slice.84
  139.7 2.0 slice.85
  141.7 21.7 %collective-permute-done.7.refs_7_.refs_3_ = bf16[896,1024]{1,0:T(8,128)(2,1)} collective-permute-done((bf16[896,1024]{1,0:T(8,128)(2,1)S(1)}, bf16[896,1024]{1,0:T(8,128)(2,1)}, u32[]{:S(2)}, u32[]{:S(2)}) %collective-permute-start.7) | collective-permute-done | bytes 1835040 | tf_op jit(solution)/shard_map/ppermute | solution.py:35
  163.4 1.5 collective-permute-done.8.refs_10_.refs_5_
  167.5 15.2 %collective-permute-done.11.refs_8_.refs_3_ = bf16[896,512]{1,0:T(8,128)(2,1)} collective-permute-done((bf16[896,512]{1,0:T(8,128)(2,1)}, bf16[896,512]{1,0:T(8,128)(2,1)}, u32[]{:S(2)}, u32[]{:S(2)}) %collective-permute-start.11) | collective-permute-done | bytes 917536 | tf_op jit(solution)/shard_map/ppermute | solution.py:35
  183.9 1.8 slice.88
  185.7 1.8 slice.89
  187.6 17.0 %shard_map.18 = bf16[4,448,896]{2,1,0:T(8,128)(2,1)} custom-call(s32[2]{0:T(128)S(1)} %pad_add_fusion.low_ref, bf16[896,768]{1,0:T(8,128)(2,1)S(1)} %bitcast.31, bf16[896,1024]{1,0:T(8,128)(2,1)} %bitcast.23, bf16[896,512]{1,0:T(8,128)(2,1)} %bitcast.7.refs_2_.refs_1_, bf16[896,768]{1,0:T(8,128)(2,1)} %collective-permute-done.2.refs_3_.refs_2_, ...), custom_call_target="tpu_custom_call" | custom-call | flops 7398752256 | bytes 19726336 | tf_op jit(solution)/shard_map/pallas_call | solution.py:103
  204.6 26.5 %all-reduce.4.cloned.1.call-done.halves.mine = bf16[3,448,896]{2,1,0:T(8,128)(2,1)} async-done(((bf16[3,448,896]{2,1,0:T(8,128)(2,1)}), bf16[3,448,896]{2,1,0:T(8,128)(2,1)}) %all-reduce.4.cloned.1.call-update) | async-done | bytes 2408464 | tf_op jit(solution)/shard_map/psum | solution.py:285
  231.4 1.5 collective-permute-start.10
  232.9 1.5 collective-permute-start.5
  235.5 16.1 %collective-permute-done.5.refs_7_ = bf16[448,768]{1,0:T(8,128)(2,1)} collective-permute-done((bf16[448,768]{1,0:T(8,128)(2,1)}, bf16[448,768]{1,0:T(8,128)(2,1)}, u32[]{:S(2)}, u32[]{:S(2)}) %collective-permute-start.5) | collective-permute-done | bytes 688160 | tf_op jit(solution)/shard_map/ppermute | solution.py:35
  251.6 16.7 %collective-permute-done.6.refs_8_ = bf16[448,768]{1,0:T(8,128)(2,1)} collective-permute-done((bf16[448,768]{1,0:T(8,128)(2,1)}, bf16[448,768]{1,0:T(8,128)(2,1)}, u32[]{:S(2)}, u32[]{:S(2)}) %collective-permute-start.6) | collective-permute-done | bytes 688160 | tf_op jit(solution)/shard_map/ppermute | solution.py:35
  268.3 1.5 collective-permute-start.13
  269.8 1.5 collective-permute-start.14
  271.3 2.5 pad_maximum_fusion.3.refs_6_
  273.8 1.5 pad_maximum_fusion.1.refs_7_
  275.3 4.6 collective-permute-done.13.refs_7_
  281.9 9.8 %shard_map.17 = bf16[2,448,896]{2,1,0:T(8,128)(2,1)} custom-call(s32[1]{0:T(128)} %bitcast.1.low_ref, bf16[896,768]{1,0:T(8,128)(2,1)S(1)} %bitcast.32, bf16[896,1024]{1,0:T(8,128)(2,1)} %bitcast.24, bf16[896,512]{1,0:T(8,128)(2,1)} %bitcast.7.refs_2_.refs_1_, bf16[896,768]{1,0:T(8,128)(2,1)} %collective-permute-done.2.refs_3_.refs_2_, ...), custom_call_target="tpu_custom_call" | custom-call | flops 3699376128 | bytes 13991936 | tf_op jit(solution)/shard_map/pallas_call | solution.py:103
  291.7 64.1 %all-reduce.6.cloned.1.call-done.mine = bf16[4,448,896]{2,1,0:T(8,128)(2,1)} async-done(((bf16[4,448,896]{2,1,0:T(8,128)(2,1)}), bf16[4,448,896]{2,1,0:T(8,128)(2,1)}) %all-reduce.6.cloned.1.call-update) | async-done | bytes 3211280 | tf_op jit(solution)/shard_map/psum | solution.py:303
  355.9 3.8 fusion.3
  359.7 1.5 collective-permute-start.22
  361.2 1.5 collective-permute-start.20
  368.3 28.5 %collective-permute-done.22.theirs = bf16[2,448,896]{2,1,0:T(8,128)(2,1)} collective-permute-done((bf16[2,448,896]{2,1,0:T(8,128)(2,1)}, bf16[2,448,896]{2,1,0:T(8,128)(2,1)}, u32[]{:S(2)}, u32[]{:S(2)}) %collective-permute-start.22) | collective-permute-done | bytes 1605664 | tf_op jit(solution)/shard_map/ppermute | solution.py:35
  396.8 2.4 shard_map.22.gram_in
  399.2 2.5 shard_map.23.gram_in
  401.7 2.5 shard_map.24.gram_in
  404.2 2.8 shard_map.25.gram_in
  406.9 23.3 %all-reduce.8.cloned.1.call-done.mine = bf16[2,448,896]{2,1,0:T(8,128)(2,1)} async-done(((bf16[2,448,896]{2,1,0:T(8,128)(2,1)}), bf16[2,448,896]{2,1,0:T(8,128)(2,1)}) %all-reduce.8.cloned.1.call-update) | async-done | bytes 1605648 | tf_op jit(solution)/shard_map/psum | solution.py:303
  430.2 2.4 collective-permute-start.25
  433.9 33.1 %collective-permute-done.25.theirs = bf16[2,448,896]{2,1,0:T(8,128)(2,1)S(1)} collective-permute-done((bf16[2,448,896]{2,1,0:T(8,128)(2,1)}, bf16[2,448,896]{2,1,0:T(8,128)(2,1)S(1)}, u32[]{:S(2)}, u32[]{:S(2)}) %collective-permute-start.25) | collective-permute-done | bytes 1605664 | tf_op jit(solution)/shard_map/ppermute | solution.py:35
  470.3 15.7 %shard_map.28.refs_3_ = bf16[896,768]{1,0:T(8,128)(2,1)} custom-call(s32[1]{0:T(128)} %bitcast.me_ref, bf16[8,896,896]{2,1,0:T(8,128)(2,1)} %shard_map.27.refs_0_, bf16[896,768]{1,0:T(8,128)(2,1)S(1)} %bitcast.33, bf16[896,768]{1,0:T(8,128)(2,1)} %collective-permute-done.2.refs_3_.refs_2_, bf16[896,768]{1,0:T(8,128)(2,1)} %copy-done.17, ...), custom_call_target="tpu_custom_call" | custom-call | flops 9865003008 | bytes 23855104 | tf_op jit(solution)/shard_map/pallas_call | solution.py:223
  487.2 5.4 collective-permute-done.28.refs_9_
  492.5 2.6 collective-permute-done.29.refs_10_
  497.7 20.1 %shard_map.30.refs_3_ = bf16[896,1024]{1,0:T(8,128)(2,1)} custom-call(s32[1]{0:T(128)} %bitcast.me_ref, bf16[8,896,896]{2,1,0:T(8,128)(2,1)} %shard_map.27.refs_0_, bf16[896,1024]{1,0:T(8,128)(2,1)} %bitcast.25, bf16[896,1024]{1,0:T(8,128)(2,1)} %collective-permute-done.3.refs_4_.refs_2_, bf16[896,1024]{1,0:T(8,128)(2,1)} %collective-permute-done.7.refs_7_.refs_3_, ...), custom_call_target="tpu_custom_call" | custom-call | flops 13153337344 | bytes 27525120 | tf_op jit(solution)/shard_map/pallas_call | solution.py:223
  519.4 2.6 collective-permute-done.32.refs_9_
  522.0 2.0 collective-permute-done.33.refs_10_
  524.0 1.8 collective-permute-done.31.refs_6_
  526.8 11.8 %shard_map.32.refs_3_ = bf16[896,512]{1,0:T(8,128)(2,1)} custom-call(s32[1]{0:T(128)} %bitcast.me_ref, bf16[8,896,896]{2,1,0:T(8,128)(2,1)} %shard_map.27.refs_0_, bf16[896,512]{1,0:T(8,128)(2,1)} %bitcast.7.refs_2_.refs_1_, bf16[896,512]{1,0:T(8,128)(2,1)} %collective-permute-done.4.refs_5_.refs_2_, ...), custom_call_target="tpu_custom_call" | custom-call | flops 6576668672 | bytes 20185088 | tf_op jit(solution)/shard_map/pallas_call | solution.py:223
  538.7 13.4 %all-gather.4.cloned.1.call-done.refs_1_ = bf16[7168,768]{1,0:T(8,128)(2,1)} async-done(((bf16[896,768]{1,0:T(8,128)(2,1)}), bf16[7168,768]{1,0:T(8,128)(2,1)}) %all-gather.4.cloned.1.call-update) | async-done | bytes 11010064 | tf_op jit(solution)/shard_map/all_gather | solution.py:319
  552.1 17.8 %shard_map.29 = bf16[896,768]{1,0:T(8,128)(2,1)} custom-call(s32[1]{0:T(128)} %bitcast.me_ref, bf16[8,896,896]{2,1,0:T(8,128)(2,1)} %shard_map.27.refs_0_, bf16[7168,768]{1,0:T(8,128)(2,1)} %all-gather.4.cloned.1.call-done.refs_1_, bf16[896,768]{1,0:T(8,128)(2,1)S(1)} %bitcast.34, bf16[896,768]{1,0:T(8,128)(2,1)} %shard_map.28.refs_3_), custom_call_target="tpu_custom_call" | custom-call | flops 9865003008 | bytes 23855104 | tf_op jit(solution)/shard_map/pallas_call | solution.py:223
  570.0 5.2 all-to-all-start.3
  575.2 59.7 %all-gather.6.cloned.1.call-done.refs_1_ = bf16[7168,1024]{1,0:T(8,128)(2,1)} async-done(((bf16[896,1024]{1,0:T(8,128)(2,1)}), bf16[7168,1024]{1,0:T(8,128)(2,1)}) %all-gather.6.cloned.1.call-update) | async-done | bytes 14680080 | tf_op jit(solution)/shard_map/all_gather | solution.py:319
  634.9 21.1 %shard_map.31 = bf16[896,1024]{1,0:T(8,128)(2,1)S(1)} custom-call(s32[1]{0:T(128)} %bitcast.me_ref, bf16[8,896,896]{2,1,0:T(8,128)(2,1)} %shard_map.27.refs_0_, bf16[7168,1024]{1,0:T(8,128)(2,1)} %all-gather.6.cloned.1.call-done.refs_1_, bf16[896,1024]{1,0:T(8,128)(2,1)S(1)} %bitcast.26, bf16[896,1024]{1,0:T(8,128)(2,1)} %shard_map.30.refs_3_), custom_call_target="tpu_custom_call" | custom-call | flops 13153337344 | bytes 27525120 | tf_op jit(solution)/shard_map/pallas_call | solution.py:223
  657.2 29.5 %all-gather.8.cloned.1.call-done.refs_1_ = bf16[7168,512]{1,0:T(8,128)(2,1)} async-done(((bf16[896,512]{1,0:T(8,128)(2,1)}), bf16[7168,512]{1,0:T(8,128)(2,1)}) %all-gather.8.cloned.1.call-update) | async-done | bytes 7340048 | tf_op jit(solution)/shard_map/all_gather | solution.py:319
  686.6 12.7 %shard_map.33 = bf16[896,512]{1,0:T(8,128)(2,1)S(1)} custom-call(s32[1]{0:T(128)} %bitcast.me_ref, bf16[8,896,896]{2,1,0:T(8,128)(2,1)} %shard_map.27.refs_0_, bf16[7168,512]{1,0:T(8,128)(2,1)} %all-gather.8.cloned.1.call-done.refs_1_, bf16[896,512]{1,0:T(8,128)(2,1)} %bitcast.7.refs_2_.refs_1_, bf16[896,512]{1,0:T(8,128)(2,1)} %shard_map.32.refs_3_), custom_call_target="tpu_custom_call" | custom-call | flops 6576668672 | bytes 20185088 | tf_op jit(solution)/shard_map/pallas_call | solution.py:223
  699.3 27.9 %all_to_all.81 = bf16[4,224,512]{2,1,0:T(8,128)(2,1)S(1)} all-to-all(bf16[4,224,512]{2,1,0:T(8,128)(2,1)S(1)} %bitcast.36), channel_id=1, replica_groups=mesh['row'=8,'col'=4] {'col'}, dimensions={0} | all-to-all | bytes 1835008 | tf_op jit(solution)/shard_map/all_to_all | solution.py:323
  727.2 44.7 %all_to_all.82 = bf16[4,224,1024]{2,1,0:T(8,128)(2,1)S(1)} all-to-all(bf16[4,224,1024]{2,1,0:T(8,128)(2,1)S(1)} %bitcast.35), channel_id=1, replica_groups=mesh['row'=8,'col'=4] {'col'}, dimensions={0} | all-to-all | bytes 3670016 | tf_op jit(solution)/shard_map/all_to_all | solution.py:323
  771.9 1.5 maximum_bitcast_fusion
  773.4 2.5 copy.10
  (115 shorter events, 34.5 us)
Async XLA Ops:
  9.1 39.1 %all-to-all-start = ((bf16[4,224,768]{2,1,0:T(8,128)(2,1)}), bf16[4,224,768]{2,1,0:T(8,128)(2,1)S(1)}, u32[]{:S(2)}, u32[]{:S(2)}) async-start(bf16[4,224,768]{2,1,0:T(8,128)(2,1)} %bitcast.2), calls=%async_computation | async-start | bytes 2752512 | tf_op jit(solution)/shard_map/all_to_all | solution.py:259
  48.2 233.7 %copy-start.4 = (bf16[4,224,768]{2,1,0:T(8,128)(2,1)}, bf16[4,224,768]{2,1,0:T(8,128)(2,1)S(1)}, u32[]{:S(2)}) copy-start(bf16[4,224,768]{2,1,0:T(8,128)(2,1)S(1)} %all-to-all-done) | copy-start | bytes 4128772
  48.2 45.6 %all-to-all-start.1 = ((bf16[4,224,1024]{2,1,0:T(8,128)(2,1)}), bf16[4,224,1024]{2,1,0:T(8,128)(2,1)S(1)}, u32[]{:S(2)}, u32[]{:S(2)}) async-start(bf16[4,224,1024]{2,1,0:T(8,128)(2,1)} %bitcast.37), calls=%async_computation.1 | async-start | bytes 3670016 | tf_op jit(solution)/shard_map/all_to_all | solution.py:259
  51.8 31.2 %collective-permute-start = (bf16[896,768]{1,0:T(8,128)(2,1)S(1)}, bf16[896,768]{1,0:T(8,128)(2,1)S(1)}, u32[]{:S(2)}, u32[]{:S(2)}) collective-permute-start(bf16[896,768]{1,0:T(8,128)(2,1)S(1)} %bitcast.27), channel_id=1, source_target_pairs={{0,8},{4,12},{8,0},{12,4},{16,24},{20,28},{24,16},{28,20},{1,9},{5... | collective-permute-start | bytes 4128776 | tf_op jit(solution)/shard_map/ppermute | solution.py:35
  53.3 31.0 %collective-permute-start.1 = (bf16[896,768]{1,0:T(8,128)(2,1)S(1)}, bf16[896,768]{1,0:T(8,128)(2,1)}, u32[]{:S(2)}, u32[]{:S(2)}) collective-permute-start(bf16[896,768]{1,0:T(8,128)(2,1)S(1)} %bitcast.28), channel_id=1, source_target_pairs={{0,16},{4,20},{8,24},{12,28},{16,0},{20,4},{24,8},{28,12},{1,17},{... | collective-permute-start | bytes 4128776 | tf_op jit(solution)/shard_map/ppermute | solution.py:35
  83.0 1.2 copy-start.17
  93.8 29.7 %copy-start.2 = (bf16[4,224,1024]{2,1,0:T(8,128)(2,1)}, bf16[4,224,1024]{2,1,0:T(8,128)(2,1)S(1)}, u32[]{:S(2)}) copy-start(bf16[4,224,1024]{2,1,0:T(8,128)(2,1)S(1)} %all-to-all-done.1) | copy-start | bytes 5505028
  93.8 26.7 %all-to-all-start.2 = ((bf16[4,224,512]{2,1,0:T(8,128)(2,1)}), bf16[4,224,512]{2,1,0:T(8,128)(2,1)}, u32[]{:S(2)}, u32[]{:S(2)}) async-start(bf16[4,224,512]{2,1,0:T(8,128)(2,1)} %bitcast.39), calls=%async_computation.2 | async-start | bytes 1835008 | tf_op jit(solution)/shard_map/all_to_all | solution.py:259
  98.1 133.0 %all-reduce.4.cloned.1.call-start = ((), (), s32[]{:S(2)}) async-start(), calls=%async_computation.6 | async-start | bytes 4816896 | tf_op jit(solution)/shard_map/psum | solution.py:285
  98.1 25.4 %collective-permute-start.3 = (bf16[896,1024]{1,0:T(8,128)(2,1)S(1)}, bf16[896,1024]{1,0:T(8,128)(2,1)}, u32[]{:S(2)}, u32[]{:S(2)}) collective-permute-start(bf16[896,1024]{1,0:T(8,128)(2,1)S(1)} %bitcast.19), channel_id=1, source_target_pairs={{0,4},{4,0},{8,12},{12,8},{16,20},{20,16},{24,28},{28,24},{1,5},{5... | collective-permute-start | bytes 5505032 | tf_op jit(solution)/shard_map/ppermute | solution.py:35
  98.2 25.4 %collective-permute-start.2 = (bf16[896,768]{1,0:T(8,128)(2,1)S(1)}, bf16[896,768]{1,0:T(8,128)(2,1)}, u32[]{:S(2)}, u32[]{:S(2)}) collective-permute-start(bf16[896,768]{1,0:T(8,128)(2,1)S(1)} %bitcast.29), channel_id=1, source_target_pairs={{0,4},{4,0},{8,12},{12,8},{16,20},{20,16},{24,28},{28,24},{1,5},{5... | collective-permute-start | bytes 4128776 | tf_op jit(solution)/shard_map/ppermute | solution.py:35
  120.5 3.0 collective-permute-start.4
  120.5 42.9 %collective-permute-start.7 = (bf16[896,1024]{1,0:T(8,128)(2,1)S(1)}, bf16[896,1024]{1,0:T(8,128)(2,1)}, u32[]{:S(2)}, u32[]{:S(2)}) collective-permute-start(bf16[896,1024]{1,0:T(8,128)(2,1)S(1)} %bitcast.20), channel_id=1, source_target_pairs={{0,8},{4,12},{8,0},{12,4},{16,24},{20,28},{24,16},{28,20},{1,9},{5... | collective-permute-start | bytes 5505032 | tf_op jit(solution)/shard_map/ppermute | solution.py:35
  122.0 43.0 %collective-permute-start.8 = (bf16[896,1024]{1,0:T(8,128)(2,1)S(1)}, bf16[896,1024]{1,0:T(8,128)(2,1)}, u32[]{:S(2)}, u32[]{:S(2)}) collective-permute-start(bf16[896,1024]{1,0:T(8,128)(2,1)S(1)} %bitcast.21), channel_id=1, source_target_pairs={{0,16},{4,20},{8,24},{12,28},{16,0},{20,4},{24,8},{28,12},{1,17},{... | collective-permute-start | bytes 5505032 | tf_op jit(solution)/shard_map/ppermute | solution.py:35
  134.8 221.1 %all-reduce.6.cloned.1.call-start = ((), (), s32[]{:S(2)}) async-start(), calls=%async_computation.7 | async-start | bytes 6422528 | tf_op jit(solution)/shard_map/psum | solution.py:303
  134.8 47.9 %collective-permute-start.11 = (bf16[896,512]{1,0:T(8,128)(2,1)}, bf16[896,512]{1,0:T(8,128)(2,1)}, u32[]{:S(2)}, u32[]{:S(2)}) collective-permute-start(bf16[896,512]{1,0:T(8,128)(2,1)} %bitcast.7.refs_2_.refs_1_), channel_id=1, source_target_pairs={{0,8},{4,12},{8,0},{12,4},{16,24},{20,28},{24,16},{28,20},{1,9},{5... | collective-permute-start | bytes 2752520 | tf_op jit(solution)/shard_map/ppermute | solution.py:35
  136.1 47.8 %collective-permute-start.12 = (bf16[896,512]{1,0:T(8,128)(2,1)}, bf16[896,512]{1,0:T(8,128)(2,1)}, u32[]{:S(2)}, u32[]{:S(2)}) collective-permute-start(bf16[896,512]{1,0:T(8,128)(2,1)} %bitcast.7.refs_2_.refs_1_), channel_id=1, source_target_pairs={{0,16},{4,20},{8,24},{12,28},{16,0},{20,4},{24,8},{28,12},{1,17},{... | collective-permute-start | bytes 2752520 | tf_op jit(solution)/shard_map/ppermute | solution.py:35
  231.1 199.1 %all-reduce.8.cloned.1.call-start = ((), (), s32[]{:S(2)}) async-start(), calls=%async_computation.8 | async-start | bytes 3211264 | tf_op jit(solution)/shard_map/psum | solution.py:303
  231.4 38.4 %collective-permute-start.10 = (bf16[448,1024]{1,0:T(8,128)(2,1)S(1)}, bf16[448,1024]{1,0:T(8,128)(2,1)S(1)}, u32[]{:S(2)}, u32[]{:S(2)}) collective-permute-start(bf16[448,1024]{1,0:T(8,128)(2,1)S(1)} %slice.87), channel_id=1, source_target_pairs={{0,8},{4,12},{8,0},{12,4},{16,24},{20,28},{24,16},{28,20},{1,9},{5... | collective-permute-start | bytes 2752520 | tf_op jit(solution)/shard_map/ppermute | solution.py:35
  232.9 18.7 %collective-permute-start.5 = (bf16[448,768]{1,0:T(8,128)(2,1)}, bf16[448,768]{1,0:T(8,128)(2,1)}, u32[]{:S(2)}, u32[]{:S(2)}) collective-permute-start(bf16[448,768]{1,0:T(8,128)(2,1)} %slice.84), channel_id=1, source_target_pairs={{0,16},{4,20},{8,24},{12,28},{16,0},{20,4},{24,8},{28,12},{1,17},{... | collective-permute-start | bytes 2064392 | tf_op jit(solution)/shard_map/ppermute | solution.py:35
  234.4 34.0 %collective-permute-start.6 = (bf16[448,768]{1,0:T(8,128)(2,1)}, bf16[448,768]{1,0:T(8,128)(2,1)}, u32[]{:S(2)}, u32[]{:S(2)}) collective-permute-start(bf16[448,768]{1,0:T(8,128)(2,1)} %slice.85), channel_id=1, source_target_pairs={{0,8},{4,12},{8,0},{12,4},{16,24},{20,28},{24,16},{28,20},{1,9},{5... | collective-permute-start | bytes 2064392 | tf_op jit(solution)/shard_map/ppermute | solution.py:35
  234.9 38.8 %collective-permute-start.9 = (bf16[448,1024]{1,0:T(8,128)(2,1)S(1)}, bf16[448,1024]{1,0:T(8,128)(2,1)S(1)}, u32[]{:S(2)}, u32[]{:S(2)}) collective-permute-start(bf16[448,1024]{1,0:T(8,128)(2,1)S(1)} %slice.86), channel_id=1, source_target_pairs={{0,16},{4,20},{8,24},{12,28},{16,0},{20,4},{24,8},{28,12},{1,17},{... | collective-permute-start | bytes 2752520 | tf_op jit(solution)/shard_map/ppermute | solution.py:35
  235.5 127.2 %collective-permute-start.15 = (bf16[896,768]{1,0:T(8,128)(2,1)}, bf16[896,768]{1,0:T(8,128)(2,1)}, u32[]{:S(2)}, u32[]{:S(2)}) collective-permute-start(bf16[896,768]{1,0:T(8,128)(2,1)} %copy-done.17), channel_id=1, source_target_pairs={{0,4},{4,0},{8,12},{12,8},{16,20},{20,16},{24,28},{28,24},{1,5},{5... | collective-permute-start | bytes 4128776 | tf_op jit(solution)/shard_map/ppermute | solution.py:35
  251.6 111.1 %collective-permute-start.16 = (bf16[896,768]{1,0:T(8,128)(2,1)}, bf16[896,768]{1,0:T(8,128)(2,1)}, u32[]{:S(2)}, u32[]{:S(2)}) collective-permute-start(bf16[896,768]{1,0:T(8,128)(2,1)} %collective-permute-done.1.refs_9_.refs_5_), channel_id=1, source_target_pairs={{0,4},{4,0},{8,12},{12,8},{16,20},{20,16},{24,28},{28,24},{1,5},{5... | collective-permute-start | bytes 4128776 | tf_op jit(solution)/shard_map/ppermute | solution.py:35
  268.3 11.5 %collective-permute-start.13 = (bf16[448,512]{1,0:T(8,128)(2,1)}, bf16[448,512]{1,0:T(8,128)(2,1)S(1)}, u32[]{:S(2)}, u32[]{:S(2)}) collective-permute-start(bf16[448,512]{1,0:T(8,128)(2,1)} %slice.88), channel_id=1, source_target_pairs={{0,16},{4,20},{8,24},{12,28},{16,0},{20,4},{24,8},{28,12},{1,17},{... | collective-permute-start | bytes 1376264 | tf_op jit(solution)/shard_map/ppermute | solution.py:35
  269.8 5.5 copy-start.9
  269.8 11.3 %collective-permute-start.14 = (bf16[448,512]{1,0:T(8,128)(2,1)}, bf16[448,512]{1,0:T(8,128)(2,1)S(1)}, u32[]{:S(2)}, u32[]{:S(2)}) collective-permute-start(bf16[448,512]{1,0:T(8,128)(2,1)} %slice.89), channel_id=1, source_target_pairs={{0,8},{4,12},{8,0},{12,4},{16,24},{20,28},{24,16},{28,20},{1,9},{5... | collective-permute-start | bytes 1376264 | tf_op jit(solution)/shard_map/ppermute | solution.py:35
  273.8 1.5 copy-start.11
  273.8 87.4 %collective-permute-start.17 = (bf16[448,768]{1,0:T(8,128)(2,1)}, bf16[448,768]{1,0:T(8,128)(2,1)}, u32[]{:S(2)}, u32[]{:S(2)}) collective-permute-start(bf16[448,768]{1,0:T(8,128)(2,1)} %collective-permute-done.5.refs_7_), channel_id=1, source_target_pairs={{0,4},{4,0},{8,12},{12,8},{16,20},{20,16},{24,28},{28,24},{1,5},{5... | collective-permute-start | bytes 2064392 | tf_op jit(solution)/shard_map/ppermute | solution.py:35
  279.9 1.2 copy-start.13
  279.9 82.8 %collective-permute-start.18 = (bf16[448,768]{1,0:T(8,128)(2,1)}, bf16[448,768]{1,0:T(8,128)(2,1)}, u32[]{:S(2)}, u32[]{:S(2)}) collective-permute-start(bf16[448,768]{1,0:T(8,128)(2,1)} %collective-permute-done.6.refs_8_), channel_id=1, source_target_pairs={{0,4},{4,0},{8,12},{12,8},{16,20},{20,16},{24,28},{28,24},{1,5},{5... | collective-permute-start | bytes 2064392 | tf_op jit(solution)/shard_map/ppermute | solution.py:35
  359.7 4.3 copy-start
  359.7 37.1 %collective-permute-start.22 = (bf16[2,448,896]{2,1,0:T(8,128)(2,1)}, bf16[2,448,896]{2,1,0:T(8,128)(2,1)}, u32[]{:S(2)}, u32[]{:S(2)}) collective-permute-start(bf16[2,448,896]{2,1,0:T(8,128)(2,1)} %get-tuple-element.63), channel_id=1, source_target_pairs={{0,8},{4,12},{8,0},{12,4},{16,24},{20,28},{24,16},{28,20},{1,9},{5... | collective-permute-start | bytes 4816904 | tf_op jit(solution)/shard_map/ppermute | solution.py:35
  361.2 40.5 %collective-permute-start.20 = (bf16[2,448,896]{2,1,0:T(8,128)(2,1)}, bf16[2,448,896]{2,1,0:T(8,128)(2,1)}, u32[]{:S(2)}, u32[]{:S(2)}) collective-permute-start(bf16[2,448,896]{2,1,0:T(8,128)(2,1)} %get-tuple-element.64), channel_id=1, source_target_pairs={{0,16},{4,20},{8,24},{12,28},{16,0},{20,4},{24,8},{28,12},{1,17},{... | collective-permute-start | bytes 4816904 | tf_op jit(solution)/shard_map/ppermute | solution.py:35
  362.7 189.4 %all-gather.4.cloned.1.call-start = ((), (), s32[]{:S(2)}) async-start(), calls=%async_computation.9 | async-start | bytes 12386304 | tf_op jit(solution)/shard_map/all_gather | solution.py:319
  363.9 1.8 copy-start.1
  364.0 3.1 collective-permute-start.23
  364.2 35.1 %collective-permute-start.21 = (bf16[1,448,896]{2,1,0:T(8,128)(2,1)S(1)}, bf16[1,448,896]{2,1,0:T(8,128)(2,1)S(1)}, u32[]{:S(2)}, u32[]{:S(2)}) collective-permute-start(bf16[1,448,896]{2,1,0:T(8,128)(2,1)S(1)} %get-tuple-element.65), channel_id=1, source_target_pairs={{0,4},{4,0},{8,12},{12,8},{16,20},{20,16},{24,28},{28,24},{1,5},{5... | collective-permute-start | bytes 2408456 | tf_op jit(solution)/shard_map/ppermute | solution.py:35
  364.7 39.4 %collective-permute-start.19 = (bf16[1,448,896]{2,1,0:T(8,128)(2,1)S(1)}, bf16[1,448,896]{2,1,0:T(8,128)(2,1)S(1)}, u32[]{:S(2)}, u32[]{:S(2)}) collective-permute-start(bf16[1,448,896]{2,1,0:T(8,128)(2,1)S(1)} %get-tuple-element.66), channel_id=1, source_target_pairs={{0,4},{4,0},{8,12},{12,8},{16,20},{20,16},{24,28},{28,24},{1,5},{5... | collective-permute-start | bytes 2408456 | tf_op jit(solution)/shard_map/ppermute | solution.py:35
  430.2 36.8 %copy-start.6 = (bf16[2,448,896]{2,1,0:T(8,128)(2,1)S(1)}, bf16[2,448,896]{2,1,0:T(8,128)(2,1)}, u32[]{:S(2)}) copy-start(bf16[2,448,896]{2,1,0:T(8,128)(2,1)} %all-reduce.8.cloned.1.call-done.mine) | copy-start | bytes 4816900
  430.2 36.8 %collective-permute-start.25 = (bf16[2,448,896]{2,1,0:T(8,128)(2,1)}, bf16[2,448,896]{2,1,0:T(8,128)(2,1)S(1)}, u32[]{:S(2)}, u32[]{:S(2)}) collective-permute-start(bf16[2,448,896]{2,1,0:T(8,128)(2,1)} %all-reduce.8.cloned.1.call-done.mine), channel_id=1, source_target_pairs={{0,24},{4,28},{8,16},{12,20},{16,8},{20,12},{24,0},{28,4},{1,25},{... | collective-permute-start | bytes 4816904 | tf_op jit(solution)/shard_map/ppermute | solution.py:35
  433.9 34.5 %collective-permute-start.24 = (bf16[1,448,896]{2,1,0:T(8,128)(2,1)S(1)}, bf16[1,448,896]{2,1,0:T(8,128)(2,1)S(1)}, u32[]{:S(2)}, u32[]{:S(2)}) collective-permute-start(bf16[1,448,896]{2,1,0:T(8,128)(2,1)S(1)} %slice.95), channel_id=1, source_target_pairs={{0,4},{4,0},{8,12},{12,8},{16,20},{20,16},{24,28},{28,24},{1,5},{5... | collective-permute-start | bytes 2408456 | tf_op jit(solution)/shard_map/ppermute | solution.py:35
  468.3 1.9 copy-start.5
  470.3 16.4 %copy-start.12 = (bf16[448,1024]{1,0:T(8,128)(2,1)S(1)}, bf16[448,1024]{1,0:T(8,128)(2,1)}, u32[]{:S(2)}) copy-start(bf16[448,1024]{1,0:T(8,128)(2,1)} %copy-done.11) | copy-start | bytes 2752516
  470.3 16.5 %copy-start.10 = (bf16[448,1024]{1,0:T(8,128)(2,1)S(1)}, bf16[448,1024]{1,0:T(8,128)(2,1)}, u32[]{:S(2)}) copy-start(bf16[448,1024]{1,0:T(8,128)(2,1)} %copy-done.9) | copy-start | bytes 2752516
  486.0 148.8 %all-gather.6.cloned.1.call-start = ((), (), s32[]{:S(2)}) async-start(), calls=%async_computation.10 | async-start | bytes 16515072 | tf_op jit(solution)/shard_map/all_gather | solution.py:319
  486.1 9.1 %collective-permute-start.26 = (bf16[896,1024]{1,0:T(8,128)(2,1)}, bf16[896,1024]{1,0:T(8,128)(2,1)S(1)}, u32[]{:S(2)}, u32[]{:S(2)}) collective-permute-start(bf16[896,1024]{1,0:T(8,128)(2,1)} %collective-permute-done.7.refs_7_.refs_3_), channel_id=1, source_target_pairs={{0,4},{4,0},{8,12},{12,8},{16,20},{20,16},{24,28},{28,24},{1,5},{5... | collective-permute-start | bytes 5505032 | tf_op jit(solution)/shard_map/ppermute | solution.py:35
  486.1 9.2 %collective-permute-start.27 = (bf16[896,1024]{1,0:T(8,128)(2,1)}, bf16[896,1024]{1,0:T(8,128)(2,1)S(1)}, u32[]{:S(2)}, u32[]{:S(2)}) collective-permute-start(bf16[896,1024]{1,0:T(8,128)(2,1)} %collective-permute-done.8.refs_10_.refs_5_), channel_id=1, source_target_pairs={{0,4},{4,0},{8,12},{12,8},{16,20},{20,16},{24,28},{28,24},{1,5},{5... | collective-permute-start | bytes 5505032 | tf_op jit(solution)/shard_map/ppermute | solution.py:35
  486.6 5.9 collective-permute-start.28
  486.7 8.4 %collective-permute-start.29 = (bf16[448,1024]{1,0:T(8,128)(2,1)S(1)}, bf16[448,1024]{1,0:T(8,128)(2,1)S(1)}, u32[]{:S(2)}, u32[]{:S(2)}) collective-permute-start(bf16[448,1024]{1,0:T(8,128)(2,1)S(1)} %copy-done.10), channel_id=1, source_target_pairs={{0,4},{4,0},{8,12},{12,8},{16,20},{20,16},{24,28},{28,24},{1,5},{5... | collective-permute-start | bytes 2752520 | tf_op jit(solution)/shard_map/ppermute | solution.py:35
  495.2 1.2 copy-start.18
  496.4 1.3 copy-start.19
  517.7 1.2 copy-start.14
  517.8 1.4 copy-start.16
  517.8 168.8 %all-gather.8.cloned.1.call-start = ((), (), s32[]{:S(2)}) async-start(), calls=%async_computation.11 | async-start | bytes 8257536 | tf_op jit(solution)/shard_map/all_gather | solution.py:319
  517.8 6.2 collective-permute-start.30
  518.0 7.8 collective-permute-start.31
  518.9 3.1 collective-permute-start.32
  519.2 4.8 collective-permute-start.33
  524.0 1.8 copy-start.20
  569.9 64.9 %copy-start.3 = (bf16[4,224,1024]{2,1,0:T(8,128)(2,1)S(1)}, bf16[4,224,1024]{2,1,0:T(8,128)(2,1)}, u32[]{:S(2)}) copy-start(bf16[4,224,1024]{2,1,0:T(8,128)(2,1)} %copy-done.2) | copy-start | bytes 5505028
  570.0 129.4 %all-to-all-start.3 = ((bf16[4,224,768]{2,1,0:T(8,128)(2,1)}), bf16[4,224,768]{2,1,0:T(8,128)(2,1)}, u32[]{:S(2)}, u32[]{:S(2)}) async-start(bf16[4,224,768]{2,1,0:T(8,128)(2,1)} %bitcast.10), calls=%async_computation.3 | async-start | bytes 2752512 | tf_op jit(solution)/shard_map/all_to_all | solution.py:323
  655.9 1.2 copy-start.7
  699.3 27.9 %copy-start.8 = (bf16[896,1024]{1,0:T(8,128)(2,1)S(1)}, bf16[896,1024]{1,0:T(8,128)(2,1)}, u32[]{:S(2)}) copy-start(bf16[896,1024]{1,0:T(8,128)(2,1)} %copy-done.7) | copy-start | bytes 5505028
  (2 other events, 1.7 us)
Sparse Core Ops, SparseCore 0:
  134.9 96.1 all-reduce.3
  233.6 122.2 all-reduce.5
  362.8 67.3 all-reduce.7
  486.1 65.9 all-gather.3
  553.8 80.9 all-gather.5
  636.6 49.9 all-gather.7

commit v6 on v5

--- a/solution.py
+++ b/solution.py
@@ -242,6 +242,33 @@
     )(me.astype(jnp.int32).reshape(1), gram, *[parts[key] for key in keys], *extra)
 
 
+def sum_on_line(piece, arrivals):
+    count = lax.axis_size("col")
+    me = lax.axis_index("col")
+    half = count // 2
+
+    def send(stage, value, pairs):
+        done = arrivals.setdefault(stage, [])
+        if len(done) > 1:
+            value = after(value, done[-2])
+        arrived = lax.ppermute(value, "col", pairs)
+        done.append(arrived)
+        return arrived
+
+    def add(left, right):
+        return (left.astype(f32) + right.astype(f32)).astype(bf16)
+
+    for s in range(half - 1):
+        pairs = [(s, s + 1), (count - 1 - s, count - 2 - s)]
+        piece = add(piece, send(s, piece, pairs))
+    piece = add(piece, send(half - 1, piece, [(half - 1, half), (half, half - 1)]))
+    for s in range(half - 2, -1, -1):
+        pairs = [(s + 1, s), (count - 2 - s, count - 1 - s)]
+        arrived = send(2 * half - 2 - s, piece, pairs)
+        piece = jnp.where((me == s) | (me == count - 1 - s), arrived, piece)
+    return piece
+
+
 def per_device(ortho_in):
     rows, cols = ortho_in.shape
     n_row = lax.axis_size("row")
@@ -262,7 +289,7 @@
     start = 0
     thirds = widths_of(width, 3)
     if width % (9 * 256) == 0:
-        thirds = [width // 9 * n for n in (3, 4, 2)]
+        thirds = [width // 9 * n for n in (4, 3, 2)]
     for k, w in enumerate(thirds):
         first = [start + c * width for c in range(n_col)]
         part = jnp.concatenate([ortho_in[:, f : f + w] for f in first], axis=0)
@@ -290,25 +317,35 @@
     panels = [
         add_cores({**parts, **sibling}) for parts, sibling in zip(gathered, siblings)
     ]
-    for stage in (chips[:2], chips[2:]):
+    corner = chips[-1]
+    corners = [part for parts in gathered for key, part in parts.items() if key[0] == corner]
+
+    def chip_pieces(stage, *held):
         blocks = list(lefts)
         for j in stage:
             peers = [whole_block(parts, j) for parts in gathered]
-            if j != chips[-1]:
-                peers[0] = after(peers[0], *tied)
             blocks.append(peers)
+        blocks[-1][0] = after(blocks[-1][0], *held) if held else blocks[-1][0]
         jobs = [(i, bit_x + n, n, 0) for n in range(len(stage)) for i in range(bit_x)]
-        pieces = gram_pieces(blocks, jobs, [low_of(j)[0] for j in stage], scale)
-        held = list(panels[0].values()) if len(stage) == 1 else []
-        last = sums = lax.psum(after(pieces, last, *held), "col")
-        if len(stage) == 1:
-            sums, gram = lax.optimization_barrier((sums, gram))
-        for n, j in enumerate(stage):
-            theirs = swap(sums[n * bit_x : (n + 1) * bit_x], j)
-            gram = put_block(gram, low_of(j), (sums, n * bit_x), (theirs, 0), j)
-            for i in cores:
-                mine = swap(sums[n * bit_x + i : n * bit_x + i + 1], i)
-                gram = put_block(gram, low_of(j), (mine, 0), (theirs, i), j | i)
+        return gram_pieces(blocks, jobs, [low_of(j)[0] for j in stage], scale)
+
+    sums = lax.psum(after(chip_pieces(chips[:2], *corners), last), "col")
+    arrivals = {}
+    far = chip_pieces(chips[2:])
+    far = [sum_on_line(far[i : i + 1], arrivals) for i in range(bit_x)]
+    far_theirs = [swap(piece, corner) for piece in far]
+    for i in cores:
+        far[i] = swap(far[i], i)
+    held = [part for panel in panels[:1] for part in panel.values()]
+    sums = after(sums, *far, *far_theirs, *held)
+    for i in range(bit_x):
+        gram = put_block(gram, low_of(corner), (far[i], 0), (far_theirs[i], 0), corner | i)
+    for n, j in enumerate(chips[:2]):
+        theirs = swap(sums[n * bit_x : (n + 1) * bit_x], j)
+        gram = put_block(gram, low_of(j), (sums, n * bit_x), (theirs, 0), j)
+        for i in cores:
+            mine = swap(sums[n * bit_x + i : n * bit_x + i + 1], i)
+            gram = put_block(gram, low_of(j), (mine, 0), (theirs, i), j | i)
 
     outs = []
     for k, w in enumerate(thirds):
@@ -318,7 +355,7 @@
         first = product(gram, me, parts, 0, w)
         first_panel = lax.all_gather(first, "row", axis=0, tiled=True)
         if k > 0:
-            first_panel = after(first_panel, result)
+            first_panel = after(first_panel, back)
         result = product(gram, me, {None: first_panel}, 0, w, (tiles[k], first))
         back = lax.all_to_all(result, "col", split_axis=0, concat_axis=1, tiled=True)
         outs.append(back.reshape(rows, n_col, w))

time: 792 us -> 899 us (1.14)
  waiting for transfers between devices: 458 us -> 575 us
  blocking collectives: 72.6 us -> 47.7 us
  starting transfers between devices: 44.5 us -> 58.2 us
    ppermute x0 -> x6, waiting for transfers between devices: none -> 145 us  [send(): arrived = lax.ppermute(value, 'col', pairs)]
    psum x2 -> x1, waiting for transfers between devices: 87.4 us -> 20 us  [per_device(): sums = lax.psum(after(chip_pieces(chips[:2], *corners), last), 'col')]
    all_gather x3, waiting for transfers between devices: 103 us -> 158 us  [per_device(): first_panel = lax.all_gather(first, 'row', axis=0, tiled=True)]
    ppermute x34 -> x35, waiting for transfers between devices: 180 us -> 137 us  [swap(): return lax.ppermute(value, 'row', [(r, r ^ bit) for r in range(count)])]
    all_to_all x2 -> x1, blocking collectives: 72.6 us -> 47.7 us  [per_device(): lax.all_to_all(result, 'col', split_axis=0, concat_axis=1, tiled=True)]
    psum x1, waiting for transfers between devices: 26.5 us -> 44.3 us  [per_device(): last = near = lax.psum(near, 'col')]
    ppermute x0 -> x6, starting transfers between devices: none -> 10.4 us  [send(): arrived = lax.ppermute(value, 'col', pairs)]
    ppermute x34 -> x35, starting transfers between devices: 24.7 us -> 23.6 us  [swap(): return lax.ppermute(value, 'row', [(r, r ^ bit) for r in range(count)])]
  transfers between devices with their start and end apart: 44 -> 51, of which waited for: 27 -> 23; matrix products, arithmetic and copies ran while one was open for 3% -> 4% of each run, Pallas kernels for 17% -> 15%
where the time goes in v6:
time: 899 us; the launch traced here: 889 us
  waiting for transfers between devices  575 us (64%)
  Pallas kernels  149 us (17%)
  starting transfers between devices  58.2 us (6%)
  blocking collectives  47.7 us (5%)
  local copies, waits for them, and re-layouts  29 us (3%)
  other arithmetic  16.3 us (2%)
  between operations  14 us (2%)
    all_gather x3, waiting for transfers between devices, per_device(): first_panel = lax.all_gather(first, 'row', axis=0, tiled=True)  158 us
    ppermute x6, waiting for transfers between devices, send(): arrived = lax.ppermute(value, 'col', pairs)  145 us
    ppermute x35, waiting for transfers between devices, swap(): return lax.ppermute(value, 'row', [(r, r ^ bit) for r in range(count)])  137 us
    pallas_call x6, Pallas kernels, product(): pl.pallas_call(functools.partial(product_kernel, keys, start, bool(extra)...  100 us
    all_to_all x3, waiting for transfers between devices, exchange(): return lax.all_to_all(value, 'col', split_axis=0, concat_axis=0, tiled=True)  69.2 us
    all_to_all x1, blocking collectives, per_device(): lax.all_to_all(result, 'col', split_axis=0, concat_axis=1, tiled=True)  47.7 us
    psum x1, waiting for transfers between devices, per_device(): last = near = lax.psum(near, 'col')  44.3 us
    pallas_call x3, Pallas kernels, gram_pieces(): pl.pallas_call(functools.partial(pieces_kernel, count, jobs, scale), out_...  38.1 us
  transfers between devices with their start and end apart: 51, of which 23 were waited for; matrix products, arithmetic and copies ran while one was open for 4% of the time, Pallas kernels for 15%

profile of v6, /device:TPU:0, one launch (start us, length us, event | category | flops | bytes accessed | tf_op | source)
XLA Modules:
  0.0 889.5 jit_solution(611283805316861058)
XLA Ops:
  6.5 1.6 fusion.2
  8.1 1.4 pad_maximum_fusion
  9.5 6.3 all-to-all-start
  15.8 1.4 fusion.1
  18.4 40.0 %all-to-all-done = bf16[4,224,1024]{2,1,0:T(8,128)(2,1)S(1)} async-done(((bf16[4,224,1024]{2,1,0:T(8,128)(2,1)}), bf16[4,224,1024]{2,1,0:T(8,128)(2,1)S(1)}, u32[]{:S(2)}, u32[]{:S(2)}) %all-to-all-start) | async-done | bytes 1835040 | tf_op jit(solution)/shard_map/all_to_all | solution.py:286
  58.4 3.5 all-to-all-start.1
  61.9 1.6 collective-permute-start
  63.5 1.5 collective-permute-start.1
  65.0 29.1 %all-to-all-done.1 = bf16[4,224,768]{2,1,0:T(8,128)(2,1)S(1)} async-done(((bf16[4,224,768]{2,1,0:T(8,128)(2,1)}), bf16[4,224,768]{2,1,0:T(8,128)(2,1)S(1)}, u32[]{:S(2)}, u32[]{:S(2)}) %all-to-all-start.1) | async-done | bytes 1376288 | tf_op jit(solution)/shard_map/all_to_all | solution.py:286
  94.2 1.5 collective-permute-start.5
  95.7 1.5 collective-permute-start.9
  97.2 1.3 fusion
  99.5 5.6 collective-permute-done.refs_6_.refs_3_
  105.1 1.5 collective-permute-done.1.refs_9_.refs_5_
  106.6 5.0 all-to-all-start.2
  111.6 21.0 %collective-permute-done.5.refs_7_.refs_3_ = bf16[896,768]{1,0:T(8,128)(2,1)} collective-permute-done((bf16[896,768]{1,0:T(8,128)(2,1)S(1)}, bf16[896,768]{1,0:T(8,128)(2,1)}, u32[]{:S(2)}, u32[]{:S(2)}) %collective-permute-start.5) | collective-permute-done | bytes 1376288 | tf_op jit(solution)/shard_map/ppermute | solution.py:35
  136.1 1.6 collective-permute-start.10
  137.7 2.2 slice.87
  139.9 2.2 slice.88
  143.1 1.5 collective-permute-start.11
  144.6 10.0 %collective-permute-done.10.refs_7_ = bf16[448,768]{1,0:T(8,128)(2,1)} collective-permute-done((bf16[448,768]{1,0:T(8,128)(2,1)S(1)}, bf16[448,768]{1,0:T(8,128)(2,1)}, u32[]{:S(2)}, u32[]{:S(2)}) %collective-permute-start.10) | collective-permute-done | bytes 688160 | tf_op jit(solution)/shard_map/ppermute | solution.py:35
  154.6 22.6 %collective-permute-done.11.refs_8_ = bf16[448,768]{1,0:T(8,128)(2,1)} collective-permute-done((bf16[448,768]{1,0:T(8,128)(2,1)S(1)}, bf16[448,768]{1,0:T(8,128)(2,1)}, u32[]{:S(2)}, u32[]{:S(2)}) %collective-permute-start.11) | collective-permute-done | bytes 688160 | tf_op jit(solution)/shard_map/ppermute | solution.py:35
  177.2 1.9 collective-permute-start.12
  179.7 2.5 pad_maximum_fusion.3.refs_7_
  182.2 2.8 pad_maximum_fusion.1.refs_6_
  185.0 11.2 %collective-permute-done.12.refs_11_.refs_5_ = bf16[896,512]{1,0:T(8,128)(2,1)} collective-permute-done((bf16[896,512]{1,0:T(8,128)(2,1)}, bf16[896,512]{1,0:T(8,128)(2,1)}, u32[]{:S(2)}, u32[]{:S(2)}) %collective-permute-start.12) | collective-permute-done | bytes 917536 | tf_op jit(solution)/shard_map/ppermute | solution.py:35
  197.4 1.8 slice.91
  199.2 1.8 slice.92
  202.6 11.1 %shard_map.18 = bf16[3,448,896]{2,1,0:T(8,128)(2,1)} custom-call(s32[1]{0:T(128)} %bitcast.9.low_ref, bf16[896,1024]{1,0:T(8,128)(2,1)} %bitcast.22, bf16[896,768]{1,0:T(8,128)(2,1)S(1)} %bitcast.30, bf16[896,512]{1,0:T(8,128)(2,1)} %bitcast.8.refs_2_.refs_1_, bf16[896,1024]{1,0:T(8,128)(2,1)} %collective-permute-done.2.refs_3_.refs_2_, ...), custom_call_target="tpu_custom_call" | custom-call | flops 5549064192 | bytes 10665984 | tf_op jit(solution)/shard_map/pallas_call | solution.py:103
  215.0 10.0 %shard_map.19 = bf16[2,448,896]{2,1,0:T(8,128)(2,1)} custom-call(s32[1]{0:T(128)} %bitcast.1.low_ref, bf16[896,1024]{1,0:T(8,128)(2,1)} %bitcast.23, bf16[896,768]{1,0:T(8,128)(2,1)S(1)} %bitcast.31, bf16[896,512]{1,0:T(8,128)(2,1)} %bitcast.8.refs_2_.refs_1_, bf16[896,1024]{1,0:T(8,128)(2,1)} %collective-permute-done.2.refs_3_.refs_2_, ...), custom_call_target="tpu_custom_call" | custom-call | flops 3699376128 | bytes 13991936 | tf_op jit(solution)/shard_map/pallas_call | solution.py:103
  225.0 2.8 fusion.5
  227.8 4.2 collective-permute-start.15
  232.1 2.2 collective-permute-start.18
  234.3 32.6 %collective-permute-done.15 = bf16[1,448,896]{2,1,0:T(8,128)(2,1)} collective-permute-done((bf16[1,448,896]{2,1,0:T(8,128)(2,1)}, bf16[1,448,896]{2,1,0:T(8,128)(2,1)}, u32[]{:S(2)}, u32[]{:S(2)}) %collective-permute-start.15) | collective-permute-done | bytes 802848 | tf_op jit(solution)/shard_map/ppermute | solution.py:254
  266.9 25.6 %collective-permute-done.18 = bf16[1,448,896]{2,1,0:T(8,128)(2,1)} collective-permute-done((bf16[1,448,896]{2,1,0:T(8,128)(2,1)}, bf16[1,448,896]{2,1,0:T(8,128)(2,1)}, u32[]{:S(2)}, u32[]{:S(2)}) %collective-permute-start.18) | collective-permute-done | bytes 802848 | tf_op jit(solution)/shard_map/ppermute | solution.py:254
  292.5 3.0 add_convert_fusion.1
  296.2 17.0 %shard_map.17 = bf16[4,448,896]{2,1,0:T(8,128)(2,1)} custom-call(s32[2]{0:T(128)S(1)} %pad_add_fusion.low_ref, bf16[896,1024]{1,0:T(8,128)(2,1)} %bitcast.24, bf16[896,768]{1,0:T(8,128)(2,1)S(1)} %bitcast.32, bf16[896,512]{1,0:T(8,128)(2,1)} %bitcast.8.refs_2_.refs_1_, bf16[896,1024]{1,0:T(8,128)(2,1)} %collective-permute-done.2.refs_3_.refs_2_, ...), custom_call_target="tpu_custom_call" | custom-call | flops 7398752256 | bytes 19726336 | tf_op jit(solution)/shard_map/pallas_call | solution.py:103
  313.2 44.3 %all-reduce.3.cloned.1.call-done.halves.mine = bf16[3,448,896]{2,1,0:T(8,128)(2,1)} async-done(((bf16[3,448,896]{2,1,0:T(8,128)(2,1)}), bf16[3,448,896]{2,1,0:T(8,128)(2,1)}) %all-reduce.3.cloned.1.call-update) | async-done | bytes 2408464 | tf_op jit(solution)/shard_map/psum | solution.py:312
  358.4 1.3 add_convert_fusion.2
  363.2 45.8 %collective-permute-done.17 = bf16[1,448,896]{2,1,0:T(8,128)(2,1)S(1)} collective-permute-done((bf16[1,448,896]{2,1,0:T(8,128)(2,1)S(1)}, bf16[1,448,896]{2,1,0:T(8,128)(2,1)S(1)}, u32[]{:S(2)}, u32[]{:S(2)}) %collective-permute-start.17) | collective-permute-done | bytes 802848 | tf_op jit(solution)/shard_map/ppermute | solution.py:254
  409.1 41.3 %collective-permute-done.20 = bf16[1,448,896]{2,1,0:T(8,128)(2,1)} collective-permute-done((bf16[1,448,896]{2,1,0:T(8,128)(2,1)S(1)}, bf16[1,448,896]{2,1,0:T(8,128)(2,1)}, u32[]{:S(2)}, u32[]{:S(2)}) %collective-permute-start.20) | collective-permute-done | bytes 802848 | tf_op jit(solution)/shard_map/ppermute | solution.py:254
  450.4 2.3 collective-permute-start.22
  454.7 17.4 %collective-permute-done.22.theirs = bf16[1,448,896]{2,1,0:T(8,128)(2,1)S(1)} collective-permute-done((bf16[1,448,896]{2,1,0:T(8,128)(2,1)S(1)}, bf16[1,448,896]{2,1,0:T(8,128)(2,1)S(1)}, u32[]{:S(2)}, u32[]{:S(2)}) %collective-permute-start.22) | collective-permute-done | bytes 802848 | tf_op jit(solution)/shard_map/ppermute | solution.py:35
  473.9 13.7 %collective-permute-done.23.theirs = bf16[1,448,896]{2,1,0:T(8,128)(2,1)S(1)} collective-permute-done((bf16[1,448,896]{2,1,0:T(8,128)(2,1)S(1)}, bf16[1,448,896]{2,1,0:T(8,128)(2,1)S(1)}, u32[]{:S(2)}, u32[]{:S(2)}) %collective-permute-start.23) | collective-permute-done | bytes 802848 | tf_op jit(solution)/shard_map/ppermute | solution.py:35
  488.6 20.0 %all-reduce.5.cloned.1.call-done.mine = bf16[4,448,896]{2,1,0:T(8,128)(2,1)} async-done(((bf16[4,448,896]{2,1,0:T(8,128)(2,1)}), bf16[4,448,896]{2,1,0:T(8,128)(2,1)}) %all-reduce.5.cloned.1.call-update) | async-done | bytes 3211280 | tf_op jit(solution)/shard_map/psum | solution.py:332
  508.6 2.3 fusion.3
  510.9 1.5 collective-permute-start.31
  512.4 1.5 collective-permute-start.29
  516.5 31.3 %collective-permute-done.31.theirs = bf16[2,448,896]{2,1,0:T(8,128)(2,1)S(1)} collective-permute-done((bf16[2,448,896]{2,1,0:T(8,128)(2,1)S(1)}, bf16[2,448,896]{2,1,0:T(8,128)(2,1)S(1)}, u32[]{:S(2)}, u32[]{:S(2)}) %collective-permute-start.31) | collective-permute-done | bytes 1605664 | tf_op jit(solution)/shard_map/ppermute | solution.py:35
  550.4 1.3 shard_map.22.gram_in
  558.9 1.6 shard_map.27.refs_0_
  560.5 20.2 %shard_map.28.refs_3_ = bf16[896,1024]{1,0:T(8,128)(2,1)} custom-call(s32[1]{0:T(128)} %bitcast.me_ref, bf16[8,896,896]{2,1,0:T(8,128)(2,1)} %shard_map.27.refs_0_, bf16[896,1024]{1,0:T(8,128)(2,1)} %bitcast.25, bf16[896,1024]{1,0:T(8,128)(2,1)} %collective-permute-done.2.refs_3_.refs_2_, bf16[896,1024]{1,0:T(8,128)(2,1)} %collective-permute-done.refs_6_.refs_3_, ...), custom_call_target="tpu_custom_call" | custom-call | flops 13153337344 | bytes 27525120 | tf_op jit(solution)/shard_map/pallas_call | solution.py:223
  581.4 15.6 %shard_map.30.refs_3_ = bf16[896,768]{1,0:T(8,128)(2,1)} custom-call(s32[1]{0:T(128)} %bitcast.me_ref, bf16[8,896,896]{2,1,0:T(8,128)(2,1)} %shard_map.27.refs_0_, bf16[896,768]{1,0:T(8,128)(2,1)S(1)} %bitcast.33, bf16[896,768]{1,0:T(8,128)(2,1)} %collective-permute-done.3.refs_4_.refs_2_, bf16[896,768]{1,0:T(8,128)(2,1)} %collective-permute-done.5.refs_7_.refs_3_, ...), custom_call_target="tpu_custom_call" | custom-call | flops 9865003008 | bytes 23855104 | tf_op jit(solution)/shard_map/pallas_call | solution.py:223
  597.0 11.8 %shard_map.32.refs_3_ = bf16[896,512]{1,0:T(8,128)(2,1)} custom-call(s32[1]{0:T(128)} %bitcast.me_ref, bf16[8,896,896]{2,1,0:T(8,128)(2,1)} %shard_map.27.refs_0_, bf16[896,512]{1,0:T(8,128)(2,1)} %bitcast.8.refs_2_.refs_1_, bf16[896,512]{1,0:T(8,128)(2,1)} %collective-permute-done.4.refs_5_.refs_2_, ...), custom_call_target="tpu_custom_call" | custom-call | flops 6576668672 | bytes 20185088 | tf_op jit(solution)/shard_map/pallas_call | solution.py:223
  610.0 49.6 %all-gather.8.cloned.1.call-done.refs_1_ = bf16[7168,512]{1,0:T(8,128)(2,1)} async-done(((bf16[896,512]{1,0:T(8,128)(2,1)}), bf16[7168,512]{1,0:T(8,128)(2,1)}) %all-gather.8.cloned.1.call-update) | async-done | bytes 7340048 | tf_op jit(solution)/shard_map/all_gather | solution.py:356
  659.7 13.6 %shard_map.33 = bf16[896,512]{1,0:T(8,128)(2,1)} custom-call(s32[1]{0:T(128)} %bitcast.me_ref, bf16[8,896,896]{2,1,0:T(8,128)(2,1)} %shard_map.27.refs_0_, bf16[7168,512]{1,0:T(8,128)(2,1)} %all-gather.8.cloned.1.call-done.refs_1_, bf16[896,512]{1,0:T(8,128)(2,1)} %bitcast.8.refs_2_.refs_1_, bf16[896,512]{1,0:T(8,128)(2,1)} %shard_map.32.refs_3_), custom_call_target="tpu_custom_call" | custom-call | flops 6576668672 | bytes 20185088 | tf_op jit(solution)/shard_map/pallas_call | solution.py:223
  673.3 4.6 all-to-all-start.5
  677.9 49.0 %all-gather.6.cloned.1.call-done.refs_1_ = bf16[7168,768]{1,0:T(8,128)(2,1)} async-done(((bf16[896,768]{1,0:T(8,128)(2,1)}), bf16[7168,768]{1,0:T(8,128)(2,1)}) %all-gather.6.cloned.1.call-update) | async-done | bytes 11010064 | tf_op jit(solution)/shard_map/all_gather | solution.py:356
  726.9 17.8 %shard_map.31 = bf16[896,768]{1,0:T(8,128)(2,1)} custom-call(s32[1]{0:T(128)} %bitcast.me_ref, bf16[8,896,896]{2,1,0:T(8,128)(2,1)} %shard_map.27.refs_0_, bf16[7168,768]{1,0:T(8,128)(2,1)} %all-gather.6.cloned.1.call-done.refs_1_, bf16[896,768]{1,0:T(8,128)(2,1)S(1)} %bitcast.34, bf16[896,768]{1,0:T(8,128)(2,1)} %shard_map.30.refs_3_), custom_call_target="tpu_custom_call" | custom-call | flops 9865003008 | bytes 23855104 | tf_op jit(solution)/shard_map/pallas_call | solution.py:223
  745.8 4.6 all-to-all-start.4
  750.4 59.3 %all-gather.4.cloned.1.call-done.refs_1_ = bf16[7168,1024]{1,0:T(8,128)(2,1)} async-done(((bf16[896,1024]{1,0:T(8,128)(2,1)}), bf16[7168,1024]{1,0:T(8,128)(2,1)}) %all-gather.4.cloned.1.call-update) | async-done | bytes 14680080 | tf_op jit(solution)/shard_map/all_gather | solution.py:356
  809.7 21.1 %shard_map.29 = bf16[896,1024]{1,0:T(8,128)(2,1)S(1)} custom-call(s32[1]{0:T(128)} %bitcast.me_ref, bf16[8,896,896]{2,1,0:T(8,128)(2,1)} %shard_map.27.refs_0_, bf16[7168,1024]{1,0:T(8,128)(2,1)} %all-gather.4.cloned.1.call-done.refs_1_, bf16[896,1024]{1,0:T(8,128)(2,1)S(1)} %bitcast.26, bf16[896,1024]{1,0:T(8,128)(2,1)} %shard_map.28.refs_3_), custom_call_target="tpu_custom_call" | custom-call | flops 13153337344 | bytes 27525120 | tf_op jit(solution)/shard_map/pallas_call | solution.py:223
  832.0 47.7 %all_to_all.81 = bf16[4,224,1024]{2,1,0:T(8,128)(2,1)S(1)} all-to-all(bf16[4,224,1024]{2,1,0:T(8,128)(2,1)} %bitcast.35), channel_id=1, replica_groups=mesh['row'=8,'col'=4] {'col'}, dimensions={0} | all-to-all | bytes 3670016 | tf_op jit(solution)/shard_map/all_to_all | solution.py:360
  880.0 2.5 copy.10
  (122 shorter events, 38.0 us)
Async XLA Ops:
  9.5 48.9 %all-to-all-start = ((bf16[4,224,1024]{2,1,0:T(8,128)(2,1)}), bf16[4,224,1024]{2,1,0:T(8,128)(2,1)S(1)}, u32[]{:S(2)}, u32[]{:S(2)}) async-start(bf16[4,224,1024]{2,1,0:T(8,128)(2,1)} %bitcast.36), calls=%async_computation | async-start | bytes 3670016 | tf_op jit(solution)/shard_map/all_to_all | solution.py:286
  58.4 84.7 %copy-start.2 = (bf16[4,224,1024]{2,1,0:T(8,128)(2,1)}, bf16[4,224,1024]{2,1,0:T(8,128)(2,1)S(1)}, u32[]{:S(2)}) copy-start(bf16[4,224,1024]{2,1,0:T(8,128)(2,1)S(1)} %all-to-all-done) | copy-start | bytes 5505028
  58.4 35.8 %all-to-all-start.1 = ((bf16[4,224,768]{2,1,0:T(8,128)(2,1)}), bf16[4,224,768]{2,1,0:T(8,128)(2,1)S(1)}, u32[]{:S(2)}, u32[]{:S(2)}) async-start(bf16[4,224,768]{2,1,0:T(8,128)(2,1)} %bitcast.38), calls=%async_computation.1 | async-start | bytes 2752512 | tf_op jit(solution)/shard_map/all_to_all | solution.py:286
  61.9 43.1 %collective-permute-start = (bf16[896,1024]{1,0:T(8,128)(2,1)S(1)}, bf16[896,1024]{1,0:T(8,128)(2,1)}, u32[]{:S(2)}, u32[]{:S(2)}) collective-permute-start(bf16[896,1024]{1,0:T(8,128)(2,1)S(1)} %bitcast.19), channel_id=1, source_target_pairs={{0,8},{4,12},{8,0},{12,4},{16,24},{20,28},{24,16},{28,20},{1,9},{5... | collective-permute-start | bytes 5505032 | tf_op jit(solution)/shard_map/ppermute | solution.py:35
  63.5 43.1 %collective-permute-start.1 = (bf16[896,1024]{1,0:T(8,128)(2,1)S(1)}, bf16[896,1024]{1,0:T(8,128)(2,1)}, u32[]{:S(2)}, u32[]{:S(2)}) collective-permute-start(bf16[896,1024]{1,0:T(8,128)(2,1)S(1)} %bitcast.20), channel_id=1, source_target_pairs={{0,16},{4,20},{8,24},{12,28},{16,0},{20,4},{24,8},{28,12},{1,17},{... | collective-permute-start | bytes 5505032 | tf_op jit(solution)/shard_map/ppermute | solution.py:35
  94.2 202.0 %copy-start.4 = (bf16[4,224,768]{2,1,0:T(8,128)(2,1)}, bf16[4,224,768]{2,1,0:T(8,128)(2,1)S(1)}, u32[]{:S(2)}) copy-start(bf16[4,224,768]{2,1,0:T(8,128)(2,1)S(1)} %all-to-all-done.1) | copy-start | bytes 4128772
  94.2 38.4 %collective-permute-start.5 = (bf16[896,768]{1,0:T(8,128)(2,1)S(1)}, bf16[896,768]{1,0:T(8,128)(2,1)}, u32[]{:S(2)}, u32[]{:S(2)}) collective-permute-start(bf16[896,768]{1,0:T(8,128)(2,1)S(1)} %bitcast.27), channel_id=1, source_target_pairs={{0,8},{4,12},{8,0},{12,4},{16,24},{20,28},{24,16},{28,20},{1,9},{5... | collective-permute-start | bytes 4128776 | tf_op jit(solution)/shard_map/ppermute | solution.py:35
  95.7 38.1 %collective-permute-start.9 = (bf16[896,768]{1,0:T(8,128)(2,1)S(1)}, bf16[896,768]{1,0:T(8,128)(2,1)}, u32[]{:S(2)}, u32[]{:S(2)}) collective-permute-start(bf16[896,768]{1,0:T(8,128)(2,1)S(1)} %bitcast.28), channel_id=1, source_target_pairs={{0,16},{4,20},{8,24},{12,28},{16,0},{20,4},{24,8},{28,12},{1,17},{... | collective-permute-start | bytes 4128776 | tf_op jit(solution)/shard_map/ppermute | solution.py:35
  106.6 70.7 %all-to-all-start.2 = ((bf16[4,224,512]{2,1,0:T(8,128)(2,1)}), bf16[4,224,512]{2,1,0:T(8,128)(2,1)}, u32[]{:S(2)}, u32[]{:S(2)}) async-start(bf16[4,224,512]{2,1,0:T(8,128)(2,1)} %bitcast.40), calls=%async_computation.2 | async-start | bytes 1835008 | tf_op jit(solution)/shard_map/all_to_all | solution.py:286
  111.6 246.0 %all-reduce.3.cloned.1.call-start = ((), (), s32[]{:S(2)}) async-start(), calls=%async_computation.6 | async-start | bytes 4816896 | tf_op jit(solution)/shard_map/psum | solution.py:312
  136.1 18.5 %collective-permute-start.10 = (bf16[448,768]{1,0:T(8,128)(2,1)S(1)}, bf16[448,768]{1,0:T(8,128)(2,1)}, u32[]{:S(2)}, u32[]{:S(2)}) collective-permute-start(bf16[448,768]{1,0:T(8,128)(2,1)S(1)} %slice.89), channel_id=1, source_target_pairs={{0,16},{4,20},{8,24},{12,28},{16,0},{20,4},{24,8},{28,12},{1,17},{... | collective-permute-start | bytes 2064392 | tf_op jit(solution)/shard_map/ppermute | solution.py:35
  142.1 37.1 %collective-permute-start.7 = (bf16[448,1024]{1,0:T(8,128)(2,1)}, bf16[448,1024]{1,0:T(8,128)(2,1)}, u32[]{:S(2)}, u32[]{:S(2)}) collective-permute-start(bf16[448,1024]{1,0:T(8,128)(2,1)} %slice.87), channel_id=1, source_target_pairs={{0,16},{4,20},{8,24},{12,28},{16,0},{20,4},{24,8},{28,12},{1,17},{... | collective-permute-start | bytes 2752520 | tf_op jit(solution)/shard_map/ppermute | solution.py:35
  142.6 37.1 %collective-permute-start.8 = (bf16[448,1024]{1,0:T(8,128)(2,1)}, bf16[448,1024]{1,0:T(8,128)(2,1)}, u32[]{:S(2)}, u32[]{:S(2)}) collective-permute-start(bf16[448,1024]{1,0:T(8,128)(2,1)} %slice.88), channel_id=1, source_target_pairs={{0,8},{4,12},{8,0},{12,4},{16,24},{20,28},{24,16},{28,20},{1,9},{5... | collective-permute-start | bytes 2752520 | tf_op jit(solution)/shard_map/ppermute | solution.py:35
  143.1 59.5 %collective-permute-start.2 = (bf16[896,1024]{1,0:T(8,128)(2,1)S(1)}, bf16[896,1024]{1,0:T(8,128)(2,1)}, u32[]{:S(2)}, u32[]{:S(2)}) collective-permute-start(bf16[896,1024]{1,0:T(8,128)(2,1)S(1)} %bitcast.21), channel_id=1, source_target_pairs={{0,4},{4,0},{8,12},{12,8},{16,20},{20,16},{24,28},{28,24},{1,5},{5... | collective-permute-start | bytes 5505032 | tf_op jit(solution)/shard_map/ppermute | solution.py:35
  143.1 34.1 %collective-permute-start.11 = (bf16[448,768]{1,0:T(8,128)(2,1)S(1)}, bf16[448,768]{1,0:T(8,128)(2,1)}, u32[]{:S(2)}, u32[]{:S(2)}) collective-permute-start(bf16[448,768]{1,0:T(8,128)(2,1)S(1)} %slice.90), channel_id=1, source_target_pairs={{0,8},{4,12},{8,0},{12,4},{16,24},{20,28},{24,16},{28,20},{1,9},{5... | collective-permute-start | bytes 2064392 | tf_op jit(solution)/shard_map/ppermute | solution.py:35
  154.6 47.9 %collective-permute-start.3 = (bf16[896,768]{1,0:T(8,128)(2,1)S(1)}, bf16[896,768]{1,0:T(8,128)(2,1)}, u32[]{:S(2)}, u32[]{:S(2)}) collective-permute-start(bf16[896,768]{1,0:T(8,128)(2,1)S(1)} %bitcast.29), channel_id=1, source_target_pairs={{0,4},{4,0},{8,12},{12,8},{16,20},{20,16},{24,28},{28,24},{1,5},{5... | collective-permute-start | bytes 4128776 | tf_op jit(solution)/shard_map/ppermute | solution.py:35
  177.2 19.0 %collective-permute-start.12 = (bf16[896,512]{1,0:T(8,128)(2,1)}, bf16[896,512]{1,0:T(8,128)(2,1)}, u32[]{:S(2)}, u32[]{:S(2)}) collective-permute-start(bf16[896,512]{1,0:T(8,128)(2,1)} %bitcast.8.refs_2_.refs_1_), channel_id=1, source_target_pairs={{0,16},{4,20},{8,24},{12,28},{16,0},{20,4},{24,8},{28,12},{1,17},{... | collective-permute-start | bytes 2752520 | tf_op jit(solution)/shard_map/ppermute | solution.py:35
  179.1 18.3 %collective-permute-start.6 = (bf16[896,512]{1,0:T(8,128)(2,1)}, bf16[896,512]{1,0:T(8,128)(2,1)}, u32[]{:S(2)}, u32[]{:S(2)}) collective-permute-start(bf16[896,512]{1,0:T(8,128)(2,1)} %bitcast.8.refs_2_.refs_1_), channel_id=1, source_target_pairs={{0,8},{4,12},{8,0},{12,4},{16,24},{20,28},{24,16},{28,20},{1,9},{5... | collective-permute-start | bytes 2752520 | tf_op jit(solution)/shard_map/ppermute | solution.py:35
  179.7 22.9 %collective-permute-start.4 = (bf16[896,512]{1,0:T(8,128)(2,1)}, bf16[896,512]{1,0:T(8,128)(2,1)}, u32[]{:S(2)}, u32[]{:S(2)}) collective-permute-start(bf16[896,512]{1,0:T(8,128)(2,1)} %bitcast.8.refs_2_.refs_1_), channel_id=1, source_target_pairs={{0,4},{4,0},{8,12},{12,8},{16,20},{20,16},{24,28},{28,24},{1,5},{5... | collective-permute-start | bytes 2752520 | tf_op jit(solution)/shard_map/ppermute | solution.py:35
  201.0 12.8 %collective-permute-start.13 = (bf16[448,512]{1,0:T(8,128)(2,1)}, bf16[448,512]{1,0:T(8,128)(2,1)}, u32[]{:S(2)}, u32[]{:S(2)}) collective-permute-start(bf16[448,512]{1,0:T(8,128)(2,1)} %slice.91), channel_id=1, source_target_pairs={{0,16},{4,20},{8,24},{12,28},{16,0},{20,4},{24,8},{28,12},{1,17},{... | collective-permute-start | bytes 1376264 | tf_op jit(solution)/shard_map/ppermute | solution.py:35
  202.0 11.8 %collective-permute-start.14 = (bf16[448,512]{1,0:T(8,128)(2,1)}, bf16[448,512]{1,0:T(8,128)(2,1)}, u32[]{:S(2)}, u32[]{:S(2)}) collective-permute-start(bf16[448,512]{1,0:T(8,128)(2,1)} %slice.92), channel_id=1, source_target_pairs={{0,8},{4,12},{8,0},{12,4},{16,24},{20,28},{24,16},{28,20},{1,9},{5... | collective-permute-start | bytes 1376264 | tf_op jit(solution)/shard_map/ppermute | solution.py:35
  213.8 294.8 %all-reduce.5.cloned.1.call-start = ((), (), s32[]{:S(2)}) async-start(), calls=%async_computation.7 | async-start | bytes 6422528 | tf_op jit(solution)/shard_map/psum | solution.py:332
  225.0 67.5 %copy-start.13 = (bf16[2,448,896]{2,1,0:T(8,128)(2,1)S(1)}, bf16[2,448,896]{2,1,0:T(8,128)(2,1)}, u32[]{:S(2)}) copy-start(bf16[2,448,896]{2,1,0:T(8,128)(2,1)} %shard_map.19) | copy-start | bytes 4816900
  227.8 39.0 %collective-permute-start.15 = (bf16[1,448,896]{2,1,0:T(8,128)(2,1)}, bf16[1,448,896]{2,1,0:T(8,128)(2,1)}, u32[]{:S(2)}, u32[]{:S(2)}) collective-permute-start(bf16[1,448,896]{2,1,0:T(8,128)(2,1)} %get-tuple-element.60), channel_id=1, source_target_pairs={{0,1},{3,2},{4,5},{7,6},{8,9},{11,10},{12,13},{15,14},{16,17},{19,... | collective-permute-start | bytes 2408456 | tf_op jit(solution)/shard_map/ppermute | solution.py:254
  232.1 60.5 %collective-permute-start.18 = (bf16[1,448,896]{2,1,0:T(8,128)(2,1)}, bf16[1,448,896]{2,1,0:T(8,128)(2,1)}, u32[]{:S(2)}, u32[]{:S(2)}) collective-permute-start(bf16[1,448,896]{2,1,0:T(8,128)(2,1)} %get-tuple-element.59), channel_id=1, source_target_pairs={{0,1},{3,2},{4,5},{7,6},{8,9},{11,10},{12,13},{15,14},{16,17},{19,... | collective-permute-start | bytes 2408456 | tf_op jit(solution)/shard_map/ppermute | solution.py:254
  295.5 62.9 %collective-permute-start.16 = (bf16[1,448,896]{2,1,0:T(8,128)(2,1)}, bf16[1,448,896]{2,1,0:T(8,128)(2,1)S(1)}, u32[]{:S(2)}, u32[]{:S(2)}) collective-permute-start(bf16[1,448,896]{2,1,0:T(8,128)(2,1)} %get-tuple-element.58), channel_id=1, source_target_pairs={{1,2},{2,1},{5,6},{6,5},{9,10},{10,9},{13,14},{14,13},{17,18},{18,... | collective-permute-start | bytes 2408456 | tf_op jit(solution)/shard_map/ppermute | solution.py:254
  313.2 44.4 %copy-start.16 = (bf16[1,448,896]{2,1,0:T(8,128)(2,1)S(1)}, bf16[1,448,896]{2,1,0:T(8,128)(2,1)}, u32[]{:S(2)}) copy-start(bf16[1,448,896]{2,1,0:T(8,128)(2,1)} %get-tuple-element.57) | copy-start | bytes 2408452
  357.6 302.1 %all-gather.8.cloned.1.call-start = ((), (), s32[]{:S(2)}) async-start(), calls=%async_computation.10 | async-start | bytes 8257536 | tf_op jit(solution)/shard_map/all_gather | solution.py:356
  357.7 3.4 collective-permute-start.19
  359.7 49.3 %collective-permute-start.17 = (bf16[1,448,896]{2,1,0:T(8,128)(2,1)S(1)}, bf16[1,448,896]{2,1,0:T(8,128)(2,1)S(1)}, u32[]{:S(2)}, u32[]{:S(2)}) collective-permute-start(bf16[1,448,896]{2,1,0:T(8,128)(2,1)S(1)} %add_convert_fusion.2), channel_id=1, source_target_pairs={{1,0},{2,3},{5,4},{6,7},{9,8},{10,11},{13,12},{14,15},{17,16},{18,... | collective-permute-start | bytes 2408456 | tf_op jit(solution)/shard_map/ppermute | solution.py:254
  361.3 89.1 %collective-permute-start.20 = (bf16[1,448,896]{2,1,0:T(8,128)(2,1)S(1)}, bf16[1,448,896]{2,1,0:T(8,128)(2,1)}, u32[]{:S(2)}, u32[]{:S(2)}) collective-permute-start(bf16[1,448,896]{2,1,0:T(8,128)(2,1)S(1)} %add_convert_fusion), channel_id=1, source_target_pairs={{1,0},{2,3},{5,4},{6,7},{9,8},{10,11},{13,12},{14,15},{17,16},{18,... | collective-permute-start | bytes 2408456 | tf_op jit(solution)/shard_map/ppermute | solution.py:254
  362.6 92.2 %collective-permute-start.24 = (bf16[896,1024]{1,0:T(8,128)(2,1)}, bf16[896,1024]{1,0:T(8,128)(2,1)}, u32[]{:S(2)}, u32[]{:S(2)}) collective-permute-start(bf16[896,1024]{1,0:T(8,128)(2,1)} %collective-permute-done.refs_6_.refs_3_), channel_id=1, source_target_pairs={{0,4},{4,0},{8,12},{12,8},{16,20},{20,16},{24,28},{28,24},{1,5},{5... | collective-permute-start | bytes 5505032 | tf_op jit(solution)/shard_map/ppermute | solution.py:35
  362.7 92.1 %collective-permute-start.25 = (bf16[896,1024]{1,0:T(8,128)(2,1)}, bf16[896,1024]{1,0:T(8,128)(2,1)}, u32[]{:S(2)}, u32[]{:S(2)}) collective-permute-start(bf16[896,1024]{1,0:T(8,128)(2,1)} %collective-permute-done.1.refs_9_.refs_5_), channel_id=1, source_target_pairs={{0,4},{4,0},{8,12},{12,8},{16,20},{20,16},{24,28},{28,24},{1,5},{5... | collective-permute-start | bytes 5505032 | tf_op jit(solution)/shard_map/ppermute | solution.py:35
  363.1 90.8 %collective-permute-start.26 = (bf16[448,1024]{1,0:T(8,128)(2,1)}, bf16[448,1024]{1,0:T(8,128)(2,1)}, u32[]{:S(2)}, u32[]{:S(2)}) collective-permute-start(bf16[448,1024]{1,0:T(8,128)(2,1)} %collective-permute-done.7.refs_7_), channel_id=1, source_target_pairs={{0,4},{4,0},{8,12},{12,8},{16,20},{20,16},{24,28},{28,24},{1,5},{5... | collective-permute-start | bytes 2752520 | tf_op jit(solution)/shard_map/ppermute | solution.py:35
  409.0 45.0 %collective-permute-start.27 = (bf16[448,1024]{1,0:T(8,128)(2,1)}, bf16[448,1024]{1,0:T(8,128)(2,1)}, u32[]{:S(2)}, u32[]{:S(2)}) collective-permute-start(bf16[448,1024]{1,0:T(8,128)(2,1)} %collective-permute-done.8.refs_8_), channel_id=1, source_target_pairs={{0,4},{4,0},{8,12},{12,8},{16,20},{20,16},{24,28},{28,24},{1,5},{5... | collective-permute-start | bytes 2752520 | tf_op jit(solution)/shard_map/ppermute | solution.py:35
  450.4 21.7 %collective-permute-start.22 = (bf16[1,448,896]{2,1,0:T(8,128)(2,1)S(1)}, bf16[1,448,896]{2,1,0:T(8,128)(2,1)S(1)}, u32[]{:S(2)}, u32[]{:S(2)}) collective-permute-start(bf16[1,448,896]{2,1,0:T(8,128)(2,1)S(1)} %broadcast_select_fusion.1.mine), channel_id=1, source_target_pairs={{0,24},{4,28},{8,16},{12,20},{16,8},{20,12},{24,0},{28,4},{1,25},{... | collective-permute-start | bytes 2408456 | tf_op jit(solution)/shard_map/ppermute | solution.py:35
  453.9 60.0 %copy-start.1 = (bf16[3,448,896]{2,1,0:T(8,128)(2,1)S(1)}, bf16[3,448,896]{2,1,0:T(8,128)(2,1)}, u32[]{:S(2)}) copy-start(bf16[3,448,896]{2,1,0:T(8,128)(2,1)} %all-reduce.3.cloned.1.call-done.halves.mine) | copy-start | bytes 7225348
  454.0 19.1 %collective-permute-start.21 = (bf16[1,448,896]{2,1,0:T(8,128)(2,1)S(1)}, bf16[1,448,896]{2,1,0:T(8,128)(2,1)S(1)}, u32[]{:S(2)}, u32[]{:S(2)}) collective-permute-start(bf16[1,448,896]{2,1,0:T(8,128)(2,1)S(1)} %broadcast_select_fusion), channel_id=1, source_target_pairs={{0,4},{4,0},{8,12},{12,8},{16,20},{20,16},{24,28},{28,24},{1,5},{5... | collective-permute-start | bytes 2408456 | tf_op jit(solution)/shard_map/ppermute | solution.py:35
  454.0 33.6 %collective-permute-start.23 = (bf16[1,448,896]{2,1,0:T(8,128)(2,1)S(1)}, bf16[1,448,896]{2,1,0:T(8,128)(2,1)S(1)}, u32[]{:S(2)}, u32[]{:S(2)}) collective-permute-start(bf16[1,448,896]{2,1,0:T(8,128)(2,1)S(1)} %broadcast_select_fusion), channel_id=1, source_target_pairs={{0,24},{4,28},{8,16},{12,20},{16,8},{20,12},{24,0},{28,4},{1,25},{... | collective-permute-start | bytes 2408456 | tf_op jit(solution)/shard_map/ppermute | solution.py:35
  508.6 5.5 copy-start
  510.9 36.9 %collective-permute-start.31 = (bf16[2,448,896]{2,1,0:T(8,128)(2,1)S(1)}, bf16[2,448,896]{2,1,0:T(8,128)(2,1)S(1)}, u32[]{:S(2)}, u32[]{:S(2)}) collective-permute-start(bf16[2,448,896]{2,1,0:T(8,128)(2,1)S(1)} %get-tuple-element.53), channel_id=1, source_target_pairs={{0,8},{4,12},{8,0},{12,4},{16,24},{20,28},{24,16},{28,20},{1,9},{5... | collective-permute-start | bytes 4816904 | tf_op jit(solution)/shard_map/ppermute | solution.py:35
  512.4 44.6 %collective-permute-start.29 = (bf16[2,448,896]{2,1,0:T(8,128)(2,1)S(1)}, bf16[2,448,896]{2,1,0:T(8,128)(2,1)S(1)}, u32[]{:S(2)}, u32[]{:S(2)}) collective-permute-start(bf16[2,448,896]{2,1,0:T(8,128)(2,1)S(1)} %get-tuple-element.54), channel_id=1, source_target_pairs={{0,16},{4,20},{8,24},{12,28},{16,0},{20,4},{24,8},{28,12},{1,17},{... | collective-permute-start | bytes 4816904 | tf_op jit(solution)/shard_map/ppermute | solution.py:35
  514.0 2.4 collective-permute-start.32
  515.1 39.9 %collective-permute-start.30 = (bf16[1,448,896]{2,1,0:T(8,128)(2,1)}, bf16[1,448,896]{2,1,0:T(8,128)(2,1)S(1)}, u32[]{:S(2)}, u32[]{:S(2)}) collective-permute-start(bf16[1,448,896]{2,1,0:T(8,128)(2,1)} %get-tuple-element.55), channel_id=1, source_target_pairs={{0,4},{4,0},{8,12},{12,8},{16,20},{20,16},{24,28},{28,24},{1,5},{5... | collective-permute-start | bytes 2408456 | tf_op jit(solution)/shard_map/ppermute | solution.py:35
  515.5 42.8 %collective-permute-start.28 = (bf16[1,448,896]{2,1,0:T(8,128)(2,1)S(1)}, bf16[1,448,896]{2,1,0:T(8,128)(2,1)S(1)}, u32[]{:S(2)}, u32[]{:S(2)}) collective-permute-start(bf16[1,448,896]{2,1,0:T(8,128)(2,1)S(1)} %get-tuple-element.56), channel_id=1, source_target_pairs={{0,4},{4,0},{8,12},{12,8},{16,20},{20,16},{24,28},{28,24},{1,5},{5... | collective-permute-start | bytes 2408456 | tf_op jit(solution)/shard_map/ppermute | solution.py:35
  516.3 64.9 %collective-permute-start.33 = (bf16[896,768]{1,0:T(8,128)(2,1)}, bf16[896,768]{1,0:T(8,128)(2,1)}, u32[]{:S(2)}, u32[]{:S(2)}) collective-permute-start(bf16[896,768]{1,0:T(8,128)(2,1)} %collective-permute-done.5.refs_7_.refs_3_), channel_id=1, source_target_pairs={{0,4},{4,0},{8,12},{12,8},{16,20},{20,16},{24,28},{28,24},{1,5},{5... | collective-permute-start | bytes 4128776 | tf_op jit(solution)/shard_map/ppermute | solution.py:35
  547.7 33.6 %collective-permute-start.34 = (bf16[896,768]{1,0:T(8,128)(2,1)}, bf16[896,768]{1,0:T(8,128)(2,1)}, u32[]{:S(2)}, u32[]{:S(2)}) collective-permute-start(bf16[896,768]{1,0:T(8,128)(2,1)} %collective-permute-done.9.refs_10_.refs_5_), channel_id=1, source_target_pairs={{0,4},{4,0},{8,12},{12,8},{16,20},{20,16},{24,28},{28,24},{1,5},{5... | collective-permute-start | bytes 4128776 | tf_op jit(solution)/shard_map/ppermute | solution.py:35
  549.0 1.4 copy-start.8
  550.4 1.4 copy-start.10
  550.4 2.0 copy-start.12
  554.9 25.7 %collective-permute-start.35 = (bf16[448,768]{1,0:T(8,128)(2,1)}, bf16[448,768]{1,0:T(8,128)(2,1)S(1)}, u32[]{:S(2)}, u32[]{:S(2)}) collective-permute-start(bf16[448,768]{1,0:T(8,128)(2,1)} %collective-permute-done.10.refs_7_), channel_id=1, source_target_pairs={{0,4},{4,0},{8,12},{12,8},{16,20},{20,16},{24,28},{28,24},{1,5},{5... | collective-permute-start | bytes 2064392 | tf_op jit(solution)/shard_map/ppermute | solution.py:35
  557.0 23.7 %collective-permute-start.36 = (bf16[448,768]{1,0:T(8,128)(2,1)}, bf16[448,768]{1,0:T(8,128)(2,1)S(1)}, u32[]{:S(2)}, u32[]{:S(2)}) collective-permute-start(bf16[448,768]{1,0:T(8,128)(2,1)} %collective-permute-done.11.refs_8_), channel_id=1, source_target_pairs={{0,4},{4,0},{8,12},{12,8},{16,20},{20,16},{24,28},{28,24},{1,5},{5... | collective-permute-start | bytes 2064392 | tf_op jit(solution)/shard_map/ppermute | solution.py:35
  558.4 38.6 %collective-permute-start.37 = (bf16[896,512]{1,0:T(8,128)(2,1)}, bf16[896,512]{1,0:T(8,128)(2,1)}, u32[]{:S(2)}, u32[]{:S(2)}) collective-permute-start(bf16[896,512]{1,0:T(8,128)(2,1)} %collective-permute-done.6.refs_8_.refs_3_), channel_id=1, source_target_pairs={{0,4},{4,0},{8,12},{12,8},{16,20},{20,16},{24,28},{28,24},{1,5},{5... | collective-permute-start | bytes 2752520 | tf_op jit(solution)/shard_map/ppermute | solution.py:35
  560.5 20.9 %copy-start.5 = (bf16[4,224,768]{2,1,0:T(8,128)(2,1)S(1)}, bf16[4,224,768]{2,1,0:T(8,128)(2,1)}, u32[]{:S(2)}) copy-start(bf16[4,224,768]{2,1,0:T(8,128)(2,1)} %copy-done.4) | copy-start | bytes 4128772
  580.7 16.3 %collective-permute-start.38 = (bf16[896,512]{1,0:T(8,128)(2,1)}, bf16[896,512]{1,0:T(8,128)(2,1)}, u32[]{:S(2)}, u32[]{:S(2)}) collective-permute-start(bf16[896,512]{1,0:T(8,128)(2,1)} %collective-permute-done.12.refs_11_.refs_5_), channel_id=1, source_target_pairs={{0,4},{4,0},{8,12},{12,8},{16,20},{20,16},{24,28},{28,24},{1,5},{5... | collective-permute-start | bytes 2752520 | tf_op jit(solution)/shard_map/ppermute | solution.py:35
  580.8 16.2 %collective-permute-start.39 = (bf16[448,512]{1,0:T(8,128)(2,1)}, bf16[448,512]{1,0:T(8,128)(2,1)S(1)}, u32[]{:S(2)}, u32[]{:S(2)}) collective-permute-start(bf16[448,512]{1,0:T(8,128)(2,1)} %collective-permute-done.13.refs_7_), channel_id=1, source_target_pairs={{0,4},{4,0},{8,12},{12,8},{16,20},{20,16},{24,28},{28,24},{1,5},{5... | collective-permute-start | bytes 1376264 | tf_op jit(solution)/shard_map/ppermute | solution.py:35
  581.3 15.7 %collective-permute-start.40 = (bf16[448,512]{1,0:T(8,128)(2,1)}, bf16[448,512]{1,0:T(8,128)(2,1)}, u32[]{:S(2)}, u32[]{:S(2)}) collective-permute-start(bf16[448,512]{1,0:T(8,128)(2,1)} %collective-permute-done.14.refs_8_), channel_id=1, source_target_pairs={{0,4},{4,0},{8,12},{12,8},{16,20},{20,16},{24,28},{28,24},{1,5},{5... | collective-permute-start | bytes 1376264 | tf_op jit(solution)/shard_map/ppermute | solution.py:35
  608.9 118.1 %all-gather.6.cloned.1.call-start = ((), (), s32[]{:S(2)}) async-start(), calls=%async_computation.9 | async-start | bytes 12386304 | tf_op jit(solution)/shard_map/all_gather | solution.py:356
  609.4 200.3 %all-gather.4.cloned.1.call-start = ((), (), s32[]{:S(2)}) async-start(), calls=%async_computation.8 | async-start | bytes 16515072 | tf_op jit(solution)/shard_map/all_gather | solution.py:356
  673.3 71.5 %all-to-all-start.5 = ((bf16[4,224,512]{2,1,0:T(8,128)(2,1)}), bf16[4,224,512]{2,1,0:T(8,128)(2,1)S(1)}, u32[]{:S(2)}, u32[]{:S(2)}) async-start(bf16[4,224,512]{2,1,0:T(8,128)(2,1)} %bitcast.14), calls=%async_computation.5 | async-start | bytes 1835008 | tf_op jit(solution)/shard_map/all_to_all | solution.py:360
  744.8 64.9 %copy-start.3 = (bf16[4,224,1024]{2,1,0:T(8,128)(2,1)S(1)}, bf16[4,224,1024]{2,1,0:T(8,128)(2,1)}, u32[]{:S(2)}) copy-start(bf16[4,224,1024]{2,1,0:T(8,128)(2,1)} %copy-done.2) | copy-start | bytes 5505028
  745.8 86.2 %all-to-all-start.4 = ((bf16[4,224,768]{2,1,0:T(8,128)(2,1)}), bf16[4,224,768]{2,1,0:T(8,128)(2,1)S(1)}, u32[]{:S(2)}, u32[]{:S(2)}) async-start(bf16[4,224,768]{2,1,0:T(8,128)(2,1)} %bitcast.12), calls=%async_computation.4 | async-start | bytes 2752512 | tf_op jit(solution)/shard_map/all_to_all | solution.py:360
  830.8 1.2 copy-start.6
  832.0 47.7 %copy-start.15 = (bf16[4,224,512]{2,1,0:T(8,128)(2,1)S(1)}, bf16[4,224,512]{2,1,0:T(8,128)(2,1)}, u32[]{:S(2)}) copy-start(bf16[4,224,512]{2,1,0:T(8,128)(2,1)} %copy-done.14) | copy-start | bytes 2752516
  (4 other events, 3.8 us)
Sparse Core Ops, SparseCore 0:
  213.9 143.6 all-reduce.2
  360.1 148.4 all-reduce.4
  609.0 50.6 all-gather.7
  661.4 65.4 all-gather.5
  728.7 80.9 all-gather.3

commit v7 on v4

--- a/solution.py
+++ b/solution.py
@@ -171,9 +171,9 @@
     )(halves)
 
 
-def product_kernel(keys, start, finish, me_ref, *refs):
+def product_kernel(keys, start, finish, n_deps, me_ref, *refs):
     gram, parts = refs[0], refs[1 : 1 + len(keys)]
-    extra = refs[1 + len(keys) : -5]
+    extra = refs[1 + len(keys) : -5 - n_deps]
     out, gbuf, xbuf, acc, sems = refs[-5:]
     count, size, width = xbuf.shape
     h = size // 2
@@ -216,16 +216,17 @@
         out[...] = acc[...].astype(bf16)
 
 
-def product(gram, me, parts, start, width, extra=()):
+def product(gram, me, parts, start, width, extra=(), deps=()):
     count, size, _ = gram.shape
     keys = sorted(parts)
     flops = 2 * count * size * size * width
     return pl.pallas_call(
-        functools.partial(product_kernel, keys, start, bool(extra)),
+        functools.partial(product_kernel, keys, start, bool(extra), len(deps)),
         out_shape=jax.ShapeDtypeStruct((size, width), bf16),
         in_specs=[pl.BlockSpec(memory_space=pltpu.SMEM)]
         + [pl.BlockSpec(memory_space=pl.ANY)] * (1 + len(keys))
-        + [pl.BlockSpec(memory_space=pltpu.VMEM)] * len(extra),
+        + [pl.BlockSpec(memory_space=pltpu.VMEM)] * len(extra)
+        + [pl.BlockSpec(memory_space=pl.ANY)] * len(deps),
         out_specs=pl.BlockSpec(memory_space=pltpu.VMEM),
         scratch_shapes=[
             pltpu.VMEM((count, size, size), bf16),
@@ -239,7 +240,7 @@
             transcendentals=0,
         ),
         compiler_params=pltpu.CompilerParams(vmem_limit_bytes=VMEM_BYTES),
-    )(me.astype(jnp.int32).reshape(1), gram, *[parts[key] for key in keys], *extra)
+    )(me.astype(jnp.int32).reshape(1), gram, *[parts[key] for key in keys], *extra, *deps)
 
 
 def per_device(ortho_in):
@@ -262,7 +263,7 @@
     start = 0
     thirds = widths_of(width, 3)
     if width % (9 * 256) == 0:
-        thirds = [width // 9 * n for n in (3, 4, 2)]
+        thirds = [width // 9 * n for n in (4, 3, 2)]
     for k, w in enumerate(thirds):
         first = [start + c * width for c in range(n_col)]
         part = jnp.concatenate([ortho_in[:, f : f + w] for f in first], axis=0)
@@ -301,6 +302,8 @@
         pieces = gram_pieces(blocks, jobs, [low_of(j)[0] for j in stage], scale)
         held = list(panels[0].values()) if len(stage) == 1 else []
         last = sums = lax.psum(after(pieces, last, *held), "col")
+        if len(stage) == 1:
+            sums, gram = lax.optimization_barrier((sums, gram))
         for n, j in enumerate(stage):
             theirs = swap(sums[n * bit_x : (n + 1) * bit_x], j)
             gram = put_block(gram, low_of(j), (sums, n * bit_x), (theirs, 0), j)
@@ -308,12 +311,15 @@
                 mine = swap(sums[n * bit_x + i : n * bit_x + i + 1], i)
                 gram = put_block(gram, low_of(j), (mine, 0), (theirs, i), j | i)
 
-    outs = []
+    outs, firsts, backs = [], [], []
     for k, w in enumerate(thirds):
-        first = product(gram, me, panels[k], 0, w)
+        first = product(gram, me, panels[k], 0, w, (), firsts[-1:])
+        firsts.append(first)
         first_panel = lax.all_gather(first, "row", axis=0, tiled=True)
-        result = product(gram, me, {None: first_panel}, 0, w, (tiles[k], first))
+        extra = (tiles[k], first)
+        result = product(gram, me, {None: first_panel}, 0, w, extra, backs[-1:])
         back = lax.all_to_all(result, "col", split_axis=0, concat_axis=1, tiled=True)
+        backs.append(back)
         outs.append(back.reshape(rows, n_col, w))
     return jnp.concatenate(outs, axis=2).reshape(rows, cols)
 

time: 787 us -> 761 us (0.967)
  waiting for transfers between devices: 471 us -> 399 us
  blocking collectives: 47.6 us -> 107 us
  starting transfers between devices: 48 us -> 37.2 us
    all_gather x3, waiting for transfers between devices: 111 us -> 34 us  [per_device(): first_panel = lax.all_gather(first, 'row', axis=0, tiled=True)]
    all_to_all x1 -> x3, blocking collectives: 47.6 us -> 107 us  [per_device(): lax.all_to_all(result, 'col', split_axis=0, concat_axis=1, tiled=True)]
    ppermute x34, waiting for transfers between devices: 144 us -> 194 us  [swap(): return lax.ppermute(value, 'row', [(r, r ^ bit) for r in range(count)])]
    psum x2, waiting for transfers between devices: 128 us -> 84.9 us  [per_device(): last = sums = lax.psum(after(pieces, last, *held), 'col')]
    all_to_all x2 -> x0, starting transfers between devices: 9.52 us -> none  [per_device(): lax.all_to_all(result, 'col', split_axis=0, concat_axis=1, tiled=True)]
  transfers between devices with their start and end apart: 45 -> 43, of which waited for: 25 -> 22; matrix products, arithmetic and copies ran while one was open for 3% -> 3% of each run, Pallas kernels for 18% -> 14%
where the time goes in v7:
time: 761 us; the launch traced here: 752 us
  waiting for transfers between devices  399 us (52%)
  Pallas kernels  150 us (20%)
  blocking collectives  107 us (14%)
  starting transfers between devices  37.2 us (5%)
  local copies, waits for them, and re-layouts  36.2 us (5%)
  between operations  14.2 us (2%)
  other arithmetic  8.25 us (1%)
    ppermute x34, waiting for transfers between devices, swap(): return lax.ppermute(value, 'row', [(r, r ^ bit) for r in range(count)])  194 us
    all_to_all x3, blocking collectives, per_device(): lax.all_to_all(result, 'col', split_axis=0, concat_axis=1, tiled=True)  107 us
    pallas_call x6, Pallas kernels, product(): pl.pallas_call(functools.partial(product_kernel, keys, start, bool(extra)...  97.6 us
    psum x2, waiting for transfers between devices, per_device(): last = sums = lax.psum(after(pieces, last, *held), 'col')  84.9 us
    all_to_all x3, waiting for transfers between devices, exchange(): return lax.all_to_all(value, 'col', split_axis=0, concat_axis=0, tiled=True)  60.6 us
    pallas_call x3, Pallas kernels, gram_pieces(): pl.pallas_call(functools.partial(pieces_kernel, count, jobs, scale), out_...  37.3 us
    all_gather x3, waiting for transfers between devices, per_device(): first_panel = lax.all_gather(first, 'row', axis=0, tiled=True)  34 us
    psum x1, waiting for transfers between devices, per_device(): last = near = lax.psum(near, 'col')  25.5 us
  transfers between devices with their start and end apart: 43, of which 22 were waited for; matrix products, arithmetic and copies ran while one was open for 3% of the time, Pallas kernels for 14%

profile of v7, /device:TPU:0, one launch (start us, length us, event | category | flops | bytes accessed | tf_op | source)
XLA Modules:
  0.0 752.4 jit_solution(15997956922365199734)
XLA Ops:
  6.5 1.6 fusion.2
  8.1 1.4 pad_maximum_fusion
  9.5 6.3 all-to-all-start
  15.8 1.4 fusion.1
  18.4 40.0 %all-to-all-done = bf16[4,224,1024]{2,1,0:T(8,128)(2,1)S(1)} async-done(((bf16[4,224,1024]{2,1,0:T(8,128)(2,1)}), bf16[4,224,1024]{2,1,0:T(8,128)(2,1)S(1)}, u32[]{:S(2)}, u32[]{:S(2)}) %all-to-all-start) | async-done | bytes 1835040 | tf_op jit(solution)/shard_map/all_to_all | solution.py:260
  58.4 3.5 all-to-all-start.1
  61.9 1.6 collective-permute-start
  63.5 1.5 collective-permute-start.1
  65.0 1.3 fusion
  67.4 35.6 %collective-permute-done.refs_6_.refs_3_ = bf16[896,1024]{1,0:T(8,128)(2,1)S(1)} collective-permute-done((bf16[896,1024]{1,0:T(8,128)(2,1)S(1)}, bf16[896,1024]{1,0:T(8,128)(2,1)S(1)}, u32[]{:S(2)}, u32[]{:S(2)}) %collective-permute-start) | collective-permute-done | bytes 1835040 | tf_op jit(solution)/shard_map/ppermute | solution.py:35
  103.0 1.3 copy-done.26
  104.3 4.7 all-to-all-start.2
  109.6 20.6 %all-to-all-done.2 = bf16[4,224,512]{2,1,0:T(8,128)(2,1)} async-done(((bf16[4,224,512]{2,1,0:T(8,128)(2,1)}), bf16[4,224,512]{2,1,0:T(8,128)(2,1)}, u32[]{:S(2)}, u32[]{:S(2)}) %all-to-all-start.2) | async-done | bytes 917536 | tf_op jit(solution)/shard_map/all_to_all | solution.py:260
  130.2 2.8 collective-permute-done.4.refs_5_.refs_2_
  133.0 11.2 %shard_map.19 = bf16[3,448,896]{2,1,0:T(8,128)(2,1)} custom-call(s32[1]{0:T(128)} %bitcast.9.low_ref, bf16[896,1024]{1,0:T(8,128)(2,1)} %bitcast.26, bf16[896,768]{1,0:T(8,128)(2,1)S(1)} %bitcast.32, bf16[896,512]{1,0:T(8,128)(2,1)} %bitcast.7.refs_2_.refs_1_, bf16[896,1024]{1,0:T(8,128)(2,1)} %collective-permute-done.2.refs_3_.refs_2_, ...), custom_call_target="tpu_custom_call" | custom-call | flops 5549064192 | bytes 10665984 | tf_op jit(solution)/shard_map/pallas_call | solution.py:103
  144.2 1.6 collective-permute-start.7
  145.8 1.5 collective-permute-start.8
  148.4 29.0 %collective-permute-done.7.refs_7_.refs_3_ = bf16[896,768]{1,0:T(8,128)(2,1)} collective-permute-done((bf16[896,768]{1,0:T(8,128)(2,1)S(1)}, bf16[896,768]{1,0:T(8,128)(2,1)}, u32[]{:S(2)}, u32[]{:S(2)}) %collective-permute-start.7) | collective-permute-done | bytes 1376288 | tf_op jit(solution)/shard_map/ppermute | solution.py:35
  177.4 1.5 collective-permute-done.8.refs_10_.refs_5_
  179.0 2.0 slice.86
  181.0 2.0 slice.87
  184.0 2.2 slice.85
  186.2 9.9 %collective-permute-done.11.refs_8_.refs_3_ = bf16[896,512]{1,0:T(8,128)(2,1)S(1)} collective-permute-done((bf16[896,512]{1,0:T(8,128)(2,1)}, bf16[896,512]{1,0:T(8,128)(2,1)S(1)}, u32[]{:S(2)}, u32[]{:S(2)}) %collective-permute-start.11) | collective-permute-done | bytes 917536 | tf_op jit(solution)/shard_map/ppermute | solution.py:35
  199.0 16.1 %shard_map.18 = bf16[4,448,896]{2,1,0:T(8,128)(2,1)} custom-call(s32[2]{0:T(128)S(1)} %pad_add_fusion.low_ref, bf16[896,1024]{1,0:T(8,128)(2,1)} %bitcast.27, bf16[896,768]{1,0:T(8,128)(2,1)S(1)} %bitcast.35, bf16[896,512]{1,0:T(8,128)(2,1)} %bitcast.7.refs_2_.refs_1_, bf16[896,1024]{1,0:T(8,128)(2,1)} %collective-permute-done.2.refs_3_.refs_2_, ...), custom_call_target="tpu_custom_call" | custom-call | flops 7398752256 | bytes 19726336 | tf_op jit(solution)/shard_map/pallas_call | solution.py:103
  215.2 25.5 %all-reduce.4.cloned.1.call-done.halves.mine = bf16[3,448,896]{2,1,0:T(8,128)(2,1)} async-done(((bf16[3,448,896]{2,1,0:T(8,128)(2,1)}), bf16[3,448,896]{2,1,0:T(8,128)(2,1)}) %all-reduce.4.cloned.1.call-update) | async-done | bytes 2408464 | tf_op jit(solution)/shard_map/psum | solution.py:286
  240.8 1.5 collective-permute-start.10
  242.3 1.5 collective-permute-start.5
  244.9 14.5 %collective-permute-done.10.refs_8_ = bf16[448,768]{1,0:T(8,128)(2,1)S(1)} collective-permute-done((bf16[448,768]{1,0:T(8,128)(2,1)}, bf16[448,768]{1,0:T(8,128)(2,1)S(1)}, u32[]{:S(2)}, u32[]{:S(2)}) %collective-permute-start.10) | collective-permute-done | bytes 688160 | tf_op jit(solution)/shard_map/ppermute | solution.py:35
  259.4 19.4 %collective-permute-done.9.refs_7_ = bf16[448,768]{1,0:T(8,128)(2,1)S(1)} collective-permute-done((bf16[448,768]{1,0:T(8,128)(2,1)}, bf16[448,768]{1,0:T(8,128)(2,1)S(1)}, u32[]{:S(2)}, u32[]{:S(2)}) %collective-permute-start.9) | collective-permute-done | bytes 688160 | tf_op jit(solution)/shard_map/ppermute | solution.py:35
  278.9 1.5 collective-permute-start.13
  282.1 8.1 %collective-permute-done.13.refs_7_ = bf16[448,512]{1,0:T(8,128)(2,1)S(1)} collective-permute-done((bf16[448,512]{1,0:T(8,128)(2,1)}, bf16[448,512]{1,0:T(8,128)(2,1)S(1)}, u32[]{:S(2)}, u32[]{:S(2)}) %collective-permute-start.13) | collective-permute-done | bytes 458784 | tf_op jit(solution)/shard_map/ppermute | solution.py:35
  290.2 3.1 pad_maximum_fusion.1.refs_6_
  294.1 10.0 %shard_map.17 = bf16[2,448,896]{2,1,0:T(8,128)(2,1)} custom-call(s32[1]{0:T(128)} %bitcast.1.low_ref, bf16[896,1024]{1,0:T(8,128)(2,1)} %bitcast.28, bf16[896,768]{1,0:T(8,128)(2,1)S(1)} %bitcast.36, bf16[896,512]{1,0:T(8,128)(2,1)} %bitcast.7.refs_2_.refs_1_, bf16[896,1024]{1,0:T(8,128)(2,1)} %collective-permute-done.2.refs_3_.refs_2_, ...), custom_call_target="tpu_custom_call" | custom-call | flops 3699376128 | bytes 13991936 | tf_op jit(solution)/shard_map/pallas_call | solution.py:103
  304.1 61.4 %all-reduce.6.cloned.1.call-done.mine = bf16[4,448,896]{2,1,0:T(8,128)(2,1)} async-done(((bf16[4,448,896]{2,1,0:T(8,128)(2,1)}), bf16[4,448,896]{2,1,0:T(8,128)(2,1)}) %all-reduce.6.cloned.1.call-update) | async-done | bytes 3211280 | tf_op jit(solution)/shard_map/psum | solution.py:304
  365.5 3.9 fusion.3
  369.4 1.5 collective-permute-start.22
  370.8 1.5 collective-permute-start.20
  375.4 1.3 shard_map.20.gram_in
  376.7 1.3 shard_map.21.gram_in
  378.0 28.5 %collective-permute-done.22.theirs = bf16[2,448,896]{2,1,0:T(8,128)(2,1)} collective-permute-done((bf16[2,448,896]{2,1,0:T(8,128)(2,1)}, bf16[2,448,896]{2,1,0:T(8,128)(2,1)}, u32[]{:S(2)}, u32[]{:S(2)}) %collective-permute-start.22) | collective-permute-done | bytes 1605664 | tf_op jit(solution)/shard_map/ppermute | solution.py:35
  406.5 2.4 shard_map.22.gram_in
  408.9 2.5 shard_map.23.gram_in
  411.3 2.5 shard_map.24.gram_in
  413.8 2.5 shard_map.25.gram_in
  416.3 23.5 %all-reduce.8.cloned.1.call-done.mine = bf16[2,448,896]{2,1,0:T(8,128)(2,1)} async-done(((bf16[2,448,896]{2,1,0:T(8,128)(2,1)}), bf16[2,448,896]{2,1,0:T(8,128)(2,1)}) %all-reduce.8.cloned.1.call-update) | async-done | bytes 1605648 | tf_op jit(solution)/shard_map/psum | solution.py:304
  439.9 2.4 collective-permute-start.25
  442.3 1.2 slice.95
  443.6 33.1 %collective-permute-done.25.theirs = bf16[2,448,896]{2,1,0:T(8,128)(2,1)S(1)} collective-permute-done((bf16[2,448,896]{2,1,0:T(8,128)(2,1)}, bf16[2,448,896]{2,1,0:T(8,128)(2,1)S(1)}, u32[]{:S(2)}, u32[]{:S(2)}) %collective-permute-start.25) | collective-permute-done | bytes 1605664 | tf_op jit(solution)/shard_map/ppermute | solution.py:35
  476.6 1.3 shard_map.26.gram_in
  477.9 1.3 shard_map.27.refs_0_
  479.2 20.2 %shard_map.28.refs_3_.refs_11_ = bf16[896,1024]{1,0:T(8,128)(2,1)} custom-call(s32[1]{0:T(128)} %bitcast.me_ref, bf16[8,896,896]{2,1,0:T(8,128)(2,1)} %shard_map.27.refs_0_, bf16[896,1024]{1,0:T(8,128)(2,1)} %bitcast.29, bf16[896,1024]{1,0:T(8,128)(2,1)} %collective-permute-done.2.refs_3_.refs_2_, bf16[896,1024]{1,0:T(8,128)(2,1)} %copy-done.26, ...), custom_call_target="tpu_custom_call" | custom-call | flops 13153337344 | bytes 27525120 | tf_op jit(solution)/shard_map/pallas_call | solution.py:223
  500.8 4.1 collective-permute-done.28.refs_9_
  504.9 2.0 collective-permute-done.29.refs_10_
  509.1 15.8 %shard_map.30.refs_3_.refs_11_ = bf16[896,768]{1,0:T(8,128)(2,1)} custom-call(s32[1]{0:T(128)} %bitcast.me_ref, bf16[8,896,896]{2,1,0:T(8,128)(2,1)} %shard_map.27.refs_0_, bf16[896,768]{1,0:T(8,128)(2,1)S(1)} %bitcast.37, bf16[896,768]{1,0:T(8,128)(2,1)} %collective-permute-done.3.refs_4_.refs_2_, bf16[896,768]{1,0:T(8,128)(2,1)} %collective-permute-done.7.refs_7_.refs_3_, ...), custom_call_target="tpu_custom_call" | custom-call | flops 9865003008 | bytes 23855104 | tf_op jit(solution)/shard_map/pallas_call | solution.py:223
  526.1 3.6 collective-permute-done.32.refs_9_
  535.5 11.2 %shard_map.32.refs_3_ = bf16[896,512]{1,0:T(8,128)(2,1)S(1)} custom-call(s32[1]{0:T(128)} %bitcast.me_ref, bf16[8,896,896]{2,1,0:T(8,128)(2,1)} %shard_map.27.refs_0_, bf16[896,512]{1,0:T(8,128)(2,1)} %bitcast.7.refs_2_.refs_1_, bf16[896,512]{1,0:T(8,128)(2,1)} %collective-permute-done.4.refs_5_.refs_2_, bf16[896,512]{1,0:T(8,128)(2,1)S(1)} %copy-done.18, ...), custom_call_target="tpu_custom_call" | custom-call | flops 6576668672 | bytes 20185088 | tf_op jit(solution)/shard_map/pallas_call | solution.py:223
  547.7 34.0 %all-gather.4.cloned.1.call-done.refs_1_ = bf16[7168,1024]{1,0:T(8,128)(2,1)} async-done(((bf16[896,1024]{1,0:T(8,128)(2,1)}), bf16[7168,1024]{1,0:T(8,128)(2,1)}) %all-gather.4.cloned.1.call-update) | async-done | bytes 14680080 | tf_op jit(solution)/shard_map/all_gather | solution.py:318
  581.7 21.1 %shard_map.29 = bf16[896,1024]{1,0:T(8,128)(2,1)S(1)} custom-call(s32[1]{0:T(128)} %bitcast.me_ref, bf16[8,896,896]{2,1,0:T(8,128)(2,1)} %shard_map.27.refs_0_, bf16[7168,1024]{1,0:T(8,128)(2,1)} %all-gather.4.cloned.1.call-done.refs_1_, bf16[896,1024]{1,0:T(8,128)(2,1)S(1)} %bitcast.30, bf16[896,1024]{1,0:T(8,128)(2,1)} %shard_map.28.refs_3_.refs_11_), custom_call_target="tpu_custom_call" | custom-call | flops 13153337344 | bytes 27525120 | tf_op jit(solution)/shard_map/pallas_call | solution.py:223
  602.7 47.4 %all_to_all.87 = bf16[4,224,1024]{2,1,0:T(8,128)(2,1)S(1)} all-to-all(bf16[4,224,1024]{2,1,0:T(8,128)(2,1)S(1)} %bitcast.40), channel_id=1, replica_groups=mesh['row'=8,'col'=4] {'col'}, dimensions={0} | all-to-all | bytes 3670016 | tf_op jit(solution)/shard_map/all_to_all | solution.py:321
  651.6 16.8 %shard_map.31 = bf16[896,768]{1,0:T(8,128)(2,1)S(1)} custom-call(s32[1]{0:T(128)} %bitcast.me_ref, bf16[8,896,896]{2,1,0:T(8,128)(2,1)} %shard_map.27.refs_0_, bf16[7168,768]{1,0:T(8,128)(2,1)} %all-gather.6.cloned.1.call-done.refs_1_, bf16[896,768]{1,0:T(8,128)(2,1)S(1)} %bitcast.38, bf16[896,768]{1,0:T(8,128)(2,1)} %shard_map.30.refs_3_.refs_11_, ...), custom_call_target="tpu_custom_call" | custom-call | flops 9865003008 | bytes 23855104 | tf_op jit(solution)/shard_map/pallas_call | solution.py:223
  668.4 34.9 %all_to_all.88 = bf16[4,224,768]{2,1,0:T(8,128)(2,1)S(1)} all-to-all(bf16[4,224,768]{2,1,0:T(8,128)(2,1)S(1)} %bitcast.42), channel_id=1, replica_groups=mesh['row'=8,'col'=4] {'col'}, dimensions={0} | all-to-all | bytes 2752512 | tf_op jit(solution)/shard_map/all_to_all | solution.py:321
  704.9 12.5 %shard_map.33 = bf16[896,512]{1,0:T(8,128)(2,1)S(1)} custom-call(s32[1]{0:T(128)} %bitcast.me_ref, bf16[8,896,896]{2,1,0:T(8,128)(2,1)} %shard_map.27.refs_0_, bf16[7168,512]{1,0:T(8,128)(2,1)} %all-gather.8.cloned.1.call-done.refs_1_, bf16[896,512]{1,0:T(8,128)(2,1)} %bitcast.7.refs_2_.refs_1_, bf16[896,512]{1,0:T(8,128)(2,1)S(1)} %copy-done.8, ...), custom_call_target="tpu_custom_call" | custom-call | flops 6576668672 | bytes 20185088 | tf_op jit(solution)/shard_map/pallas_call | solution.py:223
  717.5 24.8 %all_to_all.89 = bf16[4,224,512]{2,1,0:T(8,128)(2,1)S(1)} all-to-all(bf16[4,224,512]{2,1,0:T(8,128)(2,1)S(1)} %bitcast.43), channel_id=1, replica_groups=mesh['row'=8,'col'=4] {'col'}, dimensions={0} | all-to-all | bytes 1835008 | tf_op jit(solution)/shard_map/all_to_all | solution.py:321
  742.6 2.5 copy.19
  (136 shorter events, 29.7 us)
Async XLA Ops:
  9.5 48.9 %all-to-all-start = ((bf16[4,224,1024]{2,1,0:T(8,128)(2,1)}), bf16[4,224,1024]{2,1,0:T(8,128)(2,1)S(1)}, u32[]{:S(2)}, u32[]{:S(2)}) async-start(bf16[4,224,1024]{2,1,0:T(8,128)(2,1)} %bitcast.48), calls=%async_computation | async-start | bytes 3670016 | tf_op jit(solution)/shard_map/all_to_all | solution.py:260
  58.4 50.6 %copy-start.2 = (bf16[4,224,1024]{2,1,0:T(8,128)(2,1)}, bf16[4,224,1024]{2,1,0:T(8,128)(2,1)S(1)}, u32[]{:S(2)}) copy-start(bf16[4,224,1024]{2,1,0:T(8,128)(2,1)S(1)} %all-to-all-done) | copy-start | bytes 5505028
  58.4 45.9 %all-to-all-start.1 = ((bf16[4,224,768]{2,1,0:T(8,128)(2,1)}), bf16[4,224,768]{2,1,0:T(8,128)(2,1)S(1)}, u32[]{:S(2)}, u32[]{:S(2)}) async-start(bf16[4,224,768]{2,1,0:T(8,128)(2,1)} %bitcast.49), calls=%async_computation.1 | async-start | bytes 2752512 | tf_op jit(solution)/shard_map/all_to_all | solution.py:260
  61.9 41.0 %collective-permute-start = (bf16[896,1024]{1,0:T(8,128)(2,1)S(1)}, bf16[896,1024]{1,0:T(8,128)(2,1)S(1)}, u32[]{:S(2)}, u32[]{:S(2)}) collective-permute-start(bf16[896,1024]{1,0:T(8,128)(2,1)S(1)} %bitcast.23), channel_id=1, source_target_pairs={{0,8},{4,12},{8,0},{12,4},{16,24},{20,28},{24,16},{28,20},{1,9},{5... | collective-permute-start | bytes 5505032 | tf_op jit(solution)/shard_map/ppermute | solution.py:35
  63.5 40.8 %collective-permute-start.1 = (bf16[896,1024]{1,0:T(8,128)(2,1)S(1)}, bf16[896,1024]{1,0:T(8,128)(2,1)}, u32[]{:S(2)}, u32[]{:S(2)}) collective-permute-start(bf16[896,1024]{1,0:T(8,128)(2,1)S(1)} %bitcast.24), channel_id=1, source_target_pairs={{0,16},{4,20},{8,24},{12,28},{16,0},{20,4},{24,8},{28,12},{1,17},{... | collective-permute-start | bytes 5505032 | tf_op jit(solution)/shard_map/ppermute | solution.py:35
  103.0 1.3 copy-start.26
  104.3 189.8 %copy-start.4 = (bf16[4,224,768]{2,1,0:T(8,128)(2,1)}, bf16[4,224,768]{2,1,0:T(8,128)(2,1)S(1)}, u32[]{:S(2)}) copy-start(bf16[4,224,768]{2,1,0:T(8,128)(2,1)S(1)} %all-to-all-done.1) | copy-start | bytes 4128772
  104.3 25.9 %all-to-all-start.2 = ((bf16[4,224,512]{2,1,0:T(8,128)(2,1)}), bf16[4,224,512]{2,1,0:T(8,128)(2,1)}, u32[]{:S(2)}, u32[]{:S(2)}) async-start(bf16[4,224,512]{2,1,0:T(8,128)(2,1)} %bitcast.50), calls=%async_computation.2 | async-start | bytes 1835008 | tf_op jit(solution)/shard_map/all_to_all | solution.py:260
  109.0 131.7 %all-reduce.4.cloned.1.call-start = ((), (), s32[]{:S(2)}) async-start(), calls=%async_computation.6 | async-start | bytes 4816896 | tf_op jit(solution)/shard_map/psum | solution.py:286
  109.0 21.1 %collective-permute-start.2 = (bf16[896,1024]{1,0:T(8,128)(2,1)S(1)}, bf16[896,1024]{1,0:T(8,128)(2,1)}, u32[]{:S(2)}, u32[]{:S(2)}) collective-permute-start(bf16[896,1024]{1,0:T(8,128)(2,1)S(1)} %bitcast.25), channel_id=1, source_target_pairs={{0,4},{4,0},{8,12},{12,8},{16,20},{20,16},{24,28},{28,24},{1,5},{5... | collective-permute-start | bytes 5505032 | tf_op jit(solution)/shard_map/ppermute | solution.py:35
  109.1 21.1 %collective-permute-start.3 = (bf16[896,768]{1,0:T(8,128)(2,1)S(1)}, bf16[896,768]{1,0:T(8,128)(2,1)}, u32[]{:S(2)}, u32[]{:S(2)}) collective-permute-start(bf16[896,768]{1,0:T(8,128)(2,1)S(1)} %bitcast.31), channel_id=1, source_target_pairs={{0,4},{4,0},{8,12},{12,8},{16,20},{20,16},{24,28},{28,24},{1,5},{5... | collective-permute-start | bytes 4128776 | tf_op jit(solution)/shard_map/ppermute | solution.py:35
  130.2 2.8 collective-permute-start.4
  144.2 221.3 %all-reduce.6.cloned.1.call-start = ((), (), s32[]{:S(2)}) async-start(), calls=%async_computation.7 | async-start | bytes 6422528 | tf_op jit(solution)/shard_map/psum | solution.py:304
  144.2 33.2 %collective-permute-start.7 = (bf16[896,768]{1,0:T(8,128)(2,1)S(1)}, bf16[896,768]{1,0:T(8,128)(2,1)}, u32[]{:S(2)}, u32[]{:S(2)}) collective-permute-start(bf16[896,768]{1,0:T(8,128)(2,1)S(1)} %bitcast.33), channel_id=1, source_target_pairs={{0,8},{4,12},{8,0},{12,4},{16,24},{20,28},{24,16},{28,20},{1,9},{5... | collective-permute-start | bytes 4128776 | tf_op jit(solution)/shard_map/ppermute | solution.py:35
  145.8 33.2 %collective-permute-start.8 = (bf16[896,768]{1,0:T(8,128)(2,1)S(1)}, bf16[896,768]{1,0:T(8,128)(2,1)}, u32[]{:S(2)}, u32[]{:S(2)}) collective-permute-start(bf16[896,768]{1,0:T(8,128)(2,1)S(1)} %bitcast.34), channel_id=1, source_target_pairs={{0,16},{4,20},{8,24},{12,28},{16,0},{20,4},{24,8},{28,12},{1,17},{... | collective-permute-start | bytes 4128776 | tf_op jit(solution)/shard_map/ppermute | solution.py:35
  147.3 48.9 %collective-permute-start.11 = (bf16[896,512]{1,0:T(8,128)(2,1)}, bf16[896,512]{1,0:T(8,128)(2,1)S(1)}, u32[]{:S(2)}, u32[]{:S(2)}) collective-permute-start(bf16[896,512]{1,0:T(8,128)(2,1)} %bitcast.7.refs_2_.refs_1_), channel_id=1, source_target_pairs={{0,8},{4,12},{8,0},{12,4},{16,24},{20,28},{24,16},{28,20},{1,9},{5... | collective-permute-start | bytes 2752520 | tf_op jit(solution)/shard_map/ppermute | solution.py:35
  147.8 49.5 %collective-permute-start.12 = (bf16[896,512]{1,0:T(8,128)(2,1)}, bf16[896,512]{1,0:T(8,128)(2,1)S(1)}, u32[]{:S(2)}, u32[]{:S(2)}) collective-permute-start(bf16[896,512]{1,0:T(8,128)(2,1)} %bitcast.7.refs_2_.refs_1_), channel_id=1, source_target_pairs={{0,16},{4,20},{8,24},{12,28},{16,0},{20,4},{24,8},{28,12},{1,17},{... | collective-permute-start | bytes 2752520 | tf_op jit(solution)/shard_map/ppermute | solution.py:35
  148.3 34.7 %copy-start.27 = (bf16[896,1024]{1,0:T(8,128)(2,1)S(1)}, bf16[896,1024]{1,0:T(8,128)(2,1)}, u32[]{:S(2)}) copy-start(bf16[896,1024]{1,0:T(8,128)(2,1)} %copy-done.26) | copy-start | bytes 5505028
  196.2 19.0 %copy-start.17 = (bf16[896,512]{1,0:T(8,128)(2,1)}, bf16[896,512]{1,0:T(8,128)(2,1)S(1)}, u32[]{:S(2)}) copy-start(bf16[896,512]{1,0:T(8,128)(2,1)S(1)} %collective-permute-done.11.refs_8_.refs_3_) | copy-start | bytes 2752516
  197.4 17.8 %copy-start.19 = (bf16[896,512]{1,0:T(8,128)(2,1)}, bf16[896,512]{1,0:T(8,128)(2,1)S(1)}, u32[]{:S(2)}) copy-start(bf16[896,512]{1,0:T(8,128)(2,1)S(1)} %collective-permute-done.12.refs_11_.refs_5_) | copy-start | bytes 2752516
  215.2 27.2 %copy-start.25 = (bf16[448,1024]{1,0:T(8,128)(2,1)S(1)}, bf16[448,1024]{1,0:T(8,128)(2,1)}, u32[]{:S(2)}) copy-start(bf16[448,1024]{1,0:T(8,128)(2,1)} %slice.84) | copy-start | bytes 2752516
  215.2 29.2 %copy-start.24 = (bf16[448,1024]{1,0:T(8,128)(2,1)S(1)}, bf16[448,1024]{1,0:T(8,128)(2,1)}, u32[]{:S(2)}) copy-start(bf16[448,1024]{1,0:T(8,128)(2,1)} %slice.85) | copy-start | bytes 2752516
  240.7 199.1 %all-reduce.8.cloned.1.call-start = ((), (), s32[]{:S(2)}) async-start(), calls=%async_computation.8 | async-start | bytes 3211264 | tf_op jit(solution)/shard_map/psum | solution.py:304
  240.8 18.6 %collective-permute-start.10 = (bf16[448,768]{1,0:T(8,128)(2,1)}, bf16[448,768]{1,0:T(8,128)(2,1)S(1)}, u32[]{:S(2)}, u32[]{:S(2)}) collective-permute-start(bf16[448,768]{1,0:T(8,128)(2,1)} %slice.87), channel_id=1, source_target_pairs={{0,8},{4,12},{8,0},{12,4},{16,24},{20,28},{24,16},{28,20},{1,9},{5... | collective-permute-start | bytes 2064392 | tf_op jit(solution)/shard_map/ppermute | solution.py:35
  242.3 38.0 %collective-permute-start.5 = (bf16[448,1024]{1,0:T(8,128)(2,1)S(1)}, bf16[448,1024]{1,0:T(8,128)(2,1)}, u32[]{:S(2)}, u32[]{:S(2)}) collective-permute-start(bf16[448,1024]{1,0:T(8,128)(2,1)S(1)} %copy-done.25), channel_id=1, source_target_pairs={{0,16},{4,20},{8,24},{12,28},{16,0},{20,4},{24,8},{28,12},{1,17},{... | collective-permute-start | bytes 2752520 | tf_op jit(solution)/shard_map/ppermute | solution.py:35
  243.8 35.0 %collective-permute-start.9 = (bf16[448,768]{1,0:T(8,128)(2,1)}, bf16[448,768]{1,0:T(8,128)(2,1)S(1)}, u32[]{:S(2)}, u32[]{:S(2)}) collective-permute-start(bf16[448,768]{1,0:T(8,128)(2,1)} %slice.86), channel_id=1, source_target_pairs={{0,16},{4,20},{8,24},{12,28},{16,0},{20,4},{24,8},{28,12},{1,17},{... | collective-permute-start | bytes 2064392 | tf_op jit(solution)/shard_map/ppermute | solution.py:35
  244.4 37.7 %collective-permute-start.6 = (bf16[448,1024]{1,0:T(8,128)(2,1)S(1)}, bf16[448,1024]{1,0:T(8,128)(2,1)}, u32[]{:S(2)}, u32[]{:S(2)}) collective-permute-start(bf16[448,1024]{1,0:T(8,128)(2,1)S(1)} %copy-done.24), channel_id=1, source_target_pairs={{0,8},{4,12},{8,0},{12,4},{16,24},{20,28},{24,16},{28,20},{1,9},{5... | collective-permute-start | bytes 2752520 | tf_op jit(solution)/shard_map/ppermute | solution.py:35
  244.9 127.4 %collective-permute-start.15 = (bf16[896,1024]{1,0:T(8,128)(2,1)}, bf16[896,1024]{1,0:T(8,128)(2,1)}, u32[]{:S(2)}, u32[]{:S(2)}) collective-permute-start(bf16[896,1024]{1,0:T(8,128)(2,1)} %copy-done.26), channel_id=1, source_target_pairs={{0,4},{4,0},{8,12},{12,8},{16,20},{20,16},{24,28},{28,24},{1,5},{5... | collective-permute-start | bytes 5505032 | tf_op jit(solution)/shard_map/ppermute | solution.py:35
  259.4 21.5 %copy-start.9 = (bf16[448,768]{1,0:T(8,128)(2,1)}, bf16[448,768]{1,0:T(8,128)(2,1)S(1)}, u32[]{:S(2)}) copy-start(bf16[448,768]{1,0:T(8,128)(2,1)S(1)} %collective-permute-done.10.refs_8_) | copy-start | bytes 2064388
  259.4 112.9 %collective-permute-start.16 = (bf16[896,1024]{1,0:T(8,128)(2,1)}, bf16[896,1024]{1,0:T(8,128)(2,1)}, u32[]{:S(2)}, u32[]{:S(2)}) collective-permute-start(bf16[896,1024]{1,0:T(8,128)(2,1)} %collective-permute-done.1.refs_9_.refs_5_), channel_id=1, source_target_pairs={{0,4},{4,0},{8,12},{12,8},{16,20},{20,16},{24,28},{28,24},{1,5},{5... | collective-permute-start | bytes 5505032 | tf_op jit(solution)/shard_map/ppermute | solution.py:35
  278.8 3.2 copy-start.11
  278.9 11.3 %collective-permute-start.13 = (bf16[448,512]{1,0:T(8,128)(2,1)}, bf16[448,512]{1,0:T(8,128)(2,1)S(1)}, u32[]{:S(2)}, u32[]{:S(2)}) collective-permute-start(bf16[448,512]{1,0:T(8,128)(2,1)} %slice.88), channel_id=1, source_target_pairs={{0,16},{4,20},{8,24},{12,28},{16,0},{20,4},{24,8},{28,12},{1,17},{... | collective-permute-start | bytes 1376264 | tf_op jit(solution)/shard_map/ppermute | solution.py:35
  280.3 12.9 %collective-permute-start.14 = (bf16[448,512]{1,0:T(8,128)(2,1)}, bf16[448,512]{1,0:T(8,128)(2,1)S(1)}, u32[]{:S(2)}, u32[]{:S(2)}) collective-permute-start(bf16[448,512]{1,0:T(8,128)(2,1)} %slice.89), channel_id=1, source_target_pairs={{0,8},{4,12},{8,0},{12,4},{16,24},{20,28},{24,16},{28,20},{1,9},{5... | collective-permute-start | bytes 1376264 | tf_op jit(solution)/shard_map/ppermute | solution.py:35
  282.1 88.7 %collective-permute-start.17 = (bf16[448,1024]{1,0:T(8,128)(2,1)}, bf16[448,1024]{1,0:T(8,128)(2,1)}, u32[]{:S(2)}, u32[]{:S(2)}) collective-permute-start(bf16[448,1024]{1,0:T(8,128)(2,1)} %collective-permute-done.5.refs_7_), channel_id=1, source_target_pairs={{0,4},{4,0},{8,12},{12,8},{16,20},{20,16},{24,28},{28,24},{1,5},{5... | collective-permute-start | bytes 2752520 | tf_op jit(solution)/shard_map/ppermute | solution.py:35
  290.2 3.1 copy-start.13
  290.2 82.1 %collective-permute-start.18 = (bf16[448,1024]{1,0:T(8,128)(2,1)}, bf16[448,1024]{1,0:T(8,128)(2,1)}, u32[]{:S(2)}, u32[]{:S(2)}) collective-permute-start(bf16[448,1024]{1,0:T(8,128)(2,1)} %collective-permute-done.6.refs_8_), channel_id=1, source_target_pairs={{0,4},{4,0},{8,12},{12,8},{16,20},{20,16},{24,28},{28,24},{1,5},{5... | collective-permute-start | bytes 2752520 | tf_op jit(solution)/shard_map/ppermute | solution.py:35
  369.4 4.3 copy-start
  369.4 37.1 %collective-permute-start.22 = (bf16[2,448,896]{2,1,0:T(8,128)(2,1)}, bf16[2,448,896]{2,1,0:T(8,128)(2,1)}, u32[]{:S(2)}, u32[]{:S(2)}) collective-permute-start(bf16[2,448,896]{2,1,0:T(8,128)(2,1)} %get-tuple-element.55), channel_id=1, source_target_pairs={{0,8},{4,12},{8,0},{12,4},{16,24},{20,28},{24,16},{28,20},{1,9},{5... | collective-permute-start | bytes 4816904 | tf_op jit(solution)/shard_map/ppermute | solution.py:35
  370.8 40.5 %collective-permute-start.20 = (bf16[2,448,896]{2,1,0:T(8,128)(2,1)}, bf16[2,448,896]{2,1,0:T(8,128)(2,1)}, u32[]{:S(2)}, u32[]{:S(2)}) collective-permute-start(bf16[2,448,896]{2,1,0:T(8,128)(2,1)} %get-tuple-element.56), channel_id=1, source_target_pairs={{0,16},{4,20},{8,24},{12,28},{16,0},{20,4},{24,8},{28,12},{1,17},{... | collective-permute-start | bytes 4816904 | tf_op jit(solution)/shard_map/ppermute | solution.py:35
  372.3 209.3 %all-gather.4.cloned.1.call-start = ((), (), s32[]{:S(2)}) async-start(), calls=%async_computation.9 | async-start | bytes 16515072 | tf_op jit(solution)/shard_map/all_gather | solution.py:318
  373.6 1.8 copy-start.1
  373.6 3.1 collective-permute-start.23
  373.8 35.0 %collective-permute-start.21 = (bf16[1,448,896]{2,1,0:T(8,128)(2,1)S(1)}, bf16[1,448,896]{2,1,0:T(8,128)(2,1)S(1)}, u32[]{:S(2)}, u32[]{:S(2)}) collective-permute-start(bf16[1,448,896]{2,1,0:T(8,128)(2,1)S(1)} %get-tuple-element.57), channel_id=1, source_target_pairs={{0,4},{4,0},{8,12},{12,8},{16,20},{20,16},{24,28},{28,24},{1,5},{5... | collective-permute-start | bytes 2408456 | tf_op jit(solution)/shard_map/ppermute | solution.py:35
  374.4 39.4 %collective-permute-start.19 = (bf16[1,448,896]{2,1,0:T(8,128)(2,1)S(1)}, bf16[1,448,896]{2,1,0:T(8,128)(2,1)S(1)}, u32[]{:S(2)}, u32[]{:S(2)}) collective-permute-start(bf16[1,448,896]{2,1,0:T(8,128)(2,1)S(1)} %get-tuple-element.58), channel_id=1, source_target_pairs={{0,4},{4,0},{8,12},{12,8},{16,20},{20,16},{24,28},{28,24},{1,5},{5... | collective-permute-start | bytes 2408456 | tf_op jit(solution)/shard_map/ppermute | solution.py:35
  439.9 36.8 %copy-start.6 = (bf16[2,448,896]{2,1,0:T(8,128)(2,1)S(1)}, bf16[2,448,896]{2,1,0:T(8,128)(2,1)}, u32[]{:S(2)}) copy-start(bf16[2,448,896]{2,1,0:T(8,128)(2,1)} %all-reduce.8.cloned.1.call-done.mine) | copy-start | bytes 4816900
  439.9 36.8 %collective-permute-start.25 = (bf16[2,448,896]{2,1,0:T(8,128)(2,1)}, bf16[2,448,896]{2,1,0:T(8,128)(2,1)S(1)}, u32[]{:S(2)}, u32[]{:S(2)}) collective-permute-start(bf16[2,448,896]{2,1,0:T(8,128)(2,1)} %all-reduce.8.cloned.1.call-done.mine), channel_id=1, source_target_pairs={{0,24},{4,28},{8,16},{12,20},{16,8},{20,12},{24,0},{28,4},{1,25},{... | collective-permute-start | bytes 4816904 | tf_op jit(solution)/shard_map/ppermute | solution.py:35
  443.5 34.4 %collective-permute-start.24 = (bf16[1,448,896]{2,1,0:T(8,128)(2,1)S(1)}, bf16[1,448,896]{2,1,0:T(8,128)(2,1)S(1)}, u32[]{:S(2)}, u32[]{:S(2)}) collective-permute-start(bf16[1,448,896]{2,1,0:T(8,128)(2,1)S(1)} %slice.95), channel_id=1, source_target_pairs={{0,4},{4,0},{8,12},{12,8},{16,20},{20,16},{24,28},{28,24},{1,5},{5... | collective-permute-start | bytes 2408456 | tf_op jit(solution)/shard_map/ppermute | solution.py:35
  479.2 21.1 %copy-start.12 = (bf16[448,768]{1,0:T(8,128)(2,1)S(1)}, bf16[448,768]{1,0:T(8,128)(2,1)}, u32[]{:S(2)}) copy-start(bf16[448,768]{1,0:T(8,128)(2,1)} %copy-done.11) | copy-start | bytes 2064388
  479.2 21.2 %copy-start.10 = (bf16[448,768]{1,0:T(8,128)(2,1)S(1)}, bf16[448,768]{1,0:T(8,128)(2,1)}, u32[]{:S(2)}) copy-start(bf16[448,768]{1,0:T(8,128)(2,1)} %copy-done.9) | copy-start | bytes 2064388
  499.4 9.7 %copy-start.5 = (bf16[4,224,768]{2,1,0:T(8,128)(2,1)S(1)}, bf16[4,224,768]{2,1,0:T(8,128)(2,1)}, u32[]{:S(2)}) copy-start(bf16[4,224,768]{2,1,0:T(8,128)(2,1)} %copy-done.4) | copy-start | bytes 4128772
  499.4 152.1 %all-gather.6.cloned.1.call-start = ((), (), s32[]{:S(2)}) async-start(), calls=%async_computation.10 | async-start | bytes 12386304 | tf_op jit(solution)/shard_map/all_gather | solution.py:318
  499.8 7.1 collective-permute-start.26
  499.8 7.3 collective-permute-start.27
  500.3 4.6 collective-permute-start.28
  500.4 6.5 collective-permute-start.29
  524.9 56.7 %copy-start.3 = (bf16[4,224,1024]{2,1,0:T(8,128)(2,1)S(1)}, bf16[4,224,1024]{2,1,0:T(8,128)(2,1)}, u32[]{:S(2)}) copy-start(bf16[4,224,1024]{2,1,0:T(8,128)(2,1)} %copy-done.2) | copy-start | bytes 5505028
  525.0 179.6 %all-gather.8.cloned.1.call-start = ((), (), s32[]{:S(2)}) async-start(), calls=%async_computation.11 | async-start | bytes 8257536 | tf_op jit(solution)/shard_map/all_gather | solution.py:318
  525.0 5.4 collective-permute-start.30
  525.2 5.2 collective-permute-start.31
  525.6 4.1 collective-permute-start.32
  525.7 4.7 collective-permute-start.33
  703.3 1.7 copy-start.8
  704.9 37.4 %copy-start.23 = (bf16[4,224,768]{2,1,0:T(8,128)(2,1)S(1)}, bf16[4,224,768]{2,1,0:T(8,128)(2,1)}, u32[]{:S(2)}) copy-start(bf16[4,224,768]{2,1,0:T(8,128)(2,1)} %copy-done.22) | copy-start | bytes 4128772
  717.5 24.8 %copy-start.21 = (bf16[4,224,1024]{2,1,0:T(8,128)(2,1)S(1)}, bf16[4,224,1024]{2,1,0:T(8,128)(2,1)}, u32[]{:S(2)}) copy-start(bf16[4,224,1024]{2,1,0:T(8,128)(2,1)} %copy-done.20) | copy-start | bytes 5505028
  (11 other events, 11.4 us)
Sparse Core Ops, SparseCore 0:
  144.3 96.3 all-reduce.3
  243.2 122.2 all-reduce.5
  372.5 67.3 all-reduce.7
  499.6 82.0 all-gather.3
  583.4 65.4 all-gather.5
  650.7 49.9 all-gather.7

commit v8 on v7

--- a/solution.py
+++ b/solution.py
@@ -43,11 +43,9 @@
     parts = {(0, 0): own}
     parts[(bit_x, 0)] = swap(own, bit_x)
     parts[(bit_y, 0)] = swap(own, bit_y)
-    from_x, from_y = lax.optimization_barrier((parts[(bit_x, 0)], parts[(bit_y, 0)]))
-    upper, lower = lax.optimization_barrier((from_x[:h], from_y[h:]))
-    parts[(corner, 0)] = swap(upper, bit_y)
-    parts[(corner, h)] = swap(lower, bit_x)
-    return parts, (upper, lower)
+    parts[(corner, 0)] = swap(parts[(bit_x, 0)][:h], bit_y)
+    parts[(corner, h)] = swap(parts[(bit_y, 0)][h:], bit_x)
+    return parts
 
 
 def add_cores(parts, hold=None):
@@ -259,21 +257,16 @@
     def exchange(value):
         return lax.all_to_all(value, "col", split_axis=0, concat_axis=0, tiled=True)
 
-    tiles, gathered, siblings, tied = [], [], [], []
+    tiles, siblings = [], []
     start = 0
     thirds = widths_of(width, 3)
     if width % (9 * 256) == 0:
-        thirds = [width // 9 * n for n in (4, 3, 2)]
-    for k, w in enumerate(thirds):
+        thirds = [width // 9 * n for n in (3, 4, 2)]
+    for w in thirds:
         first = [start + c * width for c in range(n_col)]
         part = jnp.concatenate([ortho_in[:, f : f + w] for f in first], axis=0)
-        if k == 2:
-            part = after(part, gathered[0][(bit_x, 0)], gathered[0][(bit_y, 0)])
         tile = exchange(part)
         tiles.append(tile)
-        parts, tie = gather_chips(tile)
-        gathered.append(parts)
-        tied.extend(tie)
         siblings.append(add_cores({(0, 0): tile}))
         start += w
 
@@ -283,6 +276,8 @@
     lefts = [[s[(i, 0)] for s in siblings] for i in range(bit_x)]
     jobs = [(0, 0, None, 0), (0, 0, None, h)] + [(0, j, j - 1, 0) for j in cores]
     near = gram_pieces(lefts, jobs, [low_of(j)[0] for j in cores], scale)
+    gathered = [gather_chips(tile) for tile in tiles[:-1]]
+    gathered.append(gather_chips(after(tiles[-1], near)))
     last = near = lax.psum(near, "col")
     gram = start_gram(near, n_row)
     for j in cores:
@@ -291,28 +286,37 @@
     panels = [
         add_cores({**parts, **sibling}) for parts, sibling in zip(gathered, siblings)
     ]
-    for stage in (chips[:2], chips[2:]):
-        blocks = list(lefts)
-        for j in stage:
-            peers = [whole_block(parts, j) for parts in gathered]
-            if j != chips[-1]:
-                peers[0] = after(peers[0], *tied)
-            blocks.append(peers)
-        jobs = [(i, bit_x + n, n, 0) for n in range(len(stage)) for i in range(bit_x)]
-        pieces = gram_pieces(blocks, jobs, [low_of(j)[0] for j in stage], scale)
-        held = list(panels[0].values()) if len(stage) == 1 else []
-        last = sums = lax.psum(after(pieces, last, *held), "col")
-        if len(stage) == 1:
-            sums, gram = lax.optimization_barrier((sums, gram))
-        for n, j in enumerate(stage):
-            theirs = swap(sums[n * bit_x : (n + 1) * bit_x], j)
-            gram = put_block(gram, low_of(j), (sums, n * bit_x), (theirs, 0), j)
-            for i in cores:
-                mine = swap(sums[n * bit_x + i : n * bit_x + i + 1], i)
-                gram = put_block(gram, low_of(j), (mine, 0), (theirs, i), j | i)
-
-    outs, firsts, backs = [], [], []
-    for k, w in enumerate(thirds):
+    peers = [[whole_block(parts, j) for parts in gathered] for j in chips]
+    lows = [low_of(j)[0] for j in chips]
+
+    def summed(stage, *held):
+        used = sorted({n for n, _ in stage})
+        blocks = lefts + [peers[n] for n in used]
+        jobs = [(i, bit_x + used.index(n), used.index(n), 0) for n, i in stage]
+        pieces = gram_pieces(blocks, jobs, [lows[n] for n in used], scale)
+        return lax.psum(after(pieces, *held), "col")
+
+    def put_stage(gram, stage, sums):
+        for at, (n, i) in enumerate(stage):
+            mine = sums[at : at + 1]
+            theirs = swap(mine, chips[n])
+            if i > 0:
+                mine = swap(mine, i)
+            gram = put_block(gram, low_of(chips[n]), (mine, 0), (theirs, 0), chips[n] | i)
+        return gram
+
+    pairs = [(n, i) for n in range(3) for i in range(bit_x)]
+    final = [(n, bit_x - 1) for n in range(2)]
+    middle = [pair for pair in pairs if pair not in final]
+    last = sums = summed(middle, last)
+    gram = put_stage(gram, middle, sums)
+    sums = summed(final, last, *panels[1].values())
+    sums, gram = lax.optimization_barrier((sums, gram))
+    gram = put_stage(gram, final, sums)
+
+    outs, firsts, backs = {}, [], []
+    for k in (1, 0, 2):
+        w = thirds[k]
         first = product(gram, me, panels[k], 0, w, (), firsts[-1:])
         firsts.append(first)
         first_panel = lax.all_gather(first, "row", axis=0, tiled=True)
@@ -320,8 +324,8 @@
         result = product(gram, me, {None: first_panel}, 0, w, extra, backs[-1:])
         back = lax.all_to_all(result, "col", split_axis=0, concat_axis=1, tiled=True)
         backs.append(back)
-        outs.append(back.reshape(rows, n_col, w))
-    return jnp.concatenate(outs, axis=2).reshape(rows, cols)
+        outs[k] = back.reshape(rows, n_col, w)
+    return jnp.concatenate([outs[k] for k in range(3)], axis=2).reshape(rows, cols)
 
 
 def solution(mesh):

time: 761 us -> 777 us (1.021)
  waiting for transfers between devices: 399 us -> 413 us
    psum x2, waiting for transfers between devices: 84.9 us -> 116 us  [summed(): return lax.psum(after(pieces, *held), 'col')]
    all_to_all x3, waiting for transfers between devices: 60.6 us -> 91.3 us  [exchange(): return lax.all_to_all(value, 'col', split_axis=0, concat_axis=0, tiled=True)]
    psum x1, waiting for transfers between devices: 25.5 us -> 0.01 us  [per_device(): last = near = lax.psum(near, 'col')]
    ppermute x34 -> x37, waiting for transfers between devices: 194 us -> 169 us  [swap(): return lax.ppermute(value, 'row', [(r, r ^ bit) for r in range(count)])]
    ppermute x34 -> x37, starting transfers between devices: 22.2 us -> 28.1 us  [swap(): return lax.ppermute(value, 'row', [(r, r ^ bit) for r in range(count)])]
  transfers between devices with their start and end apart: 43 -> 46, of which waited for: 22 -> 22; matrix products, arithmetic and copies ran while one was open for 3% -> 3% of each run, Pallas kernels for 14% -> 15%
where the time goes in v8:
time: 777 us; the launch traced here: 768 us
  waiting for transfers between devices  413 us (53%)
  Pallas kernels  147 us (19%)
  blocking collectives  107 us (14%)
  starting transfers between devices  42.4 us (5%)
  local copies, waits for them, and re-layouts  33.8 us (4%)
  between operations  14.2 us (2%)
  other arithmetic  10.7 us (1%)
    ppermute x37, waiting for transfers between devices, swap(): return lax.ppermute(value, 'row', [(r, r ^ bit) for r in range(count)])  169 us
    psum x2, waiting for transfers between devices, summed(): return lax.psum(after(pieces, *held), 'col')  116 us
    all_to_all x3, blocking collectives, per_device(): lax.all_to_all(result, 'col', split_axis=0, concat_axis=1, tiled=True)  107 us
    pallas_call x6, Pallas kernels, product(): pl.pallas_call(functools.partial(product_kernel, keys, start, bool(extra)...  97.3 us
    all_to_all x3, waiting for transfers between devices, exchange(): return lax.all_to_all(value, 'col', split_axis=0, concat_axis=0, tiled=True)  91.3 us
    pallas_call x3, Pallas kernels, gram_pieces(): pl.pallas_call(functools.partial(pieces_kernel, count, jobs, scale), out_...  39 us
    all_gather x3, waiting for transfers between devices, per_device(): first_panel = lax.all_gather(first, 'row', axis=0, tiled=True)  36.6 us
    ppermute x37, starting transfers between devices, swap(): return lax.ppermute(value, 'row', [(r, r ^ bit) for r in range(count)])  28.1 us
  transfers between devices with their start and end apart: 46, of which 22 were waited for; matrix products, arithmetic and copies ran while one was open for 3% of the time, Pallas kernels for 15%

profile of v8, /device:TPU:0, one launch (start us, length us, event | category | flops | bytes accessed | tf_op | source)
XLA Modules:
  0.0 768.1 jit_solution(1522519738032166750)
XLA Ops:
  6.5 1.4 fusion.2
  9.1 6.3 all-to-all-start
  15.5 1.6 fusion.1
  17.0 1.4 pad_maximum_fusion
  18.4 29.8 %all-to-all-done = bf16[4,224,768]{2,1,0:T(8,128)(2,1)S(1)} async-done(((bf16[4,224,768]{2,1,0:T(8,128)(2,1)}), bf16[4,224,768]{2,1,0:T(8,128)(2,1)S(1)}, u32[]{:S(2)}, u32[]{:S(2)}) %all-to-all-start) | async-done | bytes 1376288 | tf_op jit(solution)/shard_map/all_to_all | solution.py:258
  48.2 3.6 all-to-all-start.1
  51.8 1.4 fusion
  54.2 39.7 %all-to-all-done.1 = bf16[4,224,1024]{2,1,0:T(8,128)(2,1)S(1)} async-done(((bf16[4,224,1024]{2,1,0:T(8,128)(2,1)}), bf16[4,224,1024]{2,1,0:T(8,128)(2,1)S(1)}, u32[]{:S(2)}, u32[]{:S(2)}) %all-to-all-start.1) | async-done | bytes 1835040 | tf_op jit(solution)/shard_map/all_to_all | solution.py:258
  93.9 4.2 all-to-all-start.2
  98.7 21.8 %all-to-all-done.2 = bf16[4,224,512]{2,1,0:T(8,128)(2,1)} async-done(((bf16[4,224,512]{2,1,0:T(8,128)(2,1)}), bf16[4,224,512]{2,1,0:T(8,128)(2,1)}, u32[]{:S(2)}, u32[]{:S(2)}) %all-to-all-start.2) | async-done | bytes 917536 | tf_op jit(solution)/shard_map/all_to_all | solution.py:258
  120.5 1.5 collective-permute-start.4
  122.0 1.5 collective-permute-start.7
  125.7 1.5 collective-permute-start.3
  128.4 11.0 %shard_map.17 = bf16[3,448,896]{2,1,0:T(8,128)(2,1)} custom-call(s32[1]{0:T(128)} %bitcast.9.low_ref, bf16[896,768]{1,0:T(8,128)(2,1)S(1)} %bitcast.34, bf16[896,1024]{1,0:T(8,128)(2,1)} %bitcast.26, bf16[896,512]{1,0:T(8,128)(2,1)} %bitcast.8.refs_2_.refs_1_, bf16[896,768]{1,0:T(8,128)(2,1)} %collective-permute-done.refs_3_.refs_2_, ...), custom_call_target="tpu_custom_call" | custom-call | flops 5549064192 | bytes 10665984 | tf_op jit(solution)/shard_map/pallas_call | solution.py:101
  140.0 53.8 %collective-permute-done.6.refs_9_.refs_5_ = bf16[896,768]{1,0:T(8,128)(2,1)} collective-permute-done((bf16[896,768]{1,0:T(8,128)(2,1)S(1)}, bf16[896,768]{1,0:T(8,128)(2,1)}, u32[]{:S(2)}, u32[]{:S(2)}) %collective-permute-start.6) | collective-permute-done | bytes 1376288 | tf_op jit(solution)/shard_map/ppermute | solution.py:35
  193.8 1.5 collective-permute-start.8
  197.1 2.2 slice.102
  201.0 1.5 collective-permute-start.12
  202.6 2.0 slice.100
  204.6 8.0 %collective-permute-done.5.refs_8_.refs_3_ = bf16[896,512]{1,0:T(8,128)(2,1)} collective-permute-done((bf16[896,512]{1,0:T(8,128)(2,1)}, bf16[896,512]{1,0:T(8,128)(2,1)}, u32[]{:S(2)}, u32[]{:S(2)}) %collective-permute-start.5) | collective-permute-done | bytes 917536 | tf_op jit(solution)/shard_map/ppermute | solution.py:35
  212.6 1.5 collective-permute-start.9
  214.1 1.8 slice.104
  216.0 1.3 collective-permute-done.8.refs_11_.refs_5_
  217.3 1.5 collective-permute-start.13
  220.6 6.8 collective-permute-done.10.refs_8_
  227.4 1.5 collective-permute-start.14
  228.9 22.8 %collective-permute-done.9.refs_7_ = bf16[448,768]{1,0:T(8,128)(2,1)S(1)} collective-permute-done((bf16[448,768]{1,0:T(8,128)(2,1)}, bf16[448,768]{1,0:T(8,128)(2,1)S(1)}, u32[]{:S(2)}, u32[]{:S(2)}) %collective-permute-start.9) | collective-permute-done | bytes 688160 | tf_op jit(solution)/shard_map/ppermute | solution.py:35
  251.7 2.5 pad_maximum_fusion.3.refs_12_
  254.2 2.9 pad_maximum_fusion.1.refs_13_
  257.1 2.9 collective-permute-done.13.refs_7_
  261.2 17.0 %shard_map.19 = bf16[4,448,896]{2,1,0:T(8,128)(2,1)} custom-call(s32[3]{0:T(128)S(1)} %pad_add_fusion.1.low_ref, bf16[896,768]{1,0:T(8,128)(2,1)S(1)} %bitcast.35, bf16[896,1024]{1,0:T(8,128)(2,1)} %bitcast.27, bf16[896,512]{1,0:T(8,128)(2,1)} %bitcast.8.refs_2_.refs_1_, bf16[896,768]{1,0:T(8,128)(2,1)} %collective-permute-done.refs_3_.refs_2_, ...), custom_call_target="tpu_custom_call" | custom-call | flops 7398752256 | bytes 23855104 | tf_op jit(solution)/shard_map/pallas_call | solution.py:101
  279.5 1.3 copy-done.4
  282.1 11.1 %shard_map.18 = bf16[2,448,896]{2,1,0:T(8,128)(2,1)} custom-call(s32[2]{0:T(128)S(1)} %pad_add_fusion.low_ref, bf16[896,768]{1,0:T(8,128)(2,1)S(1)} %bitcast.36, bf16[896,1024]{1,0:T(8,128)(2,1)} %bitcast.28, bf16[896,512]{1,0:T(8,128)(2,1)} %bitcast.8.refs_2_.refs_1_, bf16[896,768]{1,0:T(8,128)(2,1)} %collective-permute-done.refs_3_.refs_2_, ...), custom_call_target="tpu_custom_call" | custom-call | flops 3699376128 | bytes 18120704 | tf_op jit(solution)/shard_map/pallas_call | solution.py:101
  294.3 105.5 %all-reduce.6.cloned.1.call-done = bf16[4,448,896]{2,1,0:T(8,128)(2,1)} async-done(((bf16[4,448,896]{2,1,0:T(8,128)(2,1)}), bf16[4,448,896]{2,1,0:T(8,128)(2,1)}) %all-reduce.6.cloned.1.call-update) | async-done | bytes 3211280 | tf_op jit(solution)/shard_map/psum | solution.py:297
  399.9 2.1 fusion.3
  402.0 1.5 collective-permute-start.23
  403.6 1.5 collective-permute-start.22
  405.6 2.4 collective-permute-start.20
  410.5 12.3 %collective-permute-done.23.theirs = bf16[1,448,896]{2,1,0:T(8,128)(2,1)S(1)} collective-permute-done((bf16[1,448,896]{2,1,0:T(8,128)(2,1)S(1)}, bf16[1,448,896]{2,1,0:T(8,128)(2,1)S(1)}, u32[]{:S(2)}, u32[]{:S(2)}) %collective-permute-start.23) | collective-permute-done | bytes 802848 | tf_op jit(solution)/shard_map/ppermute | solution.py:35
  424.2 33.1 %collective-permute-done.22.theirs = bf16[1,448,896]{2,1,0:T(8,128)(2,1)S(1)} collective-permute-done((bf16[1,448,896]{2,1,0:T(8,128)(2,1)S(1)}, bf16[1,448,896]{2,1,0:T(8,128)(2,1)S(1)}, u32[]{:S(2)}, u32[]{:S(2)}) %collective-permute-start.22) | collective-permute-done | bytes 802848 | tf_op jit(solution)/shard_map/ppermute | solution.py:35
  457.3 1.3 shard_map.23.gram_in
  458.6 1.3 shard_map.24.gram_in
  461.2 10.2 %all-reduce.8.cloned.1.call-done = bf16[2,448,896]{2,1,0:T(8,128)(2,1)} async-done(((bf16[2,448,896]{2,1,0:T(8,128)(2,1)}), bf16[2,448,896]{2,1,0:T(8,128)(2,1)}) %all-reduce.8.cloned.1.call-update) | async-done | bytes 1605648 | tf_op jit(solution)/shard_map/psum | solution.py:297
  471.4 1.5 fusion.4
  473.0 1.5 collective-permute-start.28
  474.7 1.5 collective-permute-start.26
  476.2 17.1 %collective-permute-done.28.theirs = bf16[1,448,896]{2,1,0:T(8,128)(2,1)S(1)} collective-permute-done((bf16[1,448,896]{2,1,0:T(8,128)(2,1)S(1)}, bf16[1,448,896]{2,1,0:T(8,128)(2,1)S(1)}, u32[]{:S(2)}, u32[]{:S(2)}) %collective-permute-start.28) | collective-permute-done | bytes 802848 | tf_op jit(solution)/shard_map/ppermute | solution.py:35
  493.4 1.3 shard_map.26.gram_in
  494.9 1.6 shard_map.27.refs_0_
  496.5 20.1 %shard_map.28.refs_11_.refs_3_ = bf16[896,1024]{1,0:T(8,128)(2,1)} custom-call(s32[1]{0:T(128)} %bitcast.me_ref, bf16[8,896,896]{2,1,0:T(8,128)(2,1)} %shard_map.27.refs_0_, bf16[896,1024]{1,0:T(8,128)(2,1)} %bitcast.29, bf16[896,1024]{1,0:T(8,128)(2,1)} %collective-permute-done.1.refs_4_.refs_2_, bf16[896,1024]{1,0:T(8,128)(2,1)} %collective-permute-done.4.refs_7_.refs_3_, ...), custom_call_target="tpu_custom_call" | custom-call | flops 13153337344 | bytes 27525120 | tf_op jit(solution)/shard_map/pallas_call | solution.py:221
  517.8 4.1 collective-permute-done.31.refs_9_
  521.9 2.2 collective-permute-done.32.refs_10_
  526.3 15.9 %shard_map.29.refs_3_.refs_11_ = bf16[896,768]{1,0:T(8,128)(2,1)} custom-call(s32[1]{0:T(128)} %bitcast.me_ref, bf16[8,896,896]{2,1,0:T(8,128)(2,1)} %shard_map.27.refs_0_, bf16[896,768]{1,0:T(8,128)(2,1)S(1)} %bitcast.37, bf16[896,768]{1,0:T(8,128)(2,1)} %collective-permute-done.refs_3_.refs_2_, bf16[896,768]{1,0:T(8,128)(2,1)} %collective-permute-done.3.refs_6_.refs_3_, ...), custom_call_target="tpu_custom_call" | custom-call | flops 9865003008 | bytes 23855104 | tf_op jit(solution)/shard_map/pallas_call | solution.py:221
  543.4 1.7 collective-permute-done.33.refs_4_
  545.1 1.3 collective-permute-done.34.refs_6_
  548.9 10.9 %shard_map.32.refs_3_ = bf16[896,512]{1,0:T(8,128)(2,1)S(1)} custom-call(s32[1]{0:T(128)} %bitcast.me_ref, bf16[8,896,896]{2,1,0:T(8,128)(2,1)} %shard_map.27.refs_0_, bf16[896,512]{1,0:T(8,128)(2,1)} %bitcast.8.refs_2_.refs_1_, bf16[896,512]{1,0:T(8,128)(2,1)S(1)} %copy-done.14, bf16[896,512]{1,0:T(8,128)(2,1)} %collective-permute-done.5.refs_8_.refs_3_, ...), custom_call_target="tpu_custom_call" | custom-call | flops 6576668672 | bytes 20185088 | tf_op jit(solution)/shard_map/pallas_call | solution.py:221
  560.8 36.6 %all-gather.6.cloned.1.call-done.refs_1_ = bf16[7168,1024]{1,0:T(8,128)(2,1)} async-done(((bf16[896,1024]{1,0:T(8,128)(2,1)}), bf16[7168,1024]{1,0:T(8,128)(2,1)}) %all-gather.6.cloned.1.call-update) | async-done | bytes 14680080 | tf_op jit(solution)/shard_map/all_gather | solution.py:322
  597.3 21.1 %shard_map.30 = bf16[896,1024]{1,0:T(8,128)(2,1)S(1)} custom-call(s32[1]{0:T(128)} %bitcast.me_ref, bf16[8,896,896]{2,1,0:T(8,128)(2,1)} %shard_map.27.refs_0_, bf16[7168,1024]{1,0:T(8,128)(2,1)} %all-gather.6.cloned.1.call-done.refs_1_, bf16[896,1024]{1,0:T(8,128)(2,1)S(1)} %bitcast.30, bf16[896,1024]{1,0:T(8,128)(2,1)} %shard_map.28.refs_11_.refs_3_), custom_call_target="tpu_custom_call" | custom-call | flops 13153337344 | bytes 27525120 | tf_op jit(solution)/shard_map/pallas_call | solution.py:221
  618.4 47.4 %all_to_all.87 = bf16[4,224,1024]{2,1,0:T(8,128)(2,1)S(1)} all-to-all(bf16[4,224,1024]{2,1,0:T(8,128)(2,1)S(1)} %bitcast.40), channel_id=1, replica_groups=mesh['row'=8,'col'=4] {'col'}, dimensions={0} | all-to-all | bytes 3670016 | tf_op jit(solution)/shard_map/all_to_all | solution.py:325
  667.3 16.8 %shard_map.31 = bf16[896,768]{1,0:T(8,128)(2,1)S(1)} custom-call(s32[1]{0:T(128)} %bitcast.me_ref, bf16[8,896,896]{2,1,0:T(8,128)(2,1)} %shard_map.27.refs_0_, bf16[7168,768]{1,0:T(8,128)(2,1)} %all-gather.4.cloned.1.call-done.refs_1_, bf16[896,768]{1,0:T(8,128)(2,1)S(1)} %bitcast.38, bf16[896,768]{1,0:T(8,128)(2,1)} %shard_map.29.refs_3_.refs_11_, ...), custom_call_target="tpu_custom_call" | custom-call | flops 9865003008 | bytes 23855104 | tf_op jit(solution)/shard_map/pallas_call | solution.py:221
  684.0 34.9 %all_to_all.88 = bf16[4,224,768]{2,1,0:T(8,128)(2,1)S(1)} all-to-all(bf16[4,224,768]{2,1,0:T(8,128)(2,1)S(1)} %bitcast.42), channel_id=1, replica_groups=mesh['row'=8,'col'=4] {'col'}, dimensions={0} | all-to-all | bytes 2752512 | tf_op jit(solution)/shard_map/all_to_all | solution.py:325
  720.6 12.5 %shard_map.33 = bf16[896,512]{1,0:T(8,128)(2,1)S(1)} custom-call(s32[1]{0:T(128)} %bitcast.me_ref, bf16[8,896,896]{2,1,0:T(8,128)(2,1)} %shard_map.27.refs_0_, bf16[7168,512]{1,0:T(8,128)(2,1)} %all-gather.8.cloned.1.call-done.refs_1_, bf16[896,512]{1,0:T(8,128)(2,1)} %bitcast.8.refs_2_.refs_1_, bf16[896,512]{1,0:T(8,128)(2,1)S(1)} %copy-done.9, ...), custom_call_target="tpu_custom_call" | custom-call | flops 6576668672 | bytes 20185088 | tf_op jit(solution)/shard_map/pallas_call | solution.py:221
  733.2 24.8 %all_to_all.89 = bf16[4,224,512]{2,1,0:T(8,128)(2,1)S(1)} all-to-all(bf16[4,224,512]{2,1,0:T(8,128)(2,1)S(1)} %bitcast.43), channel_id=1, replica_groups=mesh['row'=8,'col'=4] {'col'}, dimensions={0} | all-to-all | bytes 1835008 | tf_op jit(solution)/shard_map/all_to_all | solution.py:325
  758.3 2.5 copy.19
  (128 shorter events, 34.6 us)
Async XLA Ops:
  9.1 39.1 %all-to-all-start = ((bf16[4,224,768]{2,1,0:T(8,128)(2,1)}), bf16[4,224,768]{2,1,0:T(8,128)(2,1)S(1)}, u32[]{:S(2)}, u32[]{:S(2)}) async-start(bf16[4,224,768]{2,1,0:T(8,128)(2,1)} %bitcast.3), calls=%async_computation | async-start | bytes 2752512 | tf_op jit(solution)/shard_map/all_to_all | solution.py:258
  48.2 213.0 %copy-start.3 = (bf16[4,224,768]{2,1,0:T(8,128)(2,1)}, bf16[4,224,768]{2,1,0:T(8,128)(2,1)S(1)}, u32[]{:S(2)}) copy-start(bf16[4,224,768]{2,1,0:T(8,128)(2,1)S(1)} %all-to-all-done) | copy-start | bytes 4128772
  48.2 45.6 %all-to-all-start.1 = ((bf16[4,224,1024]{2,1,0:T(8,128)(2,1)}), bf16[4,224,1024]{2,1,0:T(8,128)(2,1)S(1)}, u32[]{:S(2)}, u32[]{:S(2)}) async-start(bf16[4,224,1024]{2,1,0:T(8,128)(2,1)} %bitcast.48), calls=%async_computation.1 | async-start | bytes 3670016 | tf_op jit(solution)/shard_map/all_to_all | solution.py:258
  93.8 33.4 %copy-start.1 = (bf16[4,224,1024]{2,1,0:T(8,128)(2,1)}, bf16[4,224,1024]{2,1,0:T(8,128)(2,1)S(1)}, u32[]{:S(2)}) copy-start(bf16[4,224,1024]{2,1,0:T(8,128)(2,1)S(1)} %all-to-all-done.1) | copy-start | bytes 5505028
  93.9 26.7 %all-to-all-start.2 = ((bf16[4,224,512]{2,1,0:T(8,128)(2,1)}), bf16[4,224,512]{2,1,0:T(8,128)(2,1)}, u32[]{:S(2)}, u32[]{:S(2)}) async-start(bf16[4,224,512]{2,1,0:T(8,128)(2,1)} %bitcast.49), calls=%async_computation.2 | async-start | bytes 1835008 | tf_op jit(solution)/shard_map/all_to_all | solution.py:258
  98.1 180.2 %all-reduce.4.cloned.1.call-start = ((), (), s32[]{:S(2)}) async-start(), calls=%async_computation.6 | async-start | bytes 4816896 | tf_op jit(solution)/shard_map/psum | solution.py:281
  98.1 29.1 %collective-permute-start.1 = (bf16[896,1024]{1,0:T(8,128)(2,1)S(1)}, bf16[896,1024]{1,0:T(8,128)(2,1)}, u32[]{:S(2)}, u32[]{:S(2)}) collective-permute-start(bf16[896,1024]{1,0:T(8,128)(2,1)S(1)} %bitcast.23), channel_id=1, source_target_pairs={{0,4},{4,0},{8,12},{12,8},{16,20},{20,16},{24,28},{28,24},{1,5},{5... | collective-permute-start | bytes 5505032 | tf_op jit(solution)/shard_map/ppermute | solution.py:35
  98.2 27.5 %collective-permute-start = (bf16[896,768]{1,0:T(8,128)(2,1)S(1)}, bf16[896,768]{1,0:T(8,128)(2,1)}, u32[]{:S(2)}, u32[]{:S(2)}) collective-permute-start(bf16[896,768]{1,0:T(8,128)(2,1)S(1)} %bitcast.31), channel_id=1, source_target_pairs={{0,4},{4,0},{8,12},{12,8},{16,20},{20,16},{24,28},{28,24},{1,5},{5... | collective-permute-start | bytes 4128776 | tf_op jit(solution)/shard_map/ppermute | solution.py:35
  120.5 3.0 collective-permute-start.2
  120.5 75.9 %collective-permute-start.4 = (bf16[896,1024]{1,0:T(8,128)(2,1)S(1)}, bf16[896,1024]{1,0:T(8,128)(2,1)}, u32[]{:S(2)}, u32[]{:S(2)}) collective-permute-start(bf16[896,1024]{1,0:T(8,128)(2,1)S(1)} %bitcast.24), channel_id=1, source_target_pairs={{0,8},{4,12},{8,0},{12,4},{16,24},{20,28},{24,16},{28,20},{1,9},{5... | collective-permute-start | bytes 5505032 | tf_op jit(solution)/shard_map/ppermute | solution.py:35
  122.0 77.2 %collective-permute-start.7 = (bf16[896,1024]{1,0:T(8,128)(2,1)S(1)}, bf16[896,1024]{1,0:T(8,128)(2,1)}, u32[]{:S(2)}, u32[]{:S(2)}) collective-permute-start(bf16[896,1024]{1,0:T(8,128)(2,1)S(1)} %bitcast.25), channel_id=1, source_target_pairs={{0,16},{4,20},{8,24},{12,28},{16,0},{20,4},{24,8},{28,12},{1,17},{... | collective-permute-start | bytes 5505032 | tf_op jit(solution)/shard_map/ppermute | solution.py:35
  124.5 69.2 %collective-permute-start.6 = (bf16[896,768]{1,0:T(8,128)(2,1)S(1)}, bf16[896,768]{1,0:T(8,128)(2,1)}, u32[]{:S(2)}, u32[]{:S(2)}) collective-permute-start(bf16[896,768]{1,0:T(8,128)(2,1)S(1)} %bitcast.32), channel_id=1, source_target_pairs={{0,16},{4,20},{8,24},{12,28},{16,0},{20,4},{24,8},{28,12},{1,17},{... | collective-permute-start | bytes 4128776 | tf_op jit(solution)/shard_map/ppermute | solution.py:35
  125.7 75.3 %collective-permute-start.3 = (bf16[896,768]{1,0:T(8,128)(2,1)S(1)}, bf16[896,768]{1,0:T(8,128)(2,1)}, u32[]{:S(2)}, u32[]{:S(2)}) collective-permute-start(bf16[896,768]{1,0:T(8,128)(2,1)S(1)} %bitcast.33), channel_id=1, source_target_pairs={{0,8},{4,12},{8,0},{12,4},{16,24},{20,28},{24,16},{28,20},{1,9},{5... | collective-permute-start | bytes 4128776 | tf_op jit(solution)/shard_map/ppermute | solution.py:35
  127.2 1.2 copy-start.11
  139.4 73.2 %collective-permute-start.5 = (bf16[896,512]{1,0:T(8,128)(2,1)}, bf16[896,512]{1,0:T(8,128)(2,1)}, u32[]{:S(2)}, u32[]{:S(2)}) collective-permute-start(bf16[896,512]{1,0:T(8,128)(2,1)} %bitcast.8.refs_2_.refs_1_), channel_id=1, source_target_pairs={{0,8},{4,12},{8,0},{12,4},{16,24},{20,28},{24,16},{28,20},{1,9},{5... | collective-permute-start | bytes 2752520 | tf_op jit(solution)/shard_map/ppermute | solution.py:35
  139.9 259.9 %all-reduce.6.cloned.1.call-start = ((), (), s32[]{:S(2)}) async-start(), calls=%async_computation.7 | async-start | bytes 6422528 | tf_op jit(solution)/shard_map/psum | solution.py:297
  193.8 23.5 %collective-permute-start.8 = (bf16[896,512]{1,0:T(8,128)(2,1)}, bf16[896,512]{1,0:T(8,128)(2,1)S(1)}, u32[]{:S(2)}, u32[]{:S(2)}) collective-permute-start(bf16[896,512]{1,0:T(8,128)(2,1)} %bitcast.8.refs_2_.refs_1_), channel_id=1, source_target_pairs={{0,16},{4,20},{8,24},{12,28},{16,0},{20,4},{24,8},{28,12},{1,17},{... | collective-permute-start | bytes 2752520 | tf_op jit(solution)/shard_map/ppermute | solution.py:35
  196.5 30.9 %collective-permute-start.10 = (bf16[448,768]{1,0:T(8,128)(2,1)S(1)}, bf16[448,768]{1,0:T(8,128)(2,1)}, u32[]{:S(2)}, u32[]{:S(2)}) collective-permute-start(bf16[448,768]{1,0:T(8,128)(2,1)S(1)} %slice.101), channel_id=1, source_target_pairs={{0,8},{4,12},{8,0},{12,4},{16,24},{20,28},{24,16},{28,20},{1,9},{5... | collective-permute-start | bytes 2064392 | tf_op jit(solution)/shard_map/ppermute | solution.py:35
  199.2 55.0 %collective-permute-start.11 = (bf16[448,1024]{1,0:T(8,128)(2,1)}, bf16[448,1024]{1,0:T(8,128)(2,1)}, u32[]{:S(2)}, u32[]{:S(2)}) collective-permute-start(bf16[448,1024]{1,0:T(8,128)(2,1)} %slice.102), channel_id=1, source_target_pairs={{0,16},{4,20},{8,24},{12,28},{16,0},{20,4},{24,8},{28,12},{1,17},{... | collective-permute-start | bytes 2752520 | tf_op jit(solution)/shard_map/ppermute | solution.py:35
  201.0 53.2 %collective-permute-start.12 = (bf16[448,1024]{1,0:T(8,128)(2,1)S(1)}, bf16[448,1024]{1,0:T(8,128)(2,1)}, u32[]{:S(2)}, u32[]{:S(2)}) collective-permute-start(bf16[448,1024]{1,0:T(8,128)(2,1)S(1)} %slice.103), channel_id=1, source_target_pairs={{0,8},{4,12},{8,0},{12,4},{16,24},{20,28},{24,16},{28,20},{1,9},{5... | collective-permute-start | bytes 2752520 | tf_op jit(solution)/shard_map/ppermute | solution.py:35
  212.6 39.1 %collective-permute-start.9 = (bf16[448,768]{1,0:T(8,128)(2,1)}, bf16[448,768]{1,0:T(8,128)(2,1)S(1)}, u32[]{:S(2)}, u32[]{:S(2)}) collective-permute-start(bf16[448,768]{1,0:T(8,128)(2,1)} %slice.100), channel_id=1, source_target_pairs={{0,16},{4,20},{8,24},{12,28},{16,0},{20,4},{24,8},{28,12},{1,17},{... | collective-permute-start | bytes 2064392 | tf_op jit(solution)/shard_map/ppermute | solution.py:35
  217.3 42.7 %collective-permute-start.13 = (bf16[448,512]{1,0:T(8,128)(2,1)}, bf16[448,512]{1,0:T(8,128)(2,1)}, u32[]{:S(2)}, u32[]{:S(2)}) collective-permute-start(bf16[448,512]{1,0:T(8,128)(2,1)} %slice.104), channel_id=1, source_target_pairs={{0,16},{4,20},{8,24},{12,28},{16,0},{20,4},{24,8},{28,12},{1,17},{... | collective-permute-start | bytes 1376264 | tf_op jit(solution)/shard_map/ppermute | solution.py:35
  227.4 32.6 %collective-permute-start.14 = (bf16[448,512]{1,0:T(8,128)(2,1)}, bf16[448,512]{1,0:T(8,128)(2,1)}, u32[]{:S(2)}, u32[]{:S(2)}) collective-permute-start(bf16[448,512]{1,0:T(8,128)(2,1)} %slice.105), channel_id=1, source_target_pairs={{0,8},{4,12},{8,0},{12,4},{16,24},{20,28},{24,16},{28,20},{1,9},{5... | collective-permute-start | bytes 1376264 | tf_op jit(solution)/shard_map/ppermute | solution.py:35
  251.7 5.4 copy-start.15
  257.1 4.1 copy-start.7
  257.1 4.1 copy-start.12
  278.3 193.2 %all-reduce.8.cloned.1.call-start = ((), (), s32[]{:S(2)}) async-start(), calls=%async_computation.8 | async-start | bytes 3211264 | tf_op jit(solution)/shard_map/psum | solution.py:297
  278.3 16.0 %collective-permute-start.15 = (bf16[896,1024]{1,0:T(8,128)(2,1)}, bf16[896,1024]{1,0:T(8,128)(2,1)}, u32[]{:S(2)}, u32[]{:S(2)}) collective-permute-start(bf16[896,1024]{1,0:T(8,128)(2,1)} %collective-permute-done.4.refs_7_.refs_3_), channel_id=1, source_target_pairs={{0,4},{4,0},{8,12},{12,8},{16,20},{20,16},{24,28},{28,24},{1,5},{5... | collective-permute-start | bytes 5505032 | tf_op jit(solution)/shard_map/ppermute | solution.py:35
  278.4 15.9 %collective-permute-start.16 = (bf16[896,1024]{1,0:T(8,128)(2,1)}, bf16[896,1024]{1,0:T(8,128)(2,1)}, u32[]{:S(2)}, u32[]{:S(2)}) collective-permute-start(bf16[896,1024]{1,0:T(8,128)(2,1)} %collective-permute-done.7.refs_10_.refs_5_), channel_id=1, source_target_pairs={{0,4},{4,0},{8,12},{12,8},{16,20},{20,16},{24,28},{28,24},{1,5},{5... | collective-permute-start | bytes 5505032 | tf_op jit(solution)/shard_map/ppermute | solution.py:35
  278.9 15.4 %collective-permute-start.17 = (bf16[448,1024]{1,0:T(8,128)(2,1)}, bf16[448,1024]{1,0:T(8,128)(2,1)}, u32[]{:S(2)}, u32[]{:S(2)}) collective-permute-start(bf16[448,1024]{1,0:T(8,128)(2,1)} %collective-permute-done.11.refs_7_), channel_id=1, source_target_pairs={{0,4},{4,0},{8,12},{12,8},{16,20},{20,16},{24,28},{28,24},{1,5},{5... | collective-permute-start | bytes 2752520 | tf_op jit(solution)/shard_map/ppermute | solution.py:35
  279.0 15.3 %collective-permute-start.18 = (bf16[448,1024]{1,0:T(8,128)(2,1)}, bf16[448,1024]{1,0:T(8,128)(2,1)}, u32[]{:S(2)}, u32[]{:S(2)}) collective-permute-start(bf16[448,1024]{1,0:T(8,128)(2,1)} %collective-permute-done.12.refs_8_), channel_id=1, source_target_pairs={{0,4},{4,0},{8,12},{12,8},{16,20},{20,16},{24,28},{28,24},{1,5},{5... | collective-permute-start | bytes 2752520 | tf_op jit(solution)/shard_map/ppermute | solution.py:35
  279.5 1.3 copy-start.4
  280.8 1.3 copy-start.13
  282.1 11.1 %copy-start = (bf16[3,448,896]{2,1,0:T(8,128)(2,1)S(1)}, bf16[3,448,896]{2,1,0:T(8,128)(2,1)}, u32[]{:S(2)}) copy-start(bf16[3,448,896]{2,1,0:T(8,128)(2,1)} %all-reduce.4.cloned.1.call-done.halves.mine) | copy-start | bytes 7225348
  294.1 111.4 %collective-permute-start.24 = (bf16[1,448,896]{2,1,0:T(8,128)(2,1)}, bf16[1,448,896]{2,1,0:T(8,128)(2,1)S(1)}, u32[]{:S(2)}, u32[]{:S(2)}) collective-permute-start(bf16[1,448,896]{2,1,0:T(8,128)(2,1)} %slice.110), channel_id=1, source_target_pairs={{0,4},{4,0},{8,12},{12,8},{16,20},{20,16},{24,28},{28,24},{1,5},{5... | collective-permute-start | bytes 2408456 | tf_op jit(solution)/shard_map/ppermute | solution.py:35
  399.8 197.5 %all-gather.6.cloned.1.call-start = ((), (), s32[]{:S(2)}) async-start(), calls=%async_computation.10 | async-start | bytes 16515072 | tf_op jit(solution)/shard_map/all_gather | solution.py:322
  402.0 20.9 %collective-permute-start.23 = (bf16[1,448,896]{2,1,0:T(8,128)(2,1)S(1)}, bf16[1,448,896]{2,1,0:T(8,128)(2,1)S(1)}, u32[]{:S(2)}, u32[]{:S(2)}) collective-permute-start(bf16[1,448,896]{2,1,0:T(8,128)(2,1)S(1)} %get-tuple-element.27.mine), channel_id=1, source_target_pairs={{0,8},{4,12},{8,0},{12,4},{16,24},{20,28},{24,16},{28,20},{1,9},{5... | collective-permute-start | bytes 2408456 | tf_op jit(solution)/shard_map/ppermute | solution.py:35
  403.6 53.7 %collective-permute-start.22 = (bf16[1,448,896]{2,1,0:T(8,128)(2,1)S(1)}, bf16[1,448,896]{2,1,0:T(8,128)(2,1)S(1)}, u32[]{:S(2)}, u32[]{:S(2)}) collective-permute-start(bf16[1,448,896]{2,1,0:T(8,128)(2,1)S(1)} %get-tuple-element.28.mine), channel_id=1, source_target_pairs={{0,16},{4,20},{8,24},{12,28},{16,0},{20,4},{24,8},{28,12},{1,17},{... | collective-permute-start | bytes 2408456 | tf_op jit(solution)/shard_map/ppermute | solution.py:35
  405.0 53.6 %collective-permute-start.21 = (bf16[1,448,896]{2,1,0:T(8,128)(2,1)S(1)}, bf16[1,448,896]{2,1,0:T(8,128)(2,1)S(1)}, u32[]{:S(2)}, u32[]{:S(2)}) collective-permute-start(bf16[1,448,896]{2,1,0:T(8,128)(2,1)S(1)} %get-tuple-element.29.mine), channel_id=1, source_target_pairs={{0,24},{4,28},{8,16},{12,20},{16,8},{20,12},{24,0},{28,4},{1,25},{... | collective-permute-start | bytes 2408456 | tf_op jit(solution)/shard_map/ppermute | solution.py:35
  405.6 54.4 %collective-permute-start.19 = (bf16[1,448,896]{2,1,0:T(8,128)(2,1)S(1)}, bf16[1,448,896]{2,1,0:T(8,128)(2,1)S(1)}, u32[]{:S(2)}, u32[]{:S(2)}) collective-permute-start(bf16[1,448,896]{2,1,0:T(8,128)(2,1)S(1)} %get-tuple-element.30), channel_id=1, source_target_pairs={{0,4},{4,0},{8,12},{12,8},{16,20},{20,16},{24,28},{28,24},{1,5},{5... | collective-permute-start | bytes 2408456 | tf_op jit(solution)/shard_map/ppermute | solution.py:35
  405.6 54.3 %collective-permute-start.20 = (bf16[1,448,896]{2,1,0:T(8,128)(2,1)S(1)}, bf16[1,448,896]{2,1,0:T(8,128)(2,1)S(1)}, u32[]{:S(2)}, u32[]{:S(2)}) collective-permute-start(bf16[1,448,896]{2,1,0:T(8,128)(2,1)S(1)} %get-tuple-element.30), channel_id=1, source_target_pairs={{0,24},{4,28},{8,16},{12,20},{16,8},{20,12},{24,0},{28,4},{1,25},{... | collective-permute-start | bytes 2408456 | tf_op jit(solution)/shard_map/ppermute | solution.py:35
  473.0 3.3 collective-permute-start.27
  473.0 20.3 %collective-permute-start.28 = (bf16[1,448,896]{2,1,0:T(8,128)(2,1)S(1)}, bf16[1,448,896]{2,1,0:T(8,128)(2,1)S(1)}, u32[]{:S(2)}, u32[]{:S(2)}) collective-permute-start(bf16[1,448,896]{2,1,0:T(8,128)(2,1)S(1)} %get-tuple-element.31), channel_id=1, source_target_pairs={{0,8},{4,12},{8,0},{12,4},{16,24},{20,28},{24,16},{28,20},{1,9},{5... | collective-permute-start | bytes 2408456 | tf_op jit(solution)/shard_map/ppermute | solution.py:35
  474.6 20.1 %collective-permute-start.25 = (bf16[1,448,896]{2,1,0:T(8,128)(2,1)S(1)}, bf16[1,448,896]{2,1,0:T(8,128)(2,1)S(1)}, u32[]{:S(2)}, u32[]{:S(2)}) collective-permute-start(bf16[1,448,896]{2,1,0:T(8,128)(2,1)S(1)} %get-tuple-element.32), channel_id=1, source_target_pairs={{0,4},{4,0},{8,12},{12,8},{16,20},{20,16},{24,28},{28,24},{1,5},{5... | collective-permute-start | bytes 2408456 | tf_op jit(solution)/shard_map/ppermute | solution.py:35
  474.7 20.1 %collective-permute-start.26 = (bf16[1,448,896]{2,1,0:T(8,128)(2,1)S(1)}, bf16[1,448,896]{2,1,0:T(8,128)(2,1)S(1)}, u32[]{:S(2)}, u32[]{:S(2)}) collective-permute-start(bf16[1,448,896]{2,1,0:T(8,128)(2,1)S(1)} %get-tuple-element.32), channel_id=1, source_target_pairs={{0,16},{4,20},{8,24},{12,28},{16,0},{20,4},{24,8},{28,12},{1,17},{... | collective-permute-start | bytes 2408456 | tf_op jit(solution)/shard_map/ppermute | solution.py:35
  496.5 20.8 %copy-start.16 = (bf16[448,768]{1,0:T(8,128)(2,1)S(1)}, bf16[448,768]{1,0:T(8,128)(2,1)}, u32[]{:S(2)}) copy-start(bf16[448,768]{1,0:T(8,128)(2,1)} %copy-done.15) | copy-start | bytes 2064388
  516.7 9.7 %copy-start.5 = (bf16[4,224,768]{2,1,0:T(8,128)(2,1)S(1)}, bf16[4,224,768]{2,1,0:T(8,128)(2,1)}, u32[]{:S(2)}) copy-start(bf16[4,224,768]{2,1,0:T(8,128)(2,1)} %copy-done.3) | copy-start | bytes 4128772
  516.7 150.6 %all-gather.4.cloned.1.call-start = ((), (), s32[]{:S(2)}) async-start(), calls=%async_computation.9 | async-start | bytes 12386304 | tf_op jit(solution)/shard_map/all_gather | solution.py:322
  516.7 7.3 collective-permute-start.29
  516.8 7.3 collective-permute-start.30
  517.3 4.6 collective-permute-start.31
  517.4 6.7 collective-permute-start.32
  542.3 55.0 %copy-start.2 = (bf16[4,224,1024]{2,1,0:T(8,128)(2,1)S(1)}, bf16[4,224,1024]{2,1,0:T(8,128)(2,1)}, u32[]{:S(2)}) copy-start(bf16[4,224,1024]{2,1,0:T(8,128)(2,1)} %copy-done.1) | copy-start | bytes 5505028
  542.3 178.0 %all-gather.8.cloned.1.call-start = ((), (), s32[]{:S(2)}) async-start(), calls=%async_computation.11 | async-start | bytes 8257536 | tf_op jit(solution)/shard_map/all_gather | solution.py:322
  542.4 2.7 collective-permute-start.33
  542.6 3.9 collective-permute-start.34
  542.9 4.1 collective-permute-start.35
  543.1 4.7 collective-permute-start.36
  545.1 2.6 copy-start.23
  546.4 1.3 copy-start.24
  665.8 1.2 copy-start.17
  718.9 1.7 copy-start.9
  720.6 37.4 %copy-start.20 = (bf16[4,224,768]{2,1,0:T(8,128)(2,1)S(1)}, bf16[4,224,768]{2,1,0:T(8,128)(2,1)}, u32[]{:S(2)}) copy-start(bf16[4,224,768]{2,1,0:T(8,128)(2,1)} %copy-done.19) | copy-start | bytes 4128772
  733.1 24.8 %copy-start.18 = (bf16[4,224,1024]{2,1,0:T(8,128)(2,1)S(1)}, bf16[4,224,1024]{2,1,0:T(8,128)(2,1)}, u32[]{:S(2)}) copy-start(bf16[4,224,1024]{2,1,0:T(8,128)(2,1)} %copy-done.17) | copy-start | bytes 5505028
  (7 other events, 7.5 us)
Sparse Core Ops, SparseCore 0:
  140.0 95.4 all-reduce.3
  278.4 121.3 all-reduce.5
  402.2 69.2 all-reduce.7
  516.8 80.4 all-gather.5
  599.1 65.4 all-gather.3
  666.3 49.9 all-gather.7

commit v9 on v7

--- a/solution.py
+++ b/solution.py
@@ -150,25 +150,88 @@
     )(low, mine, theirs, gram)
 
 
-def own_kernel(halves, out):
-    h = halves.shape[1]
-    out[:h, :] = halves[0]
-    out[h:, :] = halves[1]
-
-
-def start_gram(halves, count):
-    _, h, size = halves.shape
+def split_of(size):
+    top = -(-(size // 2) // 128) * 128
+    return top, size - top
+
+
+def near_kernel(count, scale, low_ref, *refs):
+    out = refs[-1]
+    size = out.shape[1]
+    h = size // 2
+    top, bottom = split_of(size)
+    half = bottom // 2
+
+    def product(left, right, rows, columns):
+        total = None
+        for k in range(count):
+            a = refs[left * count + k][rows[0] : rows[1], :]
+            b = refs[right * count + k][columns[0] : columns[1], :]
+            term = dot_t(a, b)
+            total = term if total is None else total + term
+        return (total * scale).astype(bf16)
+
+    out[:top, :] = product(0, 0, (0, top), (0, size))
+    corner = product(0, 0, (top, size), (top, size))
+    out[top : top + half, :bottom] = corner[:half]
+    out[top : top + half, bottom : 2 * bottom] = corner[half:]
+    out[top : top + half, 2 * bottom :] = jnp.zeros((half, size - 2 * bottom), bf16)
+    for j in range(1, len(refs) // count):
+        start = top + half + (j - 1) * h
+
+        @pl.when(low_ref[j - 1] == 1)
+        def _():
+            out[start : start + h, :] = product(0, j, (0, h), (0, size))
+
+        @pl.when(low_ref[j - 1] == 0)
+        def _():
+            out[start : start + h, :] = product(j, 0, (h, size), (0, size))
+
+
+def near_pieces(blocks, lows, scale):
+    count = len(blocks[0])
+    size = blocks[0][0].shape[0]
+    width = sum(part.shape[1] for part in blocks[0])
+    top, bottom = split_of(size)
+    rows = top + bottom // 2 + (len(blocks) - 1) * (size // 2)
+    return pl.pallas_call(
+        functools.partial(near_kernel, count, scale),
+        out_shape=jax.ShapeDtypeStruct((rows, size), bf16),
+        in_specs=[pl.BlockSpec(memory_space=pltpu.SMEM)]
+        + [pl.BlockSpec(memory_space=pltpu.VMEM)] * (count * len(blocks)),
+        out_specs=pl.BlockSpec(memory_space=pltpu.VMEM),
+        cost_estimate=pl.CostEstimate(
+            flops=2 * rows * size * width,
+            bytes_accessed=2 * size * (len(blocks) * width + rows),
+            transcendentals=0,
+        ),
+        compiler_params=pltpu.CompilerParams(vmem_limit_bytes=VMEM_BYTES),
+    )(jnp.stack(lows).astype(jnp.int32), *[part for block in blocks for part in block])
+
+
+def own_kernel(near, out):
+    size = out.shape[1]
+    top, bottom = split_of(size)
+    half = bottom // 2
+    out[:top, :] = near[:top, :]
+    out[top:, :top] = near[:top, top:].T
+    out[top : top + half, top:] = near[top : top + half, :bottom]
+    out[top + half :, top:] = near[top : top + half, bottom : 2 * bottom]
+
+
+def start_gram(near, count):
+    rows, size = near.shape
     return pl.pallas_call(
         own_kernel,
         grid=(1,),
         out_shape=jax.ShapeDtypeStruct((count, size, size), bf16),
-        in_specs=[pl.BlockSpec((2, h, size), lambda i: (0, 0, 0))],
+        in_specs=[pl.BlockSpec((rows, size), lambda i: (0, 0))],
         out_specs=pl.BlockSpec((None, size, size), lambda i: (0, 0, 0)),
         cost_estimate=pl.CostEstimate(
             flops=0, bytes_accessed=4 * size * size, transcendentals=0
         ),
         compiler_params=pltpu.CompilerParams(vmem_limit_bytes=VMEM_BYTES),
-    )(halves)
+    )(near)
 
 
 def product_kernel(keys, start, finish, n_deps, me_ref, *refs):
@@ -263,7 +326,7 @@
     start = 0
     thirds = widths_of(width, 3)
     if width % (9 * 256) == 0:
-        thirds = [width // 9 * n for n in (4, 3, 2)]
+        thirds = [width // 9 * n for n in (3, 4, 2)]
     for k, w in enumerate(thirds):
         first = [start + c * width for c in range(n_col)]
         part = jnp.concatenate([ortho_in[:, f : f + w] for f in first], axis=0)
@@ -281,13 +344,13 @@
         return ((me & (1 << (j.bit_length() - 1))) == 0).astype(jnp.int32).reshape(1)
 
     lefts = [[s[(i, 0)] for s in siblings] for i in range(bit_x)]
-    jobs = [(0, 0, None, 0), (0, 0, None, h)] + [(0, j, j - 1, 0) for j in cores]
-    near = gram_pieces(lefts, jobs, [low_of(j)[0] for j in cores], scale)
+    near = near_pieces(lefts, [low_of(j)[0] for j in cores], scale)
     last = near = lax.psum(near, "col")
     gram = start_gram(near, n_row)
     for j in cores:
-        theirs = swap(near[1 + j : 2 + j], j)
-        gram = put_block(gram, low_of(j), (near, 1 + j), (theirs, 0), j)
+        start = near.shape[0] - (bit_x - j) * h
+        mine = near[start : start + h][None]
+        gram = put_block(gram, low_of(j), (mine, 0), (swap(mine, j), 0), j)
     panels = [
         add_cores({**parts, **sibling}) for parts, sibling in zip(gathered, siblings)
     ]
@@ -300,7 +363,7 @@
             blocks.append(peers)
         jobs = [(i, bit_x + n, n, 0) for n in range(len(stage)) for i in range(bit_x)]
         pieces = gram_pieces(blocks, jobs, [low_of(j)[0] for j in stage], scale)
-        held = list(panels[0].values()) if len(stage) == 1 else []
+        held = list(panels[1].values()) if len(stage) == 1 else []
         last = sums = lax.psum(after(pieces, last, *held), "col")
         if len(stage) == 1:
             sums, gram = lax.optimization_barrier((sums, gram))
@@ -311,8 +374,9 @@
                 mine = swap(sums[n * bit_x + i : n * bit_x + i + 1], i)
                 gram = put_block(gram, low_of(j), (mine, 0), (theirs, i), j | i)
 
-    outs, firsts, backs = [], [], []
-    for k, w in enumerate(thirds):
+    outs, firsts, backs = {}, [], []
+    for k in (1, 0, 2):
+        w = thirds[k]
         first = product(gram, me, panels[k], 0, w, (), firsts[-1:])
         firsts.append(first)
         first_panel = lax.all_gather(first, "row", axis=0, tiled=True)
@@ -320,8 +384,8 @@
         result = product(gram, me, {None: first_panel}, 0, w, extra, backs[-1:])
         back = lax.all_to_all(result, "col", split_axis=0, concat_axis=1, tiled=True)
         backs.append(back)
-        outs.append(back.reshape(rows, n_col, w))
-    return jnp.concatenate(outs, axis=2).reshape(rows, cols)
+        outs[k] = back.reshape(rows, n_col, w)
+    return jnp.concatenate([outs[k] for k in range(3)], axis=2).reshape(rows, cols)
 
 
 def solution(mesh):

time: 761 us -> 739 us (0.971)
  waiting for transfers between devices: 399 us -> 377 us
    ppermute x34, waiting for transfers between devices: 194 us -> 181 us  [swap(): return lax.ppermute(value, 'row', [(r, r ^ bit) for r in range(count)])]
    psum x1, waiting for transfers between devices: 25.5 us -> 13.8 us  [per_device(): last = near = lax.psum(near, 'col')]
    pallas_call x3 -> x2, Pallas kernels: 37.3 us -> 26.7 us  [gram_pieces(): pl.pallas_call(functools.partial(pieces_kernel, count, jobs, scale), out_...]
    pallas_call x0 -> x1, Pallas kernels: none -> 10.1 us  [near_pieces(): pl.pallas_call(functools.partial(near_kernel, count, scale), out_shape=ja...]
  transfers between devices with their start and end apart: 43 -> 43, of which waited for: 22 -> 23; matrix products, arithmetic and copies ran while one was open for 3% -> 4% of each run, Pallas kernels for 14% -> 16%
where the time goes in v9:
time: 739 us; the launch traced here: 730 us
  waiting for transfers between devices  377 us (51%)
  Pallas kernels  150 us (20%)
  blocking collectives  107 us (14%)
  starting transfers between devices  38.3 us (5%)
  local copies, waits for them, and re-layouts  35.9 us (5%)
  between operations  14.2 us (2%)
  other arithmetic  8.21 us (1%)
    ppermute x34, waiting for transfers between devices, swap(): return lax.ppermute(value, 'row', [(r, r ^ bit) for r in range(count)])  181 us
    all_to_all x3, blocking collectives, per_device(): lax.all_to_all(result, 'col', split_axis=0, concat_axis=1, tiled=True)  107 us
    pallas_call x6, Pallas kernels, product(): pl.pallas_call(functools.partial(product_kernel, keys, start, bool(extra)...  97.3 us
    psum x2, waiting for transfers between devices, per_device(): last = sums = lax.psum(after(pieces, last, *held), 'col')  84.6 us
    all_to_all x3, waiting for transfers between devices, exchange(): return lax.all_to_all(value, 'col', split_axis=0, concat_axis=0, tiled=True)  61.1 us
    all_gather x3, waiting for transfers between devices, per_device(): first_panel = lax.all_gather(first, 'row', axis=0, tiled=True)  35.7 us
    pallas_call x2, Pallas kernels, gram_pieces(): pl.pallas_call(functools.partial(pieces_kernel, count, jobs, scale), out_...  26.7 us
    ppermute x34, starting transfers between devices, swap(): return lax.ppermute(value, 'row', [(r, r ^ bit) for r in range(count)])  23.9 us
  transfers between devices with their start and end apart: 43, of which 23 were waited for; matrix products, arithmetic and copies ran while one was open for 4% of the time, Pallas kernels for 16%

profile of v9, /device:TPU:0, one launch (start us, length us, event | category | flops | bytes accessed | tf_op | source)
XLA Modules:
  0.0 729.8 jit_solution(12787813529769855457)
XLA Ops:
  6.5 1.4 fusion.2
  9.1 6.3 all-to-all-start
  15.4 1.6 fusion.1
  17.0 1.4 pad_maximum_fusion
  18.4 29.8 %all-to-all-done = bf16[4,224,768]{2,1,0:T(8,128)(2,1)S(1)} async-done(((bf16[4,224,768]{2,1,0:T(8,128)(2,1)}), bf16[4,224,768]{2,1,0:T(8,128)(2,1)S(1)}, u32[]{:S(2)}, u32[]{:S(2)}) %all-to-all-start) | async-done | bytes 1376288 | tf_op jit(solution)/shard_map/all_to_all | solution.py:323
  48.2 3.6 all-to-all-start.1
  51.8 1.6 collective-permute-start
  53.3 1.5 collective-permute-start.1
  54.8 1.3 fusion
  57.2 25.8 %collective-permute-done.refs_6_.refs_3_ = bf16[896,768]{1,0:T(8,128)(2,1)S(1)} collective-permute-done((bf16[896,768]{1,0:T(8,128)(2,1)S(1)}, bf16[896,768]{1,0:T(8,128)(2,1)S(1)}, u32[]{:S(2)}, u32[]{:S(2)}) %collective-permute-start) | collective-permute-done | bytes 1376288 | tf_op jit(solution)/shard_map/ppermute | solution.py:35
  84.3 9.5 %all-to-all-done.1 = bf16[4,224,1024]{2,1,0:T(8,128)(2,1)S(1)} async-done(((bf16[4,224,1024]{2,1,0:T(8,128)(2,1)}), bf16[4,224,1024]{2,1,0:T(8,128)(2,1)S(1)}, u32[]{:S(2)}, u32[]{:S(2)}) %all-to-all-start.1) | async-done | bytes 1835040 | tf_op jit(solution)/shard_map/all_to_all | solution.py:323
  93.8 4.2 all-to-all-start.2
  98.7 21.8 %all-to-all-done.2 = bf16[4,224,512]{2,1,0:T(8,128)(2,1)} async-done(((bf16[4,224,512]{2,1,0:T(8,128)(2,1)}), bf16[4,224,512]{2,1,0:T(8,128)(2,1)}, u32[]{:S(2)}, u32[]{:S(2)}) %all-to-all-start.2) | async-done | bytes 917536 | tf_op jit(solution)/shard_map/all_to_all | solution.py:323
  120.5 1.5 collective-permute-start.7
  122.0 1.5 collective-permute-start.8
  123.6 10.1 %shard_map.19 = bf16[1152,896]{1,0:T(8,128)(2,1)} custom-call(s32[1]{0:T(128)} %bitcast.9.low_ref, bf16[896,768]{1,0:T(8,128)(2,1)S(1)} %bitcast.36, bf16[896,1024]{1,0:T(8,128)(2,1)} %bitcast.28, bf16[896,512]{1,0:T(8,128)(2,1)} %bitcast.7.refs_2_.refs_1_, bf16[896,768]{1,0:T(8,128)(2,1)} %collective-permute-done.2.refs_3_.refs_2_, ...), custom_call_target="tpu_custom_call" | custom-call | flops 4756340736 | bytes 10321920 | tf_op jit(solution)/shard_map/pallas_call | solution.py:197
  133.8 1.3 collective-permute-start.11
  135.1 1.5 collective-permute-start.12
  136.7 2.0 slice.84
  138.7 2.0 slice.85
  140.7 22.7 %collective-permute-done.7.refs_7_.refs_3_ = bf16[896,1024]{1,0:T(8,128)(2,1)} collective-permute-done((bf16[896,1024]{1,0:T(8,128)(2,1)S(1)}, bf16[896,1024]{1,0:T(8,128)(2,1)}, u32[]{:S(2)}, u32[]{:S(2)}) %collective-permute-start.7) | collective-permute-done | bytes 1835040 | tf_op jit(solution)/shard_map/ppermute | solution.py:35
  163.4 1.5 collective-permute-done.8.refs_10_.refs_5_
  167.4 15.3 %collective-permute-done.11.refs_8_.refs_3_ = bf16[896,512]{1,0:T(8,128)(2,1)} collective-permute-done((bf16[896,512]{1,0:T(8,128)(2,1)}, bf16[896,512]{1,0:T(8,128)(2,1)}, u32[]{:S(2)}, u32[]{:S(2)}) %collective-permute-start.11) | collective-permute-done | bytes 917536 | tf_op jit(solution)/shard_map/ppermute | solution.py:35
  183.9 1.8 slice.88
  185.7 1.8 slice.89
  187.6 16.6 %shard_map.18 = bf16[4,448,896]{2,1,0:T(8,128)(2,1)} custom-call(s32[2]{0:T(128)S(1)} %pad_add_fusion.low_ref, bf16[896,768]{1,0:T(8,128)(2,1)S(1)} %bitcast.37, bf16[896,1024]{1,0:T(8,128)(2,1)} %bitcast.29, bf16[896,512]{1,0:T(8,128)(2,1)} %bitcast.7.refs_2_.refs_1_, bf16[896,768]{1,0:T(8,128)(2,1)} %collective-permute-done.2.refs_3_.refs_2_, ...), custom_call_target="tpu_custom_call" | custom-call | flops 7398752256 | bytes 19726336 | tf_op jit(solution)/shard_map/pallas_call | solution.py:103
  204.2 13.8 %all-reduce.4.cloned.1.call-done.near = bf16[1152,896]{1,0:T(8,128)(2,1)} async-done(((bf16[1152,896]{1,0:T(8,128)(2,1)}), bf16[1152,896]{1,0:T(8,128)(2,1)}) %all-reduce.4.cloned.1.call-update) | async-done | bytes 2064400 | tf_op jit(solution)/shard_map/psum | solution.py:348
  218.0 1.6 collective-permute-start.5
  219.6 1.4 collective-permute-start.10
  222.2 14.5 %collective-permute-done.5.refs_7_ = bf16[448,768]{1,0:T(8,128)(2,1)S(1)} collective-permute-done((bf16[448,768]{1,0:T(8,128)(2,1)}, bf16[448,768]{1,0:T(8,128)(2,1)S(1)}, u32[]{:S(2)}, u32[]{:S(2)}) %collective-permute-start.5) | collective-permute-done | bytes 688160 | tf_op jit(solution)/shard_map/ppermute | solution.py:35
  236.6 19.5 %collective-permute-done.6.refs_8_ = bf16[448,768]{1,0:T(8,128)(2,1)S(1)} collective-permute-done((bf16[448,768]{1,0:T(8,128)(2,1)}, bf16[448,768]{1,0:T(8,128)(2,1)S(1)}, u32[]{:S(2)}, u32[]{:S(2)}) %collective-permute-start.6) | collective-permute-done | bytes 688160 | tf_op jit(solution)/shard_map/ppermute | solution.py:35
  256.7 1.5 collective-permute-start.14
  259.4 8.2 %collective-permute-done.13.refs_7_ = bf16[448,512]{1,0:T(8,128)(2,1)S(1)} collective-permute-done((bf16[448,512]{1,0:T(8,128)(2,1)}, bf16[448,512]{1,0:T(8,128)(2,1)S(1)}, u32[]{:S(2)}, u32[]{:S(2)}) %collective-permute-start.13) | collective-permute-done | bytes 458784 | tf_op jit(solution)/shard_map/ppermute | solution.py:35
  267.6 3.0 pad_maximum_fusion.1.refs_7_
  271.4 10.1 %shard_map.17 = bf16[2,448,896]{2,1,0:T(8,128)(2,1)} custom-call(s32[1]{0:T(128)} %bitcast.1.low_ref, bf16[896,768]{1,0:T(8,128)(2,1)S(1)} %bitcast.38, bf16[896,1024]{1,0:T(8,128)(2,1)} %bitcast.30, bf16[896,512]{1,0:T(8,128)(2,1)} %bitcast.7.refs_2_.refs_1_, bf16[896,768]{1,0:T(8,128)(2,1)} %collective-permute-done.2.refs_3_.refs_2_, ...), custom_call_target="tpu_custom_call" | custom-call | flops 3699376128 | bytes 13991936 | tf_op jit(solution)/shard_map/pallas_call | solution.py:103
  281.6 61.1 %all-reduce.6.cloned.1.call-done.mine = bf16[4,448,896]{2,1,0:T(8,128)(2,1)} async-done(((bf16[4,448,896]{2,1,0:T(8,128)(2,1)}), bf16[4,448,896]{2,1,0:T(8,128)(2,1)}) %all-reduce.6.cloned.1.call-update) | async-done | bytes 3211280 | tf_op jit(solution)/shard_map/psum | solution.py:367
  342.7 3.8 fusion.3
  346.5 1.5 collective-permute-start.22
  348.0 1.5 collective-permute-start.20
  352.4 1.3 shard_map.20.gram_in
  355.0 28.6 %collective-permute-done.22.theirs = bf16[2,448,896]{2,1,0:T(8,128)(2,1)} collective-permute-done((bf16[2,448,896]{2,1,0:T(8,128)(2,1)}, bf16[2,448,896]{2,1,0:T(8,128)(2,1)}, u32[]{:S(2)}, u32[]{:S(2)}) %collective-permute-start.22) | collective-permute-done | bytes 1605664 | tf_op jit(solution)/shard_map/ppermute | solution.py:35
  383.6 2.4 shard_map.22.gram_in
  386.0 2.5 shard_map.23.gram_in
  388.5 2.5 shard_map.24.gram_in
  391.0 2.5 shard_map.25.gram_in
  393.5 23.5 %all-reduce.8.cloned.1.call-done.mine = bf16[2,448,896]{2,1,0:T(8,128)(2,1)} async-done(((bf16[2,448,896]{2,1,0:T(8,128)(2,1)}), bf16[2,448,896]{2,1,0:T(8,128)(2,1)}) %all-reduce.8.cloned.1.call-update) | async-done | bytes 1605648 | tf_op jit(solution)/shard_map/psum | solution.py:367
  417.0 2.4 collective-permute-start.25
  420.7 33.1 %collective-permute-done.25.theirs = bf16[2,448,896]{2,1,0:T(8,128)(2,1)S(1)} collective-permute-done((bf16[2,448,896]{2,1,0:T(8,128)(2,1)}, bf16[2,448,896]{2,1,0:T(8,128)(2,1)S(1)}, u32[]{:S(2)}, u32[]{:S(2)}) %collective-permute-start.25) | collective-permute-done | bytes 1605664 | tf_op jit(solution)/shard_map/ppermute | solution.py:35
  453.8 1.4 shard_map.26.gram_in
  455.1 1.5 shard_map.27.refs_0_
  456.7 20.2 %shard_map.28.refs_11_.refs_3_ = bf16[896,1024]{1,0:T(8,128)(2,1)} custom-call(s32[1]{0:T(128)} %bitcast.me_ref, bf16[8,896,896]{2,1,0:T(8,128)(2,1)} %shard_map.27.refs_0_, bf16[896,1024]{1,0:T(8,128)(2,1)} %bitcast.31, bf16[896,1024]{1,0:T(8,128)(2,1)} %collective-permute-done.3.refs_4_.refs_2_, bf16[896,1024]{1,0:T(8,128)(2,1)} %collective-permute-done.7.refs_7_.refs_3_, ...), custom_call_target="tpu_custom_call" | custom-call | flops 13153337344 | bytes 27525120 | tf_op jit(solution)/shard_map/pallas_call | solution.py:286
  478.0 4.1 collective-permute-done.28.refs_9_
  482.1 2.0 collective-permute-done.29.refs_10_
  486.3 15.9 %shard_map.29.refs_3_.refs_11_ = bf16[896,768]{1,0:T(8,128)(2,1)} custom-call(s32[1]{0:T(128)} %bitcast.me_ref, bf16[8,896,896]{2,1,0:T(8,128)(2,1)} %shard_map.27.refs_0_, bf16[896,768]{1,0:T(8,128)(2,1)S(1)} %bitcast.39, bf16[896,768]{1,0:T(8,128)(2,1)} %collective-permute-done.2.refs_3_.refs_2_, bf16[896,768]{1,0:T(8,128)(2,1)} %copy-done.21, ...), custom_call_target="tpu_custom_call" | custom-call | flops 9865003008 | bytes 23855104 | tf_op jit(solution)/shard_map/pallas_call | solution.py:286
  503.3 3.6 collective-permute-done.32.refs_9_
  511.6 10.9 %shard_map.32.refs_3_ = bf16[896,512]{1,0:T(8,128)(2,1)S(1)} custom-call(s32[1]{0:T(128)} %bitcast.me_ref, bf16[8,896,896]{2,1,0:T(8,128)(2,1)} %shard_map.27.refs_0_, bf16[896,512]{1,0:T(8,128)(2,1)} %bitcast.7.refs_2_.refs_1_, bf16[896,512]{1,0:T(8,128)(2,1)} %collective-permute-done.4.refs_5_.refs_2_, ...), custom_call_target="tpu_custom_call" | custom-call | flops 6576668672 | bytes 20185088 | tf_op jit(solution)/shard_map/pallas_call | solution.py:286
  523.4 35.7 %all-gather.6.cloned.1.call-done.refs_1_ = bf16[7168,1024]{1,0:T(8,128)(2,1)} async-done(((bf16[896,1024]{1,0:T(8,128)(2,1)}), bf16[7168,1024]{1,0:T(8,128)(2,1)}) %all-gather.6.cloned.1.call-update) | async-done | bytes 14680080 | tf_op jit(solution)/shard_map/all_gather | solution.py:382
  559.1 21.1 %shard_map.30 = bf16[896,1024]{1,0:T(8,128)(2,1)S(1)} custom-call(s32[1]{0:T(128)} %bitcast.me_ref, bf16[8,896,896]{2,1,0:T(8,128)(2,1)} %shard_map.27.refs_0_, bf16[7168,1024]{1,0:T(8,128)(2,1)} %all-gather.6.cloned.1.call-done.refs_1_, bf16[896,1024]{1,0:T(8,128)(2,1)S(1)} %bitcast.32, bf16[896,1024]{1,0:T(8,128)(2,1)} %shard_map.28.refs_11_.refs_3_), custom_call_target="tpu_custom_call" | custom-call | flops 13153337344 | bytes 27525120 | tf_op jit(solution)/shard_map/pallas_call | solution.py:286
  580.2 47.4 %all_to_all.87 = bf16[4,224,1024]{2,1,0:T(8,128)(2,1)S(1)} all-to-all(bf16[4,224,1024]{2,1,0:T(8,128)(2,1)S(1)} %bitcast.42), channel_id=1, replica_groups=mesh['row'=8,'col'=4] {'col'}, dimensions={0} | all-to-all | bytes 3670016 | tf_op jit(solution)/shard_map/all_to_all | solution.py:385
  629.0 16.8 %shard_map.31 = bf16[896,768]{1,0:T(8,128)(2,1)S(1)} custom-call(s32[1]{0:T(128)} %bitcast.me_ref, bf16[8,896,896]{2,1,0:T(8,128)(2,1)} %shard_map.27.refs_0_, bf16[7168,768]{1,0:T(8,128)(2,1)} %all-gather.4.cloned.1.call-done.refs_1_, bf16[896,768]{1,0:T(8,128)(2,1)S(1)} %bitcast.40, bf16[896,768]{1,0:T(8,128)(2,1)} %shard_map.29.refs_3_.refs_11_, ...), custom_call_target="tpu_custom_call" | custom-call | flops 9865003008 | bytes 23855104 | tf_op jit(solution)/shard_map/pallas_call | solution.py:286
  645.8 34.9 %all_to_all.88 = bf16[4,224,768]{2,1,0:T(8,128)(2,1)S(1)} all-to-all(bf16[4,224,768]{2,1,0:T(8,128)(2,1)S(1)} %bitcast.44), channel_id=1, replica_groups=mesh['row'=8,'col'=4] {'col'}, dimensions={0} | all-to-all | bytes 2752512 | tf_op jit(solution)/shard_map/all_to_all | solution.py:385
  682.4 12.5 %shard_map.33 = bf16[896,512]{1,0:T(8,128)(2,1)S(1)} custom-call(s32[1]{0:T(128)} %bitcast.me_ref, bf16[8,896,896]{2,1,0:T(8,128)(2,1)} %shard_map.27.refs_0_, bf16[7168,512]{1,0:T(8,128)(2,1)} %all-gather.8.cloned.1.call-done.refs_1_, bf16[896,512]{1,0:T(8,128)(2,1)} %bitcast.7.refs_2_.refs_1_, bf16[896,512]{1,0:T(8,128)(2,1)S(1)} %copy-done.8, ...), custom_call_target="tpu_custom_call" | custom-call | flops 6576668672 | bytes 20185088 | tf_op jit(solution)/shard_map/pallas_call | solution.py:286
  694.9 24.8 %all_to_all.89 = bf16[4,224,512]{2,1,0:T(8,128)(2,1)S(1)} all-to-all(bf16[4,224,512]{2,1,0:T(8,128)(2,1)S(1)} %bitcast.45), channel_id=1, replica_groups=mesh['row'=8,'col'=4] {'col'}, dimensions={0} | all-to-all | bytes 1835008 | tf_op jit(solution)/shard_map/all_to_all | solution.py:385
  720.1 2.5 copy.19
  (124 shorter events, 30.6 us)
Async XLA Ops:
  9.1 39.1 %all-to-all-start = ((bf16[4,224,768]{2,1,0:T(8,128)(2,1)}), bf16[4,224,768]{2,1,0:T(8,128)(2,1)S(1)}, u32[]{:S(2)}, u32[]{:S(2)}) async-start(bf16[4,224,768]{2,1,0:T(8,128)(2,1)} %bitcast.2), calls=%async_computation | async-start | bytes 2752512 | tf_op jit(solution)/shard_map/all_to_all | solution.py:323
  48.2 223.3 %copy-start.3 = (bf16[4,224,768]{2,1,0:T(8,128)(2,1)}, bf16[4,224,768]{2,1,0:T(8,128)(2,1)S(1)}, u32[]{:S(2)}) copy-start(bf16[4,224,768]{2,1,0:T(8,128)(2,1)S(1)} %all-to-all-done) | copy-start | bytes 4128772
  48.2 45.6 %all-to-all-start.1 = ((bf16[4,224,1024]{2,1,0:T(8,128)(2,1)}), bf16[4,224,1024]{2,1,0:T(8,128)(2,1)S(1)}, u32[]{:S(2)}, u32[]{:S(2)}) async-start(bf16[4,224,1024]{2,1,0:T(8,128)(2,1)} %bitcast.50), calls=%async_computation.1 | async-start | bytes 3670016 | tf_op jit(solution)/shard_map/all_to_all | solution.py:323
  51.8 31.2 %collective-permute-start = (bf16[896,768]{1,0:T(8,128)(2,1)S(1)}, bf16[896,768]{1,0:T(8,128)(2,1)S(1)}, u32[]{:S(2)}, u32[]{:S(2)}) collective-permute-start(bf16[896,768]{1,0:T(8,128)(2,1)S(1)} %bitcast.33), channel_id=1, source_target_pairs={{0,8},{4,12},{8,0},{12,4},{16,24},{20,28},{24,16},{28,20},{1,9},{5... | collective-permute-start | bytes 4128776 | tf_op jit(solution)/shard_map/ppermute | solution.py:35
  53.3 31.0 %collective-permute-start.1 = (bf16[896,768]{1,0:T(8,128)(2,1)S(1)}, bf16[896,768]{1,0:T(8,128)(2,1)}, u32[]{:S(2)}, u32[]{:S(2)}) collective-permute-start(bf16[896,768]{1,0:T(8,128)(2,1)S(1)} %bitcast.34), channel_id=1, source_target_pairs={{0,16},{4,20},{8,24},{12,28},{16,0},{20,4},{24,8},{28,12},{1,17},{... | collective-permute-start | bytes 4128776 | tf_op jit(solution)/shard_map/ppermute | solution.py:35
  83.0 1.1 copy-start.21
  93.8 29.7 %copy-start.1 = (bf16[4,224,1024]{2,1,0:T(8,128)(2,1)}, bf16[4,224,1024]{2,1,0:T(8,128)(2,1)S(1)}, u32[]{:S(2)}) copy-start(bf16[4,224,1024]{2,1,0:T(8,128)(2,1)S(1)} %all-to-all-done.1) | copy-start | bytes 5505028
  93.8 26.7 %all-to-all-start.2 = ((bf16[4,224,512]{2,1,0:T(8,128)(2,1)}), bf16[4,224,512]{2,1,0:T(8,128)(2,1)}, u32[]{:S(2)}, u32[]{:S(2)}) async-start(bf16[4,224,512]{2,1,0:T(8,128)(2,1)} %bitcast.51), calls=%async_computation.2 | async-start | bytes 1835008 | tf_op jit(solution)/shard_map/all_to_all | solution.py:323
  98.0 119.9 %all-reduce.4.cloned.1.call-start = ((), (), s32[]{:S(2)}) async-start(), calls=%async_computation.6 | async-start | bytes 4128768 | tf_op jit(solution)/shard_map/psum | solution.py:348
  98.1 25.4 %collective-permute-start.3 = (bf16[896,1024]{1,0:T(8,128)(2,1)S(1)}, bf16[896,1024]{1,0:T(8,128)(2,1)}, u32[]{:S(2)}, u32[]{:S(2)}) collective-permute-start(bf16[896,1024]{1,0:T(8,128)(2,1)S(1)} %bitcast.25), channel_id=1, source_target_pairs={{0,4},{4,0},{8,12},{12,8},{16,20},{20,16},{24,28},{28,24},{1,5},{5... | collective-permute-start | bytes 5505032 | tf_op jit(solution)/shard_map/ppermute | solution.py:35
  98.2 25.4 %collective-permute-start.2 = (bf16[896,768]{1,0:T(8,128)(2,1)S(1)}, bf16[896,768]{1,0:T(8,128)(2,1)}, u32[]{:S(2)}, u32[]{:S(2)}) collective-permute-start(bf16[896,768]{1,0:T(8,128)(2,1)S(1)} %bitcast.35), channel_id=1, source_target_pairs={{0,4},{4,0},{8,12},{12,8},{16,20},{20,16},{24,28},{28,24},{1,5},{5... | collective-permute-start | bytes 4128776 | tf_op jit(solution)/shard_map/ppermute | solution.py:35
  120.5 3.0 collective-permute-start.4
  120.5 42.9 %collective-permute-start.7 = (bf16[896,1024]{1,0:T(8,128)(2,1)S(1)}, bf16[896,1024]{1,0:T(8,128)(2,1)}, u32[]{:S(2)}, u32[]{:S(2)}) collective-permute-start(bf16[896,1024]{1,0:T(8,128)(2,1)S(1)} %bitcast.26), channel_id=1, source_target_pairs={{0,8},{4,12},{8,0},{12,4},{16,24},{20,28},{24,16},{28,20},{1,9},{5... | collective-permute-start | bytes 5505032 | tf_op jit(solution)/shard_map/ppermute | solution.py:35
  122.0 43.0 %collective-permute-start.8 = (bf16[896,1024]{1,0:T(8,128)(2,1)S(1)}, bf16[896,1024]{1,0:T(8,128)(2,1)}, u32[]{:S(2)}, u32[]{:S(2)}) collective-permute-start(bf16[896,1024]{1,0:T(8,128)(2,1)S(1)} %bitcast.27), channel_id=1, source_target_pairs={{0,16},{4,20},{8,24},{12,28},{16,0},{20,4},{24,8},{28,12},{1,17},{... | collective-permute-start | bytes 5505032 | tf_op jit(solution)/shard_map/ppermute | solution.py:35
  133.7 208.9 %all-reduce.6.cloned.1.call-start = ((), (), s32[]{:S(2)}) async-start(), calls=%async_computation.7 | async-start | bytes 6422528 | tf_op jit(solution)/shard_map/psum | solution.py:367
  133.8 48.9 %collective-permute-start.11 = (bf16[896,512]{1,0:T(8,128)(2,1)}, bf16[896,512]{1,0:T(8,128)(2,1)}, u32[]{:S(2)}, u32[]{:S(2)}) collective-permute-start(bf16[896,512]{1,0:T(8,128)(2,1)} %bitcast.7.refs_2_.refs_1_), channel_id=1, source_target_pairs={{0,8},{4,12},{8,0},{12,4},{16,24},{20,28},{24,16},{28,20},{1,9},{5... | collective-permute-start | bytes 2752520 | tf_op jit(solution)/shard_map/ppermute | solution.py:35
  135.1 48.8 %collective-permute-start.12 = (bf16[896,512]{1,0:T(8,128)(2,1)}, bf16[896,512]{1,0:T(8,128)(2,1)}, u32[]{:S(2)}, u32[]{:S(2)}) collective-permute-start(bf16[896,512]{1,0:T(8,128)(2,1)} %bitcast.7.refs_2_.refs_1_), channel_id=1, source_target_pairs={{0,16},{4,20},{8,24},{12,28},{16,0},{20,4},{24,8},{28,12},{1,17},{... | collective-permute-start | bytes 2752520 | tf_op jit(solution)/shard_map/ppermute | solution.py:35
  218.0 199.0 %all-reduce.8.cloned.1.call-start = ((), (), s32[]{:S(2)}) async-start(), calls=%async_computation.8 | async-start | bytes 3211264 | tf_op jit(solution)/shard_map/psum | solution.py:367
  218.0 18.6 %collective-permute-start.5 = (bf16[448,768]{1,0:T(8,128)(2,1)}, bf16[448,768]{1,0:T(8,128)(2,1)S(1)}, u32[]{:S(2)}, u32[]{:S(2)}) collective-permute-start(bf16[448,768]{1,0:T(8,128)(2,1)} %slice.84), channel_id=1, source_target_pairs={{0,16},{4,20},{8,24},{12,28},{16,0},{20,4},{24,8},{28,12},{1,17},{... | collective-permute-start | bytes 2064392 | tf_op jit(solution)/shard_map/ppermute | solution.py:35
  219.6 37.1 %collective-permute-start.10 = (bf16[448,1024]{1,0:T(8,128)(2,1)S(1)}, bf16[448,1024]{1,0:T(8,128)(2,1)}, u32[]{:S(2)}, u32[]{:S(2)}) collective-permute-start(bf16[448,1024]{1,0:T(8,128)(2,1)S(1)} %slice.87), channel_id=1, source_target_pairs={{0,8},{4,12},{8,0},{12,4},{16,24},{20,28},{24,16},{28,20},{1,9},{5... | collective-permute-start | bytes 2752520 | tf_op jit(solution)/shard_map/ppermute | solution.py:35
  221.0 35.1 %collective-permute-start.6 = (bf16[448,768]{1,0:T(8,128)(2,1)}, bf16[448,768]{1,0:T(8,128)(2,1)S(1)}, u32[]{:S(2)}, u32[]{:S(2)}) collective-permute-start(bf16[448,768]{1,0:T(8,128)(2,1)} %slice.85), channel_id=1, source_target_pairs={{0,8},{4,12},{8,0},{12,4},{16,24},{20,28},{24,16},{28,20},{1,9},{5... | collective-permute-start | bytes 2064392 | tf_op jit(solution)/shard_map/ppermute | solution.py:35
  221.6 37.7 %collective-permute-start.9 = (bf16[448,1024]{1,0:T(8,128)(2,1)S(1)}, bf16[448,1024]{1,0:T(8,128)(2,1)}, u32[]{:S(2)}, u32[]{:S(2)}) collective-permute-start(bf16[448,1024]{1,0:T(8,128)(2,1)S(1)} %slice.86), channel_id=1, source_target_pairs={{0,16},{4,20},{8,24},{12,28},{16,0},{20,4},{24,8},{28,12},{1,17},{... | collective-permute-start | bytes 2752520 | tf_op jit(solution)/shard_map/ppermute | solution.py:35
  222.2 127.3 %collective-permute-start.15 = (bf16[896,1024]{1,0:T(8,128)(2,1)}, bf16[896,1024]{1,0:T(8,128)(2,1)}, u32[]{:S(2)}, u32[]{:S(2)}) collective-permute-start(bf16[896,1024]{1,0:T(8,128)(2,1)} %collective-permute-done.7.refs_7_.refs_3_), channel_id=1, source_target_pairs={{0,4},{4,0},{8,12},{12,8},{16,20},{20,16},{24,28},{28,24},{1,5},{5... | collective-permute-start | bytes 5505032 | tf_op jit(solution)/shard_map/ppermute | solution.py:35
  236.6 21.5 %copy-start.9 = (bf16[448,768]{1,0:T(8,128)(2,1)}, bf16[448,768]{1,0:T(8,128)(2,1)S(1)}, u32[]{:S(2)}) copy-start(bf16[448,768]{1,0:T(8,128)(2,1)S(1)} %collective-permute-done.5.refs_7_) | copy-start | bytes 2064388
  236.6 112.8 %collective-permute-start.16 = (bf16[896,1024]{1,0:T(8,128)(2,1)}, bf16[896,1024]{1,0:T(8,128)(2,1)}, u32[]{:S(2)}, u32[]{:S(2)}) collective-permute-start(bf16[896,1024]{1,0:T(8,128)(2,1)} %collective-permute-done.8.refs_10_.refs_5_), channel_id=1, source_target_pairs={{0,4},{4,0},{8,12},{12,8},{16,20},{20,16},{24,28},{28,24},{1,5},{5... | collective-permute-start | bytes 5505032 | tf_op jit(solution)/shard_map/ppermute | solution.py:35
  256.2 3.2 copy-start.11
  256.2 11.4 %collective-permute-start.13 = (bf16[448,512]{1,0:T(8,128)(2,1)}, bf16[448,512]{1,0:T(8,128)(2,1)S(1)}, u32[]{:S(2)}, u32[]{:S(2)}) collective-permute-start(bf16[448,512]{1,0:T(8,128)(2,1)} %slice.88), channel_id=1, source_target_pairs={{0,16},{4,20},{8,24},{12,28},{16,0},{20,4},{24,8},{28,12},{1,17},{... | collective-permute-start | bytes 1376264 | tf_op jit(solution)/shard_map/ppermute | solution.py:35
  256.7 13.9 %collective-permute-start.14 = (bf16[448,512]{1,0:T(8,128)(2,1)}, bf16[448,512]{1,0:T(8,128)(2,1)S(1)}, u32[]{:S(2)}, u32[]{:S(2)}) collective-permute-start(bf16[448,512]{1,0:T(8,128)(2,1)} %slice.89), channel_id=1, source_target_pairs={{0,8},{4,12},{8,0},{12,4},{16,24},{20,28},{24,16},{28,20},{1,9},{5... | collective-permute-start | bytes 1376264 | tf_op jit(solution)/shard_map/ppermute | solution.py:35
  259.4 88.6 %collective-permute-start.17 = (bf16[448,1024]{1,0:T(8,128)(2,1)}, bf16[448,1024]{1,0:T(8,128)(2,1)}, u32[]{:S(2)}, u32[]{:S(2)}) collective-permute-start(bf16[448,1024]{1,0:T(8,128)(2,1)} %collective-permute-done.9.refs_7_), channel_id=1, source_target_pairs={{0,4},{4,0},{8,12},{12,8},{16,20},{20,16},{24,28},{28,24},{1,5},{5... | collective-permute-start | bytes 2752520 | tf_op jit(solution)/shard_map/ppermute | solution.py:35
  267.6 3.0 copy-start.13
  267.6 81.9 %collective-permute-start.18 = (bf16[448,1024]{1,0:T(8,128)(2,1)}, bf16[448,1024]{1,0:T(8,128)(2,1)}, u32[]{:S(2)}, u32[]{:S(2)}) collective-permute-start(bf16[448,1024]{1,0:T(8,128)(2,1)} %collective-permute-done.10.refs_8_), channel_id=1, source_target_pairs={{0,4},{4,0},{8,12},{12,8},{16,20},{20,16},{24,28},{28,24},{1,5},{5... | collective-permute-start | bytes 2752520 | tf_op jit(solution)/shard_map/ppermute | solution.py:35
  346.5 4.3 copy-start
  346.5 37.1 %collective-permute-start.22 = (bf16[2,448,896]{2,1,0:T(8,128)(2,1)}, bf16[2,448,896]{2,1,0:T(8,128)(2,1)}, u32[]{:S(2)}, u32[]{:S(2)}) collective-permute-start(bf16[2,448,896]{2,1,0:T(8,128)(2,1)} %get-tuple-element.55), channel_id=1, source_target_pairs={{0,8},{4,12},{8,0},{12,4},{16,24},{20,28},{24,16},{28,20},{1,9},{5... | collective-permute-start | bytes 4816904 | tf_op jit(solution)/shard_map/ppermute | solution.py:35
  348.0 40.6 %collective-permute-start.20 = (bf16[2,448,896]{2,1,0:T(8,128)(2,1)}, bf16[2,448,896]{2,1,0:T(8,128)(2,1)}, u32[]{:S(2)}, u32[]{:S(2)}) collective-permute-start(bf16[2,448,896]{2,1,0:T(8,128)(2,1)} %get-tuple-element.56), channel_id=1, source_target_pairs={{0,16},{4,20},{8,24},{12,28},{16,0},{20,4},{24,8},{28,12},{1,17},{... | collective-permute-start | bytes 4816904 | tf_op jit(solution)/shard_map/ppermute | solution.py:35
  349.5 209.6 %all-gather.6.cloned.1.call-start = ((), (), s32[]{:S(2)}) async-start(), calls=%async_computation.10 | async-start | bytes 16515072 | tf_op jit(solution)/shard_map/all_gather | solution.py:382
  350.7 1.6 copy-start.5
  350.7 3.0 collective-permute-start.23
  351.0 35.1 %collective-permute-start.21 = (bf16[1,448,896]{2,1,0:T(8,128)(2,1)S(1)}, bf16[1,448,896]{2,1,0:T(8,128)(2,1)S(1)}, u32[]{:S(2)}, u32[]{:S(2)}) collective-permute-start(bf16[1,448,896]{2,1,0:T(8,128)(2,1)S(1)} %get-tuple-element.57), channel_id=1, source_target_pairs={{0,4},{4,0},{8,12},{12,8},{16,20},{20,16},{24,28},{28,24},{1,5},{5... | collective-permute-start | bytes 2408456 | tf_op jit(solution)/shard_map/ppermute | solution.py:35
  351.5 39.5 %collective-permute-start.19 = (bf16[1,448,896]{2,1,0:T(8,128)(2,1)S(1)}, bf16[1,448,896]{2,1,0:T(8,128)(2,1)S(1)}, u32[]{:S(2)}, u32[]{:S(2)}) collective-permute-start(bf16[1,448,896]{2,1,0:T(8,128)(2,1)S(1)} %get-tuple-element.58), channel_id=1, source_target_pairs={{0,4},{4,0},{8,12},{12,8},{16,20},{20,16},{24,28},{28,24},{1,5},{5... | collective-permute-start | bytes 2408456 | tf_op jit(solution)/shard_map/ppermute | solution.py:35
  417.0 36.8 %copy-start.6 = (bf16[2,448,896]{2,1,0:T(8,128)(2,1)S(1)}, bf16[2,448,896]{2,1,0:T(8,128)(2,1)}, u32[]{:S(2)}) copy-start(bf16[2,448,896]{2,1,0:T(8,128)(2,1)} %all-reduce.8.cloned.1.call-done.mine) | copy-start | bytes 4816900
  417.0 36.8 %collective-permute-start.25 = (bf16[2,448,896]{2,1,0:T(8,128)(2,1)}, bf16[2,448,896]{2,1,0:T(8,128)(2,1)S(1)}, u32[]{:S(2)}, u32[]{:S(2)}) collective-permute-start(bf16[2,448,896]{2,1,0:T(8,128)(2,1)} %all-reduce.8.cloned.1.call-done.mine), channel_id=1, source_target_pairs={{0,24},{4,28},{8,16},{12,20},{16,8},{20,12},{24,0},{28,4},{1,25},{... | collective-permute-start | bytes 4816904 | tf_op jit(solution)/shard_map/ppermute | solution.py:35
  420.6 34.5 %collective-permute-start.24 = (bf16[1,448,896]{2,1,0:T(8,128)(2,1)S(1)}, bf16[1,448,896]{2,1,0:T(8,128)(2,1)S(1)}, u32[]{:S(2)}, u32[]{:S(2)}) collective-permute-start(bf16[1,448,896]{2,1,0:T(8,128)(2,1)S(1)} %slice.95), channel_id=1, source_target_pairs={{0,4},{4,0},{8,12},{12,8},{16,20},{20,16},{24,28},{28,24},{1,5},{5... | collective-permute-start | bytes 2408456 | tf_op jit(solution)/shard_map/ppermute | solution.py:35
  456.7 20.8 %copy-start.10 = (bf16[448,768]{1,0:T(8,128)(2,1)S(1)}, bf16[448,768]{1,0:T(8,128)(2,1)}, u32[]{:S(2)}) copy-start(bf16[448,768]{1,0:T(8,128)(2,1)} %copy-done.9) | copy-start | bytes 2064388
  456.7 20.9 %copy-start.12 = (bf16[448,768]{1,0:T(8,128)(2,1)S(1)}, bf16[448,768]{1,0:T(8,128)(2,1)}, u32[]{:S(2)}) copy-start(bf16[448,768]{1,0:T(8,128)(2,1)} %copy-done.11) | copy-start | bytes 2064388
  476.9 9.4 %copy-start.4 = (bf16[4,224,768]{2,1,0:T(8,128)(2,1)S(1)}, bf16[4,224,768]{2,1,0:T(8,128)(2,1)}, u32[]{:S(2)}) copy-start(bf16[4,224,768]{2,1,0:T(8,128)(2,1)} %copy-done.3) | copy-start | bytes 4128772
  476.9 152.1 %all-gather.4.cloned.1.call-start = ((), (), s32[]{:S(2)}) async-start(), calls=%async_computation.9 | async-start | bytes 12386304 | tf_op jit(solution)/shard_map/all_gather | solution.py:382
  477.0 7.1 collective-permute-start.26
  477.0 7.3 collective-permute-start.27
  477.5 4.6 collective-permute-start.28
  477.6 6.5 collective-permute-start.29
  484.1 1.1 copy-start.22
  485.2 1.1 copy-start.23
  502.2 56.9 %copy-start.2 = (bf16[4,224,1024]{2,1,0:T(8,128)(2,1)S(1)}, bf16[4,224,1024]{2,1,0:T(8,128)(2,1)}, u32[]{:S(2)}) copy-start(bf16[4,224,1024]{2,1,0:T(8,128)(2,1)} %copy-done.1) | copy-start | bytes 5505028
  502.2 179.8 %all-gather.8.cloned.1.call-start = ((), (), s32[]{:S(2)}) async-start(), calls=%async_computation.11 | async-start | bytes 8257536 | tf_op jit(solution)/shard_map/all_gather | solution.py:382
  502.2 5.4 collective-permute-start.30
  502.4 5.2 collective-permute-start.31
  502.8 4.1 collective-permute-start.32
  503.0 4.7 collective-permute-start.33
  509.5 1.0 copy-start.14
  627.6 1.2 copy-start.17
  680.7 1.1 copy-start.19
  680.7 1.7 copy-start.8
  682.4 37.4 %copy-start.20 = (bf16[4,224,768]{2,1,0:T(8,128)(2,1)S(1)}, bf16[4,224,768]{2,1,0:T(8,128)(2,1)}, u32[]{:S(2)}) copy-start(bf16[4,224,768]{2,1,0:T(8,128)(2,1)} %copy-done.19) | copy-start | bytes 4128772
  694.9 24.8 %copy-start.18 = (bf16[4,224,1024]{2,1,0:T(8,128)(2,1)S(1)}, bf16[4,224,1024]{2,1,0:T(8,128)(2,1)}, u32[]{:S(2)}) copy-start(bf16[4,224,1024]{2,1,0:T(8,128)(2,1)} %copy-done.17) | copy-start | bytes 5505028
  (5 other events, 4.6 us)
Sparse Core Ops, SparseCore 0:
  133.8 84.0 all-reduce.3
  220.5 122.1 all-reduce.5
  349.6 67.3 all-reduce.7
  477.0 82.0 all-gather.5
  560.8 65.4 all-gather.3
  628.1 49.9 all-gather.7

commit v10 on v9

--- a/solution.py
+++ b/solution.py
@@ -306,6 +306,33 @@
     )(me.astype(jnp.int32).reshape(1), gram, *[parts[key] for key in keys], *extra, *deps)
 
 
+def sum_on_line(piece, arrivals):
+    count = lax.axis_size("col")
+    me = lax.axis_index("col")
+    half = count // 2
+
+    def send(stage, value, pairs):
+        done = arrivals.setdefault(stage, [])
+        if len(done) > 1:
+            value = after(value, done[-2])
+        arrived = lax.ppermute(value, "col", pairs)
+        done.append(arrived)
+        return arrived
+
+    def add(left, right):
+        return (left.astype(f32) + right.astype(f32)).astype(bf16)
+
+    for s in range(half - 1):
+        pairs = [(s, s + 1), (count - 1 - s, count - 2 - s)]
+        piece = add(piece, send(s, piece, pairs))
+    piece = add(piece, send(half - 1, piece, [(half - 1, half), (half, half - 1)]))
+    for s in range(half - 2, -1, -1):
+        pairs = [(s + 1, s), (count - 2 - s, count - 1 - s)]
+        arrived = send(2 * half - 2 - s, piece, pairs)
+        piece = jnp.where((me == s) | (me == count - 1 - s), arrived, piece)
+    return piece
+
+
 def per_device(ortho_in):
     rows, cols = ortho_in.shape
     n_row = lax.axis_size("row")
@@ -354,25 +381,38 @@
     panels = [
         add_cores({**parts, **sibling}) for parts, sibling in zip(gathered, siblings)
     ]
-    for stage in (chips[:2], chips[2:]):
-        blocks = list(lefts)
-        for j in stage:
-            peers = [whole_block(parts, j) for parts in gathered]
-            if j != chips[-1]:
-                peers[0] = after(peers[0], *tied)
-            blocks.append(peers)
-        jobs = [(i, bit_x + n, n, 0) for n in range(len(stage)) for i in range(bit_x)]
-        pieces = gram_pieces(blocks, jobs, [low_of(j)[0] for j in stage], scale)
-        held = list(panels[1].values()) if len(stage) == 1 else []
-        last = sums = lax.psum(after(pieces, last, *held), "col")
-        if len(stage) == 1:
-            sums, gram = lax.optimization_barrier((sums, gram))
-        for n, j in enumerate(stage):
-            theirs = swap(sums[n * bit_x : (n + 1) * bit_x], j)
-            gram = put_block(gram, low_of(j), (sums, n * bit_x), (theirs, 0), j)
-            for i in cores:
-                mine = swap(sums[n * bit_x + i : n * bit_x + i + 1], i)
-                gram = put_block(gram, low_of(j), (mine, 0), (theirs, i), j | i)
+    def peers_of(j):
+        return [whole_block(parts, j) for parts in gathered]
+
+    blocks = list(lefts)
+    for j in chips[:2]:
+        peers = peers_of(j)
+        peers[0] = after(peers[0], *tied)
+        blocks.append(peers)
+    jobs = [(i, bit_x + n, n, 0) for n in range(2) for i in range(bit_x)]
+    pieces = gram_pieces(blocks, jobs, [low_of(j)[0] for j in chips[:2]], scale)
+    last = sums = lax.psum(after(pieces, last), "col")
+    for n, j in enumerate(chips[:2]):
+        theirs = swap(sums[n * bit_x : (n + 1) * bit_x], j)
+        gram = put_block(gram, low_of(j), (sums, n * bit_x), (theirs, 0), j)
+        for i in cores:
+            mine = swap(sums[n * bit_x + i : n * bit_x + i + 1], i)
+            gram = put_block(gram, low_of(j), (mine, 0), (theirs, i), j | i)
+
+    j = chips[-1]
+    peers = peers_of(j)
+    far = [
+        gram_pieces([lefts[i], peers], [(0, 1, 0, 0)], [low_of(j)[0]], scale)
+        for i in range(bit_x)
+    ]
+    arrivals = {}
+    lines = {i: sum_on_line(far[i], arrivals) for i in cores}
+    sums = lax.psum(after(far[0], last, *panels[1].values()), "col")
+    sums, gram = lax.optimization_barrier((sums, gram))
+    for i in cores:
+        mine, theirs = swap(lines[i], i), swap(lines[i], j)
+        gram = put_block(gram, low_of(j), (mine, 0), (theirs, 0), j | i)
+    gram = put_block(gram, low_of(j), (sums, 0), (swap(sums, j), 0), j)
 
     outs, firsts, backs = {}, [], []
     for k in (1, 0, 2):

time: 739 us -> 734 us (level)
  waiting for transfers between devices: 377 us -> 351 us
  starting transfers between devices: 38.3 us -> 46.8 us
  local copies, waits for them, and re-layouts: 35.9 us -> 44.3 us
    ppermute x34 -> x35, waiting for transfers between devices: 181 us -> 114 us  [swap(): return lax.ppermute(value, 'row', [(r, r ^ bit) for r in range(count)])]
    ppermute x0 -> x3, waiting for transfers between devices: none -> 44.4 us  [send(): arrived = lax.ppermute(value, 'col', pairs)]
    ppermute x34 -> x35, starting transfers between devices: 23.9 us -> 28.5 us  [swap(): return lax.ppermute(value, 'row', [(r, r ^ bit) for r in range(count)])]
    unnamed x52 -> x79, local copies, waits for them, and re-layouts: 12.2 us -> 16.4 us
    pallas_call x2 -> x3, Pallas kernels: 26.7 us -> 27 us  [gram_pieces(): pl.pallas_call(functools.partial(pieces_kernel, count, jobs, scale), out_...]
  transfers between devices with their start and end apart: 43 -> 47, of which waited for: 23 -> 22; matrix products, arithmetic and copies ran while one was open for 4% -> 4% of each run, Pallas kernels for 16% -> 17%
where the time goes in v10:
time: 734 us; the launch traced here: 725 us
  waiting for transfers between devices  351 us (48%)
  Pallas kernels  154 us (21%)
  blocking collectives  107 us (15%)
  starting transfers between devices  46.8 us (6%)
  local copies, waits for them, and re-layouts  44.3 us (6%)
  between operations  14.4 us (2%)
  other arithmetic  7.36 us (1%)
    ppermute x35, waiting for transfers between devices, swap(): return lax.ppermute(value, 'row', [(r, r ^ bit) for r in range(count)])  114 us
    all_to_all x3, blocking collectives, per_device(): lax.all_to_all(result, 'col', split_axis=0, concat_axis=1, tiled=True)  107 us
    pallas_call x6, Pallas kernels, product(): pl.pallas_call(functools.partial(product_kernel, keys, start, bool(extra)...  98.2 us
    psum x1, waiting for transfers between devices, per_device(): last = sums = lax.psum(after(pieces, last), 'col')  81.9 us
    all_to_all x3, waiting for transfers between devices, exchange(): return lax.all_to_all(value, 'col', split_axis=0, concat_axis=0, tiled=True)  61.1 us
    ppermute x3, waiting for transfers between devices, send(): arrived = lax.ppermute(value, 'col', pairs)  44.4 us
    all_gather x3, waiting for transfers between devices, per_device(): first_panel = lax.all_gather(first, 'row', axis=0, tiled=True)  32.9 us
    ppermute x35, starting transfers between devices, swap(): return lax.ppermute(value, 'row', [(r, r ^ bit) for r in range(count)])  28.5 us
  transfers between devices with their start and end apart: 47, of which 22 were waited for; matrix products, arithmetic and copies ran while one was open for 4% of the time, Pallas kernels for 17%

profile of v10, /device:TPU:0, one launch (start us, length us, event | category | flops | bytes accessed | tf_op | source)
XLA Modules:
  0.0 724.9 jit_solution(18430730157613098855)
XLA Ops:
  9.1 6.3 all-to-all-start
  15.4 1.6 fusion.1
  18.4 29.8 %all-to-all-done = bf16[4,224,768]{2,1,0:T(8,128)(2,1)S(1)} async-done(((bf16[4,224,768]{2,1,0:T(8,128)(2,1)}), bf16[4,224,768]{2,1,0:T(8,128)(2,1)S(1)}, u32[]{:S(2)}, u32[]{:S(2)}) %all-to-all-start) | async-done | bytes 1376288 | tf_op jit(solution)/shard_map/all_to_all | solution.py:350
  48.2 3.6 all-to-all-start.1
  51.8 1.6 collective-permute-start
  53.3 1.5 collective-permute-start.1
  57.2 25.8 %collective-permute-done.refs_6_.refs_3_ = bf16[896,768]{1,0:T(8,128)(2,1)S(1)} collective-permute-done((bf16[896,768]{1,0:T(8,128)(2,1)S(1)}, bf16[896,768]{1,0:T(8,128)(2,1)S(1)}, u32[]{:S(2)}, u32[]{:S(2)}) %collective-permute-start) | collective-permute-done | bytes 1376288 | tf_op jit(solution)/shard_map/ppermute | solution.py:35
  84.3 9.5 %all-to-all-done.1 = bf16[4,224,1024]{2,1,0:T(8,128)(2,1)S(1)} async-done(((bf16[4,224,1024]{2,1,0:T(8,128)(2,1)}), bf16[4,224,1024]{2,1,0:T(8,128)(2,1)S(1)}, u32[]{:S(2)}, u32[]{:S(2)}) %all-to-all-start.1) | async-done | bytes 1835040 | tf_op jit(solution)/shard_map/all_to_all | solution.py:350
  93.8 4.2 all-to-all-start.2
  98.7 21.8 %all-to-all-done.2 = bf16[4,224,512]{2,1,0:T(8,128)(2,1)} async-done(((bf16[4,224,512]{2,1,0:T(8,128)(2,1)}), bf16[4,224,512]{2,1,0:T(8,128)(2,1)}, u32[]{:S(2)}, u32[]{:S(2)}) %all-to-all-start.2) | async-done | bytes 917536 | tf_op jit(solution)/shard_map/all_to_all | solution.py:350
  122.0 1.5 collective-permute-start.5
  123.5 10.1 %shard_map.19 = bf16[1152,896]{1,0:T(8,128)(2,1)} custom-call(s32[1]{0:T(128)} %bitcast.9.low_ref, bf16[896,768]{1,0:T(8,128)(2,1)S(1)} %bitcast.36, bf16[896,1024]{1,0:T(8,128)(2,1)} %bitcast.28, bf16[896,512]{1,0:T(8,128)(2,1)} %bitcast.7.refs_2_.refs_1_, bf16[896,768]{1,0:T(8,128)(2,1)} %collective-permute-done.12.refs_3_.refs_0_.refs_2_, ...), custom_call_target="tpu_custom_call" | custom-call | flops 4756340736 | bytes 10321920 | tf_op jit(solution)/shard_map/pallas_call | solution.py:197
  135.1 1.5 collective-permute-start.9
  136.7 2.1 slice.81
  138.7 2.0 slice.82
  141.4 22.1 %collective-permute-done.4.refs_7_.refs_3_ = bf16[896,1024]{1,0:T(8,128)(2,1)} collective-permute-done((bf16[896,1024]{1,0:T(8,128)(2,1)S(1)}, bf16[896,1024]{1,0:T(8,128)(2,1)}, u32[]{:S(2)}, u32[]{:S(2)}) %collective-permute-start.4) | collective-permute-done | bytes 1835040 | tf_op jit(solution)/shard_map/ppermute | solution.py:35
  164.9 2.2 slice.83
  167.1 2.2 slice.84
  169.3 1.5 collective-permute-start.6
  170.9 12.2 %collective-permute-done.8.refs_8_.refs_3_ = bf16[896,512]{1,0:T(8,128)(2,1)} collective-permute-done((bf16[896,512]{1,0:T(8,128)(2,1)}, bf16[896,512]{1,0:T(8,128)(2,1)}, u32[]{:S(2)}, u32[]{:S(2)}) %collective-permute-start.8) | collective-permute-done | bytes 917536 | tf_op jit(solution)/shard_map/ppermute | solution.py:35
  184.6 1.8 slice.85
  186.4 1.8 slice.86
  188.2 16.6 %shard_map.18 = bf16[4,448,896]{2,1,0:T(8,128)(2,1)} custom-call(s32[2]{0:T(128)S(1)} %pad_add_fusion.low_ref, bf16[896,768]{1,0:T(8,128)(2,1)S(1)} %bitcast.37, bf16[896,1024]{1,0:T(8,128)(2,1)} %bitcast.29, bf16[896,512]{1,0:T(8,128)(2,1)} %bitcast.7.refs_2_.refs_1_, bf16[896,768]{1,0:T(8,128)(2,1)} %collective-permute-done.12.refs_3_.refs_0_.refs_2_, ...), custom_call_target="tpu_custom_call" | custom-call | flops 7398752256 | bytes 19726336 | tf_op jit(solution)/shard_map/pallas_call | solution.py:103
  204.8 13.1 %all-reduce.4.cloned.1.call-done.near = bf16[1152,896]{1,0:T(8,128)(2,1)} async-done(((bf16[1152,896]{1,0:T(8,128)(2,1)}), bf16[1152,896]{1,0:T(8,128)(2,1)}) %all-reduce.4.cloned.1.call-update) | async-done | bytes 2064400 | tf_op jit(solution)/shard_map/psum | solution.py:375
  218.0 1.5 collective-permute-start.10
  220.7 1.6 collective-permute-start.11
  223.6 6.7 collective-permute-done.10.refs_7_
  230.4 2.4 collective-permute-done.11.refs_8_
  233.6 5.6 shard_map.26
  239.2 1.9 collective-permute-start.25
  241.2 34.6 %collective-permute-done.25 = bf16[1,448,896]{2,1,0:T(8,128)(2,1)S(1)} collective-permute-done((bf16[1,448,896]{2,1,0:T(8,128)(2,1)S(1)}, bf16[1,448,896]{2,1,0:T(8,128)(2,1)S(1)}, u32[]{:S(2)}, u32[]{:S(2)}) %collective-permute-start.25) | collective-permute-done | bytes 802848 | tf_op jit(solution)/shard_map/ppermute | solution.py:318
  278.9 81.9 %all-reduce.6.cloned.1.call-done.mine = bf16[4,448,896]{2,1,0:T(8,128)(2,1)} async-done(((bf16[4,448,896]{2,1,0:T(8,128)(2,1)}), bf16[4,448,896]{2,1,0:T(8,128)(2,1)}) %all-reduce.6.cloned.1.call-update) | async-done | bytes 3211280 | tf_op jit(solution)/shard_map/psum | solution.py:394
  360.8 4.0 fusion.3
  369.4 4.8 shard_map.17
  375.1 2.1 slice_bitcast_fusion.mine
  379.1 9.9 %collective-permute-done.27 = bf16[1,448,896]{2,1,0:T(8,128)(2,1)} collective-permute-done((bf16[1,448,896]{2,1,0:T(8,128)(2,1)}, bf16[1,448,896]{2,1,0:T(8,128)(2,1)}, u32[]{:S(2)}, u32[]{:S(2)}) %collective-permute-start.27) | collective-permute-done | bytes 802848 | tf_op jit(solution)/shard_map/ppermute | solution.py:318
  389.0 1.6 copy-done.10
  392.0 2.1 broadcast_select_fusion
  394.6 2.7 shard_map.21.gram_in
  397.3 4.8 collective-permute-done.22.theirs
  402.1 1.7 collective-permute-start.29
  403.9 2.4 shard_map.22.gram_in
  406.3 2.7 shard_map.23.gram_in
  409.0 13.9 %collective-permute-done.20.theirs = bf16[2,448,896]{2,1,0:T(8,128)(2,1)} collective-permute-done((bf16[2,448,896]{2,1,0:T(8,128)(2,1)}, bf16[2,448,896]{2,1,0:T(8,128)(2,1)}, u32[]{:S(2)}, u32[]{:S(2)}) %collective-permute-start.20) | collective-permute-done | bytes 1605664 | tf_op jit(solution)/shard_map/ppermute | solution.py:35
  422.8 2.4 shard_map.24.gram_in
  425.3 2.8 shard_map.25.gram_in
  428.0 2.9 all-reduce.8.cloned.1.call-done.mine
  431.0 2.4 collective-permute-start.24
  433.4 2.7 shard_map.27.gram_in
  436.0 15.7 %collective-permute-done.24.theirs = bf16[1,448,896]{2,1,0:T(8,128)(2,1)S(1)} collective-permute-done((bf16[1,448,896]{2,1,0:T(8,128)(2,1)}, bf16[1,448,896]{2,1,0:T(8,128)(2,1)S(1)}, u32[]{:S(2)}, u32[]{:S(2)}) %collective-permute-start.24) | collective-permute-done | bytes 802848 | tf_op jit(solution)/shard_map/ppermute | solution.py:35
  451.8 1.6 shard_map.28.refs_0_
  453.3 20.2 %shard_map.29.refs_11_.refs_3_ = bf16[896,1024]{1,0:T(8,128)(2,1)} custom-call(s32[1]{0:T(128)} %bitcast.me_ref, bf16[8,896,896]{2,1,0:T(8,128)(2,1)} %shard_map.28.refs_0_, bf16[896,1024]{1,0:T(8,128)(2,1)} %bitcast.31, bf16[896,1024]{1,0:T(8,128)(2,1)} %collective-permute-done.13.refs_4_.refs_1_.refs_2_, ...), custom_call_target="tpu_custom_call" | custom-call | flops 13153337344 | bytes 27525120 | tf_op jit(solution)/shard_map/pallas_call | solution.py:286
  474.7 5.3 collective-permute-done.32.refs_9_
  483.2 15.9 %shard_map.30.refs_3_.refs_11_ = bf16[896,768]{1,0:T(8,128)(2,1)} custom-call(s32[1]{0:T(128)} %bitcast.me_ref, bf16[8,896,896]{2,1,0:T(8,128)(2,1)} %shard_map.28.refs_0_, bf16[896,768]{1,0:T(8,128)(2,1)S(1)} %bitcast.39, bf16[896,768]{1,0:T(8,128)(2,1)} %collective-permute-done.12.refs_3_.refs_0_.refs_2_, bf16[896,768]{1,0:T(8,128)(2,1)} %copy-done.32, ...), custom_call_target="tpu_custom_call" | custom-call | flops 9865003008 | bytes 23855104 | tf_op jit(solution)/shard_map/pallas_call | solution.py:286
  500.3 3.6 collective-permute-done.36.refs_9_
  508.5 11.7 %shard_map.33.refs_3_ = bf16[896,512]{1,0:T(8,128)(2,1)S(1)} custom-call(s32[1]{0:T(128)} %bitcast.me_ref, bf16[8,896,896]{2,1,0:T(8,128)(2,1)} %shard_map.28.refs_0_, bf16[896,512]{1,0:T(8,128)(2,1)} %bitcast.7.refs_2_.refs_1_, bf16[896,512]{1,0:T(8,128)(2,1)} %collective-permute-done.14.refs_5_.refs_2_, ...), custom_call_target="tpu_custom_call" | custom-call | flops 6576668672 | bytes 20185088 | tf_op jit(solution)/shard_map/pallas_call | solution.py:286
  521.2 32.9 %all-gather.6.cloned.1.call-done.refs_1_ = bf16[7168,1024]{1,0:T(8,128)(2,1)} async-done(((bf16[896,1024]{1,0:T(8,128)(2,1)}), bf16[7168,1024]{1,0:T(8,128)(2,1)}) %all-gather.6.cloned.1.call-update) | async-done | bytes 14680080 | tf_op jit(solution)/shard_map/all_gather | solution.py:422
  554.1 21.1 %shard_map.31 = bf16[896,1024]{1,0:T(8,128)(2,1)S(1)} custom-call(s32[1]{0:T(128)} %bitcast.me_ref, bf16[8,896,896]{2,1,0:T(8,128)(2,1)} %shard_map.28.refs_0_, bf16[7168,1024]{1,0:T(8,128)(2,1)} %all-gather.6.cloned.1.call-done.refs_1_, bf16[896,1024]{1,0:T(8,128)(2,1)S(1)} %bitcast.32, bf16[896,1024]{1,0:T(8,128)(2,1)} %shard_map.29.refs_11_.refs_3_), custom_call_target="tpu_custom_call" | custom-call | flops 13153337344 | bytes 27525120 | tf_op jit(solution)/shard_map/pallas_call | solution.py:286
  575.2 47.4 %all_to_all.87 = bf16[4,224,1024]{2,1,0:T(8,128)(2,1)S(1)} all-to-all(bf16[4,224,1024]{2,1,0:T(8,128)(2,1)S(1)} %bitcast.42), channel_id=1, replica_groups=mesh['row'=8,'col'=4] {'col'}, dimensions={0} | all-to-all | bytes 3670016 | tf_op jit(solution)/shard_map/all_to_all | solution.py:425
  624.1 16.8 %shard_map.32 = bf16[896,768]{1,0:T(8,128)(2,1)S(1)} custom-call(s32[1]{0:T(128)} %bitcast.me_ref, bf16[8,896,896]{2,1,0:T(8,128)(2,1)} %shard_map.28.refs_0_, bf16[7168,768]{1,0:T(8,128)(2,1)} %all-gather.4.cloned.1.call-done.refs_1_, bf16[896,768]{1,0:T(8,128)(2,1)S(1)} %bitcast.40, bf16[896,768]{1,0:T(8,128)(2,1)} %shard_map.30.refs_3_.refs_11_, ...), custom_call_target="tpu_custom_call" | custom-call | flops 9865003008 | bytes 23855104 | tf_op jit(solution)/shard_map/pallas_call | solution.py:286
  640.8 34.9 %all_to_all.88 = bf16[4,224,768]{2,1,0:T(8,128)(2,1)S(1)} all-to-all(bf16[4,224,768]{2,1,0:T(8,128)(2,1)S(1)} %bitcast.44), channel_id=1, replica_groups=mesh['row'=8,'col'=4] {'col'}, dimensions={0} | all-to-all | bytes 2752512 | tf_op jit(solution)/shard_map/all_to_all | solution.py:425
  677.4 12.5 %shard_map.34 = bf16[896,512]{1,0:T(8,128)(2,1)S(1)} custom-call(s32[1]{0:T(128)} %bitcast.me_ref, bf16[8,896,896]{2,1,0:T(8,128)(2,1)} %shard_map.28.refs_0_, bf16[7168,512]{1,0:T(8,128)(2,1)} %all-gather.8.cloned.1.call-done.refs_1_, bf16[896,512]{1,0:T(8,128)(2,1)} %bitcast.7.refs_2_.refs_1_, bf16[896,512]{1,0:T(8,128)(2,1)S(1)} %copy-done.17, ...), custom_call_target="tpu_custom_call" | custom-call | flops 6576668672 | bytes 20185088 | tf_op jit(solution)/shard_map/pallas_call | solution.py:286
  689.9 24.8 %all_to_all.89 = bf16[4,224,512]{2,1,0:T(8,128)(2,1)S(1)} all-to-all(bf16[4,224,512]{2,1,0:T(8,128)(2,1)S(1)} %bitcast.45), channel_id=1, replica_groups=mesh['row'=8,'col'=4] {'col'}, dimensions={0} | all-to-all | bytes 1835008 | tf_op jit(solution)/shard_map/all_to_all | solution.py:425
  715.1 2.5 copy.19
  (162 shorter events, 45.0 us)
Async XLA Ops:
  9.1 39.1 %all-to-all-start = ((bf16[4,224,768]{2,1,0:T(8,128)(2,1)}), bf16[4,224,768]{2,1,0:T(8,128)(2,1)S(1)}, u32[]{:S(2)}, u32[]{:S(2)}) async-start(bf16[4,224,768]{2,1,0:T(8,128)(2,1)} %bitcast.2), calls=%async_computation | async-start | bytes 2752512 | tf_op jit(solution)/shard_map/all_to_all | solution.py:350
  48.2 140.1 %copy-start.7 = (bf16[4,224,768]{2,1,0:T(8,128)(2,1)}, bf16[4,224,768]{2,1,0:T(8,128)(2,1)S(1)}, u32[]{:S(2)}) copy-start(bf16[4,224,768]{2,1,0:T(8,128)(2,1)S(1)} %all-to-all-done) | copy-start | bytes 4128772
  48.2 45.6 %all-to-all-start.1 = ((bf16[4,224,1024]{2,1,0:T(8,128)(2,1)}), bf16[4,224,1024]{2,1,0:T(8,128)(2,1)S(1)}, u32[]{:S(2)}, u32[]{:S(2)}) async-start(bf16[4,224,1024]{2,1,0:T(8,128)(2,1)} %bitcast.50), calls=%async_computation.1 | async-start | bytes 3670016 | tf_op jit(solution)/shard_map/all_to_all | solution.py:350
  51.8 31.2 %collective-permute-start = (bf16[896,768]{1,0:T(8,128)(2,1)S(1)}, bf16[896,768]{1,0:T(8,128)(2,1)S(1)}, u32[]{:S(2)}, u32[]{:S(2)}) collective-permute-start(bf16[896,768]{1,0:T(8,128)(2,1)S(1)} %bitcast.33), channel_id=1, source_target_pairs={{0,8},{4,12},{8,0},{12,4},{16,24},{20,28},{24,16},{28,20},{1,9},{5... | collective-permute-start | bytes 4128776 | tf_op jit(solution)/shard_map/ppermute | solution.py:35
  53.3 31.0 %collective-permute-start.1 = (bf16[896,768]{1,0:T(8,128)(2,1)S(1)}, bf16[896,768]{1,0:T(8,128)(2,1)}, u32[]{:S(2)}, u32[]{:S(2)}) collective-permute-start(bf16[896,768]{1,0:T(8,128)(2,1)S(1)} %bitcast.34), channel_id=1, source_target_pairs={{0,16},{4,20},{8,24},{12,28},{16,0},{20,4},{24,8},{28,12},{1,17},{... | collective-permute-start | bytes 4128776 | tf_op jit(solution)/shard_map/ppermute | solution.py:35
  93.8 29.7 %copy-start.3 = (bf16[4,224,1024]{2,1,0:T(8,128)(2,1)}, bf16[4,224,1024]{2,1,0:T(8,128)(2,1)S(1)}, u32[]{:S(2)}) copy-start(bf16[4,224,1024]{2,1,0:T(8,128)(2,1)S(1)} %all-to-all-done.1) | copy-start | bytes 5505028
  93.8 26.7 %all-to-all-start.2 = ((bf16[4,224,512]{2,1,0:T(8,128)(2,1)}), bf16[4,224,512]{2,1,0:T(8,128)(2,1)}, u32[]{:S(2)}, u32[]{:S(2)}) async-start(bf16[4,224,512]{2,1,0:T(8,128)(2,1)} %bitcast.51), calls=%async_computation.2 | async-start | bytes 1835008 | tf_op jit(solution)/shard_map/all_to_all | solution.py:350
  98.0 119.9 %all-reduce.4.cloned.1.call-start = ((), (), s32[]{:S(2)}) async-start(), calls=%async_computation.6 | async-start | bytes 4128768 | tf_op jit(solution)/shard_map/psum | solution.py:375
  98.1 25.4 %collective-permute-start.13 = (bf16[896,1024]{1,0:T(8,128)(2,1)S(1)}, bf16[896,1024]{1,0:T(8,128)(2,1)}, u32[]{:S(2)}, u32[]{:S(2)}) collective-permute-start(bf16[896,1024]{1,0:T(8,128)(2,1)S(1)} %bitcast.25), channel_id=1, source_target_pairs={{0,4},{4,0},{8,12},{12,8},{16,20},{20,16},{24,28},{28,24},{1,5},{5... | collective-permute-start | bytes 5505032 | tf_op jit(solution)/shard_map/ppermute | solution.py:35
  98.2 25.4 %collective-permute-start.12 = (bf16[896,768]{1,0:T(8,128)(2,1)S(1)}, bf16[896,768]{1,0:T(8,128)(2,1)}, u32[]{:S(2)}, u32[]{:S(2)}) collective-permute-start(bf16[896,768]{1,0:T(8,128)(2,1)S(1)} %bitcast.35), channel_id=1, source_target_pairs={{0,4},{4,0},{8,12},{12,8},{16,20},{20,16},{24,28},{28,24},{1,5},{5... | collective-permute-start | bytes 4128776 | tf_op jit(solution)/shard_map/ppermute | solution.py:35
  120.5 3.0 collective-permute-start.14
  120.5 42.9 %collective-permute-start.4 = (bf16[896,1024]{1,0:T(8,128)(2,1)S(1)}, bf16[896,1024]{1,0:T(8,128)(2,1)}, u32[]{:S(2)}, u32[]{:S(2)}) collective-permute-start(bf16[896,1024]{1,0:T(8,128)(2,1)S(1)} %bitcast.26), channel_id=1, source_target_pairs={{0,8},{4,12},{8,0},{12,4},{16,24},{20,28},{24,16},{28,20},{1,9},{5... | collective-permute-start | bytes 5505032 | tf_op jit(solution)/shard_map/ppermute | solution.py:35
  122.0 43.0 %collective-permute-start.5 = (bf16[896,1024]{1,0:T(8,128)(2,1)S(1)}, bf16[896,1024]{1,0:T(8,128)(2,1)}, u32[]{:S(2)}, u32[]{:S(2)}) collective-permute-start(bf16[896,1024]{1,0:T(8,128)(2,1)S(1)} %bitcast.27), channel_id=1, source_target_pairs={{0,16},{4,20},{8,24},{12,28},{16,0},{20,4},{24,8},{28,12},{1,17},{... | collective-permute-start | bytes 5505032 | tf_op jit(solution)/shard_map/ppermute | solution.py:35
  133.7 227.1 %all-reduce.6.cloned.1.call-start = ((), (), s32[]{:S(2)}) async-start(), calls=%async_computation.7 | async-start | bytes 6422528 | tf_op jit(solution)/shard_map/psum | solution.py:394
  133.7 49.3 %collective-permute-start.8 = (bf16[896,512]{1,0:T(8,128)(2,1)}, bf16[896,512]{1,0:T(8,128)(2,1)}, u32[]{:S(2)}, u32[]{:S(2)}) collective-permute-start(bf16[896,512]{1,0:T(8,128)(2,1)} %bitcast.7.refs_2_.refs_1_), channel_id=1, source_target_pairs={{0,8},{4,12},{8,0},{12,4},{16,24},{20,28},{24,16},{28,20},{1,9},{5... | collective-permute-start | bytes 2752520 | tf_op jit(solution)/shard_map/ppermute | solution.py:35
  135.1 49.5 %collective-permute-start.9 = (bf16[896,512]{1,0:T(8,128)(2,1)}, bf16[896,512]{1,0:T(8,128)(2,1)}, u32[]{:S(2)}, u32[]{:S(2)}) collective-permute-start(bf16[896,512]{1,0:T(8,128)(2,1)} %bitcast.7.refs_2_.refs_1_), channel_id=1, source_target_pairs={{0,16},{4,20},{8,24},{12,28},{16,0},{20,4},{24,8},{28,12},{1,17},{... | collective-permute-start | bytes 2752520 | tf_op jit(solution)/shard_map/ppermute | solution.py:35
  140.7 78.9 %collective-permute-start.2 = (bf16[448,768]{1,0:T(8,128)(2,1)}, bf16[448,768]{1,0:T(8,128)(2,1)}, u32[]{:S(2)}, u32[]{:S(2)}) collective-permute-start(bf16[448,768]{1,0:T(8,128)(2,1)} %slice.81), channel_id=1, source_target_pairs={{0,16},{4,20},{8,24},{12,28},{16,0},{20,4},{24,8},{28,12},{1,17},{... | collective-permute-start | bytes 2064392 | tf_op jit(solution)/shard_map/ppermute | solution.py:35
  163.4 58.9 %collective-permute-start.3 = (bf16[448,768]{1,0:T(8,128)(2,1)}, bf16[448,768]{1,0:T(8,128)(2,1)}, u32[]{:S(2)}, u32[]{:S(2)}) collective-permute-start(bf16[448,768]{1,0:T(8,128)(2,1)} %slice.82), channel_id=1, source_target_pairs={{0,8},{4,12},{8,0},{12,4},{16,24},{20,28},{24,16},{28,20},{1,9},{5... | collective-permute-start | bytes 2064392 | tf_op jit(solution)/shard_map/ppermute | solution.py:35
  169.3 54.1 %collective-permute-start.6 = (bf16[448,1024]{1,0:T(8,128)(2,1)}, bf16[448,1024]{1,0:T(8,128)(2,1)S(1)}, u32[]{:S(2)}, u32[]{:S(2)}) collective-permute-start(bf16[448,1024]{1,0:T(8,128)(2,1)} %slice.83), channel_id=1, source_target_pairs={{0,16},{4,20},{8,24},{12,28},{16,0},{20,4},{24,8},{28,12},{1,17},{... | collective-permute-start | bytes 2752520 | tf_op jit(solution)/shard_map/ppermute | solution.py:35
  183.1 40.5 %collective-permute-start.7 = (bf16[448,1024]{1,0:T(8,128)(2,1)}, bf16[448,1024]{1,0:T(8,128)(2,1)S(1)}, u32[]{:S(2)}, u32[]{:S(2)}) collective-permute-start(bf16[448,1024]{1,0:T(8,128)(2,1)} %slice.84), channel_id=1, source_target_pairs={{0,8},{4,12},{8,0},{12,4},{16,24},{20,28},{24,16},{28,20},{1,9},{5... | collective-permute-start | bytes 2752520 | tf_op jit(solution)/shard_map/ppermute | solution.py:35
  204.8 13.2 %copy-start.31 = (bf16[448,512]{1,0:T(8,128)(2,1)S(1)}, bf16[448,512]{1,0:T(8,128)(2,1)}, u32[]{:S(2)}) copy-start(bf16[448,512]{1,0:T(8,128)(2,1)} %slice.85) | copy-start | bytes 1376260
  204.8 15.9 %copy-start.30 = (bf16[448,512]{1,0:T(8,128)(2,1)S(1)}, bf16[448,512]{1,0:T(8,128)(2,1)}, u32[]{:S(2)}) copy-start(bf16[448,512]{1,0:T(8,128)(2,1)} %slice.86) | copy-start | bytes 1376260
  218.0 213.0 %all-reduce.8.cloned.1.call-start = ((), (), s32[]{:S(2)}) async-start(), calls=%async_computation.8 | async-start | bytes 1605632 | tf_op jit(solution)/shard_map/psum | solution.py:410
  218.0 12.3 %collective-permute-start.10 = (bf16[448,512]{1,0:T(8,128)(2,1)S(1)}, bf16[448,512]{1,0:T(8,128)(2,1)S(1)}, u32[]{:S(2)}, u32[]{:S(2)}) collective-permute-start(bf16[448,512]{1,0:T(8,128)(2,1)S(1)} %copy-done.31), channel_id=1, source_target_pairs={{0,16},{4,20},{8,24},{12,28},{16,0},{20,4},{24,8},{28,12},{1,17},{... | collective-permute-start | bytes 1376264 | tf_op jit(solution)/shard_map/ppermute | solution.py:35
  220.7 12.0 %collective-permute-start.11 = (bf16[448,512]{1,0:T(8,128)(2,1)S(1)}, bf16[448,512]{1,0:T(8,128)(2,1)S(1)}, u32[]{:S(2)}, u32[]{:S(2)}) collective-permute-start(bf16[448,512]{1,0:T(8,128)(2,1)S(1)} %copy-done.30), channel_id=1, source_target_pairs={{0,8},{4,12},{8,0},{12,4},{16,24},{20,28},{24,16},{28,20},{1,9},{5... | collective-permute-start | bytes 1376264 | tf_op jit(solution)/shard_map/ppermute | solution.py:35
  223.4 10.1 %copy-start.1 = (bf16[896,768]{1,0:T(8,128)(2,1)}, bf16[896,768]{1,0:T(8,128)(2,1)S(1)}, u32[]{:S(2)}) copy-start(bf16[896,768]{1,0:T(8,128)(2,1)S(1)} %constant_dynamic-update-slice_fusion.refs_3_) | copy-start | bytes 4128772
  223.4 53.8 %copy-start.12 = (bf16[448,1024]{1,0:T(8,128)(2,1)}, bf16[448,1024]{1,0:T(8,128)(2,1)S(1)}, u32[]{:S(2)}) copy-start(bf16[448,1024]{1,0:T(8,128)(2,1)S(1)} %collective-permute-done.6.refs_7_) | copy-start | bytes 2752516
  223.5 53.8 %copy-start.14 = (bf16[448,1024]{1,0:T(8,128)(2,1)}, bf16[448,1024]{1,0:T(8,128)(2,1)S(1)}, u32[]{:S(2)}) copy-start(bf16[448,1024]{1,0:T(8,128)(2,1)S(1)} %collective-permute-done.7.refs_8_) | copy-start | bytes 2752516
  223.6 10.0 %copy-start.29 = (bf16[896,1024]{1,0:T(8,128)(2,1)}, bf16[896,1024]{1,0:T(8,128)(2,1)S(1)}, u32[]{:S(2)}) copy-start(bf16[896,1024]{1,0:T(8,128)(2,1)S(1)} %constant_dynamic-update-slice_fusion.2.refs_4_) | copy-start | bytes 5505028
  239.2 36.5 %collective-permute-start.25 = (bf16[1,448,896]{2,1,0:T(8,128)(2,1)S(1)}, bf16[1,448,896]{2,1,0:T(8,128)(2,1)S(1)}, u32[]{:S(2)}, u32[]{:S(2)}) collective-permute-start(bf16[1,448,896]{2,1,0:T(8,128)(2,1)S(1)} %shard_map.26), channel_id=1, source_target_pairs={{0,1},{3,2},{4,5},{7,6},{8,9},{11,10},{12,13},{15,14},{16,17},{19,... | collective-permute-start | bytes 2408456 | tf_op jit(solution)/shard_map/ppermute | solution.py:318
  276.0 1.8 collective-permute-start.26
  276.7 100.5 %collective-permute-start.15 = (bf16[896,1024]{1,0:T(8,128)(2,1)}, bf16[896,1024]{1,0:T(8,128)(2,1)}, u32[]{:S(2)}, u32[]{:S(2)}) collective-permute-start(bf16[896,1024]{1,0:T(8,128)(2,1)} %collective-permute-done.4.refs_7_.refs_3_), channel_id=1, source_target_pairs={{0,4},{4,0},{8,12},{12,8},{16,20},{20,16},{24,28},{28,24},{1,5},{5... | collective-permute-start | bytes 5505032 | tf_op jit(solution)/shard_map/ppermute | solution.py:35
  276.8 101.8 %collective-permute-start.16 = (bf16[896,1024]{1,0:T(8,128)(2,1)}, bf16[896,1024]{1,0:T(8,128)(2,1)}, u32[]{:S(2)}, u32[]{:S(2)}) collective-permute-start(bf16[896,1024]{1,0:T(8,128)(2,1)} %collective-permute-done.5.refs_10_.refs_5_), channel_id=1, source_target_pairs={{0,4},{4,0},{8,12},{12,8},{16,20},{20,16},{24,28},{28,24},{1,5},{5... | collective-permute-start | bytes 5505032 | tf_op jit(solution)/shard_map/ppermute | solution.py:35
  277.3 89.0 %collective-permute-start.17 = (bf16[448,1024]{1,0:T(8,128)(2,1)S(1)}, bf16[448,1024]{1,0:T(8,128)(2,1)S(1)}, u32[]{:S(2)}, u32[]{:S(2)}) collective-permute-start(bf16[448,1024]{1,0:T(8,128)(2,1)S(1)} %collective-permute-done.6.refs_7_), channel_id=1, source_target_pairs={{0,4},{4,0},{8,12},{12,8},{16,20},{20,16},{24,28},{28,24},{1,5},{5... | collective-permute-start | bytes 2752520 | tf_op jit(solution)/shard_map/ppermute | solution.py:35
  277.3 91.2 %collective-permute-start.18 = (bf16[448,1024]{1,0:T(8,128)(2,1)S(1)}, bf16[448,1024]{1,0:T(8,128)(2,1)}, u32[]{:S(2)}, u32[]{:S(2)}) collective-permute-start(bf16[448,1024]{1,0:T(8,128)(2,1)S(1)} %collective-permute-done.7.refs_8_), channel_id=1, source_target_pairs={{0,4},{4,0},{8,12},{12,8},{16,20},{20,16},{24,28},{28,24},{1,5},{5... | collective-permute-start | bytes 2752520 | tf_op jit(solution)/shard_map/ppermute | solution.py:35
  364.8 37.3 %collective-permute-start.22 = (bf16[2,448,896]{2,1,0:T(8,128)(2,1)}, bf16[2,448,896]{2,1,0:T(8,128)(2,1)}, u32[]{:S(2)}, u32[]{:S(2)}) collective-permute-start(bf16[2,448,896]{2,1,0:T(8,128)(2,1)} %get-tuple-element.55), channel_id=1, source_target_pairs={{0,8},{4,12},{8,0},{12,4},{16,24},{20,28},{24,16},{28,20},{1,9},{5... | collective-permute-start | bytes 4816904 | tf_op jit(solution)/shard_map/ppermute | solution.py:35
  367.2 21.7 %collective-permute-start.27 = (bf16[1,448,896]{2,1,0:T(8,128)(2,1)}, bf16[1,448,896]{2,1,0:T(8,128)(2,1)}, u32[]{:S(2)}, u32[]{:S(2)}) collective-permute-start(bf16[1,448,896]{2,1,0:T(8,128)(2,1)} %add_convert_fusion), channel_id=1, source_target_pairs={{1,0},{2,3},{5,4},{6,7},{9,8},{10,11},{13,12},{14,15},{17,16},{18,... | collective-permute-start | bytes 2408456 | tf_op jit(solution)/shard_map/ppermute | solution.py:318
  368.5 54.3 %collective-permute-start.20 = (bf16[2,448,896]{2,1,0:T(8,128)(2,1)}, bf16[2,448,896]{2,1,0:T(8,128)(2,1)}, u32[]{:S(2)}, u32[]{:S(2)}) collective-permute-start(bf16[2,448,896]{2,1,0:T(8,128)(2,1)} %get-tuple-element.56), channel_id=1, source_target_pairs={{0,16},{4,20},{8,24},{12,28},{16,0},{20,4},{24,8},{28,12},{1,17},{... | collective-permute-start | bytes 4816904 | tf_op jit(solution)/shard_map/ppermute | solution.py:35
  377.2 16.9 %collective-permute-start.23 = (bf16[1,448,896]{2,1,0:T(8,128)(2,1)}, bf16[1,448,896]{2,1,0:T(8,128)(2,1)}, u32[]{:S(2)}, u32[]{:S(2)}) collective-permute-start(bf16[1,448,896]{2,1,0:T(8,128)(2,1)} %slice_bitcast_fusion.mine), channel_id=1, source_target_pairs={{0,4},{4,0},{8,12},{12,8},{16,20},{20,16},{24,28},{28,24},{1,5},{5... | collective-permute-start | bytes 2408456 | tf_op jit(solution)/shard_map/ppermute | solution.py:35
  378.6 27.7 %collective-permute-start.21 = (bf16[1,448,896]{2,1,0:T(8,128)(2,1)}, bf16[1,448,896]{2,1,0:T(8,128)(2,1)}, u32[]{:S(2)}, u32[]{:S(2)}) collective-permute-start(bf16[1,448,896]{2,1,0:T(8,128)(2,1)} %get-tuple-element.57), channel_id=1, source_target_pairs={{0,4},{4,0},{8,12},{12,8},{16,20},{20,16},{24,28},{28,24},{1,5},{5... | collective-permute-start | bytes 2408456 | tf_op jit(solution)/shard_map/ppermute | solution.py:35
  389.0 36.3 %collective-permute-start.19 = (bf16[1,448,896]{2,1,0:T(8,128)(2,1)}, bf16[1,448,896]{2,1,0:T(8,128)(2,1)}, u32[]{:S(2)}, u32[]{:S(2)}) collective-permute-start(bf16[1,448,896]{2,1,0:T(8,128)(2,1)} %get-tuple-element.58), channel_id=1, source_target_pairs={{0,4},{4,0},{8,12},{12,8},{16,20},{20,16},{24,28},{28,24},{1,5},{5... | collective-permute-start | bytes 2408456 | tf_op jit(solution)/shard_map/ppermute | solution.py:35
  389.0 165.1 %all-gather.6.cloned.1.call-start = ((), (), s32[]{:S(2)}) async-start(), calls=%async_computation.10 | async-start | bytes 16515072 | tf_op jit(solution)/shard_map/all_gather | solution.py:422
  394.1 39.3 %collective-permute-start.28 = (bf16[1,448,896]{2,1,0:T(8,128)(2,1)}, bf16[1,448,896]{2,1,0:T(8,128)(2,1)}, u32[]{:S(2)}, u32[]{:S(2)}) collective-permute-start(bf16[1,448,896]{2,1,0:T(8,128)(2,1)} %broadcast_select_fusion), channel_id=1, source_target_pairs={{0,4},{4,0},{8,12},{12,8},{16,20},{20,16},{24,28},{28,24},{1,5},{5... | collective-permute-start | bytes 2408456 | tf_op jit(solution)/shard_map/ppermute | solution.py:35
  402.1 31.2 %collective-permute-start.29 = (bf16[1,448,896]{2,1,0:T(8,128)(2,1)}, bf16[1,448,896]{2,1,0:T(8,128)(2,1)}, u32[]{:S(2)}, u32[]{:S(2)}) collective-permute-start(bf16[1,448,896]{2,1,0:T(8,128)(2,1)} %broadcast_select_fusion), channel_id=1, source_target_pairs={{0,24},{4,28},{8,16},{12,20},{16,8},{20,12},{24,0},{28,4},{1,25},{... | collective-permute-start | bytes 2408456 | tf_op jit(solution)/shard_map/ppermute | solution.py:35
  431.0 20.8 %copy-start.18 = (bf16[1,448,896]{2,1,0:T(8,128)(2,1)S(1)}, bf16[1,448,896]{2,1,0:T(8,128)(2,1)}, u32[]{:S(2)}) copy-start(bf16[1,448,896]{2,1,0:T(8,128)(2,1)} %all-reduce.8.cloned.1.call-done.mine) | copy-start | bytes 2408452
  431.0 20.8 %collective-permute-start.24 = (bf16[1,448,896]{2,1,0:T(8,128)(2,1)}, bf16[1,448,896]{2,1,0:T(8,128)(2,1)S(1)}, u32[]{:S(2)}, u32[]{:S(2)}) collective-permute-start(bf16[1,448,896]{2,1,0:T(8,128)(2,1)} %all-reduce.8.cloned.1.call-done.mine), channel_id=1, source_target_pairs={{0,24},{4,28},{8,16},{12,20},{16,8},{20,12},{24,0},{28,4},{1,25},{... | collective-permute-start | bytes 2408456 | tf_op jit(solution)/shard_map/ppermute | solution.py:35
  436.0 17.3 %copy-start.13 = (bf16[448,1024]{1,0:T(8,128)(2,1)S(1)}, bf16[448,1024]{1,0:T(8,128)(2,1)}, u32[]{:S(2)}) copy-start(bf16[448,1024]{1,0:T(8,128)(2,1)} %copy-done.12) | copy-start | bytes 2752516
  436.0 17.3 %copy-start.15 = (bf16[448,1024]{1,0:T(8,128)(2,1)S(1)}, bf16[448,1024]{1,0:T(8,128)(2,1)}, u32[]{:S(2)}) copy-start(bf16[448,1024]{1,0:T(8,128)(2,1)} %copy-done.14) | copy-start | bytes 2752516
  436.0 17.3 %copy-start.24 = (bf16[448,1024]{1,0:T(8,128)(2,1)S(1)}, bf16[448,1024]{1,0:T(8,128)(2,1)}, u32[]{:S(2)}) copy-start(bf16[448,1024]{1,0:T(8,128)(2,1)} %copy-done.23) | copy-start | bytes 2752516
  453.3 20.3 %copy-start.33 = (bf16[896,768]{1,0:T(8,128)(2,1)S(1)}, bf16[896,768]{1,0:T(8,128)(2,1)}, u32[]{:S(2)}) copy-start(bf16[896,768]{1,0:T(8,128)(2,1)} %copy-done.32) | copy-start | bytes 4128772
  473.5 9.7 %copy-start.9 = (bf16[4,224,768]{2,1,0:T(8,128)(2,1)S(1)}, bf16[4,224,768]{2,1,0:T(8,128)(2,1)}, u32[]{:S(2)}) copy-start(bf16[4,224,768]{2,1,0:T(8,128)(2,1)} %copy-done.7) | copy-start | bytes 4128772
  473.5 150.5 %all-gather.4.cloned.1.call-start = ((), (), s32[]{:S(2)}) async-start(), calls=%async_computation.9 | async-start | bytes 12386304 | tf_op jit(solution)/shard_map/all_gather | solution.py:422
  473.6 7.3 %collective-permute-start.30 = (bf16[896,768]{1,0:T(8,128)(2,1)S(1)}, bf16[896,768]{1,0:T(8,128)(2,1)S(1)}, u32[]{:S(2)}, u32[]{:S(2)}) collective-permute-start(bf16[896,768]{1,0:T(8,128)(2,1)S(1)} %copy-done.33), channel_id=1, source_target_pairs={{0,4},{4,0},{8,12},{12,8},{16,20},{20,16},{24,28},{28,24},{1,5},{5... | collective-permute-start | bytes 4128776 | tf_op jit(solution)/shard_map/ppermute | solution.py:35
  473.7 7.3 %collective-permute-start.31 = (bf16[896,768]{1,0:T(8,128)(2,1)}, bf16[896,768]{1,0:T(8,128)(2,1)S(1)}, u32[]{:S(2)}, u32[]{:S(2)}) collective-permute-start(bf16[896,768]{1,0:T(8,128)(2,1)} %collective-permute-done.1.refs_9_.refs_5_), channel_id=1, source_target_pairs={{0,4},{4,0},{8,12},{12,8},{16,20},{20,16},{24,28},{28,24},{1,5},{5... | collective-permute-start | bytes 4128776 | tf_op jit(solution)/shard_map/ppermute | solution.py:35
  474.2 5.8 collective-permute-start.32
  474.3 6.7 collective-permute-start.33
  499.2 55.0 %copy-start.4 = (bf16[4,224,1024]{2,1,0:T(8,128)(2,1)S(1)}, bf16[4,224,1024]{2,1,0:T(8,128)(2,1)}, u32[]{:S(2)}) copy-start(bf16[4,224,1024]{2,1,0:T(8,128)(2,1)} %copy-done.3) | copy-start | bytes 5505028
  499.2 177.9 %all-gather.8.cloned.1.call-start = ((), (), s32[]{:S(2)}) async-start(), calls=%async_computation.11 | async-start | bytes 8257536 | tf_op jit(solution)/shard_map/all_gather | solution.py:422
  499.2 5.4 collective-permute-start.34
  499.5 5.2 collective-permute-start.35
  499.8 4.1 collective-permute-start.36
  500.0 4.6 collective-permute-start.37
  677.4 37.4 %copy-start.28 = (bf16[4,224,768]{2,1,0:T(8,128)(2,1)S(1)}, bf16[4,224,768]{2,1,0:T(8,128)(2,1)}, u32[]{:S(2)}) copy-start(bf16[4,224,768]{2,1,0:T(8,128)(2,1)} %copy-done.27) | copy-start | bytes 4128772
  689.9 24.8 %copy-start.26 = (bf16[4,224,1024]{2,1,0:T(8,128)(2,1)S(1)}, bf16[4,224,1024]{2,1,0:T(8,128)(2,1)}, u32[]{:S(2)}) copy-start(bf16[4,224,1024]{2,1,0:T(8,128)(2,1)} %copy-done.25) | copy-start | bytes 5505028
  (21 other events, 58.1 us)
Sparse Core Ops, SparseCore 0:
  133.8 84.1 all-reduce.3
  220.5 140.2 all-reduce.5
  389.1 41.8 all-reduce.7
  473.7 80.4 all-gather.5
  555.9 65.4 all-gather.3
  623.1 49.9 all-gather.7

commit v11 on v10

--- a/solution.py
+++ b/solution.py
@@ -401,10 +401,9 @@
 
     j = chips[-1]
     peers = peers_of(j)
-    far = [
-        gram_pieces([lefts[i], peers], [(0, 1, 0, 0)], [low_of(j)[0]], scale)
-        for i in range(bit_x)
-    ]
+    jobs = [(i, bit_x, 0, 0) for i in range(bit_x)]
+    far = gram_pieces(lefts + [peers], jobs, [low_of(j)[0]], scale)
+    far = [far[i : i + 1] for i in range(bit_x)]
     arrivals = {}
     lines = {i: sum_on_line(far[i], arrivals) for i in cores}
     sums = lax.psum(after(far[0], last, *panels[1].values()), "col")

time: 734 us -> 734 us (level)
    psum x1, waiting for transfers between devices: 2.93 us -> 15.2 us  [per_device(): sums = lax.psum(after(far[0], last, *panels[1].values()), 'col')]
    psum x1, waiting for transfers between devices: 13.1 us -> 1.47 us  [per_device(): last = near = lax.psum(near, 'col')]
    unnamed x79 -> x52, local copies, waits for them, and re-layouts: 16.4 us -> 12.5 us
    pallas_call x3 -> x2, Pallas kernels: 27 us -> 26.8 us  [gram_pieces(): pl.pallas_call(functools.partial(pieces_kernel, count, jobs, scale), out_...]
  transfers between devices with their start and end apart: 47 -> 47, of which waited for: 22 -> 21; matrix products, arithmetic and copies ran while one was open for 4% -> 5% of each run, Pallas kernels for 17% -> 17%
where the time goes in v11:
time: 734 us; the launch traced here: 724 us
  waiting for transfers between devices  350 us (48%)
  Pallas kernels  154 us (21%)
  blocking collectives  107 us (15%)
  starting transfers between devices  45.5 us (6%)
  local copies, waits for them, and re-layouts  40.8 us (6%)
  between operations  14.3 us (2%)
  other arithmetic  12.8 us (2%)
    ppermute x35, waiting for transfers between devices, swap(): return lax.ppermute(value, 'row', [(r, r ^ bit) for r in range(count)])  108 us
    all_to_all x3, blocking collectives, per_device(): lax.all_to_all(result, 'col', split_axis=0, concat_axis=1, tiled=True)  107 us
    pallas_call x6, Pallas kernels, product(): pl.pallas_call(functools.partial(product_kernel, keys, start, bool(extra)...  98.2 us
    psum x1, waiting for transfers between devices, per_device(): last = sums = lax.psum(after(pieces, last), 'col')  80.5 us
    all_to_all x3, waiting for transfers between devices, exchange(): return lax.all_to_all(value, 'col', split_axis=0, concat_axis=0, tiled=True)  61.1 us
    ppermute x3, waiting for transfers between devices, send(): arrived = lax.ppermute(value, 'col', pairs)  50 us
    all_gather x3, waiting for transfers between devices, per_device(): first_panel = lax.all_gather(first, 'row', axis=0, tiled=True)  32.9 us
    ppermute x35, starting transfers between devices, swap(): return lax.ppermute(value, 'row', [(r, r ^ bit) for r in range(count)])  27.8 us
  transfers between devices with their start and end apart: 47, of which 21 were waited for; matrix products, arithmetic and copies ran while one was open for 5% of the time, Pallas kernels for 17%

profile of v11, /device:TPU:0, one launch (start us, length us, event | category | flops | bytes accessed | tf_op | source)
XLA Modules:
  0.0 724.0 jit_solution(9225418386338873766)
XLA Ops:
  9.1 6.3 all-to-all-start
  15.4 1.6 fusion.1
  18.4 29.8 %all-to-all-done = bf16[4,224,768]{2,1,0:T(8,128)(2,1)S(1)} async-done(((bf16[4,224,768]{2,1,0:T(8,128)(2,1)}), bf16[4,224,768]{2,1,0:T(8,128)(2,1)S(1)}, u32[]{:S(2)}, u32[]{:S(2)}) %all-to-all-start) | async-done | bytes 1376288 | tf_op jit(solution)/shard_map/all_to_all | solution.py:350
  48.2 3.6 all-to-all-start.1
  51.8 1.6 collective-permute-start
  53.3 1.5 collective-permute-start.1
  57.2 25.8 %collective-permute-done.refs_6_.refs_3_ = bf16[896,768]{1,0:T(8,128)(2,1)S(1)} collective-permute-done((bf16[896,768]{1,0:T(8,128)(2,1)S(1)}, bf16[896,768]{1,0:T(8,128)(2,1)S(1)}, u32[]{:S(2)}, u32[]{:S(2)}) %collective-permute-start) | collective-permute-done | bytes 1376288 | tf_op jit(solution)/shard_map/ppermute | solution.py:35
  84.3 9.5 %all-to-all-done.1 = bf16[4,224,1024]{2,1,0:T(8,128)(2,1)S(1)} async-done(((bf16[4,224,1024]{2,1,0:T(8,128)(2,1)}), bf16[4,224,1024]{2,1,0:T(8,128)(2,1)S(1)}, u32[]{:S(2)}, u32[]{:S(2)}) %all-to-all-start.1) | async-done | bytes 1835040 | tf_op jit(solution)/shard_map/all_to_all | solution.py:350
  93.8 4.2 all-to-all-start.2
  98.7 21.8 %all-to-all-done.2 = bf16[4,224,512]{2,1,0:T(8,128)(2,1)} async-done(((bf16[4,224,512]{2,1,0:T(8,128)(2,1)}), bf16[4,224,512]{2,1,0:T(8,128)(2,1)}, u32[]{:S(2)}, u32[]{:S(2)}) %all-to-all-start.2) | async-done | bytes 917536 | tf_op jit(solution)/shard_map/all_to_all | solution.py:350
  120.5 1.5 collective-permute-start.7
  122.0 1.5 collective-permute-start.8
  123.5 10.1 %shard_map.19 = bf16[1152,896]{1,0:T(8,128)(2,1)} custom-call(s32[1]{0:T(128)} %bitcast.9.low_ref, bf16[896,768]{1,0:T(8,128)(2,1)S(1)} %bitcast.36, bf16[896,1024]{1,0:T(8,128)(2,1)} %bitcast.28, bf16[896,512]{1,0:T(8,128)(2,1)} %bitcast.7.refs_2_.refs_1_, bf16[896,768]{1,0:T(8,128)(2,1)} %collective-permute-done.2.refs_3_.refs_2_, ...), custom_call_target="tpu_custom_call" | custom-call | flops 4756340736 | bytes 10321920 | tf_op jit(solution)/shard_map/pallas_call | solution.py:197
  135.1 1.5 collective-permute-start.12
  136.6 2.0 slice.87
  138.6 2.0 slice.88
  141.2 22.2 %collective-permute-done.7.refs_7_.refs_3_ = bf16[896,1024]{1,0:T(8,128)(2,1)} collective-permute-done((bf16[896,1024]{1,0:T(8,128)(2,1)S(1)}, bf16[896,1024]{1,0:T(8,128)(2,1)}, u32[]{:S(2)}, u32[]{:S(2)}) %collective-permute-start.7) | collective-permute-done | bytes 1835040 | tf_op jit(solution)/shard_map/ppermute | solution.py:35
  163.4 1.5 collective-permute-done.8.refs_10_.refs_5_
  164.9 2.2 slice.89
  167.1 2.2 slice.90
  169.8 1.5 collective-permute-start.9
  171.4 11.7 %collective-permute-done.11.refs_8_.refs_3_ = bf16[896,512]{1,0:T(8,128)(2,1)} collective-permute-done((bf16[896,512]{1,0:T(8,128)(2,1)}, bf16[896,512]{1,0:T(8,128)(2,1)}, u32[]{:S(2)}, u32[]{:S(2)}) %collective-permute-start.11) | collective-permute-done | bytes 917536 | tf_op jit(solution)/shard_map/ppermute | solution.py:35
  184.6 1.8 slice.91
  187.5 1.6 collective-permute-start.13
  189.1 10.3 %collective-permute-done.5.refs_7_ = bf16[448,768]{1,0:T(8,128)(2,1)} collective-permute-done((bf16[448,768]{1,0:T(8,128)(2,1)}, bf16[448,768]{1,0:T(8,128)(2,1)}, u32[]{:S(2)}, u32[]{:S(2)}) %collective-permute-start.5) | collective-permute-done | bytes 688160 | tf_op jit(solution)/shard_map/ppermute | solution.py:35
  199.9 16.6 %shard_map.18 = bf16[4,448,896]{2,1,0:T(8,128)(2,1)} custom-call(s32[2]{0:T(128)S(1)} %pad_add_fusion.low_ref, bf16[896,768]{1,0:T(8,128)(2,1)S(1)} %bitcast.37, bf16[896,1024]{1,0:T(8,128)(2,1)} %bitcast.29, bf16[896,512]{1,0:T(8,128)(2,1)} %bitcast.7.refs_2_.refs_1_, bf16[896,768]{1,0:T(8,128)(2,1)} %collective-permute-done.2.refs_3_.refs_2_, ...), custom_call_target="tpu_custom_call" | custom-call | flops 7398752256 | bytes 19726336 | tf_op jit(solution)/shard_map/pallas_call | solution.py:103
  218.0 2.5 pad_maximum_fusion.3.refs_6_
  220.6 2.9 pad_maximum_fusion.1.refs_7_
  223.5 4.5 collective-permute-done.13.refs_7_
  228.1 10.2 %shard_map.17 = bf16[2,448,896]{2,1,0:T(8,128)(2,1)} custom-call(s32[1]{0:T(128)} %bitcast.1.low_ref, bf16[896,768]{1,0:T(8,128)(2,1)S(1)} %bitcast.38, bf16[896,1024]{1,0:T(8,128)(2,1)} %bitcast.30, bf16[896,512]{1,0:T(8,128)(2,1)} %bitcast.7.refs_2_.refs_1_, bf16[896,768]{1,0:T(8,128)(2,1)} %collective-permute-done.2.refs_3_.refs_2_, ...), custom_call_target="tpu_custom_call" | custom-call | flops 3699376128 | bytes 13991936 | tf_op jit(solution)/shard_map/pallas_call | solution.py:103
  238.4 2.5 fusion.5
  242.2 35.1 %collective-permute-done.25 = bf16[1,448,896]{2,1,0:T(8,128)(2,1)S(1)} collective-permute-done((bf16[1,448,896]{2,1,0:T(8,128)(2,1)S(1)}, bf16[1,448,896]{2,1,0:T(8,128)(2,1)S(1)}, u32[]{:S(2)}, u32[]{:S(2)}) %collective-permute-start.25) | collective-permute-done | bytes 802848 | tf_op jit(solution)/shard_map/ppermute | solution.py:318
  280.4 80.5 %all-reduce.6.cloned.1.call-done.mine = bf16[4,448,896]{2,1,0:T(8,128)(2,1)} async-done(((bf16[4,448,896]{2,1,0:T(8,128)(2,1)}), bf16[4,448,896]{2,1,0:T(8,128)(2,1)}) %all-reduce.6.cloned.1.call-update) | async-done | bytes 3211280 | tf_op jit(solution)/shard_map/psum | solution.py:394
  360.8 4.0 fusion.3
  367.6 1.5 collective-permute-start.20
  369.1 2.1 slice_bitcast_fusion.mine
  373.1 15.0 %collective-permute-done.27 = bf16[1,448,896]{2,1,0:T(8,128)(2,1)} collective-permute-done((bf16[1,448,896]{2,1,0:T(8,128)(2,1)}, bf16[1,448,896]{2,1,0:T(8,128)(2,1)}, u32[]{:S(2)}, u32[]{:S(2)}) %collective-permute-start.27) | collective-permute-done | bytes 802848 | tf_op jit(solution)/shard_map/ppermute | solution.py:318
  388.1 1.6 copy-done.5
  391.0 2.1 broadcast_select_fusion
  393.7 2.7 shard_map.21.gram_in
  396.4 5.8 collective-permute-done.22.theirs
  402.2 2.4 collective-permute-start.29
  404.5 2.4 shard_map.22.gram_in
  407.0 2.7 shard_map.23.gram_in
  409.7 2.5 shard_map.24.gram_in
  412.1 2.8 shard_map.25.gram_in
  414.9 15.2 %all-reduce.8.cloned.1.call-done.mine = bf16[1,448,896]{2,1,0:T(8,128)(2,1)} async-done(((bf16[1,448,896]{2,1,0:T(8,128)(2,1)}), bf16[1,448,896]{2,1,0:T(8,128)(2,1)}) %all-reduce.8.cloned.1.call-update) | async-done | bytes 802832 | tf_op jit(solution)/shard_map/psum | solution.py:409
  430.1 2.4 collective-permute-start.24
  432.5 2.7 shard_map.26.gram_in
  435.1 15.7 %collective-permute-done.24.theirs = bf16[1,448,896]{2,1,0:T(8,128)(2,1)S(1)} collective-permute-done((bf16[1,448,896]{2,1,0:T(8,128)(2,1)}, bf16[1,448,896]{2,1,0:T(8,128)(2,1)S(1)}, u32[]{:S(2)}, u32[]{:S(2)}) %collective-permute-start.24) | collective-permute-done | bytes 802848 | tf_op jit(solution)/shard_map/ppermute | solution.py:35
  450.9 1.6 shard_map.27.refs_0_
  452.4 20.2 %shard_map.28.refs_11_.refs_3_ = bf16[896,1024]{1,0:T(8,128)(2,1)} custom-call(s32[1]{0:T(128)} %bitcast.me_ref, bf16[8,896,896]{2,1,0:T(8,128)(2,1)} %shard_map.27.refs_0_, bf16[896,1024]{1,0:T(8,128)(2,1)} %bitcast.31, bf16[896,1024]{1,0:T(8,128)(2,1)} %collective-permute-done.3.refs_4_.refs_2_, bf16[896,1024]{1,0:T(8,128)(2,1)} %collective-permute-done.7.refs_7_.refs_3_, ...), custom_call_target="tpu_custom_call" | custom-call | flops 13153337344 | bytes 27525120 | tf_op jit(solution)/shard_map/pallas_call | solution.py:286
  473.9 6.3 collective-permute-done.32.refs_9_
  482.4 15.9 %shard_map.29.refs_3_.refs_11_ = bf16[896,768]{1,0:T(8,128)(2,1)} custom-call(s32[1]{0:T(128)} %bitcast.me_ref, bf16[8,896,896]{2,1,0:T(8,128)(2,1)} %shard_map.27.refs_0_, bf16[896,768]{1,0:T(8,128)(2,1)S(1)} %bitcast.39, bf16[896,768]{1,0:T(8,128)(2,1)} %collective-permute-done.2.refs_3_.refs_2_, bf16[896,768]{1,0:T(8,128)(2,1)} %copy-done.20, ...), custom_call_target="tpu_custom_call" | custom-call | flops 9865003008 | bytes 23855104 | tf_op jit(solution)/shard_map/pallas_call | solution.py:286
  499.5 3.6 collective-permute-done.36.refs_9_
  507.7 11.8 %shard_map.32.refs_3_ = bf16[896,512]{1,0:T(8,128)(2,1)S(1)} custom-call(s32[1]{0:T(128)} %bitcast.me_ref, bf16[8,896,896]{2,1,0:T(8,128)(2,1)} %shard_map.27.refs_0_, bf16[896,512]{1,0:T(8,128)(2,1)} %bitcast.7.refs_2_.refs_1_, bf16[896,512]{1,0:T(8,128)(2,1)} %collective-permute-done.4.refs_5_.refs_2_, ...), custom_call_target="tpu_custom_call" | custom-call | flops 6576668672 | bytes 20185088 | tf_op jit(solution)/shard_map/pallas_call | solution.py:286
  520.4 32.8 %all-gather.6.cloned.1.call-done.refs_1_ = bf16[7168,1024]{1,0:T(8,128)(2,1)} async-done(((bf16[896,1024]{1,0:T(8,128)(2,1)}), bf16[7168,1024]{1,0:T(8,128)(2,1)}) %all-gather.6.cloned.1.call-update) | async-done | bytes 14680080 | tf_op jit(solution)/shard_map/all_gather | solution.py:421
  553.2 21.1 %shard_map.30 = bf16[896,1024]{1,0:T(8,128)(2,1)S(1)} custom-call(s32[1]{0:T(128)} %bitcast.me_ref, bf16[8,896,896]{2,1,0:T(8,128)(2,1)} %shard_map.27.refs_0_, bf16[7168,1024]{1,0:T(8,128)(2,1)} %all-gather.6.cloned.1.call-done.refs_1_, bf16[896,1024]{1,0:T(8,128)(2,1)S(1)} %bitcast.32, bf16[896,1024]{1,0:T(8,128)(2,1)} %shard_map.28.refs_11_.refs_3_), custom_call_target="tpu_custom_call" | custom-call | flops 13153337344 | bytes 27525120 | tf_op jit(solution)/shard_map/pallas_call | solution.py:286
  574.3 47.4 %all_to_all.87 = bf16[4,224,1024]{2,1,0:T(8,128)(2,1)S(1)} all-to-all(bf16[4,224,1024]{2,1,0:T(8,128)(2,1)S(1)} %bitcast.42), channel_id=1, replica_groups=mesh['row'=8,'col'=4] {'col'}, dimensions={0} | all-to-all | bytes 3670016 | tf_op jit(solution)/shard_map/all_to_all | solution.py:424
  623.2 16.8 %shard_map.31 = bf16[896,768]{1,0:T(8,128)(2,1)S(1)} custom-call(s32[1]{0:T(128)} %bitcast.me_ref, bf16[8,896,896]{2,1,0:T(8,128)(2,1)} %shard_map.27.refs_0_, bf16[7168,768]{1,0:T(8,128)(2,1)} %all-gather.4.cloned.1.call-done.refs_1_, bf16[896,768]{1,0:T(8,128)(2,1)S(1)} %bitcast.40, bf16[896,768]{1,0:T(8,128)(2,1)} %shard_map.29.refs_3_.refs_11_, ...), custom_call_target="tpu_custom_call" | custom-call | flops 9865003008 | bytes 23855104 | tf_op jit(solution)/shard_map/pallas_call | solution.py:286
  639.9 34.9 %all_to_all.88 = bf16[4,224,768]{2,1,0:T(8,128)(2,1)S(1)} all-to-all(bf16[4,224,768]{2,1,0:T(8,128)(2,1)S(1)} %bitcast.44), channel_id=1, replica_groups=mesh['row'=8,'col'=4] {'col'}, dimensions={0} | all-to-all | bytes 2752512 | tf_op jit(solution)/shard_map/all_to_all | solution.py:424
  676.5 12.5 %shard_map.33 = bf16[896,512]{1,0:T(8,128)(2,1)S(1)} custom-call(s32[1]{0:T(128)} %bitcast.me_ref, bf16[8,896,896]{2,1,0:T(8,128)(2,1)} %shard_map.27.refs_0_, bf16[7168,512]{1,0:T(8,128)(2,1)} %all-gather.8.cloned.1.call-done.refs_1_, bf16[896,512]{1,0:T(8,128)(2,1)} %bitcast.7.refs_2_.refs_1_, bf16[896,512]{1,0:T(8,128)(2,1)S(1)} %copy-done.7, ...), custom_call_target="tpu_custom_call" | custom-call | flops 6576668672 | bytes 20185088 | tf_op jit(solution)/shard_map/pallas_call | solution.py:286
  689.1 24.8 %all_to_all.89 = bf16[4,224,512]{2,1,0:T(8,128)(2,1)S(1)} all-to-all(bf16[4,224,512]{2,1,0:T(8,128)(2,1)S(1)} %bitcast.45), channel_id=1, replica_groups=mesh['row'=8,'col'=4] {'col'}, dimensions={0} | all-to-all | bytes 1835008 | tf_op jit(solution)/shard_map/all_to_all | solution.py:424
  714.2 2.5 copy.19
  (135 shorter events, 40.0 us)
Async XLA Ops:
  9.1 39.1 %all-to-all-start = ((bf16[4,224,768]{2,1,0:T(8,128)(2,1)}), bf16[4,224,768]{2,1,0:T(8,128)(2,1)S(1)}, u32[]{:S(2)}, u32[]{:S(2)}) async-start(bf16[4,224,768]{2,1,0:T(8,128)(2,1)} %bitcast.2), calls=%async_computation | async-start | bytes 2752512 | tf_op jit(solution)/shard_map/all_to_all | solution.py:350
  48.2 179.9 %copy-start.3 = (bf16[4,224,768]{2,1,0:T(8,128)(2,1)}, bf16[4,224,768]{2,1,0:T(8,128)(2,1)S(1)}, u32[]{:S(2)}) copy-start(bf16[4,224,768]{2,1,0:T(8,128)(2,1)S(1)} %all-to-all-done) | copy-start | bytes 4128772
  48.2 45.6 %all-to-all-start.1 = ((bf16[4,224,1024]{2,1,0:T(8,128)(2,1)}), bf16[4,224,1024]{2,1,0:T(8,128)(2,1)S(1)}, u32[]{:S(2)}, u32[]{:S(2)}) async-start(bf16[4,224,1024]{2,1,0:T(8,128)(2,1)} %bitcast.50), calls=%async_computation.1 | async-start | bytes 3670016 | tf_op jit(solution)/shard_map/all_to_all | solution.py:350
  51.8 31.2 %collective-permute-start = (bf16[896,768]{1,0:T(8,128)(2,1)S(1)}, bf16[896,768]{1,0:T(8,128)(2,1)S(1)}, u32[]{:S(2)}, u32[]{:S(2)}) collective-permute-start(bf16[896,768]{1,0:T(8,128)(2,1)S(1)} %bitcast.33), channel_id=1, source_target_pairs={{0,8},{4,12},{8,0},{12,4},{16,24},{20,28},{24,16},{28,20},{1,9},{5... | collective-permute-start | bytes 4128776 | tf_op jit(solution)/shard_map/ppermute | solution.py:35
  53.3 31.0 %collective-permute-start.1 = (bf16[896,768]{1,0:T(8,128)(2,1)S(1)}, bf16[896,768]{1,0:T(8,128)(2,1)}, u32[]{:S(2)}, u32[]{:S(2)}) collective-permute-start(bf16[896,768]{1,0:T(8,128)(2,1)S(1)} %bitcast.34), channel_id=1, source_target_pairs={{0,16},{4,20},{8,24},{12,28},{16,0},{20,4},{24,8},{28,12},{1,17},{... | collective-permute-start | bytes 4128776 | tf_op jit(solution)/shard_map/ppermute | solution.py:35
  93.8 29.7 %copy-start.1 = (bf16[4,224,1024]{2,1,0:T(8,128)(2,1)}, bf16[4,224,1024]{2,1,0:T(8,128)(2,1)S(1)}, u32[]{:S(2)}) copy-start(bf16[4,224,1024]{2,1,0:T(8,128)(2,1)S(1)} %all-to-all-done.1) | copy-start | bytes 5505028
  93.8 26.7 %all-to-all-start.2 = ((bf16[4,224,512]{2,1,0:T(8,128)(2,1)}), bf16[4,224,512]{2,1,0:T(8,128)(2,1)}, u32[]{:S(2)}, u32[]{:S(2)}) async-start(bf16[4,224,512]{2,1,0:T(8,128)(2,1)} %bitcast.51), calls=%async_computation.2 | async-start | bytes 1835008 | tf_op jit(solution)/shard_map/all_to_all | solution.py:350
  98.0 119.9 %all-reduce.4.cloned.1.call-start = ((), (), s32[]{:S(2)}) async-start(), calls=%async_computation.6 | async-start | bytes 4128768 | tf_op jit(solution)/shard_map/psum | solution.py:375
  98.1 25.4 %collective-permute-start.3 = (bf16[896,1024]{1,0:T(8,128)(2,1)S(1)}, bf16[896,1024]{1,0:T(8,128)(2,1)}, u32[]{:S(2)}, u32[]{:S(2)}) collective-permute-start(bf16[896,1024]{1,0:T(8,128)(2,1)S(1)} %bitcast.25), channel_id=1, source_target_pairs={{0,4},{4,0},{8,12},{12,8},{16,20},{20,16},{24,28},{28,24},{1,5},{5... | collective-permute-start | bytes 5505032 | tf_op jit(solution)/shard_map/ppermute | solution.py:35
  98.2 25.4 %collective-permute-start.2 = (bf16[896,768]{1,0:T(8,128)(2,1)S(1)}, bf16[896,768]{1,0:T(8,128)(2,1)}, u32[]{:S(2)}, u32[]{:S(2)}) collective-permute-start(bf16[896,768]{1,0:T(8,128)(2,1)S(1)} %bitcast.35), channel_id=1, source_target_pairs={{0,4},{4,0},{8,12},{12,8},{16,20},{20,16},{24,28},{28,24},{1,5},{5... | collective-permute-start | bytes 4128776 | tf_op jit(solution)/shard_map/ppermute | solution.py:35
  120.5 3.0 collective-permute-start.4
  120.5 42.9 %collective-permute-start.7 = (bf16[896,1024]{1,0:T(8,128)(2,1)S(1)}, bf16[896,1024]{1,0:T(8,128)(2,1)}, u32[]{:S(2)}, u32[]{:S(2)}) collective-permute-start(bf16[896,1024]{1,0:T(8,128)(2,1)S(1)} %bitcast.26), channel_id=1, source_target_pairs={{0,8},{4,12},{8,0},{12,4},{16,24},{20,28},{24,16},{28,20},{1,9},{5... | collective-permute-start | bytes 5505032 | tf_op jit(solution)/shard_map/ppermute | solution.py:35
  122.0 43.0 %collective-permute-start.8 = (bf16[896,1024]{1,0:T(8,128)(2,1)S(1)}, bf16[896,1024]{1,0:T(8,128)(2,1)}, u32[]{:S(2)}, u32[]{:S(2)}) collective-permute-start(bf16[896,1024]{1,0:T(8,128)(2,1)S(1)} %bitcast.27), channel_id=1, source_target_pairs={{0,16},{4,20},{8,24},{12,28},{16,0},{20,4},{24,8},{28,12},{1,17},{... | collective-permute-start | bytes 5505032 | tf_op jit(solution)/shard_map/ppermute | solution.py:35
  133.7 227.1 %all-reduce.6.cloned.1.call-start = ((), (), s32[]{:S(2)}) async-start(), calls=%async_computation.7 | async-start | bytes 6422528 | tf_op jit(solution)/shard_map/psum | solution.py:394
  133.7 49.3 %collective-permute-start.11 = (bf16[896,512]{1,0:T(8,128)(2,1)}, bf16[896,512]{1,0:T(8,128)(2,1)}, u32[]{:S(2)}, u32[]{:S(2)}) collective-permute-start(bf16[896,512]{1,0:T(8,128)(2,1)} %bitcast.7.refs_2_.refs_1_), channel_id=1, source_target_pairs={{0,8},{4,12},{8,0},{12,4},{16,24},{20,28},{24,16},{28,20},{1,9},{5... | collective-permute-start | bytes 2752520 | tf_op jit(solution)/shard_map/ppermute | solution.py:35
  135.1 49.5 %collective-permute-start.12 = (bf16[896,512]{1,0:T(8,128)(2,1)}, bf16[896,512]{1,0:T(8,128)(2,1)}, u32[]{:S(2)}, u32[]{:S(2)}) collective-permute-start(bf16[896,512]{1,0:T(8,128)(2,1)} %bitcast.7.refs_2_.refs_1_), channel_id=1, source_target_pairs={{0,16},{4,20},{8,24},{12,28},{16,0},{20,4},{24,8},{28,12},{1,17},{... | collective-permute-start | bytes 2752520 | tf_op jit(solution)/shard_map/ppermute | solution.py:35
  140.6 58.7 %collective-permute-start.5 = (bf16[448,768]{1,0:T(8,128)(2,1)}, bf16[448,768]{1,0:T(8,128)(2,1)}, u32[]{:S(2)}, u32[]{:S(2)}) collective-permute-start(bf16[448,768]{1,0:T(8,128)(2,1)} %slice.87), channel_id=1, source_target_pairs={{0,16},{4,20},{8,24},{12,28},{16,0},{20,4},{24,8},{28,12},{1,17},{... | collective-permute-start | bytes 2064392 | tf_op jit(solution)/shard_map/ppermute | solution.py:35
  169.3 51.3 %collective-permute-start.10 = (bf16[448,1024]{1,0:T(8,128)(2,1)}, bf16[448,1024]{1,0:T(8,128)(2,1)}, u32[]{:S(2)}, u32[]{:S(2)}) collective-permute-start(bf16[448,1024]{1,0:T(8,128)(2,1)} %slice.90), channel_id=1, source_target_pairs={{0,8},{4,12},{8,0},{12,4},{16,24},{20,28},{24,16},{28,20},{1,9},{5... | collective-permute-start | bytes 2752520 | tf_op jit(solution)/shard_map/ppermute | solution.py:35
  169.8 50.8 %collective-permute-start.9 = (bf16[448,1024]{1,0:T(8,128)(2,1)}, bf16[448,1024]{1,0:T(8,128)(2,1)}, u32[]{:S(2)}, u32[]{:S(2)}) collective-permute-start(bf16[448,1024]{1,0:T(8,128)(2,1)} %slice.89), channel_id=1, source_target_pairs={{0,16},{4,20},{8,24},{12,28},{16,0},{20,4},{24,8},{28,12},{1,17},{... | collective-permute-start | bytes 2752520 | tf_op jit(solution)/shard_map/ppermute | solution.py:35
  183.1 34.9 %collective-permute-start.6 = (bf16[448,768]{1,0:T(8,128)(2,1)}, bf16[448,768]{1,0:T(8,128)(2,1)S(1)}, u32[]{:S(2)}, u32[]{:S(2)}) collective-permute-start(bf16[448,768]{1,0:T(8,128)(2,1)} %slice.88), channel_id=1, source_target_pairs={{0,8},{4,12},{8,0},{12,4},{16,24},{20,28},{24,16},{28,20},{1,9},{5... | collective-permute-start | bytes 2064392 | tf_op jit(solution)/shard_map/ppermute | solution.py:35
  187.5 40.6 %collective-permute-start.13 = (bf16[448,512]{1,0:T(8,128)(2,1)}, bf16[448,512]{1,0:T(8,128)(2,1)S(1)}, u32[]{:S(2)}, u32[]{:S(2)}) collective-permute-start(bf16[448,512]{1,0:T(8,128)(2,1)} %slice.91), channel_id=1, source_target_pairs={{0,16},{4,20},{8,24},{12,28},{16,0},{20,4},{24,8},{28,12},{1,17},{... | collective-permute-start | bytes 1376264 | tf_op jit(solution)/shard_map/ppermute | solution.py:35
  199.4 28.7 %collective-permute-start.14 = (bf16[448,512]{1,0:T(8,128)(2,1)S(1)}, bf16[448,512]{1,0:T(8,128)(2,1)S(1)}, u32[]{:S(2)}, u32[]{:S(2)}) collective-permute-start(bf16[448,512]{1,0:T(8,128)(2,1)S(1)} %slice.92), channel_id=1, source_target_pairs={{0,8},{4,12},{8,0},{12,4},{16,24},{20,28},{24,16},{28,20},{1,9},{5... | collective-permute-start | bytes 1376264 | tf_op jit(solution)/shard_map/ppermute | solution.py:35
  218.0 212.1 %all-reduce.8.cloned.1.call-start = ((), (), s32[]{:S(2)}) async-start(), calls=%async_computation.8 | async-start | bytes 1605632 | tf_op jit(solution)/shard_map/psum | solution.py:409
  218.0 5.5 copy-start.9
  228.0 10.3 %copy-start.11 = (bf16[448,512]{1,0:T(8,128)(2,1)}, bf16[448,512]{1,0:T(8,128)(2,1)S(1)}, u32[]{:S(2)}) copy-start(bf16[448,512]{1,0:T(8,128)(2,1)S(1)} %collective-permute-done.13.refs_7_) | copy-start | bytes 1376260
  228.0 10.3 %copy-start.13 = (bf16[448,512]{1,0:T(8,128)(2,1)}, bf16[448,512]{1,0:T(8,128)(2,1)S(1)}, u32[]{:S(2)}) copy-start(bf16[448,512]{1,0:T(8,128)(2,1)S(1)} %collective-permute-done.14.refs_8_) | copy-start | bytes 1376260
  238.4 38.9 %copy-start.19 = (bf16[2,448,896]{2,1,0:T(8,128)(2,1)S(1)}, bf16[2,448,896]{2,1,0:T(8,128)(2,1)}, u32[]{:S(2)}) copy-start(bf16[2,448,896]{2,1,0:T(8,128)(2,1)} %shard_map.17) | copy-start | bytes 4816900
  240.9 36.4 %collective-permute-start.25 = (bf16[1,448,896]{2,1,0:T(8,128)(2,1)S(1)}, bf16[1,448,896]{2,1,0:T(8,128)(2,1)S(1)}, u32[]{:S(2)}, u32[]{:S(2)}) collective-permute-start(bf16[1,448,896]{2,1,0:T(8,128)(2,1)S(1)} %get-tuple-element.59), channel_id=1, source_target_pairs={{0,1},{3,2},{4,5},{7,6},{8,9},{11,10},{12,13},{15,14},{16,17},{19,... | collective-permute-start | bytes 2408456 | tf_op jit(solution)/shard_map/ppermute | solution.py:318
  277.5 1.8 collective-permute-start.26
  278.2 93.0 %collective-permute-start.15 = (bf16[896,1024]{1,0:T(8,128)(2,1)}, bf16[896,1024]{1,0:T(8,128)(2,1)}, u32[]{:S(2)}, u32[]{:S(2)}) collective-permute-start(bf16[896,1024]{1,0:T(8,128)(2,1)} %collective-permute-done.7.refs_7_.refs_3_), channel_id=1, source_target_pairs={{0,4},{4,0},{8,12},{12,8},{16,20},{20,16},{24,28},{28,24},{1,5},{5... | collective-permute-start | bytes 5505032 | tf_op jit(solution)/shard_map/ppermute | solution.py:35
  278.3 94.3 %collective-permute-start.16 = (bf16[896,1024]{1,0:T(8,128)(2,1)}, bf16[896,1024]{1,0:T(8,128)(2,1)}, u32[]{:S(2)}, u32[]{:S(2)}) collective-permute-start(bf16[896,1024]{1,0:T(8,128)(2,1)} %collective-permute-done.8.refs_10_.refs_5_), channel_id=1, source_target_pairs={{0,4},{4,0},{8,12},{12,8},{16,20},{20,16},{24,28},{28,24},{1,5},{5... | collective-permute-start | bytes 5505032 | tf_op jit(solution)/shard_map/ppermute | solution.py:35
  278.8 87.5 %collective-permute-start.17 = (bf16[448,1024]{1,0:T(8,128)(2,1)}, bf16[448,1024]{1,0:T(8,128)(2,1)}, u32[]{:S(2)}, u32[]{:S(2)}) collective-permute-start(bf16[448,1024]{1,0:T(8,128)(2,1)} %collective-permute-done.9.refs_7_), channel_id=1, source_target_pairs={{0,4},{4,0},{8,12},{12,8},{16,20},{20,16},{24,28},{28,24},{1,5},{5... | collective-permute-start | bytes 2752520 | tf_op jit(solution)/shard_map/ppermute | solution.py:35
  278.9 88.7 %collective-permute-start.18 = (bf16[448,1024]{1,0:T(8,128)(2,1)}, bf16[448,1024]{1,0:T(8,128)(2,1)}, u32[]{:S(2)}, u32[]{:S(2)}) collective-permute-start(bf16[448,1024]{1,0:T(8,128)(2,1)} %collective-permute-done.10.refs_8_), channel_id=1, source_target_pairs={{0,4},{4,0},{8,12},{12,8},{16,20},{20,16},{24,28},{28,24},{1,5},{5... | collective-permute-start | bytes 2752520 | tf_op jit(solution)/shard_map/ppermute | solution.py:35
  360.8 10.4 %copy-start = (bf16[4,448,896]{2,1,0:T(8,128)(2,1)S(1)}, bf16[4,448,896]{2,1,0:T(8,128)(2,1)}, u32[]{:S(2)}) copy-start(bf16[4,448,896]{2,1,0:T(8,128)(2,1)} %all-reduce.6.cloned.1.call-done.mine) | copy-start | bytes 9633796
  364.8 37.3 %collective-permute-start.22 = (bf16[2,448,896]{2,1,0:T(8,128)(2,1)}, bf16[2,448,896]{2,1,0:T(8,128)(2,1)}, u32[]{:S(2)}, u32[]{:S(2)}) collective-permute-start(bf16[2,448,896]{2,1,0:T(8,128)(2,1)} %get-tuple-element.55), channel_id=1, source_target_pairs={{0,8},{4,12},{8,0},{12,4},{16,24},{20,28},{24,16},{28,20},{1,9},{5... | collective-permute-start | bytes 4816904 | tf_op jit(solution)/shard_map/ppermute | solution.py:35
  366.3 21.7 %collective-permute-start.27 = (bf16[1,448,896]{2,1,0:T(8,128)(2,1)}, bf16[1,448,896]{2,1,0:T(8,128)(2,1)}, u32[]{:S(2)}, u32[]{:S(2)}) collective-permute-start(bf16[1,448,896]{2,1,0:T(8,128)(2,1)} %add_convert_fusion), channel_id=1, source_target_pairs={{1,0},{2,3},{5,4},{6,7},{9,8},{10,11},{13,12},{14,15},{17,16},{18,... | collective-permute-start | bytes 2408456 | tf_op jit(solution)/shard_map/ppermute | solution.py:318
  367.6 42.1 %collective-permute-start.20 = (bf16[2,448,896]{2,1,0:T(8,128)(2,1)}, bf16[2,448,896]{2,1,0:T(8,128)(2,1)}, u32[]{:S(2)}, u32[]{:S(2)}) collective-permute-start(bf16[2,448,896]{2,1,0:T(8,128)(2,1)} %get-tuple-element.56), channel_id=1, source_target_pairs={{0,16},{4,20},{8,24},{12,28},{16,0},{20,4},{24,8},{28,12},{1,17},{... | collective-permute-start | bytes 4816904 | tf_op jit(solution)/shard_map/ppermute | solution.py:35
  371.2 21.9 %collective-permute-start.23 = (bf16[1,448,896]{2,1,0:T(8,128)(2,1)}, bf16[1,448,896]{2,1,0:T(8,128)(2,1)}, u32[]{:S(2)}, u32[]{:S(2)}) collective-permute-start(bf16[1,448,896]{2,1,0:T(8,128)(2,1)} %slice_bitcast_fusion.mine), channel_id=1, source_target_pairs={{0,4},{4,0},{8,12},{12,8},{16,20},{20,16},{24,28},{28,24},{1,5},{5... | collective-permute-start | bytes 2408456 | tf_op jit(solution)/shard_map/ppermute | solution.py:35
  372.5 34.4 %collective-permute-start.21 = (bf16[1,448,896]{2,1,0:T(8,128)(2,1)}, bf16[1,448,896]{2,1,0:T(8,128)(2,1)}, u32[]{:S(2)}, u32[]{:S(2)}) collective-permute-start(bf16[1,448,896]{2,1,0:T(8,128)(2,1)} %get-tuple-element.57), channel_id=1, source_target_pairs={{0,4},{4,0},{8,12},{12,8},{16,20},{20,16},{24,28},{28,24},{1,5},{5... | collective-permute-start | bytes 2408456 | tf_op jit(solution)/shard_map/ppermute | solution.py:35
  388.0 24.1 %collective-permute-start.19 = (bf16[1,448,896]{2,1,0:T(8,128)(2,1)}, bf16[1,448,896]{2,1,0:T(8,128)(2,1)}, u32[]{:S(2)}, u32[]{:S(2)}) collective-permute-start(bf16[1,448,896]{2,1,0:T(8,128)(2,1)} %get-tuple-element.58), channel_id=1, source_target_pairs={{0,4},{4,0},{8,12},{12,8},{16,20},{20,16},{24,28},{28,24},{1,5},{5... | collective-permute-start | bytes 2408456 | tf_op jit(solution)/shard_map/ppermute | solution.py:35
  388.1 165.2 %all-gather.6.cloned.1.call-start = ((), (), s32[]{:S(2)}) async-start(), calls=%async_computation.10 | async-start | bytes 16515072 | tf_op jit(solution)/shard_map/all_gather | solution.py:421
  388.1 1.6 copy-start.5
  393.2 39.3 %collective-permute-start.28 = (bf16[1,448,896]{2,1,0:T(8,128)(2,1)}, bf16[1,448,896]{2,1,0:T(8,128)(2,1)}, u32[]{:S(2)}, u32[]{:S(2)}) collective-permute-start(bf16[1,448,896]{2,1,0:T(8,128)(2,1)} %broadcast_select_fusion), channel_id=1, source_target_pairs={{0,4},{4,0},{8,12},{12,8},{16,20},{20,16},{24,28},{28,24},{1,5},{5... | collective-permute-start | bytes 2408456 | tf_op jit(solution)/shard_map/ppermute | solution.py:35
  402.2 30.3 %collective-permute-start.29 = (bf16[1,448,896]{2,1,0:T(8,128)(2,1)}, bf16[1,448,896]{2,1,0:T(8,128)(2,1)}, u32[]{:S(2)}, u32[]{:S(2)}) collective-permute-start(bf16[1,448,896]{2,1,0:T(8,128)(2,1)} %broadcast_select_fusion), channel_id=1, source_target_pairs={{0,24},{4,28},{8,16},{12,20},{16,8},{20,12},{24,0},{28,4},{1,25},{... | collective-permute-start | bytes 2408456 | tf_op jit(solution)/shard_map/ppermute | solution.py:35
  430.1 20.8 %copy-start.8 = (bf16[1,448,896]{2,1,0:T(8,128)(2,1)S(1)}, bf16[1,448,896]{2,1,0:T(8,128)(2,1)}, u32[]{:S(2)}) copy-start(bf16[1,448,896]{2,1,0:T(8,128)(2,1)} %all-reduce.8.cloned.1.call-done.mine) | copy-start | bytes 2408452
  430.1 20.8 %collective-permute-start.24 = (bf16[1,448,896]{2,1,0:T(8,128)(2,1)}, bf16[1,448,896]{2,1,0:T(8,128)(2,1)S(1)}, u32[]{:S(2)}, u32[]{:S(2)}) collective-permute-start(bf16[1,448,896]{2,1,0:T(8,128)(2,1)} %all-reduce.8.cloned.1.call-done.mine), channel_id=1, source_target_pairs={{0,24},{4,28},{8,16},{12,20},{16,8},{20,12},{24,0},{28,4},{1,25},{... | collective-permute-start | bytes 2408456 | tf_op jit(solution)/shard_map/ppermute | solution.py:35
  452.4 20.3 %copy-start.21 = (bf16[896,768]{1,0:T(8,128)(2,1)S(1)}, bf16[896,768]{1,0:T(8,128)(2,1)}, u32[]{:S(2)}) copy-start(bf16[896,768]{1,0:T(8,128)(2,1)} %copy-done.20) | copy-start | bytes 4128772
  452.4 21.0 %copy-start.10 = (bf16[448,768]{1,0:T(8,128)(2,1)S(1)}, bf16[448,768]{1,0:T(8,128)(2,1)}, u32[]{:S(2)}) copy-start(bf16[448,768]{1,0:T(8,128)(2,1)} %copy-done.9) | copy-start | bytes 2064388
  472.7 9.7 %copy-start.4 = (bf16[4,224,768]{2,1,0:T(8,128)(2,1)S(1)}, bf16[4,224,768]{2,1,0:T(8,128)(2,1)}, u32[]{:S(2)}) copy-start(bf16[4,224,768]{2,1,0:T(8,128)(2,1)} %copy-done.3) | copy-start | bytes 4128772
  472.7 150.5 %all-gather.4.cloned.1.call-start = ((), (), s32[]{:S(2)}) async-start(), calls=%async_computation.9 | async-start | bytes 12386304 | tf_op jit(solution)/shard_map/all_gather | solution.py:421
  472.8 7.3 %collective-permute-start.30 = (bf16[896,768]{1,0:T(8,128)(2,1)S(1)}, bf16[896,768]{1,0:T(8,128)(2,1)S(1)}, u32[]{:S(2)}, u32[]{:S(2)}) collective-permute-start(bf16[896,768]{1,0:T(8,128)(2,1)S(1)} %copy-done.21), channel_id=1, source_target_pairs={{0,4},{4,0},{8,12},{12,8},{16,20},{20,16},{24,28},{28,24},{1,5},{5... | collective-permute-start | bytes 4128776 | tf_op jit(solution)/shard_map/ppermute | solution.py:35
  472.8 7.3 %collective-permute-start.31 = (bf16[896,768]{1,0:T(8,128)(2,1)}, bf16[896,768]{1,0:T(8,128)(2,1)S(1)}, u32[]{:S(2)}, u32[]{:S(2)}) collective-permute-start(bf16[896,768]{1,0:T(8,128)(2,1)} %collective-permute-done.1.refs_9_.refs_5_), channel_id=1, source_target_pairs={{0,4},{4,0},{8,12},{12,8},{16,20},{20,16},{24,28},{28,24},{1,5},{5... | collective-permute-start | bytes 4128776 | tf_op jit(solution)/shard_map/ppermute | solution.py:35
  473.3 6.8 collective-permute-start.32
  473.4 6.7 collective-permute-start.33
  498.3 54.9 %copy-start.2 = (bf16[4,224,1024]{2,1,0:T(8,128)(2,1)S(1)}, bf16[4,224,1024]{2,1,0:T(8,128)(2,1)}, u32[]{:S(2)}) copy-start(bf16[4,224,1024]{2,1,0:T(8,128)(2,1)} %copy-done.1) | copy-start | bytes 5505028
  498.3 177.9 %all-gather.8.cloned.1.call-start = ((), (), s32[]{:S(2)}) async-start(), calls=%async_computation.11 | async-start | bytes 8257536 | tf_op jit(solution)/shard_map/all_gather | solution.py:421
  498.4 5.4 collective-permute-start.34
  498.6 5.2 collective-permute-start.35
  498.9 4.1 collective-permute-start.36
  499.1 4.6 collective-permute-start.37
  621.7 1.2 copy-start.15
  674.8 1.7 copy-start.7
  676.5 37.4 %copy-start.18 = (bf16[4,224,768]{2,1,0:T(8,128)(2,1)S(1)}, bf16[4,224,768]{2,1,0:T(8,128)(2,1)}, u32[]{:S(2)}) copy-start(bf16[4,224,768]{2,1,0:T(8,128)(2,1)} %copy-done.17) | copy-start | bytes 4128772
  689.0 24.8 %copy-start.16 = (bf16[4,224,1024]{2,1,0:T(8,128)(2,1)S(1)}, bf16[4,224,1024]{2,1,0:T(8,128)(2,1)}, u32[]{:S(2)}) copy-start(bf16[4,224,1024]{2,1,0:T(8,128)(2,1)} %copy-done.15) | copy-start | bytes 5505028
  (9 other events, 9.4 us)
Sparse Core Ops, SparseCore 0:
  133.8 84.0 all-reduce.3
  220.4 140.3 all-reduce.5
  388.2 41.8 all-reduce.7
  472.8 80.3 all-gather.5
  555.0 65.4 all-gather.3
  622.2 49.9 all-gather.7
